TPU v7x, 32 devices: a whole 2x2x4 slice. The times are simulated.
32 devices in a mesh: rep: 8 (over y, x, core), shard: 4 (over z).
Axes of the slice: x: 2, y: 2, z: 4, core: 2. Of those that a mesh axis runs over, the one named last changes fastest.
Arguments:
- tokens: bfloat16 [16384, 576], P(('rep', 'shard')), may hold values from -6 to 6
- lengths: int32 [32, 4], P(('rep', 'shard')), may hold values from 0 to 512, as said below
- gain_attn: bfloat16 [576], P('shard'), may hold values from 0.099609375 to 1.8984375
- w_query: bfloat16 [576, 576], P('shard'), may hold values from -0.25 to 0.25
- w_key: bfloat16 [576, 192], P('shard'), may hold values from -0.25 to 0.25
- w_value: bfloat16 [576, 192], P('shard'), may hold values from -0.25 to 0.25
- w_out: bfloat16 [576, 576], P('shard'), may hold values from -0.75 to 0.75
- gain_mlp: bfloat16 [576], P('shard'), may hold values from 0.099609375 to 1.8984375
- w_gate: bfloat16 [576, 1536], P('shard'), may hold values from -0.25 to 0.25
- w_up: bfloat16 [576, 1536], P('shard'), may hold values from -0.25 to 0.25
- w_down: bfloat16 [1536, 576], P('shard'), may hold values from -0.15625 to 0.15625
- cotangent: bfloat16 [16384, 576], P(('rep', 'shard')), may hold values from -6 to 6
Outputs:
- output: bfloat16 [16384, 576], P(('rep', 'shard'))
- grad_tokens: bfloat16 [16384, 576], P(('rep', 'shard'))
- grad_gain_attn: float32 [576], P('shard')
- grad_w_query: float32 [576, 576], P('shard')
- grad_w_key: float32 [576, 192], P('shard')
- grad_w_value: float32 [576, 192], P('shard')
- grad_w_out: float32 [576, 576], P('shard')
- grad_gain_mlp: float32 [576], P('shard')
- grad_w_gate: float32 [576, 1536], P('shard')
- grad_w_up: float32 [576, 1536], P('shard')
- grad_w_down: float32 [1536, 576], P('shard')
Inputs may be any that keep to these rules, and one draw needn't show every extreme that they name: Each slab's lengths sum to between 128 and 512; lengths may be 0; in every draw some slab holds one sequence of 512 tokens and nothing else.
All inputs are finite; a program needn't handle non-finite values.
Results may differ from a plain program's by a relative error of at most 0.015.
Values may be sent and summed in bfloat16 or wider, within the bound.
No kernel may reach another device: no remote copies, remote signals or barrier semaphores. Data moves between devices by JAX's collectives and lax.ppermute only.
A program may use at most 128 MiB of HBM per device.

v0:
```python
import functools

import jax
import jax.numpy as jnp
from jax import lax
from jax.experimental import pallas as pl
from jax.experimental.pallas import tpu as pltpu
from jax.sharding import PartitionSpec as P
import numpy as np

HEADS = 9
KV = 3
HD = 64
RATIO = HEADS // KV


norm_eps = 1e-05
rope_base = 100000.0
neg_fill = -1e30

low = jnp.bfloat16
f32 = jnp.float32
QUERY_ROWS = 128


def rotation_tables(places, head_size):
    half = head_size // 2
    freq = np.float32(rope_base) ** (-(np.arange(half, dtype=np.float32) * np.float32(2.0) / head_size))
    angle = np.arange(places, dtype=np.float32)[:, None] * freq.astype(np.float32)[None, :]
    return np.concatenate([np.cos(angle)] * 4, axis=1), np.concatenate([np.sin(angle)] * 4, axis=1)


def matmul(left, right):
    return jnp.dot(left, right, preferred_element_type=f32)


def matmul_left_t(left, right):
    return lax.dot_general(left, right, (((0,), (0,)), ((), ())), preferred_element_type=f32)


def matmul_right_t(left, right):
    return lax.dot_general(left, right, (((1,), (1,)), ((), ())), preferred_element_type=f32)


def flip(value, bit, replicas):
    return lax.ppermute(value, "rep", [(i, i ^ (1 << bit)) for i in range(replicas)])


def shift_from(value, step, shards):
    return lax.ppermute(value, "shard", [((s + step) % shards, s) for s in range(shards)])


def shift_to(value, step, shards):
    return lax.ppermute(value, "shard", [(s, (s + step) % shards) for s in range(shards)])


def add_low(left, right):
    return (left.astype(f32) + right.astype(f32)).astype(low)


def after(value, *others):
    return lax.optimization_barrier((value, *others))[0]


def gather_shards(mine, shards):
    return jnp.stack([shift_from(mine, step, shards) for step in range(1, shards)])


def gather_bit(got, bit, replicas, *later):
    other = flip(got, bit, replicas)
    return jnp.stack([after(got, *later) if later else got, other])


def halve(keep, other, bit, replicas):
    sent = flip(add_low(keep[1], other[1]), bit, replicas)
    return add_low(keep[0], other[0]), sent


def scatter_over_shards(keep, other, shards, replicas):
    parts = [add_low(keep[step], other[step]) for step in range(1, shards)]
    moved = [shift_to(part, step + 1, shards) for step, part in enumerate(parts)]
    total = keep[0].astype(f32) + other[0].astype(f32)
    for part in moved:
        total = total + part.astype(f32)
    total = total.astype(low)
    bit = 3
    while (1 << bit) < replicas:
        total = add_low(total, flip(total, bit, replicas))
        bit += 1
    return total


def spread(total, order, replicas):
    for bit in order[:-1]:
        total = jnp.stack([total, flip(total, bit, replicas)])
    return total, flip(total, order[-1], replicas)


class Copies:
    def __init__(self, sems):
        self.sems = sems
        self.made = []

    def start(self, source, target):
        copy = pltpu.make_async_copy(source, target, self.sems.at[len(self.made)])
        copy.start()
        self.made.append(copy)

    def wait(self, first=0, last=None):
        for copy in self.made[first:last]:
            copy.wait()


def rows_at(start, count, unit=16):
    return pl.ds(pl.multiple_of(start, unit), count)


def relative(bit, rel):
    return 1 - bit if rel else bit


def shard_at(shard, step, shards):
    at = shard + step
    return jnp.where(at >= shards, at - shards, at)


def swap_halves(values):
    lane = lax.broadcasted_iota(jnp.int32, values.shape, 1)
    return jnp.where(
        lane % HD < HD // 2,
        pltpu.roll(values, 2 * HD - HD // 2, 1),
        pltpu.roll(values, HD // 2, 1),
    )


def norm_recip(values):
    return lax.rsqrt(jnp.mean(values * values, axis=-1, keepdims=True) + norm_eps)


def norm_back(values, recip, gain, grad_normed):
    scaled = grad_normed * gain
    inner = jnp.mean(scaled * values, axis=-1, keepdims=True)
    grad_values = recip * scaled - values * (recip * recip * recip * inner)
    grad_gain = jnp.sum(grad_normed * values * recip, axis=0, keepdims=True)
    return (grad_values, grad_gain)


def pack_kernel(
    where_ref,
    w_out,
    w_query,
    w_key,
    w_value,
    both_gains,
    gate,
    up,
    down_t,
    own,
    attn_mine,
    pair_mine,
    down_mine,
    down,
):
    core, x, y, shard = (where_ref[i] for i in range(4))
    block = 2 * core + x
    part = gate.shape[0]
    packed = own.shape[1]
    columns = rows_at(384 * block, 384, 128)
    pair_mine[...] = jnp.where(y == 0, gate[:, columns], up[:, columns])
    own[0:part] = jnp.concatenate([w_out[...], w_query[...], w_key[...], w_value[...]], axis=1)
    row = lax.broadcasted_iota(jnp.int32, (16, part), 0)
    gains = jnp.where(
        row == 0,
        jnp.broadcast_to(both_gains[0:1].astype(f32), row.shape),
        jnp.where(row == 1, jnp.broadcast_to(both_gains[1:2].astype(f32), row.shape), 0.0),
    )
    gains = jnp.concatenate([gains, jnp.zeros((16, packed - part), f32)], axis=1)
    own[part : part + 16] = pltpu.roll(gains, part * shard, 1).astype(low)
    attn_mine[...] = own[rows_at(80 * y, 80), columns]
    down[...] = down_t[...].T
    eighth = down_mine.shape[0]
    down_mine[...] = down[rows_at(eighth * (2 * block + y), eighth), :]


def fold(value):
    rest = value[..., 384:]
    pad = [(0, 0)] * (value.ndim - 1) + [(0, 384 - rest.shape[-1])]
    return jnp.concatenate([value[..., :384], jnp.pad(rest, pad)], axis=-2)


def unfold(value, width):
    half = value.shape[-2] // 2
    return jnp.concatenate([value[..., :half, :], value[..., half:, : width - 384]], axis=-1)


def prepare_kernel(
    lengths,
    tokens_t,
    cotangent_t,
    table_cos,
    table_sin,
    cosine,
    sine,
    bias,
    hidden,
    scaled,
    grad_low,
):
    rows = hidden.shape[0]
    count = lengths.shape[1]
    ends = []
    for i in range(count):
        ends.append(lengths[0, i] + (ends[-1] if ends else 0))
    place = lax.broadcasted_iota(jnp.int32, cosine.shape, 0)
    start_cos = jnp.broadcast_to(table_cos[0:1], cosine.shape)
    start_sin = jnp.broadcast_to(table_sin[0:1], cosine.shape)
    for end in ends:
        start_cos = jnp.where(place >= end, table_cos[pl.ds(end, 1)], start_cos)
        start_sin = jnp.where(place >= end, table_sin[pl.ds(end, 1)], start_sin)
    cos, sin = table_cos[0:rows], table_sin[0:rows]
    cosine[...] = cos * start_cos + sin * start_sin
    signed = sin * start_cos - cos * start_sin
    lane = lax.broadcasted_iota(jnp.int32, cosine.shape, 1)
    sine[...] = jnp.where(lane % HD < HD // 2, -signed, signed)
    query = lax.broadcasted_iota(jnp.int32, bias.shape, 0)
    key = lax.broadcasted_iota(jnp.int32, bias.shape, 1)
    allowed = query >= key
    for end in ends:
        allowed = allowed & ((query < end) | (key >= end))
    bias[...] = jnp.where(allowed, 0.0, neg_fill)
    values = tokens_t[...].T.astype(f32)
    hidden[...] = values
    scaled[...] = values * norm_recip(values)
    wide = lax.broadcasted_iota(jnp.int32, grad_low.shape, 0)
    grad_low[...] = jnp.where(wide < ends[-1], cotangent_t[...].T, jnp.zeros((), low))


def project_kernel(
    shards,
    part,
    where_ref,
    scaled,
    cosine,
    sine,
    own,
    pieces,
    other,
    weights,
    gains,
    normed,
    query,
    keys,
    values,
    sems,
):
    core, x, y, shard = (where_ref[i] for i in range(4))
    width = scaled.shape[1]
    copies = Copies(sems)
    copies.start(own.at[pl.ds(0, part)], weights.at[rows_at(part * shard, part)])
    copies.start(own.at[pl.ds(part, 16)], weights.at[rows_at(width + 16 * shard, 16)])
    for rel_core, source in enumerate((pieces, other)):
        for rel_x in range(2):
            for rel_y in range(2):
                at_y = relative(y, rel_y)
                block = 2 * relative(core, rel_core) + relative(x, rel_x)
                columns = rows_at(384 * block, 384, 128)
                for step in range(1, shards):
                    at = shard_at(shard, step, shards)
                    piece = source.at[rel_x, rel_y, step - 1]
                    copies.start(
                        piece.at[pl.ds(0, 64)], weights.at[rows_at(part * at + 80 * at_y, 64), columns]
                    )
                    last = jnp.where(at_y == 0, part * at + 64, width + 16 * at)
                    copies.start(piece.at[pl.ds(64, 16)], weights.at[rows_at(last, 16), columns])
    copies.wait()
    total = sum(
        weights[width + 16 * s : width + 16 * s + 16, :width].astype(f32) for s in range(shards)
    )
    gains[...] = total[:8]
    n1 = (scaled[...] * total[0:1]).astype(low)
    normed[...] = n1
    for block in range(8):
        start = 512 + 128 * block
        result = matmul(n1, weights[0:width, start : start + 128])
        heads = [2 * block - 1, 2 * block]
        if heads[0] < HEADS + KV:
            turned = result * cosine[...] + swap_halves(result) * sine[...]
        for side, head in enumerate(heads):
            lanes = slice(HD * side, HD * side + HD)
            if head < 0:
                continue
            if head < HEADS:
                query[head] = (turned[:, lanes] * HD**-0.5).astype(low)
            elif head < HEADS + KV:
                keys[head - HEADS] = turned[:, lanes].astype(low)
            else:
                values[head - HEADS - KV] = result[:, lanes].astype(low)


def attend_kernel(kv, bias, query, keys, values, mixed, log_total):
    rows = bias.shape[0]
    for block in range(rows // QUERY_ROWS):
        at = slice(QUERY_ROWS * block, QUERY_ROWS * (block + 1))
        reach = QUERY_ROWS * (block + 1)
        stacked = jnp.concatenate([query[RATIO * kv + i, at] for i in range(RATIO)], axis=0)
        scores = matmul_right_t(stacked, keys[kv, :reach])
        logits = scores.reshape(RATIO, QUERY_ROWS, reach) + bias[at, :reach][None]
        top = jnp.max(logits, axis=-1, keepdims=True)
        expo = jnp.exp(logits - top)
        total = jnp.sum(expo, axis=-1, keepdims=True)
        probs = (expo * (1.0 / total)).astype(low).reshape(RATIO * QUERY_ROWS, reach)
        log_total[:, at] = top + jnp.log(total)
        result = matmul(probs, values[kv, :reach]).astype(low)
        for i in range(RATIO):
            mixed[at, HD * i : HD * i + HD] = result[QUERY_ROWS * i : QUERY_ROWS * (i + 1)]


def attend_last_kernel(
    kv,
    bias,
    query,
    keys,
    values,
    hidden_in,
    gains,
    weights,
    *rest,
):
    before, (mixed, log_total, hidden_one, normed_two) = rest[:kv], rest[kv:]
    attend_kernel(kv, bias, query, keys, values, mixed, log_total)
    width = hidden_in.shape[1]
    every = jnp.concatenate([item[...] for item in before] + [mixed[...]], axis=1)
    hidden = hidden_in[...] + matmul(every, weights[0:width, 0:width])
    hidden_one[...] = hidden
    normed_two[...] = (hidden * norm_recip(hidden) * gains[1:2]).astype(low)


def feed_kernel(
    shards,
    part,
    where_ref,
    hidden_one,
    normed_two,
    gains,
    lengths,
    cotangent,
    own_gate,
    own_up,
    own_down,
    pair_pieces,
    pair_other,
    down_pieces,
    down_other,
    result,
    grad_one,
    grad_gain,
    pair_keep,
    pair_send,
    down_keep,
    down_send,
    pair,
    down,
    hidden,
    grad_gate,
    grad_up,
    grad_pair,
    grad_down,
    sems,
):
    core, x, y, shard = (where_ref[i] for i in range(4))
    width = hidden_one.shape[1]
    down_part = own_down.shape[0]
    eighth = down_part // 8
    copies = Copies(sems)
    copies.start(own_gate, pair.at[0, rows_at(part * shard, part)])
    copies.start(own_up, pair.at[1, rows_at(part * shard, part)])
    for rel_core, source in enumerate((pair_pieces, pair_other)):
        for rel_x in range(2):
            block = 2 * relative(core, rel_core) + relative(x, rel_x)
            columns = rows_at(384 * block, 384, 128)
            for rel_y in range(2):
                at_y = relative(y, rel_y)
                for step in range(1, shards):
                    at = shard_at(shard, step, shards)
                    copies.start(
                        source.at[rel_x, rel_y, step - 1],
                        pair.at[at_y, rows_at(part * at, part), columns],
                    )
    first = len(copies.made)
    copies.start(own_down, down.at[rows_at(down_part * shard, down_part)])
    for rel_core, source in enumerate((down_pieces, down_other)):
        for rel_x in range(2):
            block = 2 * relative(core, rel_core) + relative(x, rel_x)
            for rel_y in range(2):
                place = eighth * (2 * block + relative(y, rel_y))
                for step in range(1, shards):
                    at = shard_at(shard, step, shards)
                    copies.start(
                        source.at[rel_y, rel_x, step - 1],
                        down.at[rows_at(down_part * at + place, eighth)],
                    )
    grad_low = cotangent[...]
    n2 = normed_two[...]
    copies.wait(0, first)
    hidden_width = pair.shape[2]
    for start in range(0, hidden_width, 512):
        at = slice(start, start + 512)
        gate = matmul(n2, pair[0, :, at])
        upward = matmul(n2, pair[1, :, at])
        if start == 0:
            copies.wait(first)
        grad_hidden = matmul_right_t(grad_low, down[at, :])
        sigma = jax.nn.sigmoid(gate)
        active = gate * sigma
        hidden[:, at] = (active * upward).astype(low)
        grad_up[:, at] = (grad_hidden * active).astype(low)
        grad_gate[:, at] = (grad_hidden * upward * (sigma + active * (1.0 - sigma))).astype(low)
    turned = n2.T
    sent = Copies(sems)
    for unit, grads in enumerate((grad_gate, grad_up)):
        for start in range(0, hidden_width, 512):
            at = slice(start, start + 512)
            grad_pair[unit, :, at] = matmul(turned, grads[:, at]).astype(low)
    for start in range(0, hidden_width, 512):
        at = slice(start, start + 512)
        grad_down[at, :] = matmul_left_t(hidden[:, at], grad_low).astype(low)
    for rel_core, (target, down_target) in enumerate(((pair_keep, down_keep), (pair_send, down_send))):
        at_core = relative(core, rel_core)
        for rel_x in range(2):
            at_x = relative(x, rel_x)
            block = 2 * at_core + at_x
            columns = rows_at(384 * block, 384, 128)
            for rel_y in range(2):
                at_y = relative(y, rel_y)
                for step in range(shards):
                    at = shard_at(shard, step, shards)
                    sent.start(
                        grad_pair.at[at_y, rows_at(part * at, part), columns],
                        target.at[rel_x, rel_y, step],
                    )
                    sent.start(
                        grad_down.at[rows_at(down_part * at + eighth * (2 * block + at_y), eighth)],
                        down_target.at[rel_y, rel_x, step],
                    )
    h1 = hidden_one[...]
    total = lengths[0, 0]
    for i in range(1, lengths.shape[1]):
        total = total + lengths[0, i]
    row = lax.broadcasted_iota(jnp.int32, h1.shape, 0)
    summed = h1 + matmul(hidden[...], down[...])
    result[...] = jnp.where(row < total, summed, 0.0).astype(low).T
    grad_normed = matmul_right_t(grad_gate[...], pair[0]) + matmul_right_t(grad_up[...], pair[1])
    grad_from, gain_row = norm_back(h1, norm_recip(h1), gains[1:2], grad_normed)
    grad_one[...] = grad_low.astype(f32) + grad_from
    grad_gain[...] = jnp.broadcast_to(gain_row, grad_gain.shape)
    sent.wait()


def back_heads_kernel(
    kv,
    bias,
    cosine,
    sine,
    weights,
    query,
    keys,
    values,
    mixed,
    log_total,
    grad_one,
    grad_turned,
    grad_values_out,
    grad_out,
    grad_mixed,
    grad_heads,
):
    rows, width = grad_one.shape
    span = RATIO * HD
    da = grad_one[...].astype(low)
    grad_mixed[...] = matmul_right_t(da, weights[span * kv : span * kv + span, 0:width]).astype(low)
    grad_out[...] = matmul_left_t(mixed[...], da).astype(low)
    grad_keys = [None] * (rows // QUERY_ROWS)
    grad_values = [None] * (rows // QUERY_ROWS)
    for block in range(rows // QUERY_ROWS):
        at = slice(QUERY_ROWS * block, QUERY_ROWS * (block + 1))
        reach = QUERY_ROWS * (block + 1)
        stacked = jnp.concatenate([query[RATIO * kv + i, at] for i in range(RATIO)], axis=0)
        grads = jnp.concatenate([grad_mixed[at, HD * i : HD * i + HD] for i in range(RATIO)], axis=0)
        out = jnp.concatenate([mixed[at, HD * i : HD * i + HD] for i in range(RATIO)], axis=0)
        delta = jnp.sum(grads.astype(f32) * out.astype(f32), axis=-1, keepdims=True)
        scores = matmul_right_t(stacked, keys[kv, :reach]).reshape(RATIO, QUERY_ROWS, reach)
        probs = jnp.exp(scores + bias[at, :reach][None] - log_total[:, at]).reshape(-1, reach)
        grad_probs = matmul_right_t(grads, values[kv, :reach])
        grad_scores = (probs * (grad_probs - delta)).astype(low)
        grad_query = matmul(grad_scores, keys[kv, :reach])
        for i in range(RATIO):
            grad_heads[at, HD * i : HD * i + HD] = (
                grad_query[QUERY_ROWS * i : QUERY_ROWS * (i + 1)] * HD**-0.5
            )
        key_part = matmul_left_t(grad_scores, stacked)
        value_part = matmul_left_t(probs.astype(low), grads)
        for j in range(block + 1):
            at_j = slice(QUERY_ROWS * j, QUERY_ROWS * (j + 1))
            if grad_keys[j] is None:
                grad_keys[j], grad_values[j] = key_part[at_j], value_part[at_j]
            else:
                grad_keys[j] = grad_keys[j] + key_part[at_j]
                grad_values[j] = grad_values[j] + value_part[at_j]
    grad_heads[:, span : span + HD] = jnp.concatenate(grad_keys, axis=0)
    grad_values_out[...] = jnp.concatenate(grad_values, axis=0).astype(low)
    for start in range(0, span + HD, 2 * HD):
        value = grad_heads[:, start : start + 2 * HD]
        turned = value * cosine[...] - swap_halves(value) * sine[...]
        grad_turned[:, start : start + 2 * HD] = turned.astype(low)


def back_last_kernel(
    shards,
    part,
    where_ref,
    hidden_in,
    gains,
    weights,
    normed,
    grad_one,
    grad_gain_two,
    *rest,
):
    core, x, y, shard = (where_ref[i] for i in range(4))
    rows, width = hidden_in.shape
    turned, values, outs = rest[0:KV], rest[KV : 2 * KV], rest[2 * KV : 3 * KV]
    grad_tokens, keep, send, grad_low, grad_weights, sems = rest[3 * KV :]
    span = RATIO * HD
    grad_low[...] = jnp.concatenate(
        [jnp.zeros((rows, HD), low)]
        + [item[:, 0:span] for item in turned]
        + [item[:, span : span + HD] for item in turned]
        + [item[...] for item in values],
        axis=1,
    )
    normed_t = normed[...].T
    for start in range(0, 1024, 512):
        at = slice(start, start + 512)
        grad_weights[0:width, 512 + start : 1024 + start] = matmul(normed_t, grad_low[:, at]).astype(low)
    for kv in range(KV):
        grad_weights[span * kv : span * kv + span, 0:width] = outs[kv][...]
    grad_normed = matmul_right_t(grad_low[...], weights[0:width, 512:1536])
    hidden = hidden_in[...]
    grad_from, gain_row = norm_back(hidden, norm_recip(hidden), gains[0:1], grad_normed)
    grad_tokens[...] = (grad_one[...] + grad_from).astype(low).T
    row = lax.broadcasted_iota(jnp.int32, (16, width), 0)
    both = jnp.where(
        row == 0,
        jnp.broadcast_to(gain_row, (16, width)),
        jnp.where(row == 1, jnp.broadcast_to(grad_gain_two[0:1], (16, width)), 0.0),
    )
    grad_weights[width : width + 16, :] = jnp.zeros((16, grad_weights.shape[1]), low)
    grad_weights[width : width + 16, 0:width] = both.astype(low)
    copies = Copies(sems)
    for rel_core, target in enumerate((keep, send)):
        for rel_x in range(2):
            for rel_y in range(2):
                at_y = relative(y, rel_y)
                block = 2 * relative(core, rel_core) + relative(x, rel_x)
                columns = rows_at(384 * block, 384, 128)
                for step in range(shards):
                    at = shard_at(shard, step, shards)
                    piece = target.at[rel_x, rel_y, step]
                    copies.start(
                        grad_weights.at[rows_at(part * at + 80 * at_y, 64), columns],
                        piece.at[pl.ds(0, 64)],
                    )
                    last = jnp.where(at_y == 0, part * at + 64, width)
                    copies.start(grad_weights.at[rows_at(last, 16), columns], piece.at[pl.ds(64, 16)])
    copies.wait()


def finish_kernel(
    where_ref,
    pair_pieces,
    pair_other,
    rest_pieces,
    rest_other,
    out_query,
    out_key,
    out_value,
    out_out,
    out_gains,
    out_gate,
    out_up,
    out_down,
    attn,
    pair,
    down,
    sems,
):
    core, x, y = (where_ref[i] for i in range(3))
    part, width = out_out.shape
    copies = Copies(sems)
    for rel_core, (p_from, r_from) in enumerate(((pair_pieces, rest_pieces), (pair_other, rest_other))):
        for rel_x in range(2):
            for rel_y in range(2):
                at_y = relative(y, rel_y)
                block = 2 * relative(core, rel_core) + relative(x, rel_x)
                columns = rows_at(384 * block, 384, 128)
                piece = r_from.at[rel_y, rel_x]
                copies.start(p_from.at[rel_x, rel_y], pair.at[at_y, :, columns])
                copies.start(piece.at[pl.ds(0, 80)], attn.at[rows_at(80 * at_y, 80), columns])
                copies.start(piece.at[pl.ds(80, down.shape[1])], down.at[2 * block + at_y])
    copies.wait()
    kv_width = out_key.shape[1]
    out_out[...] = attn[0:part, 0:width].astype(f32)
    rest = attn[0:part, 512:].astype(f32)
    at = width - 512
    out_query[...] = rest[:, at : at + width]
    out_key[...] = rest[:, at + width : at + width + kv_width]
    out_value[...] = rest[:, at + width + kv_width :]
    out_gains[...] = attn[part : part + 16, 0:width].astype(f32)[:8]
    out_gate[...] = pair[0].astype(f32)
    out_up[...] = pair[1].astype(f32)
    half = down.shape[1] // 2
    whole = [
        jnp.concatenate([down[i, :half], down[i, half:, : width - 384]], axis=1)
        for i in range(down.shape[0])
    ]
    out_down[...] = jnp.concatenate(whole, axis=0).T.astype(f32)


VM = pl.BlockSpec(memory_space=pltpu.VMEM)
SM = pl.BlockSpec(memory_space=pltpu.SMEM)
HB = pl.BlockSpec(memory_space=pl.ANY)


def shape(sizes, kind):
    return jax.ShapeDtypeStruct(tuple(sizes), kind)


def call(kernel, name, operands, in_specs, out_shape, out_specs, scratch, micros, room):
    moved = sum(item.size * item.dtype.itemsize for item in out_shape)
    return pl.pallas_call(
        kernel,
        name=name,
        in_specs=in_specs,
        out_shape=out_shape,
        out_specs=out_specs,
        scratch_shapes=scratch,
        cost_estimate=pl.CostEstimate(
            flops=int(micros * 1e7), bytes_accessed=moved, transcendentals=0
        ),
        compiler_params=pltpu.CompilerParams(vmem_limit_bytes=room << 20),
    )(*operands)


def local(
    replicas,
    shards,
    tokens,
    lengths,
    gain_attn,
    w_query,
    w_key,
    w_value,
    w_out,
    gain_mlp,
    w_gate,
    w_up,
    w_down,
    cotangent,
):
    rows, width = tokens.shape
    part = w_gate.shape[0]
    hidden_width = w_gate.shape[1]
    down_part = w_down.shape[0]
    eighth = down_part // 8
    packed = 2 * width + 2 * w_key.shape[1]
    rep_index = lax.axis_index("rep")
    shard = lax.axis_index("shard")
    core, x, y = ((rep_index >> bit) & 1 for bit in range(3))
    where = jnp.stack([core, x, y, shard]).astype(jnp.int32)

    own, attn_mine, pair_mine, down_mine, own_down = call(
        pack_kernel,
        "pack",
        (
            where,
            w_out,
            w_query,
            w_key,
            w_value,
            jnp.stack([gain_attn, gain_mlp]),
            w_gate,
            w_up,
            w_down.T,
        ),
        [SM] + [VM] * 8,
        (
            shape((part + 16, packed), low),
            shape((80, 384), low),
            shape((part, 384), low),
            shape((eighth, width), low),
            shape((down_part, width), low),
        ),
        [VM] * 5,
        [],
        2,
        60,
    )
    attn_got = gather_shards(attn_mine, shards)
    table_cos, table_sin = rotation_tables(rows + 8, HD)
    cosine, sine, bias, hidden_in, scaled, grad_low = call(
        prepare_kernel,
        "prepare",
        (lengths, tokens.T, cotangent.T, table_cos, table_sin),
        [SM] + [VM] * 4,
        (
            shape((rows, 2 * HD), f32),
            shape((rows, 2 * HD), f32),
            shape((rows, rows), f32),
            shape((rows, width), f32),
            shape((rows, width), f32),
            shape((rows, width), low),
        ),
        [VM] * 6,
        [],
        5,
        60,
    )
    pair_got = gather_shards(after(pair_mine, scaled), shards)
    down_got = gather_shards(after(down_mine, attn_got), shards)
    attn_got = gather_bit(after(attn_got, scaled), 2, replicas)
    attn_got = gather_bit(after(attn_got, pair_got), 1, replicas)
    attn_other = flip(attn_got, 0, replicas)
    pair_got = gather_bit(pair_got, 2, replicas)
    scaled = after(scaled, down_got)
    weights, gains, normed, query, keys, values = call(
        functools.partial(project_kernel, shards, part),
        "project",
        (where, scaled, cosine, sine, own, attn_got, attn_other),
        [SM, VM, VM, VM, HB, HB, HB],
        (
            shape((width + 16 * shards, packed), low),
            shape((8, width), f32),
            shape((rows, width), low),
            shape((HEADS, rows, HD), low),
            shape((KV, rows, HD), low),
            shape((KV, rows, HD), low),
        ),
        [VM] * 6,
        [pltpu.SemaphoreType.DMA((2 + 16 * (shards - 1),))],
        5,
        24,
    )
    keys = after(keys, pair_got)
    down_got = gather_bit(down_got, 1, replicas, normed)
    mixed, log_total = [], []
    for kv in range(KV):
        outs = [shape((rows, RATIO * HD), low), shape((RATIO, rows, 1), f32)]
        operands = (bias, query, keys, values)
        if kv < KV - 1:
            one, two = call(
                functools.partial(attend_kernel, kv),
                f"attend_{kv}",
                operands,
                [VM] * 4,
                outs,
                [VM] * 2,
                [],
                3,
                24,
            )
        else:
            down_got = gather_bit(down_got, 2, replicas, *mixed)
            operands += (after(hidden_in, down_got), gains, weights, *mixed)
            one, two, hidden_one, normed_two = call(
                functools.partial(attend_last_kernel, kv),
                f"attend_{kv}",
                operands,
                [VM] * len(operands),
                outs + [shape((rows, width), f32), shape((rows, width), low)],
                [VM] * 4,
                [],
                4,
                24,
            )
        mixed.append(one)
        log_total.append(two)
    pair_got = gather_bit(pair_got, 1, replicas, normed_two)
    pair_other = flip(pair_got, 0, replicas)
    down_other = flip(down_got, 0, replicas)
    pair_shape = shape((2, 2, shards, part, 384), low)
    down_shape = shape((2, 2, shards, eighth, width), low)
    result, grad_one, grad_gain_two, pair_keep, pair_send, down_keep, down_send = call(
        functools.partial(feed_kernel, shards, part),
        "feed",
        (
            where,
            hidden_one,
            normed_two,
            gains,
            lengths,
            grad_low,
            w_gate,
            w_up,
            own_down,
            pair_got,
            pair_other,
            down_got,
            down_other,
        ),
        [SM] + [VM] * 3 + [SM, VM] + [HB] * 7,
        (
            shape((width, rows), low),
            shape((rows, width), f32),
            shape((8, width), f32),
            pair_shape,
            pair_shape,
            down_shape,
            down_shape,
        ),
        [VM] * 3 + [HB] * 4,
        [
            pltpu.VMEM((2, shards * part, hidden_width), low),
            pltpu.VMEM((hidden_width, width), low),
            pltpu.VMEM((rows, hidden_width), low),
            pltpu.VMEM((rows, hidden_width), low),
            pltpu.VMEM((rows, hidden_width), low),
            pltpu.VMEM((2, shards * part, hidden_width), low),
            pltpu.VMEM((hidden_width, width), low),
            pltpu.SemaphoreType.DMA((16 * shards + 3,)),
        ],
        19,
        60,
    )
    pair_sent = flip(pair_send, 0, replicas)
    down_sent = flip(down_send, 0, replicas)
    grad_turned, grad_values, grad_out = [], [], []
    for kv in range(KV):
        if kv == 1:
            pair_left = halve(pair_keep, after(pair_sent, grad_turned[0]), 1, replicas)
            down_left = halve(down_keep, after(down_sent, grad_turned[0]), 2, replicas)
            grad_one = after(grad_one, pair_sent, down_sent)
        one, two, three = call(
            functools.partial(back_heads_kernel, kv),
            f"back_{kv}",
            (bias, cosine, sine, weights, query, keys, values, mixed[kv], log_total[kv], grad_one),
            [VM] * 10,
            (
                shape((rows, RATIO * HD + HD), low),
                shape((rows, HD), low),
                shape((RATIO * HD, width), low),
            ),
            [VM] * 3,
            [pltpu.VMEM((rows, RATIO * HD), low), pltpu.VMEM((rows, RATIO * HD + HD), f32)],
            5,
            24,
        )
        grad_turned.append(one)
        grad_values.append(two)
        grad_out.append(three)
    attn_shape = shape((2, 2, shards, 80, 384), low)
    grad_tokens, attn_keep, attn_send = call(
        functools.partial(back_last_kernel, shards, part),
        "back_last",
        (
            where,
            hidden_in,
            gains,
            weights,
            normed,
            grad_one,
            grad_gain_two,
            *grad_turned,
            *grad_values,
            *grad_out,
        ),
        [SM] + [VM] * (6 + 3 * KV),
        (shape((width, rows), low), attn_shape, attn_shape),
        [VM, HB, HB],
        [
            pltpu.VMEM((rows, 1024), low),
            pltpu.VMEM((width + 16, packed), low),
            pltpu.SemaphoreType.DMA((16 * shards,)),
        ],
        6,
        24,
    )
    attn_left = halve(attn_keep, flip(after(attn_send, down_left[1]), 0, replicas), 1, replicas)
    pair_left = halve(*pair_left, 2, replicas)
    down_left = halve(down_left[0], after(down_left[1], grad_tokens), 1, replicas)
    attn_left = halve(*attn_left, 2, replicas)
    feed_left = tuple(
        jnp.concatenate([one, fold(two)], axis=1) for one, two in zip(pair_left, down_left)
    )
    feed_total = scatter_over_shards(*feed_left, shards, replicas)
    attn_total = scatter_over_shards(*attn_left, shards, replicas)
    pair_pieces = spread(feed_total[:part], (2, 1, 0), replicas)
    rest_pieces = spread(jnp.concatenate([attn_total, feed_total[part:]]), (1, 2, 0), replicas)
    g_query, g_key, g_value, g_out, g_gains, g_gate, g_up, g_down = call(
        finish_kernel,
        "finish",
        (where, *pair_pieces, *rest_pieces),
        [SM] + [HB] * 4,
        (
            shape(w_query.shape, f32),
            shape(w_key.shape, f32),
            shape(w_value.shape, f32),
            shape(w_out.shape, f32),
            shape((8, width), f32),
            shape(w_gate.shape, f32),
            shape(w_up.shape, f32),
            shape((width, down_part), f32),
        ),
        [VM] * 8,
        [
            pltpu.VMEM((160, packed), low),
            pltpu.VMEM((2, part, hidden_width), low),
            pltpu.VMEM((8, 2 * eighth, 384), low),
            pltpu.SemaphoreType.DMA((24,)),
        ],
        5,
        60,
    )
    g_gains = lax.dynamic_slice(g_gains, (0, part * shard), (2, part))
    return (
        result.T,
        grad_tokens.T,
        g_gains[0],
        g_query,
        g_key,
        g_value,
        g_out,
        g_gains[1],
        g_gate,
        g_up,
        g_down.T,
    )


def solution(mesh):
    in_specs = (
        P(("rep", "shard"), None),
        P(("rep", "shard"), None),
        P("shard"),
        P("shard", None),
        P("shard", None),
        P("shard", None),
        P("shard", None),
        P("shard"),
        P("shard", None),
        P("shard", None),
        P("shard", None),
        P(("rep", "shard"), None),
    )
    out_specs = (
        P(("rep", "shard"), None),
        P(("rep", "shard"), None),
        P("shard"),
        P("shard", None),
        P("shard", None),
        P("shard", None),
        P("shard", None),
        P("shard"),
        P("shard", None),
        P("shard", None),
        P("shard", None),
    )
    part = functools.partial(local, mesh.shape["rep"], mesh.shape["shard"])
    return jax.shard_map(part, mesh=mesh, in_specs=in_specs, out_specs=out_specs, check_vma=False)
```

profile of v0, /device:TPU:0, one launch (start us, length us, event | category | flops | bytes accessed | tf_op | source)
XLA Modules:
  0.0 194.5 jit_solution(7445990382467678538)
XLA Ops:
  3.2 2.7 %pack.1 = (bf16[160,1536]{1,0:T(8,128)(2,1)}, bf16[80,384]{1,0:T(8,128)(2,1)}, bf16[144,384]{1,0:T(8,128)(2,1)}, bf16[48,576]{1,0:T(8,128)(2,1)}, bf16[384,576]{1,0:T(8,128)(2,1)}) custom-call(s32[4]{0:T(128)} %pad_add_fusion.where_ref, bf16[144,576]{1,0:T(8,128)(2,1)} %w_out.1, bf16[144,576]{1,0:T(8,128)(2,1)} %w_query.1, bf16[144,192]{1,0:T(8,128)(2,1)} %w_key.1, ...), custom_call_target="tpu_custom_call" | custom-call | flops 20000000 | bytes 1161216 | tf_op jit(solution)/shard_map/pack/pallas_call | solution.py:640
  5.9 5.0 %collective-permute-start = (bf16[80,384]{1,0:T(8,128)(2,1)}, bf16[80,384]{1,0:T(8,128)(2,1)S(1)}, u32[]{:S(2)}, u32[]{:S(2)}) collective-permute-start(bf16[80,384]{1,0:T(8,128)(2,1)} %get-tuple-element.81), channel_id=1, source_target_pairs={{1,0},{2,1},{3,2},{0,3},{5,4},{6,5},{7,6},{4,7},{9,8},{10,9},{11,1... | collective-permute-start | bytes 184328 | tf_op jit(solution)/shard_map/ppermute | solution.py:50
  11.0 1.0 collective-permute-start.2
  12.0 3.9 %prepare.1 = (f32[512,128]{1,0:T(8,128)}, f32[512,128]{1,0:T(8,128)}, f32[512,512]{1,0:T(8,128)}, f32[512,576]{1,0:T(8,128)}, f32[512,576]{1,0:T(8,128)}, /*index=5*/bf16[512,576]{1,0:T(8,128)(2,1)}) custom-call(s32[1,4]{1,0:T(1,128)} %lengths.3, bf16[576,512]{1,0:T(8,128)(2,1)} %bitcast.148, bf16[576,512]{1,0:T(8,128)(2,1)} %bitcast.149, ...), custom_call_target="tpu_custom_call" | custom-call | flops 50000000 | bytes 4521984 | tf_op jit(solution)/shard_map/prepare/pallas_call | solution.py:640
  15.9 2.8 %collective-permute-start.7 = (bf16[144,384]{1,0:T(8,128)(2,1)S(1)}, bf16[144,384]{1,0:T(8,128)(2,1)S(1)}, u32[]{:S(2)}, u32[]{:S(2)}) collective-permute-start(bf16[144,384]{1,0:T(8,128)(2,1)S(1)} %copy-done.43), channel_id=1, source_target_pairs={{1,0},{2,1},{3,2},{0,3},{5,4},{6,5},{7,6},{4,7},{9,8},{10,9},{11,1... | collective-permute-start | bytes 331784 | tf_op jit(solution)/shard_map/ppermute | solution.py:50
  18.7 1.1 collective-permute-start.8
  19.9 1.6 collective-permute-start.6
  22.2 6.7 %collective-permute-done.8 = bf16[144,384]{1,0:T(8,128)(2,1)S(1)} collective-permute-done((bf16[144,384]{1,0:T(8,128)(2,1)S(1)}, bf16[144,384]{1,0:T(8,128)(2,1)S(1)}, u32[]{:S(2)}, u32[]{:S(2)}) %collective-permute-start.8) | collective-permute-done | bytes 110624 | tf_op jit(solution)/shard_map/ppermute | solution.py:50
  29.0 1.6 collective-permute-start.10
  30.6 7.5 %collective-permute-done.10 = bf16[2,3,80,384]{3,2,1,0:T(8,128)(2,1)S(1)} collective-permute-done((bf16[2,3,80,384]{3,2,1,0:T(8,128)(2,1)S(1)}, bf16[2,3,80,384]{3,2,1,0:T(8,128)(2,1)S(1)}, u32[]{:S(2)}, u32[]{:S(2)}) %collective-permute-start.10) | collective-permute-done | bytes 368672 | tf_op jit(solution)/shard_map/ppermute | solution.py:46
  38.3 1.6 collective-permute-start.12
  39.9 2.2 %collective-permute-start.4 = (bf16[48,576]{1,0:T(8,128)(2,1)S(1)}, bf16[48,576]{1,0:T(8,128)(2,1)S(1)}, u32[]{:S(2)}, u32[]{:S(2)}) collective-permute-start(bf16[48,576]{1,0:T(8,128)(2,1)S(1)} %copy-done.44), channel_id=1, source_target_pairs={{2,0},{3,1},{0,2},{1,3},{6,4},{7,5},{4,6},{5,7},{10,8},{11,9},{8,1... | collective-permute-start | bytes 165896 | tf_op jit(solution)/shard_map/ppermute | solution.py:50
  42.1 2.0 %collective-permute-start.5 = (bf16[48,576]{1,0:T(8,128)(2,1)S(1)}, bf16[48,576]{1,0:T(8,128)(2,1)S(1)}, u32[]{:S(2)}, u32[]{:S(2)}) collective-permute-start(bf16[48,576]{1,0:T(8,128)(2,1)S(1)} %copy-done.44), channel_id=1, source_target_pairs={{3,0},{0,1},{1,2},{2,3},{7,4},{4,5},{5,6},{6,7},{11,8},{8,9},{9,10... | collective-permute-start | bytes 165896 | tf_op jit(solution)/shard_map/ppermute | solution.py:50
  44.2 4.2 %collective-permute-done.4 = bf16[48,576]{1,0:T(8,128)(2,1)S(1)} collective-permute-done((bf16[48,576]{1,0:T(8,128)(2,1)S(1)}, bf16[48,576]{1,0:T(8,128)(2,1)S(1)}, u32[]{:S(2)}, u32[]{:S(2)}) %collective-permute-start.4) | collective-permute-done | bytes 55328 | tf_op jit(solution)/shard_map/ppermute | solution.py:50
  48.4 1.6 collective-permute-start.13
  50.7 3.9 %project.1 = (bf16[640,1536]{1,0:T(8,128)(2,1)S(1)}, f32[8,576]{1,0:T(8,128)S(1)}, bf16[512,576]{1,0:T(8,128)(2,1)S(1)}, bf16[9,512,64]{2,1,0:T(8,128)(2,1)S(1)}...) custom-call(s32[4]{0:T(128)S(1)} %copy-done.31, f32[512,576]{1,0:T(8,128)S(1)} %copy-done.10, ...), custom_call_target="tpu_custom_call" | custom-call | flops 50000000 | bytes 3557376 | tf_op jit(solution)/shard_map/project/pallas_call | solution.py:640
  54.7 1.4 collective-permute-done.13
  56.7 1.9 attend_1.1
  58.6 0.9 copy-done.16
  59.5 1.9 attend_0.1
  61.4 0.9 copy-done.20
  62.3 1.9 collective-permute-done.14
  64.3 2.7 %attend_2.1 = (bf16[512,192]{1,0:T(8,128)(2,1)S(1)}, f32[3,512,1]{2,1,0:T(8,128)S(1)}, f32[512,576]{1,0:T(8,128)S(1)}, bf16[512,576]{1,0:T(8,128)(2,1)S(1)}) custom-call(f32[512,512]{1,0:T(8,128)S(1)} %copy-done, bf16[9,512,64]{2,1,0:T(8,128)(2,1)S(1)} %get-tuple-element.91.query, bf16[3,512,64]{2,1,0:T(8,128)(2,1)S(1)} %get-tuple-element.93.keys, ...), custom_call_target="tpu_custom_call" | custom-call | flops 40000000 | bytes 1972224 | tf_op jit(solution)/shard_map/attend_2/pallas_call | solution.py:640
  67.0 1.1 copy-done.11
  68.1 0.9 copy-done.18
  69.0 0.9 copy-done.24
  70.7 1.1 copy-done.33
  72.3 3.6 %collective-permute-done.17.down_other = bf16[2,2,3,48,576]{4,3,2,1,0:T(8,128)(2,1)S(1)} collective-permute-done((bf16[2,2,3,48,576]{4,3,2,1,0:T(8,128)(2,1)S(1)}, bf16[2,2,3,48,576]{4,3,2,1,0:T(8,128)(2,1)S(1)}, u32[]{:S(2)}, u32[]{:S(2)}) %collective-permute-start.17) | collective-permute-done | bytes 663584 | tf_op jit(solution)/shard_map/ppermute | solution.py:46
  75.9 1.1 copy-done.38
  77.2 17.6 %feed.1 = (bf16[576,512]{1,0:T(8,128)(2,1)}, f32[512,576]{1,0:T(8,128)}, f32[8,576]{1,0:T(8,128)}, bf16[2,2,4,144,384]{4,3,2,1,0:T(8,128)(2,1)}, bf16[2,2,4,144,...) custom-call(s32[4]{0:T(128)} %pad_add_fusion.where_ref, ...), custom_call_target="tpu_custom_call" | custom-call | flops 190000000 | bytes 7096320 | tf_op jit(solution)/shard_map/feed/pallas_call | solution.py:640
  95.4 1.2 copy-done.1
  96.7 1.3 copy-done.2
  98.0 0.9 copy-done.7
  98.9 0.9 copy-done.9
  99.9 0.9 copy-done.15
  100.8 1.1 copy-done.21
  102.0 2.8 %back_0.1 = (bf16[512,256]{1,0:T(8,128)(2,1)S(1)}, bf16[512,64]{1,0:T(8,128)(2,1)S(1)}, bf16[192,576]{1,0:T(8,128)(2,1)S(1)}) custom-call(f32[512,512]{1,0:T(8,128)S(1)} %copy-done.1, f32[512,128]{1,0:T(8,128)S(1)} %copy-done.7, f32[512,128]{1,0:T(8,128)S(1)} %copy-done.9, bf16[640,1536]{1,0:T(8,128)(2,1)S(1)} %get-tuple-element.103.weights, ...), custom_call_target="tpu_custom_call" | custom-call | flops 50000000 | bytes 548864 | tf_op jit(solution)/shard_map/back_0/pallas_call | solution.py:640
  105.1 1.6 collective-permute-start.21
  107.2 1.2 collective-permute-start.20
  108.4 3.1 %back_1.1 = (bf16[512,256]{1,0:T(8,128)(2,1)S(1)}, bf16[512,64]{1,0:T(8,128)(2,1)S(1)}, bf16[192,576]{1,0:T(8,128)(2,1)S(1)}) custom-call(f32[512,512]{1,0:T(8,128)S(1)} %copy-done.1, f32[512,128]{1,0:T(8,128)S(1)} %copy-done.7, f32[512,128]{1,0:T(8,128)S(1)} %copy-done.9, bf16[640,1536]{1,0:T(8,128)(2,1)S(1)} %get-tuple-element.103.weights, ...), custom_call_target="tpu_custom_call" | custom-call | flops 50000000 | bytes 548864 | tf_op jit(solution)/shard_map/back_1/pallas_call | solution.py:640
  111.6 2.9 %back_2.1 = (bf16[512,256]{1,0:T(8,128)(2,1)S(1)}, bf16[512,64]{1,0:T(8,128)(2,1)S(1)}, bf16[192,576]{1,0:T(8,128)(2,1)S(1)}) custom-call(f32[512,512]{1,0:T(8,128)S(1)} %copy-done.1, f32[512,128]{1,0:T(8,128)S(1)} %copy-done.7, f32[512,128]{1,0:T(8,128)S(1)} %copy-done.9, bf16[640,1536]{1,0:T(8,128)(2,1)S(1)} %get-tuple-element.103.weights, ...), custom_call_target="tpu_custom_call" | custom-call | flops 50000000 | bytes 548864 | tf_op jit(solution)/shard_map/back_2/pallas_call | solution.py:640
  114.5 4.8 %back_last.1 = (bf16[576,512]{1,0:T(8,128)(2,1)}, bf16[2,2,4,80,384]{4,3,2,1,0:T(8,128)(2,1)S(1)}, bf16[2,2,4,80,384]{4,3,2,1,0:T(8,128)(2,1)S(1)}) custom-call(s32[4]{0:T(128)S(1)} %copy-done.32, f32[512,576]{1,0:T(8,128)S(1)} %copy-done.5, f32[8,576]{1,0:T(8,128)S(1)} %copy-done.29, bf16[640,1536]{1,0:T(8,128)(2,1)S(1)} %get-tuple-element.103.weights, ...), custom_call_target="tpu_custom_call" | custom-call | flops 60000000 | bytes 2555904 | tf_op jit(solution)/shard_map/back_last/pallas_call | solution.py:640
  119.4 9.2 %collective-permute-done.20 = bf16[2,4,144,384]{3,2,1,0:T(8,128)(2,1)S(1)} collective-permute-done((bf16[2,4,144,384]{3,2,1,0:T(8,128)(2,1)S(1)}, bf16[2,4,144,384]{3,2,1,0:T(8,128)(2,1)S(1)}, u32[]{:S(2)}, u32[]{:S(2)}) %collective-permute-start.20) | collective-permute-done | bytes 884768 | tf_op jit(solution)/shard_map/ppermute | solution.py:46
  128.9 1.5 collective-permute-start.22
  130.6 0.9 collective-permute-start.31
  131.7 1.2 collective-permute-start.23
  132.9 15.2 %collective-permute-done.23 = bf16[4,48,576]{2,1,0:T(8,128)(2,1)S(1)} collective-permute-done((bf16[4,48,576]{2,1,0:T(8,128)(2,1)S(1)}, bf16[4,48,576]{2,1,0:T(8,128)(2,1)S(1)}, u32[]{:S(2)}, u32[]{:S(2)}) %collective-permute-start.23) | collective-permute-done | bytes 221216 | tf_op jit(solution)/shard_map/ppermute | solution.py:46
  149.3 2.0 %collective-permute-start.25 = (bf16[240,384]{1,0:T(8,128)(2,1)S(1)}, bf16[240,384]{1,0:T(8,128)(2,1)S(1)}, u32[]{:S(2)}, u32[]{:S(2)}) collective-permute-start(bf16[240,384]{1,0:T(8,128)(2,1)S(1)} %get-tuple-element.155), channel_id=1, source_target_pairs={{0,2},{1,3},{2,0},{3,1},{4,6},{5,7},{6,4},{7,5},{8,10},{9,11},{10,... | collective-permute-start | bytes 552968 | tf_op jit(solution)/shard_map/ppermute | solution.py:54
  151.3 2.8 %collective-permute-start.26 = (bf16[240,384]{1,0:T(8,128)(2,1)S(1)}, bf16[240,384]{1,0:T(8,128)(2,1)S(1)}, u32[]{:S(2)}, u32[]{:S(2)}) collective-permute-start(bf16[240,384]{1,0:T(8,128)(2,1)S(1)} %get-tuple-element.154), channel_id=1, source_target_pairs={{0,3},{1,0},{2,1},{3,2},{4,7},{5,4},{6,5},{7,6},{8,11},{9,8},{10,9... | collective-permute-start | bytes 552968 | tf_op jit(solution)/shard_map/ppermute | solution.py:54
  155.1 2.0 %collective-permute-start.34 = (bf16[80,384]{1,0:T(8,128)(2,1)S(1)}, bf16[80,384]{1,0:T(8,128)(2,1)S(1)}, u32[]{:S(2)}, u32[]{:S(2)}) collective-permute-start(bf16[80,384]{1,0:T(8,128)(2,1)S(1)} %get-tuple-element.162), channel_id=1, source_target_pairs={{0,2},{1,3},{2,0},{3,1},{4,6},{5,7},{6,4},{7,5},{8,10},{9,11},{10,... | collective-permute-start | bytes 184328 | tf_op jit(solution)/shard_map/ppermute | solution.py:54
  157.1 1.3 collective-permute-done.24
  158.4 1.5 collective-permute-start.35
  160.0 4.7 %collective-permute-done.25 = bf16[240,384]{1,0:T(8,128)(2,1)S(1)} collective-permute-done((bf16[240,384]{1,0:T(8,128)(2,1)S(1)}, bf16[240,384]{1,0:T(8,128)(2,1)S(1)}, u32[]{:S(2)}, u32[]{:S(2)}) %collective-permute-start.25) | collective-permute-done | bytes 184352 | tf_op jit(solution)/shard_map/ppermute | solution.py:54
  164.8 1.1 collective-permute-done.33
  165.9 5.0 %collective-permute-done.34 = bf16[80,384]{1,0:T(8,128)(2,1)S(1)} collective-permute-done((bf16[80,384]{1,0:T(8,128)(2,1)S(1)}, bf16[80,384]{1,0:T(8,128)(2,1)S(1)}, u32[]{:S(2)}, u32[]{:S(2)}) %collective-permute-start.34) | collective-permute-done | bytes 61472 | tf_op jit(solution)/shard_map/ppermute | solution.py:54
  171.0 1.8 collective-permute-start.36
  172.8 1.0 collective-permute-start.27
  173.7 2.3 %collective-permute-done.36 = bf16[176,384]{1,0:T(8,128)(2,1)S(1)} collective-permute-done((bf16[176,384]{1,0:T(8,128)(2,1)S(1)}, bf16[176,384]{1,0:T(8,128)(2,1)S(1)}, u32[]{:S(2)}, u32[]{:S(2)}) %collective-permute-start.36) | collective-permute-done | bytes 135200 | tf_op jit(solution)/shard_map/ppermute | solution.py:46
  176.1 1.8 collective-permute-start.37
  178.9 3.9 %collective-permute-done.37 = bf16[2,176,384]{2,1,0:T(8,128)(2,1)S(1)} collective-permute-done((bf16[2,176,384]{2,1,0:T(8,128)(2,1)S(1)}, bf16[2,176,384]{2,1,0:T(8,128)(2,1)S(1)}, u32[]{:S(2)}, u32[]{:S(2)}) %collective-permute-start.37) | collective-permute-done | bytes 270368 | tf_op jit(solution)/shard_map/ppermute | solution.py:46
  182.9 1.8 collective-permute-done.28
  184.9 1.8 collective-permute-done.29.pair_other
  188.3 4.4 %finish.1 = (f32[144,576]{1,0:T(8,128)}, f32[144,192]{1,0:T(8,128)}, f32[144,192]{1,0:T(8,128)}, f32[144,576]{1,0:T(8,128)}, f32[8,576]{1,0:T(8,128)}, /*index=5...) custom-call(s32[4]{0:T(128)} %pad_add_fusion.where_ref, bf16[2,2,144,384]{3,2,1,0:T(8,128)(2,1)} %copy-done.36, ...), custom_call_target="tpu_custom_call" | custom-call | flops 50000000 | bytes 3557376 | tf_op jit(solution)/shard_map/finish/pallas_call | solution.py:640
  192.6 1.4 fusion.39
  (153 shorter events, 14.1 us)
Async XLA Ops:
  5.9 9.9 %copy-start.43 = (bf16[144,384]{1,0:T(8,128)(2,1)S(1)}, bf16[144,384]{1,0:T(8,128)(2,1)}, u32[]{:S(2)}) copy-start(bf16[144,384]{1,0:T(8,128)(2,1)} %get-tuple-element.89) | copy-start | bytes 331780
  5.9 13.9 %collective-permute-start = (bf16[80,384]{1,0:T(8,128)(2,1)}, bf16[80,384]{1,0:T(8,128)(2,1)S(1)}, u32[]{:S(2)}, u32[]{:S(2)}) collective-permute-start(bf16[80,384]{1,0:T(8,128)(2,1)} %get-tuple-element.81), channel_id=1, source_target_pairs={{1,0},{2,1},{3,2},{0,3},{5,4},{6,5},{7,6},{4,7},{9,8},{10,9},{11,1... | collective-permute-start | bytes 184328 | tf_op jit(solution)/shard_map/ppermute | solution.py:50
  11.0 8.8 %collective-permute-start.1 = (bf16[80,384]{1,0:T(8,128)(2,1)}, bf16[80,384]{1,0:T(8,128)(2,1)S(1)}, u32[]{:S(2)}, u32[]{:S(2)}) collective-permute-start(bf16[80,384]{1,0:T(8,128)(2,1)} %get-tuple-element.81), channel_id=1, source_target_pairs={{2,0},{3,1},{0,2},{1,3},{6,4},{7,5},{4,6},{5,7},{10,8},{11,9},{8,1... | collective-permute-start | bytes 184328 | tf_op jit(solution)/shard_map/ppermute | solution.py:50
  11.0 8.8 %collective-permute-start.2 = (bf16[80,384]{1,0:T(8,128)(2,1)}, bf16[80,384]{1,0:T(8,128)(2,1)S(1)}, u32[]{:S(2)}, u32[]{:S(2)}) collective-permute-start(bf16[80,384]{1,0:T(8,128)(2,1)} %get-tuple-element.81), channel_id=1, source_target_pairs={{3,0},{0,1},{1,2},{2,3},{7,4},{4,5},{5,6},{6,7},{11,8},{8,9},{9,10... | collective-permute-start | bytes 184328 | tf_op jit(solution)/shard_map/ppermute | solution.py:50
  15.9 6.3 %collective-permute-start.7 = (bf16[144,384]{1,0:T(8,128)(2,1)S(1)}, bf16[144,384]{1,0:T(8,128)(2,1)S(1)}, u32[]{:S(2)}, u32[]{:S(2)}) collective-permute-start(bf16[144,384]{1,0:T(8,128)(2,1)S(1)} %copy-done.43), channel_id=1, source_target_pairs={{1,0},{2,1},{3,2},{0,3},{5,4},{6,5},{7,6},{4,7},{9,8},{10,9},{11,1... | collective-permute-start | bytes 331784 | tf_op jit(solution)/shard_map/ppermute | solution.py:50
  18.7 10.2 %collective-permute-start.8 = (bf16[144,384]{1,0:T(8,128)(2,1)S(1)}, bf16[144,384]{1,0:T(8,128)(2,1)S(1)}, u32[]{:S(2)}, u32[]{:S(2)}) collective-permute-start(bf16[144,384]{1,0:T(8,128)(2,1)S(1)} %copy-done.43), channel_id=1, source_target_pairs={{2,0},{3,1},{0,2},{1,3},{6,4},{7,5},{4,6},{5,7},{10,8},{11,9},{8,1... | collective-permute-start | bytes 331784 | tf_op jit(solution)/shard_map/ppermute | solution.py:50
  19.8 9.1 %collective-permute-start.9 = (bf16[144,384]{1,0:T(8,128)(2,1)S(1)}, bf16[144,384]{1,0:T(8,128)(2,1)S(1)}, u32[]{:S(2)}, u32[]{:S(2)}) collective-permute-start(bf16[144,384]{1,0:T(8,128)(2,1)S(1)} %copy-done.43), channel_id=1, source_target_pairs={{3,0},{0,1},{1,2},{2,3},{7,4},{4,5},{5,6},{6,7},{11,8},{8,9},{9,10... | collective-permute-start | bytes 331784 | tf_op jit(solution)/shard_map/ppermute | solution.py:50
  19.9 9.1 %collective-permute-start.6 = (bf16[3,80,384]{2,1,0:T(8,128)(2,1)S(1)}, bf16[3,80,384]{2,1,0:T(8,128)(2,1)S(1)}, u32[]{:S(2)}, u32[]{:S(2)}) collective-permute-start(bf16[3,80,384]{2,1,0:T(8,128)(2,1)S(1)} %pad_maximum_fusion.11), channel_id=1, source_target_pairs={{0,16},{4,20},{8,24},{12,28},{16,0},{20,4},{24,8},{28,12},{1,17},{... | collective-permute-start | bytes 552968 | tf_op jit(solution)/shard_map/ppermute | solution.py:46
  28.9 11.0 %copy-start.44 = (bf16[48,576]{1,0:T(8,128)(2,1)S(1)}, bf16[48,576]{1,0:T(8,128)(2,1)}, u32[]{:S(2)}) copy-start(bf16[48,576]{1,0:T(8,128)(2,1)} %get-tuple-element.82) | copy-start | bytes 165892
  29.0 9.1 %collective-permute-start.10 = (bf16[2,3,80,384]{3,2,1,0:T(8,128)(2,1)S(1)}, bf16[2,3,80,384]{3,2,1,0:T(8,128)(2,1)S(1)}, u32[]{:S(2)}, u32[]{:S(2)}) collective-permute-start(bf16[2,3,80,384]{3,2,1,0:T(8,128)(2,1)S(1)} %pad_maximum_fusion.6), channel_id=1, source_target_pairs={{0,8},{4,12},{8,0},{12,4},{16,24},{20,28},{24,16},{28,20},{1,9},{5... | collective-permute-start | bytes 1105928 | tf_op jit(solution)/shard_map/ppermute | solution.py:46
  38.1 12.6 %copy-start.6 = (f32[512,128]{1,0:T(8,128)S(1)}, f32[512,128]{1,0:T(8,128)}, u32[]{:S(2)}) copy-start(f32[512,128]{1,0:T(8,128)} %get-tuple-element.84.cosine) | copy-start | bytes 786436
  38.1 12.6 %copy-start.8 = (f32[512,128]{1,0:T(8,128)S(1)}, f32[512,128]{1,0:T(8,128)}, u32[]{:S(2)}) copy-start(f32[512,128]{1,0:T(8,128)} %get-tuple-element.85.sine) | copy-start | bytes 786436
  38.1 12.6 %copy-start.10 = (f32[512,576]{1,0:T(8,128)S(1)}, f32[512,576]{1,0:T(8,128)}, u32[]{:S(2)}) copy-start(f32[512,576]{1,0:T(8,128)} %get-tuple-element.83.scaled) | copy-start | bytes 3538948
  38.1 12.6 %copy-start.25 = (bf16[160,1536]{1,0:T(8,128)(2,1)S(1)}, bf16[160,1536]{1,0:T(8,128)(2,1)}, u32[]{:S(2)}) copy-start(bf16[160,1536]{1,0:T(8,128)(2,1)} %get-tuple-element.86.own) | copy-start | bytes 1474564
  38.1 12.6 %copy-start.31 = (s32[4]{0:T(128)S(1)}, s32[4]{0:T(128)}, u32[]{:S(2)}) copy-start(s32[4]{0:T(128)} %pad_add_fusion.where_ref) | copy-start | bytes 52
  38.2 12.5 %collective-permute-start.11 = (bf16[2,2,3,80,384]{4,3,2,1,0:T(8,128)(2,1)S(1)}, bf16[2,2,3,80,384]{4,3,2,1,0:T(8,128)(2,1)S(1)}, u32[]{:S(2)}, u32[]{:S(2)}) collective-permute-start(bf16[2,2,3,80,384]{4,3,2,1,0:T(8,128)(2,1)S(1)} %pad_maximum_fusion.1.pieces), channel_id=1, source_target_pairs={{0,4},{4,0},{8,12},{12,8},{16,20},{20,16},{24,28},{28,24},{1,5},{5... | collective-permute-start | bytes 2211848 | tf_op jit(solution)/shard_map/ppermute | solution.py:46
  38.3 11.7 %collective-permute-start.12 = (bf16[3,144,384]{2,1,0:T(8,128)(2,1)S(1)}, bf16[3,144,384]{2,1,0:T(8,128)(2,1)S(1)}, u32[]{:S(2)}, u32[]{:S(2)}) collective-permute-start(bf16[3,144,384]{2,1,0:T(8,128)(2,1)S(1)} %get-tuple-element.164), channel_id=1, source_target_pairs={{0,16},{4,20},{8,24},{12,28},{16,0},{20,4},{24,8},{28,12},{1,17},{... | collective-permute-start | bytes 995336 | tf_op jit(solution)/shard_map/ppermute | solution.py:46
  39.9 4.3 %collective-permute-start.3 = (bf16[48,576]{1,0:T(8,128)(2,1)S(1)}, bf16[48,576]{1,0:T(8,128)(2,1)S(1)}, u32[]{:S(2)}, u32[]{:S(2)}) collective-permute-start(bf16[48,576]{1,0:T(8,128)(2,1)S(1)} %copy-done.44), channel_id=1, source_target_pairs={{1,0},{2,1},{3,2},{0,3},{5,4},{6,5},{7,6},{4,7},{9,8},{10,9},{11,1... | collective-permute-start | bytes 165896 | tf_op jit(solution)/shard_map/ppermute | solution.py:50
  39.9 8.5 %collective-permute-start.4 = (bf16[48,576]{1,0:T(8,128)(2,1)S(1)}, bf16[48,576]{1,0:T(8,128)(2,1)S(1)}, u32[]{:S(2)}, u32[]{:S(2)}) collective-permute-start(bf16[48,576]{1,0:T(8,128)(2,1)S(1)} %copy-done.44), channel_id=1, source_target_pairs={{2,0},{3,1},{0,2},{1,3},{6,4},{7,5},{4,6},{5,7},{10,8},{11,9},{8,1... | collective-permute-start | bytes 165896 | tf_op jit(solution)/shard_map/ppermute | solution.py:50
  42.1 6.3 %collective-permute-start.5 = (bf16[48,576]{1,0:T(8,128)(2,1)S(1)}, bf16[48,576]{1,0:T(8,128)(2,1)S(1)}, u32[]{:S(2)}, u32[]{:S(2)}) collective-permute-start(bf16[48,576]{1,0:T(8,128)(2,1)S(1)} %copy-done.44), channel_id=1, source_target_pairs={{3,0},{0,1},{1,2},{2,3},{7,4},{4,5},{5,6},{6,7},{11,8},{8,9},{9,10... | collective-permute-start | bytes 165896 | tf_op jit(solution)/shard_map/ppermute | solution.py:50
  48.4 7.6 %collective-permute-start.13 = (bf16[3,48,576]{2,1,0:T(8,128)(2,1)S(1)}, bf16[3,48,576]{2,1,0:T(8,128)(2,1)S(1)}, u32[]{:S(2)}, u32[]{:S(2)}) collective-permute-start(bf16[3,48,576]{2,1,0:T(8,128)(2,1)S(1)} %pad_maximum_fusion.12), channel_id=1, source_target_pairs={{0,8},{4,12},{8,0},{12,4},{16,24},{20,28},{24,16},{28,20},{1,9},{5... | collective-permute-start | bytes 497672 | tf_op jit(solution)/shard_map/ppermute | solution.py:46
  50.1 20.5 %collective-permute-start.15 = (bf16[2,3,144,384]{3,2,1,0:T(8,128)(2,1)S(1)}, bf16[2,3,144,384]{3,2,1,0:T(8,128)(2,1)S(1)}, u32[]{:S(2)}, u32[]{:S(2)}) collective-permute-start(bf16[2,3,144,384]{3,2,1,0:T(8,128)(2,1)S(1)} %pad_maximum_fusion.3), channel_id=1, source_target_pairs={{0,8},{4,12},{8,0},{12,4},{16,24},{20,28},{24,16},{28,20},{1,9},{5... | collective-permute-start | bytes 1990664 | tf_op jit(solution)/shard_map/ppermute | solution.py:46
  50.7 6.0 %copy-start = (f32[512,512]{1,0:T(8,128)S(1)}, f32[512,512]{1,0:T(8,128)}, u32[]{:S(2)}) copy-start(f32[512,512]{1,0:T(8,128)} %get-tuple-element.78.bias) | copy-start | bytes 3145732
  54.7 4.0 %copy-start.22 = (bf16[512,576]{1,0:T(8,128)(2,1)}, bf16[512,576]{1,0:T(8,128)(2,1)S(1)}, u32[]{:S(2)}) copy-start(bf16[512,576]{1,0:T(8,128)(2,1)S(1)} %get-tuple-element.96.normed) | copy-start | bytes 1769476
  54.7 9.6 %copy-start.28 = (f32[8,576]{1,0:T(8,128)}, f32[8,576]{1,0:T(8,128)S(1)}, u32[]{:S(2)}) copy-start(f32[8,576]{1,0:T(8,128)S(1)} %get-tuple-element.102.gains) | copy-start | bytes 55300
  56.1 8.0 %collective-permute-start.14 = (bf16[2,3,48,576]{3,2,1,0:T(8,128)(2,1)S(1)}, bf16[2,3,48,576]{3,2,1,0:T(8,128)(2,1)S(1)}, u32[]{:S(2)}, u32[]{:S(2)}) collective-permute-start(bf16[2,3,48,576]{3,2,1,0:T(8,128)(2,1)S(1)} %pad_maximum_fusion.7), channel_id=1, source_target_pairs={{0,16},{4,20},{8,24},{12,28},{16,0},{20,4},{24,8},{28,12},{1,17},{... | collective-permute-start | bytes 995336 | tf_op jit(solution)/shard_map/ppermute | solution.py:46
  59.5 4.8 %copy-start.12 = (bf16[512,192]{1,0:T(8,128)(2,1)}, bf16[512,192]{1,0:T(8,128)(2,1)S(1)}, u32[]{:S(2)}) copy-start(bf16[512,192]{1,0:T(8,128)(2,1)S(1)} %get-tuple-element.99.rest_1_.mixed) | copy-start | bytes 589828
  62.3 4.7 %copy-start.14 = (bf16[512,192]{1,0:T(8,128)(2,1)}, bf16[512,192]{1,0:T(8,128)(2,1)S(1)}, u32[]{:S(2)}) copy-start(bf16[512,192]{1,0:T(8,128)(2,1)S(1)} %get-tuple-element.98.rest_0_.mixed) | copy-start | bytes 589828
  62.3 2.0 %copy-start.4 = (f32[512,576]{1,0:T(8,128)S(1)}, f32[512,576]{1,0:T(8,128)}, u32[]{:S(2)}) copy-start(f32[512,576]{1,0:T(8,128)} %get-tuple-element.101.hidden_in) | copy-start | bytes 3538948
  64.3 7.5 %copy-start.34 = (bf16[2,2,3,48,576]{4,3,2,1,0:T(8,128)(2,1)}, bf16[2,2,3,48,576]{4,3,2,1,0:T(8,128)(2,1)S(1)}, u32[]{:S(2)}) copy-start(bf16[2,2,3,48,576]{4,3,2,1,0:T(8,128)(2,1)S(1)} %pad_maximum_fusion.2.down_pieces) | copy-start | bytes 1990660
  71.8 4.1 %collective-permute-start.16 = (bf16[2,2,3,144,384]{4,3,2,1,0:T(8,128)(2,1)S(1)}, bf16[2,2,3,144,384]{4,3,2,1,0:T(8,128)(2,1)S(1)}, u32[]{:S(2)}, u32[]{:S(2)}) collective-permute-start(bf16[2,2,3,144,384]{4,3,2,1,0:T(8,128)(2,1)S(1)} %pad_maximum_fusion.pair_pieces), channel_id=1, source_target_pairs={{0,4},{4,0},{8,12},{12,8},{16,20},{20,16},{24,28},{28,24},{1,5},{5... | collective-permute-start | bytes 3981320 | tf_op jit(solution)/shard_map/ppermute | solution.py:46
  71.8 4.1 %collective-permute-start.17 = (bf16[2,2,3,48,576]{4,3,2,1,0:T(8,128)(2,1)S(1)}, bf16[2,2,3,48,576]{4,3,2,1,0:T(8,128)(2,1)S(1)}, u32[]{:S(2)}, u32[]{:S(2)}) collective-permute-start(bf16[2,2,3,48,576]{4,3,2,1,0:T(8,128)(2,1)S(1)} %pad_maximum_fusion.2.down_pieces), channel_id=1, source_target_pairs={{0,4},{4,0},{8,12},{12,8},{16,20},{20,16},{24,28},{28,24},{1,5},{5... | collective-permute-start | bytes 1990664 | tf_op jit(solution)/shard_map/ppermute | solution.py:46
  94.9 11.8 %collective-permute-start.18 = (bf16[2,2,4,144,384]{4,3,2,1,0:T(8,128)(2,1)}, bf16[2,2,4,144,384]{4,3,2,1,0:T(8,128)(2,1)S(1)}, u32[]{:S(2)}, u32[]{:S(2)}) collective-permute-start(bf16[2,2,4,144,384]{4,3,2,1,0:T(8,128)(2,1)} %get-tuple-element.111), channel_id=1, source_target_pairs={{0,4},{4,0},{8,12},{12,8},{16,20},{20,16},{24,28},{28,24},{1,5},{5... | collective-permute-start | bytes 5308424 | tf_op jit(solution)/shard_map/ppermute | solution.py:46
  95.1 9.8 %collective-permute-start.19 = (bf16[2,2,4,48,576]{4,3,2,1,0:T(8,128)(2,1)}, bf16[2,2,4,48,576]{4,3,2,1,0:T(8,128)(2,1)S(1)}, u32[]{:S(2)}, u32[]{:S(2)}) collective-permute-start(bf16[2,2,4,48,576]{4,3,2,1,0:T(8,128)(2,1)} %get-tuple-element.112), channel_id=1, source_target_pairs={{0,4},{4,0},{8,12},{12,8},{16,20},{20,16},{24,28},{28,24},{1,5},{5... | collective-permute-start | bytes 2654216 | tf_op jit(solution)/shard_map/ppermute | solution.py:46
  102.0 2.9 %copy-start.39 = (bf16[2,2,4,48,576]{4,3,2,1,0:T(8,128)(2,1)S(1)}, bf16[2,2,4,48,576]{4,3,2,1,0:T(8,128)(2,1)}, u32[]{:S(2)}) copy-start(bf16[2,2,4,48,576]{4,3,2,1,0:T(8,128)(2,1)} %get-tuple-element.131) | copy-start | bytes 2654212
  105.1 14.2 %collective-permute-start.21 = (bf16[2,4,48,576]{3,2,1,0:T(8,128)(2,1)S(1)}, bf16[2,4,48,576]{3,2,1,0:T(8,128)(2,1)S(1)}, u32[]{:S(2)}, u32[]{:S(2)}) collective-permute-start(bf16[2,4,48,576]{3,2,1,0:T(8,128)(2,1)S(1)} %get-tuple-element.149), channel_id=1, source_target_pairs={{0,16},{4,20},{8,24},{12,28},{16,0},{20,4},{24,8},{28,12},{1,17},{... | collective-permute-start | bytes 1327112 | tf_op jit(solution)/shard_map/ppermute | solution.py:46
  107.2 21.5 %collective-permute-start.20 = (bf16[2,4,144,384]{3,2,1,0:T(8,128)(2,1)S(1)}, bf16[2,4,144,384]{3,2,1,0:T(8,128)(2,1)S(1)}, u32[]{:S(2)}, u32[]{:S(2)}) collective-permute-start(bf16[2,4,144,384]{3,2,1,0:T(8,128)(2,1)S(1)} %get-tuple-element.146), channel_id=1, source_target_pairs={{0,8},{4,12},{8,0},{12,4},{16,24},{20,28},{24,16},{28,20},{1,9},{5... | collective-permute-start | bytes 2654216 | tf_op jit(solution)/shard_map/ppermute | solution.py:46
  108.4 3.1 %copy-start.19 = (f32[3,512,1]{2,1,0:T(8,128)S(1)}, f32[3,512,1]{2,1,0:T(8,128)}, u32[]{:S(2)}) copy-start(f32[3,512,1]{2,1,0:T(8,128)} %copy-done.18) | copy-start | bytes 18436
  108.4 3.1 %copy-start.27 = (bf16[512,192]{1,0:T(8,128)(2,1)S(1)}, bf16[512,192]{1,0:T(8,128)(2,1)}, u32[]{:S(2)}) copy-start(bf16[512,192]{1,0:T(8,128)(2,1)} %copy-done.26) | copy-start | bytes 589828
  111.5 2.9 %copy-start.3 = (f32[512,576]{1,0:T(8,128)S(1)}, f32[512,576]{1,0:T(8,128)}, u32[]{:S(2)}) copy-start(f32[512,576]{1,0:T(8,128)} %get-tuple-element.113.grad_one) | copy-start | bytes 3538948
  111.5 2.9 %copy-start.5 = (f32[512,576]{1,0:T(8,128)S(1)}, f32[512,576]{1,0:T(8,128)}, u32[]{:S(2)}) copy-start(f32[512,576]{1,0:T(8,128)} %get-tuple-element.101.hidden_in) | copy-start | bytes 3538948
  111.5 2.9 %copy-start.23 = (bf16[512,576]{1,0:T(8,128)(2,1)S(1)}, bf16[512,576]{1,0:T(8,128)(2,1)}, u32[]{:S(2)}) copy-start(bf16[512,576]{1,0:T(8,128)(2,1)} %copy-done.22) | copy-start | bytes 1769476
  111.5 2.9 %copy-start.29 = (f32[8,576]{1,0:T(8,128)S(1)}, f32[8,576]{1,0:T(8,128)}, u32[]{:S(2)}) copy-start(f32[8,576]{1,0:T(8,128)} %copy-done.28) | copy-start | bytes 55300
  111.5 2.9 %copy-start.30 = (f32[8,576]{1,0:T(8,128)S(1)}, f32[8,576]{1,0:T(8,128)}, u32[]{:S(2)}) copy-start(f32[8,576]{1,0:T(8,128)} %get-tuple-element.114.grad_gain_two) | copy-start | bytes 55300
  111.6 2.9 %copy-start.32 = (s32[4]{0:T(128)S(1)}, s32[4]{0:T(128)}, u32[]{:S(2)}) copy-start(s32[4]{0:T(128)} %pad_add_fusion.where_ref) | copy-start | bytes 52
  119.3 11.0 %collective-permute-start.30 = (bf16[2,2,4,80,384]{4,3,2,1,0:T(8,128)(2,1)S(1)}, bf16[2,2,4,80,384]{4,3,2,1,0:T(8,128)(2,1)S(1)}, u32[]{:S(2)}, u32[]{:S(2)}) collective-permute-start(bf16[2,2,4,80,384]{4,3,2,1,0:T(8,128)(2,1)S(1)} %get-tuple-element.136), channel_id=1, source_target_pairs={{0,4},{4,0},{8,12},{12,8},{16,20},{20,16},{24,28},{28,24},{1,5},{5... | collective-permute-start | bytes 2949128 | tf_op jit(solution)/shard_map/ppermute | solution.py:46
  128.9 19.4 %collective-permute-start.22 = (bf16[4,144,384]{2,1,0:T(8,128)(2,1)S(1)}, bf16[4,144,384]{2,1,0:T(8,128)(2,1)S(1)}, u32[]{:S(2)}, u32[]{:S(2)}) collective-permute-start(bf16[4,144,384]{2,1,0:T(8,128)(2,1)S(1)} %get-tuple-element.152), channel_id=1, source_target_pairs={{0,16},{4,20},{8,24},{12,28},{16,0},{20,4},{24,8},{28,12},{1,17},{... | collective-permute-start | bytes 1327112 | tf_op jit(solution)/shard_map/ppermute | solution.py:46
  130.6 17.7 %collective-permute-start.31 = (bf16[2,4,80,384]{3,2,1,0:T(8,128)(2,1)S(1)}, bf16[2,4,80,384]{3,2,1,0:T(8,128)(2,1)S(1)}, u32[]{:S(2)}, u32[]{:S(2)}) collective-permute-start(bf16[2,4,80,384]{3,2,1,0:T(8,128)(2,1)S(1)} %get-tuple-element.148), channel_id=1, source_target_pairs={{0,8},{4,12},{8,0},{12,4},{16,24},{20,28},{24,16},{28,20},{1,9},{5... | collective-permute-start | bytes 1474568 | tf_op jit(solution)/shard_map/ppermute | solution.py:46
  131.7 16.4 %collective-permute-start.23 = (bf16[4,48,576]{2,1,0:T(8,128)(2,1)S(1)}, bf16[4,48,576]{2,1,0:T(8,128)(2,1)S(1)}, u32[]{:S(2)}, u32[]{:S(2)}) collective-permute-start(bf16[4,48,576]{2,1,0:T(8,128)(2,1)S(1)} %get-tuple-element.159), channel_id=1, source_target_pairs={{0,8},{4,12},{8,0},{12,4},{16,24},{20,28},{24,16},{28,20},{1,9},{5... | collective-permute-start | bytes 663560 | tf_op jit(solution)/shard_map/ppermute | solution.py:46
  148.4 6.3 %collective-permute-start.32 = (bf16[4,80,384]{2,1,0:T(8,128)(2,1)S(1)}, bf16[4,80,384]{2,1,0:T(8,128)(2,1)S(1)}, u32[]{:S(2)}, u32[]{:S(2)}) collective-permute-start(bf16[4,80,384]{2,1,0:T(8,128)(2,1)S(1)} %get-tuple-element.157), channel_id=1, source_target_pairs={{0,16},{4,20},{8,24},{12,28},{16,0},{20,4},{24,8},{28,12},{1,17},{... | collective-permute-start | bytes 737288 | tf_op jit(solution)/shard_map/ppermute | solution.py:46
  148.9 9.5 %collective-permute-start.24 = (bf16[240,384]{1,0:T(8,128)(2,1)S(1)}, bf16[240,384]{1,0:T(8,128)(2,1)S(1)}, u32[]{:S(2)}, u32[]{:S(2)}) collective-permute-start(bf16[240,384]{1,0:T(8,128)(2,1)S(1)} %get-tuple-element.153), channel_id=1, source_target_pairs={{0,1},{1,2},{2,3},{3,0},{4,5},{5,6},{6,7},{7,4},{8,9},{9,10},{10,1... | collective-permute-start | bytes 552968 | tf_op jit(solution)/shard_map/ppermute | solution.py:54
  149.3 15.3 %collective-permute-start.25 = (bf16[240,384]{1,0:T(8,128)(2,1)S(1)}, bf16[240,384]{1,0:T(8,128)(2,1)S(1)}, u32[]{:S(2)}, u32[]{:S(2)}) collective-permute-start(bf16[240,384]{1,0:T(8,128)(2,1)S(1)} %get-tuple-element.155), channel_id=1, source_target_pairs={{0,2},{1,3},{2,0},{3,1},{4,6},{5,7},{6,4},{7,5},{8,10},{9,11},{10,... | collective-permute-start | bytes 552968 | tf_op jit(solution)/shard_map/ppermute | solution.py:54
  151.3 13.3 %collective-permute-start.26 = (bf16[240,384]{1,0:T(8,128)(2,1)S(1)}, bf16[240,384]{1,0:T(8,128)(2,1)S(1)}, u32[]{:S(2)}, u32[]{:S(2)}) collective-permute-start(bf16[240,384]{1,0:T(8,128)(2,1)S(1)} %get-tuple-element.154), channel_id=1, source_target_pairs={{0,3},{1,0},{2,1},{3,2},{4,7},{5,4},{6,5},{7,6},{8,11},{9,8},{10,9... | collective-permute-start | bytes 552968 | tf_op jit(solution)/shard_map/ppermute | solution.py:54
  154.8 11.1 %collective-permute-start.33 = (bf16[80,384]{1,0:T(8,128)(2,1)S(1)}, bf16[80,384]{1,0:T(8,128)(2,1)S(1)}, u32[]{:S(2)}, u32[]{:S(2)}) collective-permute-start(bf16[80,384]{1,0:T(8,128)(2,1)S(1)} %get-tuple-element.160), channel_id=1, source_target_pairs={{0,1},{1,2},{2,3},{3,0},{4,5},{5,6},{6,7},{7,4},{8,9},{9,10},{10,1... | collective-permute-start | bytes 184328 | tf_op jit(solution)/shard_map/ppermute | solution.py:54
  155.1 15.8 %collective-permute-start.34 = (bf16[80,384]{1,0:T(8,128)(2,1)S(1)}, bf16[80,384]{1,0:T(8,128)(2,1)S(1)}, u32[]{:S(2)}, u32[]{:S(2)}) collective-permute-start(bf16[80,384]{1,0:T(8,128)(2,1)S(1)} %get-tuple-element.162), channel_id=1, source_target_pairs={{0,2},{1,3},{2,0},{3,1},{4,6},{5,7},{6,4},{7,5},{8,10},{9,11},{10,... | collective-permute-start | bytes 184328 | tf_op jit(solution)/shard_map/ppermute | solution.py:54
  158.4 12.4 %collective-permute-start.35 = (bf16[80,384]{1,0:T(8,128)(2,1)S(1)}, bf16[80,384]{1,0:T(8,128)(2,1)S(1)}, u32[]{:S(2)}, u32[]{:S(2)}) collective-permute-start(bf16[80,384]{1,0:T(8,128)(2,1)S(1)} %get-tuple-element.161), channel_id=1, source_target_pairs={{0,3},{1,0},{2,1},{3,2},{4,7},{5,4},{6,5},{7,6},{8,11},{9,8},{10,9... | collective-permute-start | bytes 184328 | tf_op jit(solution)/shard_map/ppermute | solution.py:54
  171.0 5.1 %collective-permute-start.36 = (bf16[176,384]{1,0:T(8,128)(2,1)S(1)}, bf16[176,384]{1,0:T(8,128)(2,1)S(1)}, u32[]{:S(2)}, u32[]{:S(2)}) collective-permute-start(bf16[176,384]{1,0:T(8,128)(2,1)S(1)} %get-tuple-element.172), channel_id=1, source_target_pairs={{0,8},{4,12},{8,0},{12,4},{16,24},{20,28},{24,16},{28,20},{1,9},{5... | collective-permute-start | bytes 405512 | tf_op jit(solution)/shard_map/ppermute | solution.py:46
  172.8 5.9 %collective-permute-start.27 = (bf16[144,384]{1,0:T(8,128)(2,1)S(1)}, bf16[144,384]{1,0:T(8,128)(2,1)S(1)}, u32[]{:S(2)}, u32[]{:S(2)}) collective-permute-start(bf16[144,384]{1,0:T(8,128)(2,1)S(1)} %get-tuple-element.170), channel_id=1, source_target_pairs={{0,16},{4,20},{8,24},{12,28},{16,0},{20,4},{24,8},{28,12},{1,17},{... | collective-permute-start | bytes 331784 | tf_op jit(solution)/shard_map/ppermute | solution.py:46
  176.1 6.7 %collective-permute-start.37 = (bf16[2,176,384]{2,1,0:T(8,128)(2,1)S(1)}, bf16[2,176,384]{2,1,0:T(8,128)(2,1)S(1)}, u32[]{:S(2)}, u32[]{:S(2)}) collective-permute-start(bf16[2,176,384]{2,1,0:T(8,128)(2,1)S(1)} %get-tuple-element.166), channel_id=1, source_target_pairs={{0,16},{4,20},{8,24},{12,28},{16,0},{20,4},{24,8},{28,12},{1,17},{... | collective-permute-start | bytes 811016 | tf_op jit(solution)/shard_map/ppermute | solution.py:46
  178.8 6.0 %collective-permute-start.28 = (bf16[2,144,384]{2,1,0:T(8,128)(2,1)S(1)}, bf16[2,144,384]{2,1,0:T(8,128)(2,1)S(1)}, u32[]{:S(2)}, u32[]{:S(2)}) collective-permute-start(bf16[2,144,384]{2,1,0:T(8,128)(2,1)S(1)} %get-tuple-element.168), channel_id=1, source_target_pairs={{0,8},{4,12},{8,0},{12,4},{16,24},{20,28},{24,16},{28,20},{1,9},{5... | collective-permute-start | bytes 663560 | tf_op jit(solution)/shard_map/ppermute | solution.py:46
  182.8 3.9 %copy-start.35 = (bf16[2,2,176,384]{3,2,1,0:T(8,128)(2,1)}, bf16[2,2,176,384]{3,2,1,0:T(8,128)(2,1)S(1)}, u32[]{:S(2)}) copy-start(bf16[2,2,176,384]{3,2,1,0:T(8,128)(2,1)S(1)} %pad_maximum_fusion.4.rest_pieces) | copy-start | bytes 1622020
  182.8 3.8 %collective-permute-start.38 = (bf16[2,2,176,384]{3,2,1,0:T(8,128)(2,1)S(1)}, bf16[2,2,176,384]{3,2,1,0:T(8,128)(2,1)S(1)}, u32[]{:S(2)}, u32[]{:S(2)}) collective-permute-start(bf16[2,2,176,384]{3,2,1,0:T(8,128)(2,1)S(1)} %pad_maximum_fusion.4.rest_pieces), channel_id=1, source_target_pairs={{0,4},{4,0},{8,12},{12,8},{16,20},{20,16},{24,28},{28,24},{1,5},{5... | collective-permute-start | bytes 1622024 | tf_op jit(solution)/shard_map/ppermute | solution.py:46
  184.8 1.9 copy-start.36
  184.8 1.9 collective-permute-start.29
  (20 other events, 22.1 us)
where the time goes:
time: 198 us; the launch traced here: 195 us
  waiting for transfers between devices  73.8 us (37%)
  Pallas kernels  52.6 us (27%)
  starting transfers between devices  43.6 us (22%)
  local copies, waits for them, and re-layouts  18.7 us (9%)
  other arithmetic  4.04 us (2%)
    pallas_call x12, Pallas kernels, call(): pl.pallas_call(kernel, name=name, in_specs=in_specs, out_shape=out_shape,...  52.6 us
    ppermute x24, waiting for transfers between devices, flip(): lax.ppermute(value, 'rep', [(i, i ^ 1 << bit) for i in range(replicas)])  50 us
    ppermute x24, starting transfers between devices, flip(): lax.ppermute(value, 'rep', [(i, i ^ 1 << bit) for i in range(replicas)])  20.3 us
    unnamed x90, local copies, waits for them, and re-layouts  15.8 us
    ppermute x9, starting transfers between devices, shift_from(): lax.ppermute(value, 'shard', [((s + step) % shards, s) for s in range(sha...  14.2 us
    ppermute x6, waiting for transfers between devices, shift_to(): lax.ppermute(value, 'shard', [(s, (s + step) % shards) for s in range(sha...  12.1 us
    ppermute x9, waiting for transfers between devices, shift_from(): lax.ppermute(value, 'shard', [((s + step) % shards, s) for s in range(sha...  11.7 us
    ppermute x6, starting transfers between devices, shift_to(): lax.ppermute(value, 'shard', [(s, (s + step) % shards) for s in range(sha...  9.1 us
  transfers between devices with their start and end apart: 39, of which 20 were waited for; matrix products, arithmetic and copies ran while one was open for 1% of the time, Pallas kernels for 14%

commit v1 on v0

--- a/solution.py
+++ b/solution.py
@@ -186,11 +186,6 @@
     rest = value[..., 384:]
     pad = [(0, 0)] * (value.ndim - 1) + [(0, 384 - rest.shape[-1])]
     return jnp.concatenate([value[..., :384], jnp.pad(rest, pad)], axis=-2)
-
-
-def unfold(value, width):
-    half = value.shape[-2] // 2
-    return jnp.concatenate([value[..., :half, :], value[..., half:, : width - 384]], axis=-1)
 
 
 def prepare_kernel(
@@ -297,20 +292,20 @@
                 values[head - HEADS - KV] = result[:, lanes].astype(low)
 
 
-def attend_kernel(kv, bias, query, keys, values, mixed, log_total):
+def attend_kernel(bias, query, keys, values, mixed, log_total):
     rows = bias.shape[0]
     for block in range(rows // QUERY_ROWS):
         at = slice(QUERY_ROWS * block, QUERY_ROWS * (block + 1))
         reach = QUERY_ROWS * (block + 1)
-        stacked = jnp.concatenate([query[RATIO * kv + i, at] for i in range(RATIO)], axis=0)
-        scores = matmul_right_t(stacked, keys[kv, :reach])
+        stacked = jnp.concatenate([query[i, at] for i in range(RATIO)], axis=0)
+        scores = matmul_right_t(stacked, keys[0, :reach])
         logits = scores.reshape(RATIO, QUERY_ROWS, reach) + bias[at, :reach][None]
         top = jnp.max(logits, axis=-1, keepdims=True)
         expo = jnp.exp(logits - top)
         total = jnp.sum(expo, axis=-1, keepdims=True)
         probs = (expo * (1.0 / total)).astype(low).reshape(RATIO * QUERY_ROWS, reach)
         log_total[:, at] = top + jnp.log(total)
-        result = matmul(probs, values[kv, :reach]).astype(low)
+        result = matmul(probs, values[0, :reach]).astype(low)
         for i in range(RATIO):
             mixed[at, HD * i : HD * i + HD] = result[QUERY_ROWS * i : QUERY_ROWS * (i + 1)]
 
@@ -327,7 +322,7 @@
     *rest,
 ):
     before, (mixed, log_total, hidden_one, normed_two) = rest[:kv], rest[kv:]
-    attend_kernel(kv, bias, query, keys, values, mixed, log_total)
+    attend_kernel(bias, query, keys, values, mixed, log_total)
     width = hidden_in.shape[1]
     every = jnp.concatenate([item[...] for item in before] + [mixed[...]], axis=1)
     hidden = hidden_in[...] + matmul(every, weights[0:width, 0:width])
@@ -457,7 +452,6 @@
 
 
 def back_heads_kernel(
-    kv,
     bias,
     cosine,
     sine,
@@ -477,22 +471,22 @@
     rows, width = grad_one.shape
     span = RATIO * HD
     da = grad_one[...].astype(low)
-    grad_mixed[...] = matmul_right_t(da, weights[span * kv : span * kv + span, 0:width]).astype(low)
+    grad_mixed[...] = matmul_right_t(da, weights[:, 0:width]).astype(low)
     grad_out[...] = matmul_left_t(mixed[...], da).astype(low)
     grad_keys = [None] * (rows // QUERY_ROWS)
     grad_values = [None] * (rows // QUERY_ROWS)
     for block in range(rows // QUERY_ROWS):
         at = slice(QUERY_ROWS * block, QUERY_ROWS * (block + 1))
         reach = QUERY_ROWS * (block + 1)
-        stacked = jnp.concatenate([query[RATIO * kv + i, at] for i in range(RATIO)], axis=0)
+        stacked = jnp.concatenate([query[i, at] for i in range(RATIO)], axis=0)
         grads = jnp.concatenate([grad_mixed[at, HD * i : HD * i + HD] for i in range(RATIO)], axis=0)
         out = jnp.concatenate([mixed[at, HD * i : HD * i + HD] for i in range(RATIO)], axis=0)
         delta = jnp.sum(grads.astype(f32) * out.astype(f32), axis=-1, keepdims=True)
-        scores = matmul_right_t(stacked, keys[kv, :reach]).reshape(RATIO, QUERY_ROWS, reach)
+        scores = matmul_right_t(stacked, keys[0, :reach]).reshape(RATIO, QUERY_ROWS, reach)
         probs = jnp.exp(scores + bias[at, :reach][None] - log_total[:, at]).reshape(-1, reach)
-        grad_probs = matmul_right_t(grads, values[kv, :reach])
+        grad_probs = matmul_right_t(grads, values[0, :reach])
         grad_scores = (probs * (grad_probs - delta)).astype(low)
-        grad_query = matmul(grad_scores, keys[kv, :reach])
+        grad_query = matmul(grad_scores, keys[0, :reach])
         for i in range(RATIO):
             grad_heads[at, HD * i : HD * i + HD] = (
                 grad_query[QUERY_ROWS * i : QUERY_ROWS * (i + 1)] * HD**-0.5
@@ -520,7 +514,8 @@
     where_ref,
     hidden_in,
     gains,
-    weights,
+    weights_one,
+    weights_two,
     normed,
     grad_one,
     grad_gain_two,
@@ -544,7 +539,8 @@
         grad_weights[0:width, 512 + start : 1024 + start] = matmul(normed_t, grad_low[:, at]).astype(low)
     for kv in range(KV):
         grad_weights[span * kv : span * kv + span, 0:width] = outs[kv][...]
-    grad_normed = matmul_right_t(grad_low[...], weights[0:width, 512:1536])
+    grad_normed = matmul_right_t(grad_low[:, :512], weights_one[...])
+    grad_normed = grad_normed + matmul_right_t(grad_low[:, 512:], weights_two[...])
     hidden = hidden_in[...]
     grad_from, gain_row = norm_back(hidden, norm_recip(hidden), gains[0:1], grad_normed)
     grad_tokens[...] = (grad_one[...] + grad_from).astype(low).T
@@ -565,7 +561,7 @@
                 columns = rows_at(384 * block, 384, 128)
                 for step in range(shards):
                     at = shard_at(shard, step, shards)
-                    piece = target.at[rel_x, rel_y, step]
+                    piece = target.at[rel_y, rel_x, step]
                     copies.start(
                         grad_weights.at[rows_at(part * at + 80 * at_y, 64), columns],
                         piece.at[pl.ds(0, 64)],
@@ -631,14 +627,20 @@
 HB = pl.BlockSpec(memory_space=pl.ANY)
 
 
+def block_of(sizes, *place):
+    return pl.BlockSpec(tuple(sizes), lambda step: place)
+
+
 def shape(sizes, kind):
     return jax.ShapeDtypeStruct(tuple(sizes), kind)
 
 
 def call(kernel, name, operands, in_specs, out_shape, out_specs, scratch, micros, room):
     moved = sum(item.size * item.dtype.itemsize for item in out_shape)
+    blocks = any(spec.block_shape is not None for spec in in_specs)
     return pl.pallas_call(
         kernel,
+        grid=(1,) if blocks else (),
         name=name,
         in_specs=in_specs,
         out_shape=out_shape,
@@ -728,10 +730,10 @@
     pair_got = gather_shards(after(pair_mine, scaled), shards)
     down_got = gather_shards(after(down_mine, attn_got), shards)
     attn_got = gather_bit(after(attn_got, scaled), 2, replicas)
-    attn_got = gather_bit(after(attn_got, pair_got), 1, replicas)
+    attn_got = gather_bit(after(attn_got, pair_got, down_got), 1, replicas)
+    pair_got = gather_bit(pair_got, 2, replicas)
+    attn_got = after(attn_got, pair_got)
     attn_other = flip(attn_got, 0, replicas)
-    pair_got = gather_bit(pair_got, 2, replicas)
-    scaled = after(scaled, down_got)
     weights, gains, normed, query, keys, values = call(
         functools.partial(project_kernel, shards, part),
         "project",
@@ -748,25 +750,30 @@
         [VM] * 6,
         [pltpu.SemaphoreType.DMA((2 + 16 * (shards - 1),))],
         5,
-        24,
-    )
-    keys = after(keys, pair_got)
+        60,
+    )
     down_got = gather_bit(down_got, 1, replicas, normed)
     mixed, log_total = [], []
     for kv in range(KV):
         outs = [shape((rows, RATIO * HD), low), shape((RATIO, rows, 1), f32)]
         operands = (bias, query, keys, values)
+        head_blocks = [
+            VM,
+            block_of((RATIO, rows, HD), kv, 0, 0),
+            block_of((1, rows, HD), kv, 0, 0),
+            block_of((1, rows, HD), kv, 0, 0),
+        ]
         if kv < KV - 1:
             one, two = call(
-                functools.partial(attend_kernel, kv),
+                attend_kernel,
                 f"attend_{kv}",
                 operands,
-                [VM] * 4,
+                head_blocks,
                 outs,
                 [VM] * 2,
                 [],
                 3,
-                24,
+                60,
             )
         else:
             down_got = gather_bit(down_got, 2, replicas, *mixed)
@@ -775,12 +782,12 @@
                 functools.partial(attend_last_kernel, kv),
                 f"attend_{kv}",
                 operands,
-                [VM] * len(operands),
+                head_blocks + [VM, VM, block_of((width, 640), 0, 0)] + [VM] * kv,
                 outs + [shape((rows, width), f32), shape((rows, width), low)],
                 [VM] * 4,
                 [],
                 4,
-                24,
+                60,
             )
         mixed.append(one)
         log_total.append(two)
@@ -840,10 +847,21 @@
             down_left = halve(down_keep, after(down_sent, grad_turned[0]), 2, replicas)
             grad_one = after(grad_one, pair_sent, down_sent)
         one, two, three = call(
-            functools.partial(back_heads_kernel, kv),
+            back_heads_kernel,
             f"back_{kv}",
             (bias, cosine, sine, weights, query, keys, values, mixed[kv], log_total[kv], grad_one),
-            [VM] * 10,
+            [
+                VM,
+                VM,
+                VM,
+                block_of((RATIO * HD, 640), kv, 0),
+                block_of((RATIO, rows, HD), kv, 0, 0),
+                block_of((1, rows, HD), kv, 0, 0),
+                block_of((1, rows, HD), kv, 0, 0),
+                VM,
+                VM,
+                VM,
+            ],
             (
                 shape((rows, RATIO * HD + HD), low),
                 shape((rows, HD), low),
@@ -852,7 +870,7 @@
             [VM] * 3,
             [pltpu.VMEM((rows, RATIO * HD), low), pltpu.VMEM((rows, RATIO * HD + HD), f32)],
             5,
-            24,
+            60,
         )
         grad_turned.append(one)
         grad_values.append(two)
@@ -866,6 +884,7 @@
             hidden_in,
             gains,
             weights,
+            weights,
             normed,
             grad_one,
             grad_gain_two,
@@ -873,7 +892,8 @@
             *grad_values,
             *grad_out,
         ),
-        [SM] + [VM] * (6 + 3 * KV),
+        [SM, VM, VM, block_of((width, 512), 0, 1), block_of((width, 512), 0, 2)]
+        + [VM] * (3 + 3 * KV),
         (shape((width, rows), low), attn_shape, attn_shape),
         [VM, HB, HB],
         [
@@ -882,19 +902,17 @@
             pltpu.SemaphoreType.DMA((16 * shards,)),
         ],
         6,
-        24,
-    )
-    attn_left = halve(attn_keep, flip(after(attn_send, down_left[1]), 0, replicas), 1, replicas)
+        60,
+    )
+    attn_left = halve(attn_keep, flip(after(attn_send, down_left[1], pair_left[1]), 0, replicas), 2, replicas)
     pair_left = halve(*pair_left, 2, replicas)
     down_left = halve(down_left[0], after(down_left[1], grad_tokens), 1, replicas)
-    attn_left = halve(*attn_left, 2, replicas)
-    feed_left = tuple(
-        jnp.concatenate([one, fold(two)], axis=1) for one, two in zip(pair_left, down_left)
-    )
-    feed_total = scatter_over_shards(*feed_left, shards, replicas)
+    attn_left = halve(*attn_left, 1, replicas)
+    down_total = scatter_over_shards(*down_left, shards, replicas)
+    pair_total = scatter_over_shards(*pair_left, shards, replicas)
     attn_total = scatter_over_shards(*attn_left, shards, replicas)
-    pair_pieces = spread(feed_total[:part], (2, 1, 0), replicas)
-    rest_pieces = spread(jnp.concatenate([attn_total, feed_total[part:]]), (1, 2, 0), replicas)
+    pair_pieces = spread(pair_total, (2, 1, 0), replicas)
+    rest_pieces = spread(jnp.concatenate([attn_total, fold(down_total)]), (1, 2, 0), replicas)
     g_query, g_key, g_value, g_out, g_gains, g_gate, g_up, g_down = call(
         finish_kernel,
         "finish",

time: 198 us -> 197 us (level)
  waiting for transfers between devices: 73.8 us -> 50.6 us
  Pallas kernels: 52.6 us -> 75.7 us
  local copies, waits for them, and re-layouts: 18.7 us -> 6.6 us
  starting transfers between devices: 43.6 us -> 52 us
  other arithmetic: 4.04 us -> 7.49 us
    pallas_call x12, Pallas kernels: 52.6 us -> 75.7 us  [call(): pl.pallas_call(kernel, grid=(1,) if blocks else (), name=name, in_specs=i...]
    unnamed x90 -> x26, local copies, waits for them, and re-layouts: 15.8 us -> 3.84 us
    ppermute x9, waiting for transfers between devices: 11.7 us -> 1.68 us  [shift_from(): lax.ppermute(value, 'shard', [((s + step) % shards, s) for s in range(sha...]
    ppermute x24, waiting for transfers between devices: 50 us -> 42.6 us  [flip(): lax.ppermute(value, 'rep', [(i, i ^ 1 << bit) for i in range(replicas)])]
    ppermute x9, starting transfers between devices: 14.2 us -> 21.4 us  [shift_from(): lax.ppermute(value, 'shard', [((s + step) % shards, s) for s in range(sha...]
    ppermute x6 -> x9, waiting for transfers between devices: 12.1 us -> 6.32 us  [shift_to(): lax.ppermute(value, 'shard', [(s, (s + step) % shards) for s in range(sha...]
    convert_element_type x8 -> x9, other arithmetic: 1.6 us -> 5.19 us  [add_low(): return (left.astype(f32) + right.astype(f32)).astype(low)]
    ppermute x6 -> x9, starting transfers between devices: 9.1 us -> 11.8 us  [shift_to(): lax.ppermute(value, 'shard', [(s, (s + step) % shards) for s in range(sha...]
  transfers between devices with their start and end apart: 39 -> 42, of which waited for: 20 -> 20; matrix products, arithmetic and copies ran while one was open for 1% -> 2% of each run, Pallas kernels for 14% -> 26%
where the time goes in v1:
time: 197 us; the launch traced here: 194 us
  Pallas kernels  75.7 us (38%)
  starting transfers between devices  52 us (26%)
  waiting for transfers between devices  50.6 us (26%)
  other arithmetic  7.49 us (4%)
  local copies, waits for them, and re-layouts  6.6 us (3%)
    pallas_call x12, Pallas kernels, call(): pl.pallas_call(kernel, grid=(1,) if blocks else (), name=name, in_specs=i...  75.7 us
    ppermute x24, waiting for transfers between devices, flip(): lax.ppermute(value, 'rep', [(i, i ^ 1 << bit) for i in range(replicas)])  42.6 us
    ppermute x9, starting transfers between devices, shift_from(): lax.ppermute(value, 'shard', [((s + step) % shards, s) for s in range(sha...  21.4 us
    ppermute x24, starting transfers between devices, flip(): lax.ppermute(value, 'rep', [(i, i ^ 1 << bit) for i in range(replicas)])  18.8 us
    ppermute x9, starting transfers between devices, shift_to(): lax.ppermute(value, 'shard', [(s, (s + step) % shards) for s in range(sha...  11.8 us
    ppermute x9, waiting for transfers between devices, shift_to(): lax.ppermute(value, 'shard', [(s, (s + step) % shards) for s in range(sha...  6.32 us
    convert_element_type x9, other arithmetic, add_low(): return (left.astype(f32) + right.astype(f32)).astype(low)  5.19 us
  transfers between devices with their start and end apart: 42, of which 20 were waited for; matrix products, arithmetic and copies ran while one was open for 2% of the time, Pallas kernels for 26%

profile of v1, /device:TPU:0, one launch (start us, length us, event | category | flops | bytes accessed | tf_op | source)
XLA Modules:
  0.0 193.9 jit_solution(11345120331170625974)
XLA Ops:
  0.7 0.7 stack.155
  1.3 0.7 stack.156
  2.0 0.6 pad_maximum_fusion.13.both_gains
  2.5 0.7 pad_add_fusion.where_ref
  3.2 2.7 %pack.1 = (bf16[160,1536]{1,0:T(8,128)(2,1)}, bf16[80,384]{1,0:T(8,128)(2,1)}, bf16[144,384]{1,0:T(8,128)(2,1)}, bf16[48,576]{1,0:T(8,128)(2,1)}, bf16[384,576]{1,0:T(8,128)(2,1)}) custom-call(s32[4]{0:T(128)} %pad_add_fusion.where_ref, bf16[144,576]{1,0:T(8,128)(2,1)} %w_out.1, bf16[144,576]{1,0:T(8,128)(2,1)} %w_query.1, bf16[144,192]{1,0:T(8,128)(2,1)} %w_key.1, ...), custom_call_target="tpu_custom_call" | custom-call | flops 20000000 | bytes 1161216 | tf_op jit(solution)/shard_map/pack/pallas_call | solution.py:641
  5.9 5.0 %collective-permute-start = (bf16[80,384]{1,0:T(8,128)(2,1)}, bf16[80,384]{1,0:T(8,128)(2,1)S(1)}, u32[]{:S(2)}, u32[]{:S(2)}) collective-permute-start(bf16[80,384]{1,0:T(8,128)(2,1)} %get-tuple-element.82), channel_id=1, source_target_pairs={{1,0},{2,1},{3,2},{0,3},{5,4},{6,5},{7,6},{4,7},{9,8},{10,9},{11,1... | collective-permute-start | bytes 184328 | tf_op jit(solution)/shard_map/ppermute | solution.py:50
  11.0 1.0 collective-permute-start.2
  12.0 3.9 %prepare.1 = (f32[512,128]{1,0:T(8,128)}, f32[512,128]{1,0:T(8,128)}, f32[512,512]{1,0:T(8,128)}, f32[512,576]{1,0:T(8,128)}, f32[512,576]{1,0:T(8,128)}, /*index=5*/bf16[512,576]{1,0:T(8,128)(2,1)}) custom-call(s32[1,4]{1,0:T(1,128)} %lengths.3, bf16[576,512]{1,0:T(8,128)(2,1)} %bitcast.201, bf16[576,512]{1,0:T(8,128)(2,1)} %bitcast.202, ...), custom_call_target="tpu_custom_call" | custom-call | flops 50000000 | bytes 4521984 | tf_op jit(solution)/shard_map/prepare/pallas_call | solution.py:641
  15.8 2.8 %collective-permute-start.4 = (bf16[144,384]{1,0:T(8,128)(2,1)}, bf16[144,384]{1,0:T(8,128)(2,1)S(1)}, u32[]{:S(2)}, u32[]{:S(2)}) collective-permute-start(bf16[144,384]{1,0:T(8,128)(2,1)} %get-tuple-element.85), channel_id=1, source_target_pairs={{1,0},{2,1},{3,2},{0,3},{5,4},{6,5},{7,6},{4,7},{9,8},{10,9},{11,1... | collective-permute-start | bytes 331784 | tf_op jit(solution)/shard_map/ppermute | solution.py:50
  18.7 1.1 collective-permute-start.5
  19.9 3.9 %collective-permute-start.7 = (bf16[48,576]{1,0:T(8,128)(2,1)S(1)}, bf16[48,576]{1,0:T(8,128)(2,1)S(1)}, u32[]{:S(2)}, u32[]{:S(2)}) collective-permute-start(bf16[48,576]{1,0:T(8,128)(2,1)S(1)} %copy-done.12), channel_id=1, source_target_pairs={{1,0},{2,1},{3,2},{0,3},{5,4},{6,5},{7,6},{4,7},{9,8},{10,9},{11,1... | collective-permute-start | bytes 165896 | tf_op jit(solution)/shard_map/ppermute | solution.py:50
  23.7 7.5 %collective-permute-start.9 = (bf16[48,576]{1,0:T(8,128)(2,1)S(1)}, bf16[48,576]{1,0:T(8,128)(2,1)S(1)}, u32[]{:S(2)}, u32[]{:S(2)}) collective-permute-start(bf16[48,576]{1,0:T(8,128)(2,1)S(1)} %copy-done.12), channel_id=1, source_target_pairs={{3,0},{0,1},{1,2},{2,3},{7,4},{4,5},{5,6},{6,7},{11,8},{8,9},{9,10... | collective-permute-start | bytes 165896 | tf_op jit(solution)/shard_map/ppermute | solution.py:50
  31.2 1.7 collective-permute-done.5
  32.9 1.5 collective-permute-start.3
  35.1 5.4 %collective-permute-done.3 = bf16[3,80,384]{2,1,0:T(8,128)(2,1)S(1)} collective-permute-done((bf16[3,80,384]{2,1,0:T(8,128)(2,1)S(1)}, bf16[3,80,384]{2,1,0:T(8,128)(2,1)S(1)}, u32[]{:S(2)}, u32[]{:S(2)}) %collective-permute-start.3) | collective-permute-done | bytes 184352 | tf_op jit(solution)/shard_map/ppermute | solution.py:46
  40.5 1.6 collective-permute-start.10
  42.1 2.1 %collective-permute-done.11 = bf16[3,144,384]{2,1,0:T(8,128)(2,1)S(1)} collective-permute-done((bf16[3,144,384]{2,1,0:T(8,128)(2,1)S(1)}, bf16[3,144,384]{2,1,0:T(8,128)(2,1)S(1)}, u32[]{:S(2)}, u32[]{:S(2)}) %collective-permute-start.11) | collective-permute-done | bytes 331808 | tf_op jit(solution)/shard_map/ppermute | solution.py:46
  44.2 3.9 %collective-permute-done.10 = bf16[2,3,80,384]{3,2,1,0:T(8,128)(2,1)S(1)} collective-permute-done((bf16[2,3,80,384]{3,2,1,0:T(8,128)(2,1)S(1)}, bf16[2,3,80,384]{3,2,1,0:T(8,128)(2,1)S(1)}, u32[]{:S(2)}, u32[]{:S(2)}) %collective-permute-start.10) | collective-permute-done | bytes 368672 | tf_op jit(solution)/shard_map/ppermute | solution.py:46
  48.3 1.6 collective-permute-start.13
  50.5 0.9 copy-done.8
  51.3 6.1 %project.1 = (bf16[640,1536]{1,0:T(8,128)(2,1)}, f32[8,576]{1,0:T(8,128)}, bf16[512,576]{1,0:T(8,128)(2,1)}, bf16[9,512,64]{2,1,0:T(8,128)(2,1)}, bf16[3,512,64]...) custom-call(s32[4]{0:T(128)} %pad_add_fusion.where_ref, f32[512,576]{1,0:T(8,128)} %get-tuple-element.78.scaled, ...), custom_call_target="tpu_custom_call" | custom-call | flops 50000000 | bytes 3557376 | tf_op jit(solution)/shard_map/project/pallas_call | solution.py:641
  57.5 1.6 collective-permute-start.14
  59.1 4.1 %attend_1.1 = (bf16[512,192]{1,0:T(8,128)(2,1)}, f32[3,512,1]{2,1,0:T(8,128)}) custom-call(f32[512,512]{1,0:T(8,128)} %get-tuple-element.77.bias, bf16[9,512,64]{2,1,0:T(8,128)(2,1)} %get-tuple-element.90.query, bf16[3,512,64]{2,1,0:T(8,128)(2,1)} %get-tuple-element.91.keys, bf16[3,512,64]{2,1,0:T(8,128)(2,1)} %get-tuple-element.92.values), custom_call_target="tpu_custom_call" | custom-call | flops 30000000 | bytes 202752 | tf_op jit(solution)/shard_map/attend_1/pallas_call | solution.py:641
  63.3 4.1 %attend_0.1 = (bf16[512,192]{1,0:T(8,128)(2,1)}, f32[3,512,1]{2,1,0:T(8,128)}) custom-call(f32[512,512]{1,0:T(8,128)} %get-tuple-element.77.bias, bf16[9,512,64]{2,1,0:T(8,128)(2,1)} %get-tuple-element.90.query, bf16[3,512,64]{2,1,0:T(8,128)(2,1)} %get-tuple-element.91.keys, bf16[3,512,64]{2,1,0:T(8,128)(2,1)} %get-tuple-element.92.values), custom_call_target="tpu_custom_call" | custom-call | flops 30000000 | bytes 202752 | tf_op jit(solution)/shard_map/attend_0/pallas_call | solution.py:641
  67.4 0.9 collective-permute-done.14
  68.4 6.3 %attend_2.1 = (bf16[512,192]{1,0:T(8,128)(2,1)}, f32[3,512,1]{2,1,0:T(8,128)}, f32[512,576]{1,0:T(8,128)}, bf16[512,576]{1,0:T(8,128)(2,1)}) custom-call(f32[512,512]{1,0:T(8,128)} %get-tuple-element.77.bias, bf16[9,512,64]{2,1,0:T(8,128)(2,1)} %get-tuple-element.90.query, bf16[3,512,64]{2,1,0:T(8,128)(2,1)} %get-tuple-element.91.keys, ...), custom_call_target="tpu_custom_call" | custom-call | flops 40000000 | bytes 1972224 | tf_op jit(solution)/shard_map/attend_2/pallas_call | solution.py:641
  75.4 3.6 %collective-permute-done.17.down_other = bf16[2,2,3,48,576]{4,3,2,1,0:T(8,128)(2,1)S(1)} collective-permute-done((bf16[2,2,3,48,576]{4,3,2,1,0:T(8,128)(2,1)S(1)}, bf16[2,2,3,48,576]{4,3,2,1,0:T(8,128)(2,1)S(1)}, u32[]{:S(2)}, u32[]{:S(2)}) %collective-permute-start.17) | collective-permute-done | bytes 663584 | tf_op jit(solution)/shard_map/ppermute | solution.py:46
  79.0 0.9 copy-done.9
  80.4 17.7 %feed.1 = (bf16[576,512]{1,0:T(8,128)(2,1)}, f32[512,576]{1,0:T(8,128)}, f32[8,576]{1,0:T(8,128)}, bf16[2,2,4,144,384]{4,3,2,1,0:T(8,128)(2,1)}, bf16[2,2,4,144,...) custom-call(s32[4]{0:T(128)} %pad_add_fusion.where_ref, ...), custom_call_target="tpu_custom_call" | custom-call | flops 190000000 | bytes 7096320 | tf_op jit(solution)/shard_map/feed/pallas_call | solution.py:641
  98.6 6.2 %back_0.1 = (bf16[512,256]{1,0:T(8,128)(2,1)}, bf16[512,64]{1,0:T(8,128)(2,1)}, bf16[192,576]{1,0:T(8,128)(2,1)}) custom-call(f32[512,512]{1,0:T(8,128)} %get-tuple-element.77.bias, f32[512,128]{1,0:T(8,128)} %get-tuple-element.79.cosine, f32[512,128]{1,0:T(8,128)} %get-tuple-element.80.sine, ...), custom_call_target="tpu_custom_call" | custom-call | flops 50000000 | bytes 548864 | tf_op jit(solution)/shard_map/back_0/pallas_call | solution.py:641
  104.8 2.9 %add_convert_fusion.1 = (bf16[1,2,4,144,384]{4,3,2,1,0:T(8,128)(2,1)S(1)}, bf16[2,4,144,384]{3,2,1,0:T(8,128)(2,1)}) fusion(bf16[2,2,4,144,384]{4,3,2,1,0:T(8,128)(2,1)} %collective-permute-done.18, bf16[2,2,4,144,384]{4,3,2,1,0:T(8,128)(2,1)S(1)} %copy-done.5), kind=kLoop, calls=%fused_computation.1 | loop fusion | flops 3538944 | bytes 5308416 | tf_op jit(solution)/shard_map/convert_element_type | solution.py:58
  107.7 1.5 collective-permute-start.20
  109.4 1.6 collective-permute-start.28
  111.0 6.4 %back_1.1 = (bf16[512,256]{1,0:T(8,128)(2,1)}, bf16[512,64]{1,0:T(8,128)(2,1)}, bf16[192,576]{1,0:T(8,128)(2,1)}) custom-call(f32[512,512]{1,0:T(8,128)} %get-tuple-element.77.bias, f32[512,128]{1,0:T(8,128)} %get-tuple-element.79.cosine, f32[512,128]{1,0:T(8,128)} %get-tuple-element.80.sine, ...), custom_call_target="tpu_custom_call" | custom-call | flops 50000000 | bytes 548864 | tf_op jit(solution)/shard_map/back_1/pallas_call | solution.py:641
  117.4 6.1 %back_2.1 = (bf16[512,256]{1,0:T(8,128)(2,1)}, bf16[512,64]{1,0:T(8,128)(2,1)}, bf16[192,576]{1,0:T(8,128)(2,1)}) custom-call(f32[512,512]{1,0:T(8,128)} %get-tuple-element.77.bias, f32[512,128]{1,0:T(8,128)} %get-tuple-element.79.cosine, f32[512,128]{1,0:T(8,128)} %get-tuple-element.80.sine, ...), custom_call_target="tpu_custom_call" | custom-call | flops 50000000 | bytes 548864 | tf_op jit(solution)/shard_map/back_2/pallas_call | solution.py:641
  123.5 7.8 %back_last.1 = (bf16[576,512]{1,0:T(8,128)(2,1)}, bf16[2,2,4,80,384]{4,3,2,1,0:T(8,128)(2,1)}, bf16[2,2,4,80,384]{4,3,2,1,0:T(8,128)(2,1)}) custom-call(s32[4]{0:T(128)} %pad_add_fusion.where_ref, f32[512,576]{1,0:T(8,128)} %get-tuple-element.99.hidden_in, f32[8,576]{1,0:T(8,128)} %get-tuple-element.100.gains, ...), custom_call_target="tpu_custom_call" | custom-call | flops 60000000 | bytes 2555904 | tf_op jit(solution)/shard_map/back_last/pallas_call | solution.py:641
  131.4 2.8 %collective-permute-done.29 = bf16[2,2,4,80,384]{4,3,2,1,0:T(8,128)(2,1)S(1)} collective-permute-done((bf16[2,2,4,80,384]{4,3,2,1,0:T(8,128)(2,1)}, bf16[2,2,4,80,384]{4,3,2,1,0:T(8,128)(2,1)S(1)}, u32[]{:S(2)}, u32[]{:S(2)}) %collective-permute-start.29) | collective-permute-done | bytes 983072 | tf_op jit(solution)/shard_map/ppermute | solution.py:46
  134.2 1.4 add_convert_fusion.4
  135.6 0.6 collective-permute-start.30
  136.3 0.8 collective-permute-start.35
  137.1 7.0 %collective-permute-done.35 = bf16[4,48,576]{2,1,0:T(8,128)(2,1)S(1)} collective-permute-done((bf16[4,48,576]{2,1,0:T(8,128)(2,1)S(1)}, bf16[4,48,576]{2,1,0:T(8,128)(2,1)S(1)}, u32[]{:S(2)}, u32[]{:S(2)}) %collective-permute-start.35) | collective-permute-done | bytes 221216 | tf_op jit(solution)/shard_map/ppermute | solution.py:46
  144.3 3.7 %collective-permute-start.38 = (bf16[48,576]{1,0:T(8,128)(2,1)S(1)}, bf16[48,576]{1,0:T(8,128)(2,1)S(1)}, u32[]{:S(2)}, u32[]{:S(2)}) collective-permute-start(bf16[48,576]{1,0:T(8,128)(2,1)S(1)} %get-tuple-element.162), channel_id=1, source_target_pairs={{0,3},{1,0},{2,1},{3,2},{4,7},{5,4},{6,5},{7,6},{8,11},{9,8},{10,9... | collective-permute-start | bytes 165896 | tf_op jit(solution)/shard_map/ppermute | solution.py:54
  148.0 0.9 collective-permute-done.30
  149.1 0.6 collective-permute-start.31
  149.9 0.7 collective-permute-start.21
  150.6 0.7 collective-permute-done.37
  151.4 4.9 %collective-permute-done.31 = bf16[4,80,384]{2,1,0:T(8,128)(2,1)S(1)} collective-permute-done((bf16[4,80,384]{2,1,0:T(8,128)(2,1)S(1)}, bf16[4,80,384]{2,1,0:T(8,128)(2,1)S(1)}, u32[]{:S(2)}, u32[]{:S(2)}) %collective-permute-start.31) | collective-permute-done | bytes 245792 | tf_op jit(solution)/shard_map/ppermute | solution.py:46
  156.6 3.6 %collective-permute-start.34 = (bf16[80,384]{1,0:T(8,128)(2,1)S(1)}, bf16[80,384]{1,0:T(8,128)(2,1)S(1)}, u32[]{:S(2)}, u32[]{:S(2)}) collective-permute-start(bf16[80,384]{1,0:T(8,128)(2,1)S(1)} %get-tuple-element.159), channel_id=1, source_target_pairs={{0,3},{1,0},{2,1},{3,2},{4,7},{5,4},{6,5},{7,6},{8,11},{9,8},{10,9... | collective-permute-start | bytes 184328 | tf_op jit(solution)/shard_map/ppermute | solution.py:54
  160.2 0.8 collective-permute-done.21
  161.2 1.3 collective-permute-start.23
  162.5 2.8 %collective-permute-start.24 = (bf16[144,384]{1,0:T(8,128)(2,1)S(1)}, bf16[144,384]{1,0:T(8,128)(2,1)S(1)}, u32[]{:S(2)}, u32[]{:S(2)}) collective-permute-start(bf16[144,384]{1,0:T(8,128)(2,1)S(1)} %get-tuple-element.156), channel_id=1, source_target_pairs={{0,3},{1,0},{2,1},{3,2},{4,7},{5,4},{6,5},{7,6},{8,11},{9,8},{10,9... | collective-permute-start | bytes 331784 | tf_op jit(solution)/shard_map/ppermute | solution.py:54
  165.4 1.3 collective-permute-start.39
  166.7 1.9 collective-permute-done.22
  168.6 3.6 %collective-permute-done.23 = bf16[144,384]{1,0:T(8,128)(2,1)S(1)} collective-permute-done((bf16[144,384]{1,0:T(8,128)(2,1)S(1)}, bf16[144,384]{1,0:T(8,128)(2,1)S(1)}, u32[]{:S(2)}, u32[]{:S(2)}) %collective-permute-start.23) | collective-permute-done | bytes 110624 | tf_op jit(solution)/shard_map/ppermute | solution.py:54
  172.9 1.6 collective-permute-start.40
  174.5 3.5 %collective-permute-done.25 = bf16[144,384]{1,0:T(8,128)(2,1)S(1)} collective-permute-done((bf16[144,384]{1,0:T(8,128)(2,1)S(1)}, bf16[144,384]{1,0:T(8,128)(2,1)S(1)}, u32[]{:S(2)}, u32[]{:S(2)}) %collective-permute-start.25) | collective-permute-done | bytes 110624 | tf_op jit(solution)/shard_map/ppermute | solution.py:46
  178.1 0.9 collective-permute-start.26
  179.0 2.0 %collective-permute-done.40 = bf16[2,176,384]{2,1,0:T(8,128)(2,1)S(1)} collective-permute-done((bf16[2,176,384]{2,1,0:T(8,128)(2,1)S(1)}, bf16[2,176,384]{2,1,0:T(8,128)(2,1)S(1)}, u32[]{:S(2)}, u32[]{:S(2)}) %collective-permute-start.40) | collective-permute-done | bytes 270368 | tf_op jit(solution)/shard_map/ppermute | solution.py:46
  181.1 3.0 %collective-permute-done.26 = bf16[2,144,384]{2,1,0:T(8,128)(2,1)S(1)} collective-permute-done((bf16[2,144,384]{2,1,0:T(8,128)(2,1)S(1)}, bf16[2,144,384]{2,1,0:T(8,128)(2,1)S(1)}, u32[]{:S(2)}, u32[]{:S(2)}) %collective-permute-start.26) | collective-permute-done | bytes 221216 | tf_op jit(solution)/shard_map/ppermute | solution.py:46
  184.2 1.8 collective-permute-done.27.pair_other
  186.0 0.8 copy-done.11
  186.8 0.8 copy-done.10
  187.6 4.4 %finish.1 = (f32[144,576]{1,0:T(8,128)}, f32[144,192]{1,0:T(8,128)}, f32[144,192]{1,0:T(8,128)}, f32[144,576]{1,0:T(8,128)}, f32[8,576]{1,0:T(8,128)}, /*index=5...) custom-call(s32[4]{0:T(128)} %pad_add_fusion.where_ref, bf16[2,2,144,384]{3,2,1,0:T(8,128)(2,1)} %copy-done.4, ...), custom_call_target="tpu_custom_call" | custom-call | flops 50000000 | bytes 3557376 | tf_op jit(solution)/shard_map/finish/pallas_call | solution.py:641
  192.0 1.4 fusion.51
  (91 shorter events, 6.3 us)
Async XLA Ops:
  5.9 13.9 %copy-start.12 = (bf16[48,576]{1,0:T(8,128)(2,1)S(1)}, bf16[48,576]{1,0:T(8,128)(2,1)}, u32[]{:S(2)}) copy-start(bf16[48,576]{1,0:T(8,128)(2,1)} %get-tuple-element.87) | copy-start | bytes 165892
  5.9 13.9 %collective-permute-start = (bf16[80,384]{1,0:T(8,128)(2,1)}, bf16[80,384]{1,0:T(8,128)(2,1)S(1)}, u32[]{:S(2)}, u32[]{:S(2)}) collective-permute-start(bf16[80,384]{1,0:T(8,128)(2,1)} %get-tuple-element.82), channel_id=1, source_target_pairs={{1,0},{2,1},{3,2},{0,3},{5,4},{6,5},{7,6},{4,7},{9,8},{10,9},{11,1... | collective-permute-start | bytes 184328 | tf_op jit(solution)/shard_map/ppermute | solution.py:50
  11.0 8.8 %collective-permute-start.1 = (bf16[80,384]{1,0:T(8,128)(2,1)}, bf16[80,384]{1,0:T(8,128)(2,1)S(1)}, u32[]{:S(2)}, u32[]{:S(2)}) collective-permute-start(bf16[80,384]{1,0:T(8,128)(2,1)} %get-tuple-element.82), channel_id=1, source_target_pairs={{2,0},{3,1},{0,2},{1,3},{6,4},{7,5},{4,6},{5,7},{10,8},{11,9},{8,1... | collective-permute-start | bytes 184328 | tf_op jit(solution)/shard_map/ppermute | solution.py:50
  11.0 8.8 %collective-permute-start.2 = (bf16[80,384]{1,0:T(8,128)(2,1)}, bf16[80,384]{1,0:T(8,128)(2,1)S(1)}, u32[]{:S(2)}, u32[]{:S(2)}) collective-permute-start(bf16[80,384]{1,0:T(8,128)(2,1)} %get-tuple-element.82), channel_id=1, source_target_pairs={{3,0},{0,1},{1,2},{2,3},{7,4},{4,5},{5,6},{6,7},{11,8},{8,9},{9,10... | collective-permute-start | bytes 184328 | tf_op jit(solution)/shard_map/ppermute | solution.py:50
  15.8 7.9 %collective-permute-start.4 = (bf16[144,384]{1,0:T(8,128)(2,1)}, bf16[144,384]{1,0:T(8,128)(2,1)S(1)}, u32[]{:S(2)}, u32[]{:S(2)}) collective-permute-start(bf16[144,384]{1,0:T(8,128)(2,1)} %get-tuple-element.85), channel_id=1, source_target_pairs={{1,0},{2,1},{3,2},{0,3},{5,4},{6,5},{7,6},{4,7},{9,8},{10,9},{11,1... | collective-permute-start | bytes 331784 | tf_op jit(solution)/shard_map/ppermute | solution.py:50
  18.7 14.2 %collective-permute-start.5 = (bf16[144,384]{1,0:T(8,128)(2,1)}, bf16[144,384]{1,0:T(8,128)(2,1)S(1)}, u32[]{:S(2)}, u32[]{:S(2)}) collective-permute-start(bf16[144,384]{1,0:T(8,128)(2,1)} %get-tuple-element.85), channel_id=1, source_target_pairs={{2,0},{3,1},{0,2},{1,3},{6,4},{7,5},{4,6},{5,7},{10,8},{11,9},{8,1... | collective-permute-start | bytes 331784 | tf_op jit(solution)/shard_map/ppermute | solution.py:50
  19.8 14.6 %collective-permute-start.6 = (bf16[144,384]{1,0:T(8,128)(2,1)}, bf16[144,384]{1,0:T(8,128)(2,1)S(1)}, u32[]{:S(2)}, u32[]{:S(2)}) collective-permute-start(bf16[144,384]{1,0:T(8,128)(2,1)} %get-tuple-element.85), channel_id=1, source_target_pairs={{3,0},{0,1},{1,2},{2,3},{7,4},{4,5},{5,6},{6,7},{11,8},{8,9},{9,10... | collective-permute-start | bytes 331784 | tf_op jit(solution)/shard_map/ppermute | solution.py:50
  19.9 15.2 %collective-permute-start.7 = (bf16[48,576]{1,0:T(8,128)(2,1)S(1)}, bf16[48,576]{1,0:T(8,128)(2,1)S(1)}, u32[]{:S(2)}, u32[]{:S(2)}) collective-permute-start(bf16[48,576]{1,0:T(8,128)(2,1)S(1)} %copy-done.12), channel_id=1, source_target_pairs={{1,0},{2,1},{3,2},{0,3},{5,4},{6,5},{7,6},{4,7},{9,8},{10,9},{11,1... | collective-permute-start | bytes 165896 | tf_op jit(solution)/shard_map/ppermute | solution.py:50
  23.7 11.3 %collective-permute-start.8 = (bf16[48,576]{1,0:T(8,128)(2,1)S(1)}, bf16[48,576]{1,0:T(8,128)(2,1)S(1)}, u32[]{:S(2)}, u32[]{:S(2)}) collective-permute-start(bf16[48,576]{1,0:T(8,128)(2,1)S(1)} %copy-done.12), channel_id=1, source_target_pairs={{2,0},{3,1},{0,2},{1,3},{6,4},{7,5},{4,6},{5,7},{10,8},{11,9},{8,1... | collective-permute-start | bytes 165896 | tf_op jit(solution)/shard_map/ppermute | solution.py:50
  23.7 11.3 %collective-permute-start.9 = (bf16[48,576]{1,0:T(8,128)(2,1)S(1)}, bf16[48,576]{1,0:T(8,128)(2,1)S(1)}, u32[]{:S(2)}, u32[]{:S(2)}) collective-permute-start(bf16[48,576]{1,0:T(8,128)(2,1)S(1)} %copy-done.12), channel_id=1, source_target_pairs={{3,0},{0,1},{1,2},{2,3},{7,4},{4,5},{5,6},{6,7},{11,8},{8,9},{9,10... | collective-permute-start | bytes 165896 | tf_op jit(solution)/shard_map/ppermute | solution.py:50
  32.9 7.6 %collective-permute-start.3 = (bf16[3,80,384]{2,1,0:T(8,128)(2,1)S(1)}, bf16[3,80,384]{2,1,0:T(8,128)(2,1)S(1)}, u32[]{:S(2)}, u32[]{:S(2)}) collective-permute-start(bf16[3,80,384]{2,1,0:T(8,128)(2,1)S(1)} %pad_maximum_fusion.11), channel_id=1, source_target_pairs={{0,16},{4,20},{8,24},{12,28},{16,0},{20,4},{24,8},{28,12},{1,17},{... | collective-permute-start | bytes 552968 | tf_op jit(solution)/shard_map/ppermute | solution.py:46
  34.5 9.7 %collective-permute-start.11 = (bf16[3,144,384]{2,1,0:T(8,128)(2,1)S(1)}, bf16[3,144,384]{2,1,0:T(8,128)(2,1)S(1)}, u32[]{:S(2)}, u32[]{:S(2)}) collective-permute-start(bf16[3,144,384]{2,1,0:T(8,128)(2,1)S(1)} %get-tuple-element.165), channel_id=1, source_target_pairs={{0,16},{4,20},{8,24},{12,28},{16,0},{20,4},{24,8},{28,12},{1,17},{... | collective-permute-start | bytes 995336 | tf_op jit(solution)/shard_map/ppermute | solution.py:46
  40.5 7.6 %collective-permute-start.10 = (bf16[2,3,80,384]{3,2,1,0:T(8,128)(2,1)S(1)}, bf16[2,3,80,384]{3,2,1,0:T(8,128)(2,1)S(1)}, u32[]{:S(2)}, u32[]{:S(2)}) collective-permute-start(bf16[2,3,80,384]{3,2,1,0:T(8,128)(2,1)S(1)} %pad_maximum_fusion.6), channel_id=1, source_target_pairs={{0,8},{4,12},{8,0},{12,4},{16,24},{20,28},{24,16},{28,20},{1,9},{5... | collective-permute-start | bytes 1105928 | tf_op jit(solution)/shard_map/ppermute | solution.py:46
  48.2 2.3 %copy-start.1 = (bf16[2,2,3,80,384]{4,3,2,1,0:T(8,128)(2,1)}, bf16[2,2,3,80,384]{4,3,2,1,0:T(8,128)(2,1)S(1)}, u32[]{:S(2)}) copy-start(bf16[2,2,3,80,384]{4,3,2,1,0:T(8,128)(2,1)S(1)} %pad_maximum_fusion.1.pieces) | copy-start | bytes 2211844
  48.2 2.3 %collective-permute-start.12 = (bf16[2,2,3,80,384]{4,3,2,1,0:T(8,128)(2,1)S(1)}, bf16[2,2,3,80,384]{4,3,2,1,0:T(8,128)(2,1)S(1)}, u32[]{:S(2)}, u32[]{:S(2)}) collective-permute-start(bf16[2,2,3,80,384]{4,3,2,1,0:T(8,128)(2,1)S(1)} %pad_maximum_fusion.1.pieces), channel_id=1, source_target_pairs={{0,4},{4,0},{8,12},{12,8},{16,20},{20,16},{24,28},{28,24},{1,5},{5... | collective-permute-start | bytes 2211848 | tf_op jit(solution)/shard_map/ppermute | solution.py:46
  48.3 9.2 %collective-permute-start.13 = (bf16[3,48,576]{2,1,0:T(8,128)(2,1)S(1)}, bf16[3,48,576]{2,1,0:T(8,128)(2,1)S(1)}, u32[]{:S(2)}, u32[]{:S(2)}) collective-permute-start(bf16[3,48,576]{2,1,0:T(8,128)(2,1)S(1)} %pad_maximum_fusion.12), channel_id=1, source_target_pairs={{0,8},{4,12},{8,0},{12,4},{16,24},{20,28},{24,16},{28,20},{1,9},{5... | collective-permute-start | bytes 497672 | tf_op jit(solution)/shard_map/ppermute | solution.py:46
  49.8 24.8 %collective-permute-start.15 = (bf16[2,3,144,384]{3,2,1,0:T(8,128)(2,1)S(1)}, bf16[2,3,144,384]{3,2,1,0:T(8,128)(2,1)S(1)}, u32[]{:S(2)}, u32[]{:S(2)}) collective-permute-start(bf16[2,3,144,384]{3,2,1,0:T(8,128)(2,1)S(1)} %pad_maximum_fusion.3), channel_id=1, source_target_pairs={{0,8},{4,12},{8,0},{12,4},{16,24},{20,28},{24,16},{28,20},{1,9},{5... | collective-permute-start | bytes 1990664 | tf_op jit(solution)/shard_map/ppermute | solution.py:46
  50.5 0.9 copy-start.8
  57.5 10.7 %collective-permute-start.14 = (bf16[2,3,48,576]{3,2,1,0:T(8,128)(2,1)S(1)}, bf16[2,3,48,576]{3,2,1,0:T(8,128)(2,1)S(1)}, u32[]{:S(2)}, u32[]{:S(2)}) collective-permute-start(bf16[2,3,48,576]{3,2,1,0:T(8,128)(2,1)S(1)} %pad_maximum_fusion.7), channel_id=1, source_target_pairs={{0,16},{4,20},{8,24},{12,28},{16,0},{20,4},{24,8},{28,12},{1,17},{... | collective-permute-start | bytes 995336 | tf_op jit(solution)/shard_map/ppermute | solution.py:46
  68.4 6.6 %copy-start.2 = (bf16[2,2,3,48,576]{4,3,2,1,0:T(8,128)(2,1)}, bf16[2,2,3,48,576]{4,3,2,1,0:T(8,128)(2,1)S(1)}, u32[]{:S(2)}) copy-start(bf16[2,2,3,48,576]{4,3,2,1,0:T(8,128)(2,1)S(1)} %pad_maximum_fusion.2.down_pieces) | copy-start | bytes 1990660
  74.8 4.2 %copy-start = (bf16[2,2,3,144,384]{4,3,2,1,0:T(8,128)(2,1)}, bf16[2,2,3,144,384]{4,3,2,1,0:T(8,128)(2,1)S(1)}, u32[]{:S(2)}) copy-start(bf16[2,2,3,144,384]{4,3,2,1,0:T(8,128)(2,1)S(1)} %pad_maximum_fusion.pair_pieces) | copy-start | bytes 3981316
  74.8 4.2 %collective-permute-start.16 = (bf16[2,2,3,144,384]{4,3,2,1,0:T(8,128)(2,1)S(1)}, bf16[2,2,3,144,384]{4,3,2,1,0:T(8,128)(2,1)S(1)}, u32[]{:S(2)}, u32[]{:S(2)}) collective-permute-start(bf16[2,2,3,144,384]{4,3,2,1,0:T(8,128)(2,1)S(1)} %pad_maximum_fusion.pair_pieces), channel_id=1, source_target_pairs={{0,4},{4,0},{8,12},{12,8},{16,20},{20,16},{24,28},{28,24},{1,5},{5... | collective-permute-start | bytes 3981320 | tf_op jit(solution)/shard_map/ppermute | solution.py:46
  74.9 4.1 %collective-permute-start.17 = (bf16[2,2,3,48,576]{4,3,2,1,0:T(8,128)(2,1)S(1)}, bf16[2,2,3,48,576]{4,3,2,1,0:T(8,128)(2,1)S(1)}, u32[]{:S(2)}, u32[]{:S(2)}) collective-permute-start(bf16[2,2,3,48,576]{4,3,2,1,0:T(8,128)(2,1)S(1)} %pad_maximum_fusion.2.down_pieces), channel_id=1, source_target_pairs={{0,4},{4,0},{8,12},{12,8},{16,20},{20,16},{24,28},{28,24},{1,5},{5... | collective-permute-start | bytes 1990664 | tf_op jit(solution)/shard_map/ppermute | solution.py:46
  79.0 0.9 copy-start.9
  79.0 1.4 copy-start.6
  98.1 6.8 %collective-permute-start.18 = (bf16[2,2,4,144,384]{4,3,2,1,0:T(8,128)(2,1)}, bf16[2,2,4,144,384]{4,3,2,1,0:T(8,128)(2,1)}, u32[]{:S(2)}, u32[]{:S(2)}) collective-permute-start(bf16[2,2,4,144,384]{4,3,2,1,0:T(8,128)(2,1)} %get-tuple-element.109), channel_id=1, source_target_pairs={{0,4},{4,0},{8,12},{12,8},{16,20},{20,16},{24,28},{28,24},{1,5},{5... | collective-permute-start | bytes 5308424 | tf_op jit(solution)/shard_map/ppermute | solution.py:46
  98.3 10.9 %collective-permute-start.19 = (bf16[2,2,4,48,576]{4,3,2,1,0:T(8,128)(2,1)}, bf16[2,2,4,48,576]{4,3,2,1,0:T(8,128)(2,1)S(1)}, u32[]{:S(2)}, u32[]{:S(2)}) collective-permute-start(bf16[2,2,4,48,576]{4,3,2,1,0:T(8,128)(2,1)} %get-tuple-element.110), channel_id=1, source_target_pairs={{0,4},{4,0},{8,12},{12,8},{16,20},{20,16},{24,28},{28,24},{1,5},{5... | collective-permute-start | bytes 2654216 | tf_op jit(solution)/shard_map/ppermute | solution.py:46
  98.6 6.2 %copy-start.5 = (bf16[2,2,4,144,384]{4,3,2,1,0:T(8,128)(2,1)S(1)}, bf16[2,2,4,144,384]{4,3,2,1,0:T(8,128)(2,1)}, u32[]{:S(2)}) copy-start(bf16[2,2,4,144,384]{4,3,2,1,0:T(8,128)(2,1)} %get-tuple-element.127) | copy-start | bytes 5308420
  104.8 4.4 %copy-start.7 = (bf16[2,2,4,48,576]{4,3,2,1,0:T(8,128)(2,1)S(1)}, bf16[2,2,4,48,576]{4,3,2,1,0:T(8,128)(2,1)}, u32[]{:S(2)}) copy-start(bf16[2,2,4,48,576]{4,3,2,1,0:T(8,128)(2,1)} %get-tuple-element.131) | copy-start | bytes 2654212
  107.7 23.6 %collective-permute-start.20 = (bf16[2,4,144,384]{3,2,1,0:T(8,128)(2,1)}, bf16[2,4,144,384]{3,2,1,0:T(8,128)(2,1)S(1)}, u32[]{:S(2)}, u32[]{:S(2)}) collective-permute-start(bf16[2,4,144,384]{3,2,1,0:T(8,128)(2,1)} %get-tuple-element.144), channel_id=1, source_target_pairs={{0,8},{4,12},{8,0},{12,4},{16,24},{20,28},{24,16},{28,20},{1,9},{5... | collective-permute-start | bytes 2654216 | tf_op jit(solution)/shard_map/ppermute | solution.py:46
  109.4 21.9 %collective-permute-start.28 = (bf16[2,4,48,576]{3,2,1,0:T(8,128)(2,1)S(1)}, bf16[2,4,48,576]{3,2,1,0:T(8,128)(2,1)S(1)}, u32[]{:S(2)}, u32[]{:S(2)}) collective-permute-start(bf16[2,4,48,576]{3,2,1,0:T(8,128)(2,1)S(1)} %get-tuple-element.147), channel_id=1, source_target_pairs={{0,16},{4,20},{8,24},{12,28},{16,0},{20,4},{24,8},{28,12},{1,17},{... | collective-permute-start | bytes 1327112 | tf_op jit(solution)/shard_map/ppermute | solution.py:46
  131.3 2.8 %collective-permute-start.29 = (bf16[2,2,4,80,384]{4,3,2,1,0:T(8,128)(2,1)}, bf16[2,2,4,80,384]{4,3,2,1,0:T(8,128)(2,1)S(1)}, u32[]{:S(2)}, u32[]{:S(2)}) collective-permute-start(bf16[2,2,4,80,384]{4,3,2,1,0:T(8,128)(2,1)} %get-tuple-element.133), channel_id=1, source_target_pairs={{0,4},{4,0},{8,12},{12,8},{16,20},{20,16},{24,28},{28,24},{1,5},{5... | collective-permute-start | bytes 2949128 | tf_op jit(solution)/shard_map/ppermute | solution.py:46
  135.6 13.3 %collective-permute-start.30 = (bf16[2,4,80,384]{3,2,1,0:T(8,128)(2,1)S(1)}, bf16[2,4,80,384]{3,2,1,0:T(8,128)(2,1)S(1)}, u32[]{:S(2)}, u32[]{:S(2)}) collective-permute-start(bf16[2,4,80,384]{3,2,1,0:T(8,128)(2,1)S(1)} %get-tuple-element.146), channel_id=1, source_target_pairs={{0,16},{4,20},{8,24},{12,28},{16,0},{20,4},{24,8},{28,12},{1,17},{... | collective-permute-start | bytes 1474568 | tf_op jit(solution)/shard_map/ppermute | solution.py:46
  136.3 7.8 %collective-permute-start.35 = (bf16[4,48,576]{2,1,0:T(8,128)(2,1)S(1)}, bf16[4,48,576]{2,1,0:T(8,128)(2,1)S(1)}, u32[]{:S(2)}, u32[]{:S(2)}) collective-permute-start(bf16[4,48,576]{2,1,0:T(8,128)(2,1)S(1)} %get-tuple-element.154), channel_id=1, source_target_pairs={{0,8},{4,12},{8,0},{12,4},{16,24},{20,28},{24,16},{28,20},{1,9},{5... | collective-permute-start | bytes 663560 | tf_op jit(solution)/shard_map/ppermute | solution.py:46
  144.1 6.5 %collective-permute-start.36 = (bf16[48,576]{1,0:T(8,128)(2,1)S(1)}, bf16[48,576]{1,0:T(8,128)(2,1)S(1)}, u32[]{:S(2)}, u32[]{:S(2)}) collective-permute-start(bf16[48,576]{1,0:T(8,128)(2,1)S(1)} %get-tuple-element.161), channel_id=1, source_target_pairs={{0,1},{1,2},{2,3},{3,0},{4,5},{5,6},{6,7},{7,4},{8,9},{9,10},{10,1... | collective-permute-start | bytes 165896 | tf_op jit(solution)/shard_map/ppermute | solution.py:54
  144.2 7.2 %collective-permute-start.37 = (bf16[48,576]{1,0:T(8,128)(2,1)S(1)}, bf16[48,576]{1,0:T(8,128)(2,1)S(1)}, u32[]{:S(2)}, u32[]{:S(2)}) collective-permute-start(bf16[48,576]{1,0:T(8,128)(2,1)S(1)} %get-tuple-element.163), channel_id=1, source_target_pairs={{0,2},{1,3},{2,0},{3,1},{4,6},{5,7},{6,4},{7,5},{8,10},{9,11},{10,... | collective-permute-start | bytes 165896 | tf_op jit(solution)/shard_map/ppermute | solution.py:54
  144.3 7.1 %collective-permute-start.38 = (bf16[48,576]{1,0:T(8,128)(2,1)S(1)}, bf16[48,576]{1,0:T(8,128)(2,1)S(1)}, u32[]{:S(2)}, u32[]{:S(2)}) collective-permute-start(bf16[48,576]{1,0:T(8,128)(2,1)S(1)} %get-tuple-element.162), channel_id=1, source_target_pairs={{0,3},{1,0},{2,1},{3,2},{4,7},{5,4},{6,5},{7,6},{8,11},{9,8},{10,9... | collective-permute-start | bytes 165896 | tf_op jit(solution)/shard_map/ppermute | solution.py:54
  149.1 7.2 %collective-permute-start.31 = (bf16[4,80,384]{2,1,0:T(8,128)(2,1)S(1)}, bf16[4,80,384]{2,1,0:T(8,128)(2,1)S(1)}, u32[]{:S(2)}, u32[]{:S(2)}) collective-permute-start(bf16[4,80,384]{2,1,0:T(8,128)(2,1)S(1)} %get-tuple-element.152), channel_id=1, source_target_pairs={{0,8},{4,12},{8,0},{12,4},{16,24},{20,28},{24,16},{28,20},{1,9},{5... | collective-permute-start | bytes 737288 | tf_op jit(solution)/shard_map/ppermute | solution.py:46
  149.9 11.2 %collective-permute-start.21 = (bf16[4,144,384]{2,1,0:T(8,128)(2,1)S(1)}, bf16[4,144,384]{2,1,0:T(8,128)(2,1)S(1)}, u32[]{:S(2)}, u32[]{:S(2)}) collective-permute-start(bf16[4,144,384]{2,1,0:T(8,128)(2,1)S(1)} %get-tuple-element.150), channel_id=1, source_target_pairs={{0,16},{4,20},{8,24},{12,28},{16,0},{20,4},{24,8},{28,12},{1,17},{... | collective-permute-start | bytes 1327112 | tf_op jit(solution)/shard_map/ppermute | solution.py:46
  156.4 6.2 %collective-permute-start.32 = (bf16[80,384]{1,0:T(8,128)(2,1)S(1)}, bf16[80,384]{1,0:T(8,128)(2,1)S(1)}, u32[]{:S(2)}, u32[]{:S(2)}) collective-permute-start(bf16[80,384]{1,0:T(8,128)(2,1)S(1)} %get-tuple-element.158), channel_id=1, source_target_pairs={{0,1},{1,2},{2,3},{3,0},{4,5},{5,6},{6,7},{7,4},{8,9},{9,10},{10,1... | collective-permute-start | bytes 184328 | tf_op jit(solution)/shard_map/ppermute | solution.py:54
  156.4 8.9 %collective-permute-start.33 = (bf16[80,384]{1,0:T(8,128)(2,1)S(1)}, bf16[80,384]{1,0:T(8,128)(2,1)S(1)}, u32[]{:S(2)}, u32[]{:S(2)}) collective-permute-start(bf16[80,384]{1,0:T(8,128)(2,1)S(1)} %get-tuple-element.160), channel_id=1, source_target_pairs={{0,2},{1,3},{2,0},{3,1},{4,6},{5,7},{6,4},{7,5},{8,10},{9,11},{10,... | collective-permute-start | bytes 184328 | tf_op jit(solution)/shard_map/ppermute | solution.py:54
  156.6 8.7 %collective-permute-start.34 = (bf16[80,384]{1,0:T(8,128)(2,1)S(1)}, bf16[80,384]{1,0:T(8,128)(2,1)S(1)}, u32[]{:S(2)}, u32[]{:S(2)}) collective-permute-start(bf16[80,384]{1,0:T(8,128)(2,1)S(1)} %get-tuple-element.159), channel_id=1, source_target_pairs={{0,3},{1,0},{2,1},{3,2},{4,7},{5,4},{6,5},{7,6},{8,11},{9,8},{10,9... | collective-permute-start | bytes 184328 | tf_op jit(solution)/shard_map/ppermute | solution.py:54
  161.2 7.5 %collective-permute-start.22 = (bf16[144,384]{1,0:T(8,128)(2,1)S(1)}, bf16[144,384]{1,0:T(8,128)(2,1)S(1)}, u32[]{:S(2)}, u32[]{:S(2)}) collective-permute-start(bf16[144,384]{1,0:T(8,128)(2,1)S(1)} %get-tuple-element.155), channel_id=1, source_target_pairs={{0,1},{1,2},{2,3},{3,0},{4,5},{5,6},{6,7},{7,4},{8,9},{9,10},{10,1... | collective-permute-start | bytes 331784 | tf_op jit(solution)/shard_map/ppermute | solution.py:54
  161.2 11.0 %collective-permute-start.23 = (bf16[144,384]{1,0:T(8,128)(2,1)S(1)}, bf16[144,384]{1,0:T(8,128)(2,1)S(1)}, u32[]{:S(2)}, u32[]{:S(2)}) collective-permute-start(bf16[144,384]{1,0:T(8,128)(2,1)S(1)} %get-tuple-element.157), channel_id=1, source_target_pairs={{0,2},{1,3},{2,0},{3,1},{4,6},{5,7},{6,4},{7,5},{8,10},{9,11},{10,... | collective-permute-start | bytes 331784 | tf_op jit(solution)/shard_map/ppermute | solution.py:54
  162.5 9.6 %collective-permute-start.24 = (bf16[144,384]{1,0:T(8,128)(2,1)S(1)}, bf16[144,384]{1,0:T(8,128)(2,1)S(1)}, u32[]{:S(2)}, u32[]{:S(2)}) collective-permute-start(bf16[144,384]{1,0:T(8,128)(2,1)S(1)} %get-tuple-element.156), channel_id=1, source_target_pairs={{0,3},{1,0},{2,1},{3,2},{4,7},{5,4},{6,5},{7,6},{8,11},{9,8},{10,9... | collective-permute-start | bytes 331784 | tf_op jit(solution)/shard_map/ppermute | solution.py:54
  165.4 7.4 %collective-permute-start.39 = (bf16[176,384]{1,0:T(8,128)(2,1)S(1)}, bf16[176,384]{1,0:T(8,128)(2,1)S(1)}, u32[]{:S(2)}, u32[]{:S(2)}) collective-permute-start(bf16[176,384]{1,0:T(8,128)(2,1)S(1)} %get-tuple-element.171), channel_id=1, source_target_pairs={{0,8},{4,12},{8,0},{12,4},{16,24},{20,28},{24,16},{28,20},{1,9},{5... | collective-permute-start | bytes 405512 | tf_op jit(solution)/shard_map/ppermute | solution.py:46
  172.3 5.8 %collective-permute-start.25 = (bf16[144,384]{1,0:T(8,128)(2,1)S(1)}, bf16[144,384]{1,0:T(8,128)(2,1)S(1)}, u32[]{:S(2)}, u32[]{:S(2)}) collective-permute-start(bf16[144,384]{1,0:T(8,128)(2,1)S(1)} %fusion.20), channel_id=1, source_target_pairs={{0,16},{4,20},{8,24},{12,28},{16,0},{20,4},{24,8},{28,12},{1,17},{... | collective-permute-start | bytes 331784 | tf_op jit(solution)/shard_map/ppermute | solution.py:46
  172.9 8.1 %collective-permute-start.40 = (bf16[2,176,384]{2,1,0:T(8,128)(2,1)S(1)}, bf16[2,176,384]{2,1,0:T(8,128)(2,1)S(1)}, u32[]{:S(2)}, u32[]{:S(2)}) collective-permute-start(bf16[2,176,384]{2,1,0:T(8,128)(2,1)S(1)} %get-tuple-element.167), channel_id=1, source_target_pairs={{0,16},{4,20},{8,24},{12,28},{16,0},{20,4},{24,8},{28,12},{1,17},{... | collective-permute-start | bytes 811016 | tf_op jit(solution)/shard_map/ppermute | solution.py:46
  178.1 6.0 %collective-permute-start.26 = (bf16[2,144,384]{2,1,0:T(8,128)(2,1)S(1)}, bf16[2,144,384]{2,1,0:T(8,128)(2,1)S(1)}, u32[]{:S(2)}, u32[]{:S(2)}) collective-permute-start(bf16[2,144,384]{2,1,0:T(8,128)(2,1)S(1)} %get-tuple-element.169), channel_id=1, source_target_pairs={{0,8},{4,12},{8,0},{12,4},{16,24},{20,28},{24,16},{28,20},{1,9},{5... | collective-permute-start | bytes 663560 | tf_op jit(solution)/shard_map/ppermute | solution.py:46
  181.0 5.0 %copy-start.3 = (bf16[2,2,176,384]{3,2,1,0:T(8,128)(2,1)}, bf16[2,2,176,384]{3,2,1,0:T(8,128)(2,1)S(1)}, u32[]{:S(2)}) copy-start(bf16[2,2,176,384]{3,2,1,0:T(8,128)(2,1)S(1)} %pad_maximum_fusion.4.rest_pieces) | copy-start | bytes 1622020
  181.0 5.0 %collective-permute-start.41 = (bf16[2,2,176,384]{3,2,1,0:T(8,128)(2,1)S(1)}, bf16[2,2,176,384]{3,2,1,0:T(8,128)(2,1)S(1)}, u32[]{:S(2)}, u32[]{:S(2)}) collective-permute-start(bf16[2,2,176,384]{3,2,1,0:T(8,128)(2,1)S(1)} %pad_maximum_fusion.4.rest_pieces), channel_id=1, source_target_pairs={{0,4},{4,0},{8,12},{12,8},{16,20},{20,16},{24,28},{28,24},{1,5},{5... | collective-permute-start | bytes 1622024 | tf_op jit(solution)/shard_map/ppermute | solution.py:46
  184.1 1.9 copy-start.4
  184.1 1.9 collective-permute-start.27
  186.0 0.8 copy-start.11
  186.8 0.8 copy-start.10

commit v2 on v0

--- a/solution.py
+++ b/solution.py
@@ -115,6 +115,11 @@
     return pl.ds(pl.multiple_of(start, unit), count)
 
 
+def position():
+    index = lax.axis_index("rep")
+    return index % 2, index // 2 % 2, index // 4 % 2, lax.axis_index("shard")
+
+
 def relative(bit, rel):
     return 1 - bit if rel else bit
 
@@ -146,7 +151,6 @@
 
 
 def pack_kernel(
-    where_ref,
     w_out,
     w_query,
     w_key,
@@ -161,7 +165,7 @@
     down_mine,
     down,
 ):
-    core, x, y, shard = (where_ref[i] for i in range(4))
+    core, x, y, shard = position()
     block = 2 * core + x
     part = gate.shape[0]
     packed = own.shape[1]
@@ -186,11 +190,6 @@
     rest = value[..., 384:]
     pad = [(0, 0)] * (value.ndim - 1) + [(0, 384 - rest.shape[-1])]
     return jnp.concatenate([value[..., :384], jnp.pad(rest, pad)], axis=-2)
-
-
-def unfold(value, width):
-    half = value.shape[-2] // 2
-    return jnp.concatenate([value[..., :half, :], value[..., half:, : width - 384]], axis=-1)
 
 
 def prepare_kernel(
@@ -238,7 +237,6 @@
 def project_kernel(
     shards,
     part,
-    where_ref,
     scaled,
     cosine,
     sine,
@@ -253,7 +251,7 @@
     values,
     sems,
 ):
-    core, x, y, shard = (where_ref[i] for i in range(4))
+    core, x, y, shard = position()
     width = scaled.shape[1]
     copies = Copies(sems)
     copies.start(own.at[pl.ds(0, part)], weights.at[rows_at(part * shard, part)])
@@ -338,7 +336,6 @@
 def feed_kernel(
     shards,
     part,
-    where_ref,
     hidden_one,
     normed_two,
     gains,
@@ -367,7 +364,7 @@
     grad_down,
     sems,
 ):
-    core, x, y, shard = (where_ref[i] for i in range(4))
+    core, x, y, shard = position()
     width = hidden_one.shape[1]
     down_part = own_down.shape[0]
     eighth = down_part // 8
@@ -517,7 +514,6 @@
 def back_last_kernel(
     shards,
     part,
-    where_ref,
     hidden_in,
     gains,
     weights,
@@ -526,7 +522,7 @@
     grad_gain_two,
     *rest,
 ):
-    core, x, y, shard = (where_ref[i] for i in range(4))
+    core, x, y, shard = position()
     rows, width = hidden_in.shape
     turned, values, outs = rest[0:KV], rest[KV : 2 * KV], rest[2 * KV : 3 * KV]
     grad_tokens, keep, send, grad_low, grad_weights, sems = rest[3 * KV :]
@@ -565,7 +561,7 @@
                 columns = rows_at(384 * block, 384, 128)
                 for step in range(shards):
                     at = shard_at(shard, step, shards)
-                    piece = target.at[rel_x, rel_y, step]
+                    piece = target.at[rel_y, rel_x, step]
                     copies.start(
                         grad_weights.at[rows_at(part * at + 80 * at_y, 64), columns],
                         piece.at[pl.ds(0, 64)],
@@ -576,7 +572,6 @@
 
 
 def finish_kernel(
-    where_ref,
     pair_pieces,
     pair_other,
     rest_pieces,
@@ -585,7 +580,8 @@
     out_key,
     out_value,
     out_out,
-    out_gains,
+    out_gain_one,
+    out_gain_two,
     out_gate,
     out_up,
     out_down,
@@ -594,7 +590,7 @@
     down,
     sems,
 ):
-    core, x, y = (where_ref[i] for i in range(3))
+    core, x, y, shard = position()
     part, width = out_out.shape
     copies = Copies(sems)
     for rel_core, (p_from, r_from) in enumerate(((pair_pieces, rest_pieces), (pair_other, rest_other))):
@@ -615,7 +611,10 @@
     out_query[...] = rest[:, at : at + width]
     out_key[...] = rest[:, at + width : at + width + kv_width]
     out_value[...] = rest[:, at + width + kv_width :]
-    out_gains[...] = attn[part : part + 16, 0:width].astype(f32)[:8]
+    gains = attn[part : part + 16, :].astype(f32)
+    gains = pltpu.roll(gains, gains.shape[1] - part * shard, 1)
+    out_gain_one[...] = gains[0:1, :part]
+    out_gain_two[...] = gains[1:2, :part]
     out_gate[...] = pair[0].astype(f32)
     out_up[...] = pair[1].astype(f32)
     half = down.shape[1] // 2
@@ -628,7 +627,7 @@
 
 VM = pl.BlockSpec(memory_space=pltpu.VMEM)
 SM = pl.BlockSpec(memory_space=pltpu.SMEM)
-HB = pl.BlockSpec(memory_space=pl.ANY)
+HB = pl.BlockSpec(memory_space=pltpu.HBM)
 
 
 def shape(sizes, kind):
@@ -673,16 +672,10 @@
     down_part = w_down.shape[0]
     eighth = down_part // 8
     packed = 2 * width + 2 * w_key.shape[1]
-    rep_index = lax.axis_index("rep")
-    shard = lax.axis_index("shard")
-    core, x, y = ((rep_index >> bit) & 1 for bit in range(3))
-    where = jnp.stack([core, x, y, shard]).astype(jnp.int32)
-
     own, attn_mine, pair_mine, down_mine, own_down = call(
         pack_kernel,
         "pack",
         (
-            where,
             w_out,
             w_query,
             w_key,
@@ -692,7 +685,7 @@
             w_up,
             w_down.T,
         ),
-        [SM] + [VM] * 8,
+        [VM] * 8,
         (
             shape((part + 16, packed), low),
             shape((80, 384), low),
@@ -723,20 +716,20 @@
         [VM] * 6,
         [],
         5,
-        60,
+        24,
     )
     pair_got = gather_shards(after(pair_mine, scaled), shards)
     down_got = gather_shards(after(down_mine, attn_got), shards)
     attn_got = gather_bit(after(attn_got, scaled), 2, replicas)
-    attn_got = gather_bit(after(attn_got, pair_got), 1, replicas)
+    attn_got = gather_bit(after(attn_got, pair_got, down_got), 1, replicas)
+    pair_got = gather_bit(pair_got, 2, replicas)
+    attn_got = after(attn_got, pair_got)
     attn_other = flip(attn_got, 0, replicas)
-    pair_got = gather_bit(pair_got, 2, replicas)
-    scaled = after(scaled, down_got)
     weights, gains, normed, query, keys, values = call(
         functools.partial(project_kernel, shards, part),
         "project",
-        (where, scaled, cosine, sine, own, attn_got, attn_other),
-        [SM, VM, VM, VM, HB, HB, HB],
+        (scaled, cosine, sine, own, attn_got, attn_other),
+        [VM, VM, VM, HB, HB, HB],
         (
             shape((width + 16 * shards, packed), low),
             shape((8, width), f32),
@@ -750,7 +743,6 @@
         5,
         24,
     )
-    keys = after(keys, pair_got)
     down_got = gather_bit(down_got, 1, replicas, normed)
     mixed, log_total = [], []
     for kv in range(KV):
@@ -793,7 +785,6 @@
         functools.partial(feed_kernel, shards, part),
         "feed",
         (
-            where,
             hidden_one,
             normed_two,
             gains,
@@ -807,7 +798,7 @@
             down_got,
             down_other,
         ),
-        [SM] + [VM] * 3 + [SM, VM] + [HB] * 7,
+        [VM] * 3 + [SM, VM] + [HB] * 7,
         (
             shape((width, rows), low),
             shape((rows, width), f32),
@@ -829,7 +820,7 @@
             pltpu.SemaphoreType.DMA((16 * shards + 3,)),
         ],
         19,
-        60,
+        40,
     )
     pair_sent = flip(pair_send, 0, replicas)
     down_sent = flip(down_send, 0, replicas)
@@ -862,7 +853,6 @@
         functools.partial(back_last_kernel, shards, part),
         "back_last",
         (
-            where,
             hidden_in,
             gains,
             weights,
@@ -873,7 +863,7 @@
             *grad_values,
             *grad_out,
         ),
-        [SM] + [VM] * (6 + 3 * KV),
+        [VM] * (6 + 3 * KV),
         (shape((width, rows), low), attn_shape, attn_shape),
         [VM, HB, HB],
         [
@@ -884,33 +874,32 @@
         6,
         24,
     )
-    attn_left = halve(attn_keep, flip(after(attn_send, down_left[1]), 0, replicas), 1, replicas)
+    attn_left = halve(attn_keep, flip(after(attn_send, down_left[1], pair_left[1]), 0, replicas), 2, replicas)
     pair_left = halve(*pair_left, 2, replicas)
     down_left = halve(down_left[0], after(down_left[1], grad_tokens), 1, replicas)
-    attn_left = halve(*attn_left, 2, replicas)
-    feed_left = tuple(
-        jnp.concatenate([one, fold(two)], axis=1) for one, two in zip(pair_left, down_left)
-    )
-    feed_total = scatter_over_shards(*feed_left, shards, replicas)
+    attn_left = halve(*attn_left, 1, replicas)
+    down_total = scatter_over_shards(*down_left, shards, replicas)
+    pair_total = scatter_over_shards(*pair_left, shards, replicas)
     attn_total = scatter_over_shards(*attn_left, shards, replicas)
-    pair_pieces = spread(feed_total[:part], (2, 1, 0), replicas)
-    rest_pieces = spread(jnp.concatenate([attn_total, feed_total[part:]]), (1, 2, 0), replicas)
-    g_query, g_key, g_value, g_out, g_gains, g_gate, g_up, g_down = call(
+    pair_pieces = spread(pair_total, (2, 1, 0), replicas)
+    rest_pieces = spread(jnp.concatenate([attn_total, fold(down_total)]), (1, 2, 0), replicas)
+    g_query, g_key, g_value, g_out, g_gain_one, g_gain_two, g_gate, g_up, g_down = call(
         finish_kernel,
         "finish",
-        (where, *pair_pieces, *rest_pieces),
-        [SM] + [HB] * 4,
+        (*pair_pieces, *rest_pieces),
+        [HB] * 4,
         (
             shape(w_query.shape, f32),
             shape(w_key.shape, f32),
             shape(w_value.shape, f32),
             shape(w_out.shape, f32),
-            shape((8, width), f32),
+            shape((1, part), f32),
+            shape((1, part), f32),
             shape(w_gate.shape, f32),
             shape(w_up.shape, f32),
             shape((width, down_part), f32),
         ),
-        [VM] * 8,
+        [VM] * 9,
         [
             pltpu.VMEM((160, packed), low),
             pltpu.VMEM((2, part, hidden_width), low),
@@ -918,18 +907,17 @@
             pltpu.SemaphoreType.DMA((24,)),
         ],
         5,
-        60,
-    )
-    g_gains = lax.dynamic_slice(g_gains, (0, part * shard), (2, part))
+        24,
+    )
     return (
         result.T,
         grad_tokens.T,
-        g_gains[0],
+        g_gain_one.reshape(part),
         g_query,
         g_key,
         g_value,
         g_out,
-        g_gains[1],
+        g_gain_two.reshape(part),
         g_gate,
         g_up,
         g_down.T,

time: 198 us -> 181 us (0.914)
  local copies, waits for them, and re-layouts: 18.7 us -> 1.5 us
  starting transfers between devices: 43.6 us -> 52.4 us
  waiting for transfers between devices: 73.8 us -> 67 us
    unnamed x90 -> x20, local copies, waits for them, and re-layouts: 15.8 us -> 0.05 us
    ppermute x6 -> x9, starting transfers between devices: 9.1 us -> 15.1 us  [shift_to(): lax.ppermute(value, 'shard', [(s, (s + step) % shards) for s in range(sha...]
    ppermute x9, waiting for transfers between devices: 11.7 us -> 7.71 us  [shift_from(): lax.ppermute(value, 'shard', [((s + step) % shards, s) for s in range(sha...]
    ppermute x6 -> x9, waiting for transfers between devices: 12.1 us -> 8.46 us  [shift_to(): lax.ppermute(value, 'shard', [(s, (s + step) % shards) for s in range(sha...]
    ppermute x24, starting transfers between devices: 20.3 us -> 23 us  [flip(): lax.ppermute(value, 'rep', [(i, i ^ 1 << bit) for i in range(replicas)])]
  transfers between devices with their start and end apart: 39 -> 42, of which waited for: 20 -> 25; matrix products, arithmetic and copies ran while one was open for 1% -> 1% of each run, Pallas kernels for 14% -> 14%
where the time goes in v2:
time: 181 us; the launch traced here: 178 us
  waiting for transfers between devices  67 us (37%)
  Pallas kernels  52.9 us (29%)
  starting transfers between devices  52.4 us (29%)
  other arithmetic  3.24 us (2%)
    pallas_call x12, Pallas kernels, call(): pl.pallas_call(kernel, name=name, in_specs=in_specs, out_shape=out_shape,...  52.9 us
    ppermute x24, waiting for transfers between devices, flip(): lax.ppermute(value, 'rep', [(i, i ^ 1 << bit) for i in range(replicas)])  50.8 us
    ppermute x24, starting transfers between devices, flip(): lax.ppermute(value, 'rep', [(i, i ^ 1 << bit) for i in range(replicas)])  23 us
    ppermute x9, starting transfers between devices, shift_to(): lax.ppermute(value, 'shard', [(s, (s + step) % shards) for s in range(sha...  15.1 us
    ppermute x9, starting transfers between devices, shift_from(): lax.ppermute(value, 'shard', [((s + step) % shards, s) for s in range(sha...  14.3 us
    ppermute x9, waiting for transfers between devices, shift_to(): lax.ppermute(value, 'shard', [(s, (s + step) % shards) for s in range(sha...  8.46 us
    ppermute x9, waiting for transfers between devices, shift_from(): lax.ppermute(value, 'shard', [((s + step) % shards, s) for s in range(sha...  7.71 us
  transfers between devices with their start and end apart: 42, of which 25 were waited for; matrix products, arithmetic and copies ran while one was open for 1% of the time, Pallas kernels for 14%

profile of v2, /device:TPU:0, one launch (start us, length us, event | category | flops | bytes accessed | tf_op | source)
XLA Modules:
  0.0 178.4 jit_solution(16295679823851602085)
XLA Ops:
  0.7 0.8 stack.135
  1.5 0.7 stack.136
  2.7 2.7 %pack.1 = (bf16[160,1536]{1,0:T(8,128)(2,1)}, bf16[80,384]{1,0:T(8,128)(2,1)}, bf16[144,384]{1,0:T(8,128)(2,1)}, bf16[48,576]{1,0:T(8,128)(2,1)}, bf16[384,576]{1,0:T(8,128)(2,1)}) custom-call(bf16[144,576]{1,0:T(8,128)(2,1)} %w_out.1, bf16[144,576]{1,0:T(8,128)(2,1)} %w_query.1, bf16[144,192]{1,0:T(8,128)(2,1)} %w_key.1, bf16[144,192]{1,0:T(8,128)(2,1)} %w_value.1, ...), custom_call_target="tpu_custom_call" | custom-call | flops 20000000 | bytes 1161216 | tf_op jit(solution)/shard_map/pack/pallas_call | solution.py:639
  5.4 3.0 %collective-permute-start.2 = (bf16[80,384]{1,0:T(8,128)(2,1)}, bf16[80,384]{1,0:T(8,128)(2,1)S(1)}, u32[]{:S(2)}, u32[]{:S(2)}) collective-permute-start(bf16[80,384]{1,0:T(8,128)(2,1)} %get-tuple-element.83), channel_id=1, source_target_pairs={{3,0},{0,1},{1,2},{2,3},{7,4},{4,5},{5,6},{6,7},{11,8},{8,9},{9,10... | collective-permute-start | bytes 184328 | tf_op jit(solution)/shard_map/ppermute | solution.py:50
  8.4 2.6 %collective-permute-start.1 = (bf16[80,384]{1,0:T(8,128)(2,1)}, bf16[80,384]{1,0:T(8,128)(2,1)S(1)}, u32[]{:S(2)}, u32[]{:S(2)}) collective-permute-start(bf16[80,384]{1,0:T(8,128)(2,1)} %get-tuple-element.83), channel_id=1, source_target_pairs={{2,0},{3,1},{0,2},{1,3},{6,4},{7,5},{4,6},{5,7},{10,8},{11,9},{8,1... | collective-permute-start | bytes 184328 | tf_op jit(solution)/shard_map/ppermute | solution.py:50
  11.0 1.3 collective-permute-start
  12.4 1.6 prepare.1
  14.0 0.7 collective-permute-start.6
  15.0 2.8 %collective-permute-start.4 = (bf16[144,384]{1,0:T(8,128)(2,1)}, bf16[144,384]{1,0:T(8,128)(2,1)S(1)}, u32[]{:S(2)}, u32[]{:S(2)}) collective-permute-start(bf16[144,384]{1,0:T(8,128)(2,1)} %get-tuple-element.86), channel_id=1, source_target_pairs={{1,0},{2,1},{3,2},{0,3},{5,4},{6,5},{7,6},{4,7},{9,8},{10,9},{11,1... | collective-permute-start | bytes 331784 | tf_op jit(solution)/shard_map/ppermute | solution.py:50
  18.5 1.5 collective-permute-start.8
  20.0 2.0 %collective-permute-done.6 = bf16[144,384]{1,0:T(8,128)(2,1)S(1)} collective-permute-done((bf16[144,384]{1,0:T(8,128)(2,1)}, bf16[144,384]{1,0:T(8,128)(2,1)S(1)}, u32[]{:S(2)}, u32[]{:S(2)}) %collective-permute-start.6) | collective-permute-done | bytes 110624 | tf_op jit(solution)/shard_map/ppermute | solution.py:50
  22.1 1.3 collective-permute-start.7
  23.4 2.8 %collective-permute-done.5 = bf16[144,384]{1,0:T(8,128)(2,1)S(1)} collective-permute-done((bf16[144,384]{1,0:T(8,128)(2,1)}, bf16[144,384]{1,0:T(8,128)(2,1)S(1)}, u32[]{:S(2)}, u32[]{:S(2)}) %collective-permute-start.5) | collective-permute-done | bytes 110624 | tf_op jit(solution)/shard_map/ppermute | solution.py:50
  26.2 1.5 collective-permute-start.3
  28.4 2.8 %collective-permute-done.8 = bf16[48,576]{1,0:T(8,128)(2,1)S(1)} collective-permute-done((bf16[48,576]{1,0:T(8,128)(2,1)S(1)}, bf16[48,576]{1,0:T(8,128)(2,1)S(1)}, u32[]{:S(2)}, u32[]{:S(2)}) %collective-permute-start.8) | collective-permute-done | bytes 55328 | tf_op jit(solution)/shard_map/ppermute | solution.py:50
  31.3 2.5 %collective-permute-done.3 = bf16[3,80,384]{2,1,0:T(8,128)(2,1)S(1)} collective-permute-done((bf16[3,80,384]{2,1,0:T(8,128)(2,1)S(1)}, bf16[3,80,384]{2,1,0:T(8,128)(2,1)S(1)}, u32[]{:S(2)}, u32[]{:S(2)}) %collective-permute-start.3) | collective-permute-done | bytes 184352 | tf_op jit(solution)/shard_map/ppermute | solution.py:46
  33.9 1.6 collective-permute-start.10
  35.4 2.8 %collective-permute-done.11 = bf16[3,144,384]{2,1,0:T(8,128)(2,1)S(1)} collective-permute-done((bf16[3,144,384]{2,1,0:T(8,128)(2,1)S(1)}, bf16[3,144,384]{2,1,0:T(8,128)(2,1)S(1)}, u32[]{:S(2)}, u32[]{:S(2)}) %collective-permute-start.11) | collective-permute-done | bytes 331808 | tf_op jit(solution)/shard_map/ppermute | solution.py:46
  38.3 3.2 %collective-permute-done.10 = bf16[2,3,80,384]{3,2,1,0:T(8,128)(2,1)S(1)} collective-permute-done((bf16[2,3,80,384]{3,2,1,0:T(8,128)(2,1)S(1)}, bf16[2,3,80,384]{3,2,1,0:T(8,128)(2,1)S(1)}, u32[]{:S(2)}, u32[]{:S(2)}) %collective-permute-start.10) | collective-permute-done | bytes 368672 | tf_op jit(solution)/shard_map/ppermute | solution.py:46
  41.6 1.6 collective-permute-start.13
  43.8 3.2 %project.1 = (bf16[640,1536]{1,0:T(8,128)(2,1)S(1)}, f32[8,576]{1,0:T(8,128)S(1)}, bf16[512,576]{1,0:T(8,128)(2,1)S(1)}, bf16[9,512,64]{2,1,0:T(8,128)(2,1)S(1)}...) custom-call(f32[512,576]{1,0:T(8,128)S(1)} %get-tuple-element.79.scaled, ...), custom_call_target="tpu_custom_call" | custom-call | flops 50000000 | bytes 3557376 | tf_op jit(solution)/shard_map/project/pallas_call | solution.py:639
  47.0 2.1 %collective-permute-done.13 = bf16[3,48,576]{2,1,0:T(8,128)(2,1)S(1)} collective-permute-done((bf16[3,48,576]{2,1,0:T(8,128)(2,1)S(1)}, bf16[3,48,576]{2,1,0:T(8,128)(2,1)S(1)}, u32[]{:S(2)}, u32[]{:S(2)}) %collective-permute-start.13) | collective-permute-done | bytes 165920 | tf_op jit(solution)/shard_map/ppermute | solution.py:46
  49.2 1.1 collective-permute-start.14
  50.3 1.9 %attend_1.1 = (bf16[512,192]{1,0:T(8,128)(2,1)S(1)}, f32[3,512,1]{2,1,0:T(8,128)S(1)}) custom-call(f32[512,512]{1,0:T(8,128)S(1)} %get-tuple-element.78.bias, bf16[9,512,64]{2,1,0:T(8,128)(2,1)S(1)} %get-tuple-element.91.query, bf16[3,512,64]{2,1,0:T(8,128)(2,1)S(1)} %get-tuple-element.92.keys, bf16[3,512,64]{2,1,0:T(8,128)(2,1)S(1)} %get-tuple-element.93.values), custom_call_target="tpu_custom_call" | custom-call | flops 30000000 | bytes 202752 | tf_op jit(solution)/shard_map/attend_1/pallas_call | solution.py:639
  52.2 1.9 %attend_0.1 = (bf16[512,192]{1,0:T(8,128)(2,1)S(1)}, f32[3,512,1]{2,1,0:T(8,128)S(1)}) custom-call(f32[512,512]{1,0:T(8,128)S(1)} %get-tuple-element.78.bias, bf16[9,512,64]{2,1,0:T(8,128)(2,1)S(1)} %get-tuple-element.91.query, bf16[3,512,64]{2,1,0:T(8,128)(2,1)S(1)} %get-tuple-element.92.keys, bf16[3,512,64]{2,1,0:T(8,128)(2,1)S(1)} %get-tuple-element.93.values), custom_call_target="tpu_custom_call" | custom-call | flops 30000000 | bytes 202752 | tf_op jit(solution)/shard_map/attend_0/pallas_call | solution.py:639
  54.1 4.8 %collective-permute-done.14 = bf16[2,3,48,576]{3,2,1,0:T(8,128)(2,1)S(1)} collective-permute-done((bf16[2,3,48,576]{3,2,1,0:T(8,128)(2,1)S(1)}, bf16[2,3,48,576]{3,2,1,0:T(8,128)(2,1)S(1)}, u32[]{:S(2)}, u32[]{:S(2)}) %collective-permute-start.14) | collective-permute-done | bytes 331808 | tf_op jit(solution)/shard_map/ppermute | solution.py:46
  59.1 2.7 %attend_2.1 = (bf16[512,192]{1,0:T(8,128)(2,1)S(1)}, f32[3,512,1]{2,1,0:T(8,128)S(1)}, f32[512,576]{1,0:T(8,128)S(1)}, bf16[512,576]{1,0:T(8,128)(2,1)S(1)}) custom-call(f32[512,512]{1,0:T(8,128)S(1)} %get-tuple-element.78.bias, bf16[9,512,64]{2,1,0:T(8,128)(2,1)S(1)} %get-tuple-element.91.query, bf16[3,512,64]{2,1,0:T(8,128)(2,1)S(1)} %get-tuple-element.92.keys, ...), custom_call_target="tpu_custom_call" | custom-call | flops 40000000 | bytes 1972224 | tf_op jit(solution)/shard_map/attend_2/pallas_call | solution.py:639
  61.8 1.1 collective-permute-done.15
  63.6 3.6 %collective-permute-done.17.down_other = bf16[2,2,3,48,576]{4,3,2,1,0:T(8,128)(2,1)S(1)} collective-permute-done((bf16[2,2,3,48,576]{4,3,2,1,0:T(8,128)(2,1)S(1)}, bf16[2,2,3,48,576]{4,3,2,1,0:T(8,128)(2,1)S(1)}, u32[]{:S(2)}, u32[]{:S(2)}) %collective-permute-start.17) | collective-permute-done | bytes 663584 | tf_op jit(solution)/shard_map/ppermute | solution.py:46
  67.2 22.5 %feed.1 = (bf16[576,512]{1,0:T(8,128)(2,1)}, f32[512,576]{1,0:T(8,128)S(1)}, f32[8,576]{1,0:T(8,128)S(1)}, bf16[2,2,4,144,384]{4,3,2,1,0:T(8,128)(2,1)S(1)}, bf1...) custom-call(f32[512,576]{1,0:T(8,128)S(1)} %get-tuple-element.103.hi, ...), custom_call_target="tpu_custom_call" | custom-call | flops 190000000 | bytes 7096320 | tf_op jit(solution)/shard_map/feed/pallas_call | solution.py:639
  90.4 2.9 %back_0.1 = (bf16[512,256]{1,0:T(8,128)(2,1)S(1)}, bf16[512,64]{1,0:T(8,128)(2,1)S(1)}, bf16[192,576]{1,0:T(8,128)(2,1)S(1)}) custom-call(f32[512,512]{1,0:T(8,128)S(1)} %get-tuple-element.78.bias, f32[512,128]{1,0:T(8,128)S(1)} %get-tuple-element.80.cosine, f32[512,128]{1,0:T(8,128)S(1)} %get-tuple-element.81.sine, ...), custom_call_target="tpu_custom_call" | custom-call | flops 50000000 | bytes 548864 | tf_op jit(solution)/shard_map/back_0/pallas_call | solution.py:639
  93.2 1.7 collective-permute-done.18
  95.4 1.6 collective-permute-start.20
  97.3 1.7 collective-permute-start.28
  98.9 2.9 %back_1.1 = (bf16[512,256]{1,0:T(8,128)(2,1)S(1)}, bf16[512,64]{1,0:T(8,128)(2,1)S(1)}, bf16[192,576]{1,0:T(8,128)(2,1)S(1)}) custom-call(f32[512,512]{1,0:T(8,128)S(1)} %get-tuple-element.78.bias, f32[512,128]{1,0:T(8,128)S(1)} %get-tuple-element.80.cosine, f32[512,128]{1,0:T(8,128)S(1)} %get-tuple-element.81.sine, ...), custom_call_target="tpu_custom_call" | custom-call | flops 50000000 | bytes 548864 | tf_op jit(solution)/shard_map/back_1/pallas_call | solution.py:639
  101.8 3.1 %back_2.1 = (bf16[512,256]{1,0:T(8,128)(2,1)S(1)}, bf16[512,64]{1,0:T(8,128)(2,1)S(1)}, bf16[192,576]{1,0:T(8,128)(2,1)S(1)}) custom-call(f32[512,512]{1,0:T(8,128)S(1)} %get-tuple-element.78.bias, f32[512,128]{1,0:T(8,128)S(1)} %get-tuple-element.80.cosine, f32[512,128]{1,0:T(8,128)S(1)} %get-tuple-element.81.sine, ...), custom_call_target="tpu_custom_call" | custom-call | flops 50000000 | bytes 548864 | tf_op jit(solution)/shard_map/back_2/pallas_call | solution.py:639
  105.0 4.4 %back_last.1 = (bf16[576,512]{1,0:T(8,128)(2,1)}, bf16[2,2,4,80,384]{4,3,2,1,0:T(8,128)(2,1)S(1)}, bf16[2,2,4,80,384]{4,3,2,1,0:T(8,128)(2,1)S(1)}) custom-call(f32[512,576]{1,0:T(8,128)S(1)} %get-tuple-element.100.hidden_in, f32[8,576]{1,0:T(8,128)S(1)} %get-tuple-element.101.gains, bf16[640,1536]{1,0:T(8,128)(2,1)S(1)} %get-tuple-element.102.weights, ...), custom_call_target="tpu_custom_call" | custom-call | flops 60000000 | bytes 2555904 | tf_op jit(solution)/shard_map/back_last/pallas_call | solution.py:639
  109.4 0.9 collective-permute-done.28
  110.3 6.9 %collective-permute-done.20 = bf16[2,4,144,384]{3,2,1,0:T(8,128)(2,1)S(1)} collective-permute-done((bf16[2,4,144,384]{3,2,1,0:T(8,128)(2,1)S(1)}, bf16[2,4,144,384]{3,2,1,0:T(8,128)(2,1)S(1)}, u32[]{:S(2)}, u32[]{:S(2)}) %collective-permute-start.20) | collective-permute-done | bytes 884768 | tf_op jit(solution)/shard_map/ppermute | solution.py:46
  117.2 2.6 %collective-permute-done.29 = bf16[2,2,4,80,384]{4,3,2,1,0:T(8,128)(2,1)S(1)} collective-permute-done((bf16[2,2,4,80,384]{4,3,2,1,0:T(8,128)(2,1)S(1)}, bf16[2,2,4,80,384]{4,3,2,1,0:T(8,128)(2,1)S(1)}, u32[]{:S(2)}, u32[]{:S(2)}) %collective-permute-start.29) | collective-permute-done | bytes 983072 | tf_op jit(solution)/shard_map/ppermute | solution.py:46
  120.0 1.4 collective-permute-start.30
  121.6 1.8 %collective-permute-start.35 = (bf16[4,48,576]{2,1,0:T(8,128)(2,1)S(1)}, bf16[4,48,576]{2,1,0:T(8,128)(2,1)S(1)}, u32[]{:S(2)}, u32[]{:S(2)}) collective-permute-start(bf16[4,48,576]{2,1,0:T(8,128)(2,1)S(1)} %get-tuple-element.156), channel_id=1, source_target_pairs={{0,8},{4,12},{8,0},{12,4},{16,24},{20,28},{24,16},{28,20},{1,9},{5... | collective-permute-start | bytes 663560 | tf_op jit(solution)/shard_map/ppermute | solution.py:46
  123.4 6.0 %collective-permute-done.35 = bf16[4,48,576]{2,1,0:T(8,128)(2,1)S(1)} collective-permute-done((bf16[4,48,576]{2,1,0:T(8,128)(2,1)S(1)}, bf16[4,48,576]{2,1,0:T(8,128)(2,1)S(1)}, u32[]{:S(2)}, u32[]{:S(2)}) %collective-permute-start.35) | collective-permute-done | bytes 221216 | tf_op jit(solution)/shard_map/ppermute | solution.py:46
  129.4 2.5 %collective-permute-start.36 = (bf16[48,576]{1,0:T(8,128)(2,1)S(1)}, bf16[48,576]{1,0:T(8,128)(2,1)S(1)}, u32[]{:S(2)}, u32[]{:S(2)}) collective-permute-start(bf16[48,576]{1,0:T(8,128)(2,1)S(1)} %get-tuple-element.163), channel_id=1, source_target_pairs={{0,1},{1,2},{2,3},{3,0},{4,5},{5,6},{6,7},{7,4},{8,9},{9,10},{10,1... | collective-permute-start | bytes 165896 | tf_op jit(solution)/shard_map/ppermute | solution.py:54
  131.9 2.7 %collective-permute-start.38 = (bf16[48,576]{1,0:T(8,128)(2,1)S(1)}, bf16[48,576]{1,0:T(8,128)(2,1)S(1)}, u32[]{:S(2)}, u32[]{:S(2)}) collective-permute-start(bf16[48,576]{1,0:T(8,128)(2,1)S(1)} %get-tuple-element.164), channel_id=1, source_target_pairs={{0,3},{1,0},{2,1},{3,2},{4,7},{5,4},{6,5},{7,6},{8,11},{9,8},{10,9... | collective-permute-start | bytes 165896 | tf_op jit(solution)/shard_map/ppermute | solution.py:54
  135.2 1.6 collective-permute-start.31
  137.6 2.7 %collective-permute-done.37 = bf16[48,576]{1,0:T(8,128)(2,1)S(1)} collective-permute-done((bf16[48,576]{1,0:T(8,128)(2,1)S(1)}, bf16[48,576]{1,0:T(8,128)(2,1)S(1)}, u32[]{:S(2)}, u32[]{:S(2)}) %collective-permute-start.37) | collective-permute-done | bytes 55328 | tf_op jit(solution)/shard_map/ppermute | solution.py:54
  140.4 1.2 collective-permute-done.31
  141.6 2.0 %collective-permute-start.32 = (bf16[80,384]{1,0:T(8,128)(2,1)S(1)}, bf16[80,384]{1,0:T(8,128)(2,1)S(1)}, u32[]{:S(2)}, u32[]{:S(2)}) collective-permute-start(bf16[80,384]{1,0:T(8,128)(2,1)S(1)} %get-tuple-element.160), channel_id=1, source_target_pairs={{0,1},{1,2},{2,3},{3,0},{4,5},{5,6},{6,7},{7,4},{8,9},{9,10},{10,1... | collective-permute-start | bytes 184328 | tf_op jit(solution)/shard_map/ppermute | solution.py:54
  143.6 2.3 %collective-permute-start.34 = (bf16[80,384]{1,0:T(8,128)(2,1)S(1)}, bf16[80,384]{1,0:T(8,128)(2,1)S(1)}, u32[]{:S(2)}, u32[]{:S(2)}) collective-permute-start(bf16[80,384]{1,0:T(8,128)(2,1)S(1)} %get-tuple-element.161), channel_id=1, source_target_pairs={{0,3},{1,0},{2,1},{3,2},{4,7},{5,4},{6,5},{7,6},{8,11},{9,8},{10,9... | collective-permute-start | bytes 184328 | tf_op jit(solution)/shard_map/ppermute | solution.py:54
  146.4 0.9 collective-permute-done.21
  147.4 1.8 %collective-permute-start.22 = (bf16[144,384]{1,0:T(8,128)(2,1)S(1)}, bf16[144,384]{1,0:T(8,128)(2,1)S(1)}, u32[]{:S(2)}, u32[]{:S(2)}) collective-permute-start(bf16[144,384]{1,0:T(8,128)(2,1)S(1)} %get-tuple-element.157), channel_id=1, source_target_pairs={{0,1},{1,2},{2,3},{3,0},{4,5},{5,6},{6,7},{7,4},{8,9},{9,10},{10,1... | collective-permute-start | bytes 331784 | tf_op jit(solution)/shard_map/ppermute | solution.py:54
  149.2 2.3 %collective-permute-start.24 = (bf16[144,384]{1,0:T(8,128)(2,1)S(1)}, bf16[144,384]{1,0:T(8,128)(2,1)S(1)}, u32[]{:S(2)}, u32[]{:S(2)}) collective-permute-start(bf16[144,384]{1,0:T(8,128)(2,1)S(1)} %get-tuple-element.158), channel_id=1, source_target_pairs={{0,3},{1,0},{2,1},{3,2},{4,7},{5,4},{6,5},{7,6},{8,11},{9,8},{10,9... | collective-permute-start | bytes 331784 | tf_op jit(solution)/shard_map/ppermute | solution.py:54
  152.0 1.2 collective-permute-done.33
  153.3 3.0 %collective-permute-start.39 = (bf16[176,384]{1,0:T(8,128)(2,1)S(1)}, bf16[176,384]{1,0:T(8,128)(2,1)S(1)}, u32[]{:S(2)}, u32[]{:S(2)}) collective-permute-start(bf16[176,384]{1,0:T(8,128)(2,1)S(1)} %get-tuple-element.173), channel_id=1, source_target_pairs={{0,8},{4,12},{8,0},{12,4},{16,24},{20,28},{24,16},{28,20},{1,9},{5... | collective-permute-start | bytes 405512 | tf_op jit(solution)/shard_map/ppermute | solution.py:46
  156.3 4.5 %collective-permute-done.23 = bf16[144,384]{1,0:T(8,128)(2,1)S(1)} collective-permute-done((bf16[144,384]{1,0:T(8,128)(2,1)S(1)}, bf16[144,384]{1,0:T(8,128)(2,1)S(1)}, u32[]{:S(2)}, u32[]{:S(2)}) %collective-permute-start.23) | collective-permute-done | bytes 110624 | tf_op jit(solution)/shard_map/ppermute | solution.py:54
  160.9 1.5 collective-permute-start.25
  162.5 0.7 collective-permute-start.40
  163.1 3.8 %collective-permute-done.25 = bf16[144,384]{1,0:T(8,128)(2,1)S(1)} collective-permute-done((bf16[144,384]{1,0:T(8,128)(2,1)S(1)}, bf16[144,384]{1,0:T(8,128)(2,1)S(1)}, u32[]{:S(2)}, u32[]{:S(2)}) %collective-permute-start.25) | collective-permute-done | bytes 110624 | tf_op jit(solution)/shard_map/ppermute | solution.py:46
  167.0 1.1 collective-permute-start.26
  168.1 3.1 %collective-permute-done.40 = bf16[2,176,384]{2,1,0:T(8,128)(2,1)S(1)} collective-permute-done((bf16[2,176,384]{2,1,0:T(8,128)(2,1)S(1)}, bf16[2,176,384]{2,1,0:T(8,128)(2,1)S(1)}, u32[]{:S(2)}, u32[]{:S(2)}) %collective-permute-start.40) | collective-permute-done | bytes 270368 | tf_op jit(solution)/shard_map/ppermute | solution.py:46
  171.3 1.7 collective-permute-done.26
  173.2 1.8 collective-permute-done.27.pair_other
  174.9 3.1 %finish.1 = (f32[144,576]{1,0:T(8,128)}, f32[144,192]{1,0:T(8,128)}, f32[144,192]{1,0:T(8,128)}, f32[144,576]{1,0:T(8,128)}, f32[1,144]{1,0:T(1,128)}, /*index=5...) custom-call(bf16[2,2,144,384]{3,2,1,0:T(8,128)(2,1)S(1)} %pad_maximum_fusion.5.pair_pieces, ...), custom_call_target="tpu_custom_call" | custom-call | flops 50000000 | bytes 3540096 | tf_op jit(solution)/shard_map/finish/pallas_call | solution.py:639
  (83 shorter events, 8.9 us)
Async XLA Ops:
  0.6 11.7 %copy-start.6 = (f32[520,128]{1,0:T(8,128)S(1)}, f32[520,128]{1,0:T(8,128)}, u32[]{:S(2)}) copy-start(f32[520,128]{1,0:T(8,128)} %constant.8.clone.table_sin) | copy-start | bytes 798724
  0.7 11.7 %copy-start.7 = (f32[520,128]{1,0:T(8,128)S(1)}, f32[520,128]{1,0:T(8,128)}, u32[]{:S(2)}) copy-start(f32[520,128]{1,0:T(8,128)} %constant.7.clone.table_cos) | copy-start | bytes 798724
  0.7 11.7 %copy-start.8 = (s32[1,4]{1,0:T(1,128)S(1)}, s32[1,4]{1,0:T(1,128)}, u32[]{:S(2)}) copy-start(s32[1,4]{1,0:T(1,128)} %lengths.3) | copy-start | bytes 52
  0.7 11.7 %copy-start.3 = (bf16[512,576]{0,1:T(8,128)(2,1)S(1)}, bf16[512,576]{0,1:T(8,128)(2,1)}, u32[]{:S(2)}) copy-start(bf16[512,576]{0,1:T(8,128)(2,1)} %param.25) | copy-start | bytes 1769476
  0.7 11.7 %copy-start.2 = (bf16[512,576]{0,1:T(8,128)(2,1)S(1)}, bf16[512,576]{0,1:T(8,128)(2,1)}, u32[]{:S(2)}) copy-start(bf16[512,576]{0,1:T(8,128)(2,1)} %param.14) | copy-start | bytes 1769476
  5.4 12.5 %copy-start.9 = (bf16[48,576]{1,0:T(8,128)(2,1)S(1)}, bf16[48,576]{1,0:T(8,128)(2,1)}, u32[]{:S(2)}) copy-start(bf16[48,576]{1,0:T(8,128)(2,1)} %get-tuple-element.88) | copy-start | bytes 165892
  5.4 9.6 %collective-permute-start.2 = (bf16[80,384]{1,0:T(8,128)(2,1)}, bf16[80,384]{1,0:T(8,128)(2,1)S(1)}, u32[]{:S(2)}, u32[]{:S(2)}) collective-permute-start(bf16[80,384]{1,0:T(8,128)(2,1)} %get-tuple-element.83), channel_id=1, source_target_pairs={{3,0},{0,1},{1,2},{2,3},{7,4},{4,5},{5,6},{6,7},{11,8},{8,9},{9,10... | collective-permute-start | bytes 184328 | tf_op jit(solution)/shard_map/ppermute | solution.py:50
  8.4 9.4 %collective-permute-start.1 = (bf16[80,384]{1,0:T(8,128)(2,1)}, bf16[80,384]{1,0:T(8,128)(2,1)S(1)}, u32[]{:S(2)}, u32[]{:S(2)}) collective-permute-start(bf16[80,384]{1,0:T(8,128)(2,1)} %get-tuple-element.83), channel_id=1, source_target_pairs={{2,0},{3,1},{0,2},{1,3},{6,4},{7,5},{4,6},{5,7},{10,8},{11,9},{8,1... | collective-permute-start | bytes 184328 | tf_op jit(solution)/shard_map/ppermute | solution.py:50
  11.0 6.8 %collective-permute-start = (bf16[80,384]{1,0:T(8,128)(2,1)}, bf16[80,384]{1,0:T(8,128)(2,1)S(1)}, u32[]{:S(2)}, u32[]{:S(2)}) collective-permute-start(bf16[80,384]{1,0:T(8,128)(2,1)} %get-tuple-element.83), channel_id=1, source_target_pairs={{1,0},{2,1},{3,2},{0,3},{5,4},{6,5},{7,6},{4,7},{9,8},{10,9},{11,1... | collective-permute-start | bytes 184328 | tf_op jit(solution)/shard_map/ppermute | solution.py:50
  14.0 8.1 %collective-permute-start.6 = (bf16[144,384]{1,0:T(8,128)(2,1)}, bf16[144,384]{1,0:T(8,128)(2,1)S(1)}, u32[]{:S(2)}, u32[]{:S(2)}) collective-permute-start(bf16[144,384]{1,0:T(8,128)(2,1)} %get-tuple-element.86), channel_id=1, source_target_pairs={{3,0},{0,1},{1,2},{2,3},{7,4},{4,5},{5,6},{6,7},{11,8},{8,9},{9,10... | collective-permute-start | bytes 331784 | tf_op jit(solution)/shard_map/ppermute | solution.py:50
  14.7 11.5 %collective-permute-start.5 = (bf16[144,384]{1,0:T(8,128)(2,1)}, bf16[144,384]{1,0:T(8,128)(2,1)S(1)}, u32[]{:S(2)}, u32[]{:S(2)}) collective-permute-start(bf16[144,384]{1,0:T(8,128)(2,1)} %get-tuple-element.86), channel_id=1, source_target_pairs={{2,0},{3,1},{0,2},{1,3},{6,4},{7,5},{4,6},{5,7},{10,8},{11,9},{8,1... | collective-permute-start | bytes 331784 | tf_op jit(solution)/shard_map/ppermute | solution.py:50
  15.0 12.7 %collective-permute-start.4 = (bf16[144,384]{1,0:T(8,128)(2,1)}, bf16[144,384]{1,0:T(8,128)(2,1)S(1)}, u32[]{:S(2)}, u32[]{:S(2)}) collective-permute-start(bf16[144,384]{1,0:T(8,128)(2,1)} %get-tuple-element.86), channel_id=1, source_target_pairs={{1,0},{2,1},{3,2},{0,3},{5,4},{6,5},{7,6},{4,7},{9,8},{10,9},{11,1... | collective-permute-start | bytes 331784 | tf_op jit(solution)/shard_map/ppermute | solution.py:50
  17.9 10.5 %collective-permute-start.9 = (bf16[48,576]{1,0:T(8,128)(2,1)S(1)}, bf16[48,576]{1,0:T(8,128)(2,1)S(1)}, u32[]{:S(2)}, u32[]{:S(2)}) collective-permute-start(bf16[48,576]{1,0:T(8,128)(2,1)S(1)} %copy-done.9), channel_id=1, source_target_pairs={{3,0},{0,1},{1,2},{2,3},{7,4},{4,5},{5,6},{6,7},{11,8},{8,9},{9,10... | collective-permute-start | bytes 165896 | tf_op jit(solution)/shard_map/ppermute | solution.py:50
  18.5 12.7 %collective-permute-start.8 = (bf16[48,576]{1,0:T(8,128)(2,1)S(1)}, bf16[48,576]{1,0:T(8,128)(2,1)S(1)}, u32[]{:S(2)}, u32[]{:S(2)}) collective-permute-start(bf16[48,576]{1,0:T(8,128)(2,1)S(1)} %copy-done.9), channel_id=1, source_target_pairs={{2,0},{3,1},{0,2},{1,3},{6,4},{7,5},{4,6},{5,7},{10,8},{11,9},{8,1... | collective-permute-start | bytes 165896 | tf_op jit(solution)/shard_map/ppermute | solution.py:50
  22.1 9.2 %collective-permute-start.7 = (bf16[48,576]{1,0:T(8,128)(2,1)S(1)}, bf16[48,576]{1,0:T(8,128)(2,1)S(1)}, u32[]{:S(2)}, u32[]{:S(2)}) collective-permute-start(bf16[48,576]{1,0:T(8,128)(2,1)S(1)} %copy-done.9), channel_id=1, source_target_pairs={{1,0},{2,1},{3,2},{0,3},{5,4},{6,5},{7,6},{4,7},{9,8},{10,9},{11,1... | collective-permute-start | bytes 165896 | tf_op jit(solution)/shard_map/ppermute | solution.py:50
  26.2 7.6 %collective-permute-start.3 = (bf16[3,80,384]{2,1,0:T(8,128)(2,1)S(1)}, bf16[3,80,384]{2,1,0:T(8,128)(2,1)S(1)}, u32[]{:S(2)}, u32[]{:S(2)}) collective-permute-start(bf16[3,80,384]{2,1,0:T(8,128)(2,1)S(1)} %pad_maximum_fusion.11), channel_id=1, source_target_pairs={{0,16},{4,20},{8,24},{12,28},{16,0},{20,4},{24,8},{28,12},{1,17},{... | collective-permute-start | bytes 552968 | tf_op jit(solution)/shard_map/ppermute | solution.py:46
  27.8 10.3 %collective-permute-start.11 = (bf16[3,144,384]{2,1,0:T(8,128)(2,1)S(1)}, bf16[3,144,384]{2,1,0:T(8,128)(2,1)S(1)}, u32[]{:S(2)}, u32[]{:S(2)}) collective-permute-start(bf16[3,144,384]{2,1,0:T(8,128)(2,1)S(1)} %get-tuple-element.167), channel_id=1, source_target_pairs={{0,16},{4,20},{8,24},{12,28},{16,0},{20,4},{24,8},{28,12},{1,17},{... | collective-permute-start | bytes 995336 | tf_op jit(solution)/shard_map/ppermute | solution.py:46
  33.8 10.0 %copy-start.4 = (bf16[160,1536]{1,0:T(8,128)(2,1)S(1)}, bf16[160,1536]{1,0:T(8,128)(2,1)}, u32[]{:S(2)}) copy-start(bf16[160,1536]{1,0:T(8,128)(2,1)} %get-tuple-element.82.own) | copy-start | bytes 1474564
  33.9 7.6 %collective-permute-start.10 = (bf16[2,3,80,384]{3,2,1,0:T(8,128)(2,1)S(1)}, bf16[2,3,80,384]{3,2,1,0:T(8,128)(2,1)S(1)}, u32[]{:S(2)}, u32[]{:S(2)}) collective-permute-start(bf16[2,3,80,384]{3,2,1,0:T(8,128)(2,1)S(1)} %pad_maximum_fusion.6), channel_id=1, source_target_pairs={{0,8},{4,12},{8,0},{12,4},{16,24},{20,28},{24,16},{28,20},{1,9},{5... | collective-permute-start | bytes 1105928 | tf_op jit(solution)/shard_map/ppermute | solution.py:46
  41.5 2.3 %collective-permute-start.12 = (bf16[2,2,3,80,384]{4,3,2,1,0:T(8,128)(2,1)S(1)}, bf16[2,2,3,80,384]{4,3,2,1,0:T(8,128)(2,1)S(1)}, u32[]{:S(2)}, u32[]{:S(2)}) collective-permute-start(bf16[2,2,3,80,384]{4,3,2,1,0:T(8,128)(2,1)S(1)} %pad_maximum_fusion.1.pieces), channel_id=1, source_target_pairs={{0,4},{4,0},{8,12},{12,8},{16,20},{20,16},{24,28},{28,24},{1,5},{5... | collective-permute-start | bytes 2211848 | tf_op jit(solution)/shard_map/ppermute | solution.py:46
  41.6 7.5 %collective-permute-start.13 = (bf16[3,48,576]{2,1,0:T(8,128)(2,1)S(1)}, bf16[3,48,576]{2,1,0:T(8,128)(2,1)S(1)}, u32[]{:S(2)}, u32[]{:S(2)}) collective-permute-start(bf16[3,48,576]{2,1,0:T(8,128)(2,1)S(1)} %pad_maximum_fusion.12), channel_id=1, source_target_pairs={{0,8},{4,12},{8,0},{12,4},{16,24},{20,28},{24,16},{28,20},{1,9},{5... | collective-permute-start | bytes 497672 | tf_op jit(solution)/shard_map/ppermute | solution.py:46
  43.2 19.7 %collective-permute-start.15 = (bf16[2,3,144,384]{3,2,1,0:T(8,128)(2,1)S(1)}, bf16[2,3,144,384]{3,2,1,0:T(8,128)(2,1)S(1)}, u32[]{:S(2)}, u32[]{:S(2)}) collective-permute-start(bf16[2,3,144,384]{3,2,1,0:T(8,128)(2,1)S(1)} %pad_maximum_fusion.3), channel_id=1, source_target_pairs={{0,8},{4,12},{8,0},{12,4},{16,24},{20,28},{24,16},{28,20},{1,9},{5... | collective-permute-start | bytes 1990664 | tf_op jit(solution)/shard_map/ppermute | solution.py:46
  49.2 9.8 %collective-permute-start.14 = (bf16[2,3,48,576]{3,2,1,0:T(8,128)(2,1)S(1)}, bf16[2,3,48,576]{3,2,1,0:T(8,128)(2,1)S(1)}, u32[]{:S(2)}, u32[]{:S(2)}) collective-permute-start(bf16[2,3,48,576]{3,2,1,0:T(8,128)(2,1)S(1)} %pad_maximum_fusion.7), channel_id=1, source_target_pairs={{0,16},{4,20},{8,24},{12,28},{16,0},{20,4},{24,8},{28,12},{1,17},{... | collective-permute-start | bytes 995336 | tf_op jit(solution)/shard_map/ppermute | solution.py:46
  61.7 5.5 %copy-start = (bf16[144,1536]{1,0:T(8,128)(2,1)S(1)}, bf16[144,1536]{1,0:T(8,128)(2,1)}, u32[]{:S(2)}) copy-start(bf16[144,1536]{1,0:T(8,128)(2,1)} %own_gate.1) | copy-start | bytes 1327108
  61.8 5.5 %copy-start.1 = (bf16[144,1536]{1,0:T(8,128)(2,1)S(1)}, bf16[144,1536]{1,0:T(8,128)(2,1)}, u32[]{:S(2)}) copy-start(bf16[144,1536]{1,0:T(8,128)(2,1)} %own_up.1) | copy-start | bytes 1327108
  61.8 5.5 %copy-start.5 = (bf16[384,576]{1,0:T(8,128)(2,1)S(1)}, bf16[384,576]{1,0:T(8,128)(2,1)}, u32[]{:S(2)}) copy-start(bf16[384,576]{1,0:T(8,128)(2,1)} %get-tuple-element.106.own_down) | copy-start | bytes 1327108
  63.0 4.2 %collective-permute-start.16 = (bf16[2,2,3,144,384]{4,3,2,1,0:T(8,128)(2,1)S(1)}, bf16[2,2,3,144,384]{4,3,2,1,0:T(8,128)(2,1)S(1)}, u32[]{:S(2)}, u32[]{:S(2)}) collective-permute-start(bf16[2,2,3,144,384]{4,3,2,1,0:T(8,128)(2,1)S(1)} %pad_maximum_fusion.pair_pieces), channel_id=1, source_target_pairs={{0,4},{4,0},{8,12},{12,8},{16,20},{20,16},{24,28},{28,24},{1,5},{5... | collective-permute-start | bytes 3981320 | tf_op jit(solution)/shard_map/ppermute | solution.py:46
  63.1 4.1 %collective-permute-start.17 = (bf16[2,2,3,48,576]{4,3,2,1,0:T(8,128)(2,1)S(1)}, bf16[2,2,3,48,576]{4,3,2,1,0:T(8,128)(2,1)S(1)}, u32[]{:S(2)}, u32[]{:S(2)}) collective-permute-start(bf16[2,2,3,48,576]{4,3,2,1,0:T(8,128)(2,1)S(1)} %pad_maximum_fusion.2.down_pieces), channel_id=1, source_target_pairs={{0,4},{4,0},{8,12},{12,8},{16,20},{20,16},{24,28},{28,24},{1,5},{5... | collective-permute-start | bytes 1990664 | tf_op jit(solution)/shard_map/ppermute | solution.py:46
  89.8 5.2 %collective-permute-start.18 = (bf16[2,2,4,144,384]{4,3,2,1,0:T(8,128)(2,1)}, bf16[2,2,4,144,384]{4,3,2,1,0:T(8,128)(2,1)S(1)}, u32[]{:S(2)}, u32[]{:S(2)}) collective-permute-start(bf16[2,2,4,144,384]{4,3,2,1,0:T(8,128)(2,1)} %get-tuple-element.110), channel_id=1, source_target_pairs={{0,4},{4,0},{8,12},{12,8},{16,20},{20,16},{24,28},{28,24},{1,5},{5... | collective-permute-start | bytes 5308424 | tf_op jit(solution)/shard_map/ppermute | solution.py:46
  90.0 7.0 %collective-permute-start.19 = (bf16[2,2,4,48,576]{4,3,2,1,0:T(8,128)(2,1)S(1)}, bf16[2,2,4,48,576]{4,3,2,1,0:T(8,128)(2,1)S(1)}, u32[]{:S(2)}, u32[]{:S(2)}) collective-permute-start(bf16[2,2,4,48,576]{4,3,2,1,0:T(8,128)(2,1)S(1)} %get-tuple-element.111), channel_id=1, source_target_pairs={{0,4},{4,0},{8,12},{12,8},{16,20},{20,16},{24,28},{28,24},{1,5},{5... | collective-permute-start | bytes 2654216 | tf_op jit(solution)/shard_map/ppermute | solution.py:46
  95.4 21.8 %collective-permute-start.20 = (bf16[2,4,144,384]{3,2,1,0:T(8,128)(2,1)S(1)}, bf16[2,4,144,384]{3,2,1,0:T(8,128)(2,1)S(1)}, u32[]{:S(2)}, u32[]{:S(2)}) collective-permute-start(bf16[2,4,144,384]{3,2,1,0:T(8,128)(2,1)S(1)} %get-tuple-element.146), channel_id=1, source_target_pairs={{0,8},{4,12},{8,0},{12,4},{16,24},{20,28},{24,16},{28,20},{1,9},{5... | collective-permute-start | bytes 2654216 | tf_op jit(solution)/shard_map/ppermute | solution.py:46
  97.3 13.0 %collective-permute-start.28 = (bf16[2,4,48,576]{3,2,1,0:T(8,128)(2,1)S(1)}, bf16[2,4,48,576]{3,2,1,0:T(8,128)(2,1)S(1)}, u32[]{:S(2)}, u32[]{:S(2)}) collective-permute-start(bf16[2,4,48,576]{3,2,1,0:T(8,128)(2,1)S(1)} %get-tuple-element.149), channel_id=1, source_target_pairs={{0,16},{4,20},{8,24},{12,28},{16,0},{20,4},{24,8},{28,12},{1,17},{... | collective-permute-start | bytes 1327112 | tf_op jit(solution)/shard_map/ppermute | solution.py:46
  117.2 2.6 %collective-permute-start.29 = (bf16[2,2,4,80,384]{4,3,2,1,0:T(8,128)(2,1)S(1)}, bf16[2,2,4,80,384]{4,3,2,1,0:T(8,128)(2,1)S(1)}, u32[]{:S(2)}, u32[]{:S(2)}) collective-permute-start(bf16[2,2,4,80,384]{4,3,2,1,0:T(8,128)(2,1)S(1)} %get-tuple-element.134), channel_id=1, source_target_pairs={{0,4},{4,0},{8,12},{12,8},{16,20},{20,16},{24,28},{28,24},{1,5},{5... | collective-permute-start | bytes 2949128 | tf_op jit(solution)/shard_map/ppermute | solution.py:46
  120.0 15.1 %collective-permute-start.30 = (bf16[2,4,80,384]{3,2,1,0:T(8,128)(2,1)S(1)}, bf16[2,4,80,384]{3,2,1,0:T(8,128)(2,1)S(1)}, u32[]{:S(2)}, u32[]{:S(2)}) collective-permute-start(bf16[2,4,80,384]{3,2,1,0:T(8,128)(2,1)S(1)} %get-tuple-element.148), channel_id=1, source_target_pairs={{0,16},{4,20},{8,24},{12,28},{16,0},{20,4},{24,8},{28,12},{1,17},{... | collective-permute-start | bytes 1474568 | tf_op jit(solution)/shard_map/ppermute | solution.py:46
  121.6 7.8 %collective-permute-start.35 = (bf16[4,48,576]{2,1,0:T(8,128)(2,1)S(1)}, bf16[4,48,576]{2,1,0:T(8,128)(2,1)S(1)}, u32[]{:S(2)}, u32[]{:S(2)}) collective-permute-start(bf16[4,48,576]{2,1,0:T(8,128)(2,1)S(1)} %get-tuple-element.156), channel_id=1, source_target_pairs={{0,8},{4,12},{8,0},{12,4},{16,24},{20,28},{24,16},{28,20},{1,9},{5... | collective-permute-start | bytes 663560 | tf_op jit(solution)/shard_map/ppermute | solution.py:46
  129.4 8.2 %collective-permute-start.36 = (bf16[48,576]{1,0:T(8,128)(2,1)S(1)}, bf16[48,576]{1,0:T(8,128)(2,1)S(1)}, u32[]{:S(2)}, u32[]{:S(2)}) collective-permute-start(bf16[48,576]{1,0:T(8,128)(2,1)S(1)} %get-tuple-element.163), channel_id=1, source_target_pairs={{0,1},{1,2},{2,3},{3,0},{4,5},{5,6},{6,7},{7,4},{8,9},{9,10},{10,1... | collective-permute-start | bytes 165896 | tf_op jit(solution)/shard_map/ppermute | solution.py:54
  131.9 5.7 %collective-permute-start.38 = (bf16[48,576]{1,0:T(8,128)(2,1)S(1)}, bf16[48,576]{1,0:T(8,128)(2,1)S(1)}, u32[]{:S(2)}, u32[]{:S(2)}) collective-permute-start(bf16[48,576]{1,0:T(8,128)(2,1)S(1)} %get-tuple-element.164), channel_id=1, source_target_pairs={{0,3},{1,0},{2,1},{3,2},{4,7},{5,4},{6,5},{7,6},{8,11},{9,8},{10,9... | collective-permute-start | bytes 165896 | tf_op jit(solution)/shard_map/ppermute | solution.py:54
  134.6 5.7 %collective-permute-start.37 = (bf16[48,576]{1,0:T(8,128)(2,1)S(1)}, bf16[48,576]{1,0:T(8,128)(2,1)S(1)}, u32[]{:S(2)}, u32[]{:S(2)}) collective-permute-start(bf16[48,576]{1,0:T(8,128)(2,1)S(1)} %get-tuple-element.165), channel_id=1, source_target_pairs={{0,2},{1,3},{2,0},{3,1},{4,6},{5,7},{6,4},{7,5},{8,10},{9,11},{10,... | collective-permute-start | bytes 165896 | tf_op jit(solution)/shard_map/ppermute | solution.py:54
  135.2 6.4 %collective-permute-start.31 = (bf16[4,80,384]{2,1,0:T(8,128)(2,1)S(1)}, bf16[4,80,384]{2,1,0:T(8,128)(2,1)S(1)}, u32[]{:S(2)}, u32[]{:S(2)}) collective-permute-start(bf16[4,80,384]{2,1,0:T(8,128)(2,1)S(1)} %get-tuple-element.154), channel_id=1, source_target_pairs={{0,8},{4,12},{8,0},{12,4},{16,24},{20,28},{24,16},{28,20},{1,9},{5... | collective-permute-start | bytes 737288 | tf_op jit(solution)/shard_map/ppermute | solution.py:46
  137.0 10.3 %collective-permute-start.21 = (bf16[4,144,384]{2,1,0:T(8,128)(2,1)S(1)}, bf16[4,144,384]{2,1,0:T(8,128)(2,1)S(1)}, u32[]{:S(2)}, u32[]{:S(2)}) collective-permute-start(bf16[4,144,384]{2,1,0:T(8,128)(2,1)S(1)} %get-tuple-element.152), channel_id=1, source_target_pairs={{0,16},{4,20},{8,24},{12,28},{16,0},{20,4},{24,8},{28,12},{1,17},{... | collective-permute-start | bytes 1327112 | tf_op jit(solution)/shard_map/ppermute | solution.py:46
  141.6 9.9 %collective-permute-start.32 = (bf16[80,384]{1,0:T(8,128)(2,1)S(1)}, bf16[80,384]{1,0:T(8,128)(2,1)S(1)}, u32[]{:S(2)}, u32[]{:S(2)}) collective-permute-start(bf16[80,384]{1,0:T(8,128)(2,1)S(1)} %get-tuple-element.160), channel_id=1, source_target_pairs={{0,1},{1,2},{2,3},{3,0},{4,5},{5,6},{6,7},{7,4},{8,9},{9,10},{10,1... | collective-permute-start | bytes 184328 | tf_op jit(solution)/shard_map/ppermute | solution.py:54
  143.6 8.4 %collective-permute-start.34 = (bf16[80,384]{1,0:T(8,128)(2,1)S(1)}, bf16[80,384]{1,0:T(8,128)(2,1)S(1)}, u32[]{:S(2)}, u32[]{:S(2)}) collective-permute-start(bf16[80,384]{1,0:T(8,128)(2,1)S(1)} %get-tuple-element.161), channel_id=1, source_target_pairs={{0,3},{1,0},{2,1},{3,2},{4,7},{5,4},{6,5},{7,6},{8,11},{9,8},{10,9... | collective-permute-start | bytes 184328 | tf_op jit(solution)/shard_map/ppermute | solution.py:54
  145.9 7.4 %collective-permute-start.33 = (bf16[80,384]{1,0:T(8,128)(2,1)S(1)}, bf16[80,384]{1,0:T(8,128)(2,1)S(1)}, u32[]{:S(2)}, u32[]{:S(2)}) collective-permute-start(bf16[80,384]{1,0:T(8,128)(2,1)S(1)} %get-tuple-element.162), channel_id=1, source_target_pairs={{0,2},{1,3},{2,0},{3,1},{4,6},{5,7},{6,4},{7,5},{8,10},{9,11},{10,... | collective-permute-start | bytes 184328 | tf_op jit(solution)/shard_map/ppermute | solution.py:54
  147.4 8.9 %collective-permute-start.22 = (bf16[144,384]{1,0:T(8,128)(2,1)S(1)}, bf16[144,384]{1,0:T(8,128)(2,1)S(1)}, u32[]{:S(2)}, u32[]{:S(2)}) collective-permute-start(bf16[144,384]{1,0:T(8,128)(2,1)S(1)} %get-tuple-element.157), channel_id=1, source_target_pairs={{0,1},{1,2},{2,3},{3,0},{4,5},{5,6},{6,7},{7,4},{8,9},{9,10},{10,1... | collective-permute-start | bytes 331784 | tf_op jit(solution)/shard_map/ppermute | solution.py:54
  149.2 7.2 %collective-permute-start.24 = (bf16[144,384]{1,0:T(8,128)(2,1)S(1)}, bf16[144,384]{1,0:T(8,128)(2,1)S(1)}, u32[]{:S(2)}, u32[]{:S(2)}) collective-permute-start(bf16[144,384]{1,0:T(8,128)(2,1)S(1)} %get-tuple-element.158), channel_id=1, source_target_pairs={{0,3},{1,0},{2,1},{3,2},{4,7},{5,4},{6,5},{7,6},{8,11},{9,8},{10,9... | collective-permute-start | bytes 331784 | tf_op jit(solution)/shard_map/ppermute | solution.py:54
  151.5 9.3 %collective-permute-start.23 = (bf16[144,384]{1,0:T(8,128)(2,1)S(1)}, bf16[144,384]{1,0:T(8,128)(2,1)S(1)}, u32[]{:S(2)}, u32[]{:S(2)}) collective-permute-start(bf16[144,384]{1,0:T(8,128)(2,1)S(1)} %get-tuple-element.159), channel_id=1, source_target_pairs={{0,2},{1,3},{2,0},{3,1},{4,6},{5,7},{6,4},{7,5},{8,10},{9,11},{10,... | collective-permute-start | bytes 331784 | tf_op jit(solution)/shard_map/ppermute | solution.py:54
  153.3 9.1 %collective-permute-start.39 = (bf16[176,384]{1,0:T(8,128)(2,1)S(1)}, bf16[176,384]{1,0:T(8,128)(2,1)S(1)}, u32[]{:S(2)}, u32[]{:S(2)}) collective-permute-start(bf16[176,384]{1,0:T(8,128)(2,1)S(1)} %get-tuple-element.173), channel_id=1, source_target_pairs={{0,8},{4,12},{8,0},{12,4},{16,24},{20,28},{24,16},{28,20},{1,9},{5... | collective-permute-start | bytes 405512 | tf_op jit(solution)/shard_map/ppermute | solution.py:46
  160.9 6.1 %collective-permute-start.25 = (bf16[144,384]{1,0:T(8,128)(2,1)S(1)}, bf16[144,384]{1,0:T(8,128)(2,1)S(1)}, u32[]{:S(2)}, u32[]{:S(2)}) collective-permute-start(bf16[144,384]{1,0:T(8,128)(2,1)S(1)} %fusion.20), channel_id=1, source_target_pairs={{0,16},{4,20},{8,24},{12,28},{16,0},{20,4},{24,8},{28,12},{1,17},{... | collective-permute-start | bytes 331784 | tf_op jit(solution)/shard_map/ppermute | solution.py:46
  162.5 8.7 %collective-permute-start.40 = (bf16[2,176,384]{2,1,0:T(8,128)(2,1)S(1)}, bf16[2,176,384]{2,1,0:T(8,128)(2,1)S(1)}, u32[]{:S(2)}, u32[]{:S(2)}) collective-permute-start(bf16[2,176,384]{2,1,0:T(8,128)(2,1)S(1)} %get-tuple-element.169), channel_id=1, source_target_pairs={{0,16},{4,20},{8,24},{12,28},{16,0},{20,4},{24,8},{28,12},{1,17},{... | collective-permute-start | bytes 811016 | tf_op jit(solution)/shard_map/ppermute | solution.py:46
  167.0 6.0 %collective-permute-start.26 = (bf16[2,144,384]{2,1,0:T(8,128)(2,1)S(1)}, bf16[2,144,384]{2,1,0:T(8,128)(2,1)S(1)}, u32[]{:S(2)}, u32[]{:S(2)}) collective-permute-start(bf16[2,144,384]{2,1,0:T(8,128)(2,1)S(1)} %get-tuple-element.171), channel_id=1, source_target_pairs={{0,8},{4,12},{8,0},{12,4},{16,24},{20,28},{24,16},{28,20},{1,9},{5... | collective-permute-start | bytes 663560 | tf_op jit(solution)/shard_map/ppermute | solution.py:46
  171.2 3.7 %collective-permute-start.41 = (bf16[2,2,176,384]{3,2,1,0:T(8,128)(2,1)S(1)}, bf16[2,2,176,384]{3,2,1,0:T(8,128)(2,1)S(1)}, u32[]{:S(2)}, u32[]{:S(2)}) collective-permute-start(bf16[2,2,176,384]{3,2,1,0:T(8,128)(2,1)S(1)} %pad_maximum_fusion.4.rest_pieces), channel_id=1, source_target_pairs={{0,4},{4,0},{8,12},{12,8},{16,20},{20,16},{24,28},{28,24},{1,5},{5... | collective-permute-start | bytes 1622024 | tf_op jit(solution)/shard_map/ppermute | solution.py:46
  173.1 1.9 %collective-permute-start.27 = (bf16[2,2,144,384]{3,2,1,0:T(8,128)(2,1)S(1)}, bf16[2,2,144,384]{3,2,1,0:T(8,128)(2,1)S(1)}, u32[]{:S(2)}, u32[]{:S(2)}) collective-permute-start(bf16[2,2,144,384]{3,2,1,0:T(8,128)(2,1)S(1)} %pad_maximum_fusion.5.pair_pieces), channel_id=1, source_target_pairs={{0,4},{4,0},{8,12},{12,8},{16,20},{20,16},{24,28},{28,24},{1,5},{5... | collective-permute-start | bytes 1327112 | tf_op jit(solution)/shard_map/ppermute | solution.py:46

commit v3 on v2

--- a/solution.py
+++ b/solution.py
@@ -96,19 +96,8 @@
     return total, flip(total, order[-1], replicas)
 
 
-class Copies:
-    def __init__(self, sems):
-        self.sems = sems
-        self.made = []
-
-    def start(self, source, target):
-        copy = pltpu.make_async_copy(source, target, self.sems.at[len(self.made)])
-        copy.start()
-        self.made.append(copy)
-
-    def wait(self, first=0, last=None):
-        for copy in self.made[first:last]:
-            copy.wait()
+def place(source, target):
+    target[...] = source[...]
 
 
 def rows_at(start, count, unit=16):
@@ -249,13 +238,11 @@
     query,
     keys,
     values,
-    sems,
 ):
     core, x, y, shard = position()
     width = scaled.shape[1]
-    copies = Copies(sems)
-    copies.start(own.at[pl.ds(0, part)], weights.at[rows_at(part * shard, part)])
-    copies.start(own.at[pl.ds(part, 16)], weights.at[rows_at(width + 16 * shard, 16)])
+    place(own.at[pl.ds(0, part)], weights.at[rows_at(part * shard, part)])
+    place(own.at[pl.ds(part, 16)], weights.at[rows_at(width + 16 * shard, 16)])
     for rel_core, source in enumerate((pieces, other)):
         for rel_x in range(2):
             for rel_y in range(2):
@@ -265,12 +252,11 @@
                 for step in range(1, shards):
                     at = shard_at(shard, step, shards)
                     piece = source.at[rel_x, rel_y, step - 1]
-                    copies.start(
+                    place(
                         piece.at[pl.ds(0, 64)], weights.at[rows_at(part * at + 80 * at_y, 64), columns]
                     )
                     last = jnp.where(at_y == 0, part * at + 64, width + 16 * at)
-                    copies.start(piece.at[pl.ds(64, 16)], weights.at[rows_at(last, 16), columns])
-    copies.wait()
+                    place(piece.at[pl.ds(64, 16)], weights.at[rows_at(last, 16), columns])
     total = sum(
         weights[width + 16 * s : width + 16 * s + 16, :width].astype(f32) for s in range(shards)
     )
@@ -362,15 +348,13 @@
     grad_up,
     grad_pair,
     grad_down,
-    sems,
 ):
     core, x, y, shard = position()
     width = hidden_one.shape[1]
     down_part = own_down.shape[0]
     eighth = down_part // 8
-    copies = Copies(sems)
-    copies.start(own_gate, pair.at[0, rows_at(part * shard, part)])
-    copies.start(own_up, pair.at[1, rows_at(part * shard, part)])
+    place(own_gate, pair.at[0, rows_at(part * shard, part)])
+    place(own_up, pair.at[1, rows_at(part * shard, part)])
     for rel_core, source in enumerate((pair_pieces, pair_other)):
         for rel_x in range(2):
             block = 2 * relative(core, rel_core) + relative(x, rel_x)
@@ -379,33 +363,29 @@
                 at_y = relative(y, rel_y)
                 for step in range(1, shards):
                     at = shard_at(shard, step, shards)
-                    copies.start(
+                    place(
                         source.at[rel_x, rel_y, step - 1],
                         pair.at[at_y, rows_at(part * at, part), columns],
                     )
-    first = len(copies.made)
-    copies.start(own_down, down.at[rows_at(down_part * shard, down_part)])
+    place(own_down, down.at[rows_at(down_part * shard, down_part)])
     for rel_core, source in enumerate((down_pieces, down_other)):
         for rel_x in range(2):
             block = 2 * relative(core, rel_core) + relative(x, rel_x)
             for rel_y in range(2):
-                place = eighth * (2 * block + relative(y, rel_y))
+                start = eighth * (2 * block + relative(y, rel_y))
                 for step in range(1, shards):
                     at = shard_at(shard, step, shards)
-                    copies.start(
+                    place(
                         source.at[rel_y, rel_x, step - 1],
-                        down.at[rows_at(down_part * at + place, eighth)],
+                        down.at[rows_at(down_part * at + start, eighth)],
                     )
     grad_low = cotangent[...]
     n2 = normed_two[...]
-    copies.wait(0, first)
     hidden_width = pair.shape[2]
     for start in range(0, hidden_width, 512):
         at = slice(start, start + 512)
         gate = matmul(n2, pair[0, :, at])
         upward = matmul(n2, pair[1, :, at])
-        if start == 0:
-            copies.wait(first)
         grad_hidden = matmul_right_t(grad_low, down[at, :])
         sigma = jax.nn.sigmoid(gate)
         active = gate * sigma
@@ -413,7 +393,6 @@
         grad_up[:, at] = (grad_hidden * active).astype(low)
         grad_gate[:, at] = (grad_hidden * upward * (sigma + active * (1.0 - sigma))).astype(low)
     turned = n2.T
-    sent = Copies(sems)
     for unit, grads in enumerate((grad_gate, grad_up)):
         for start in range(0, hidden_width, 512):
             at = slice(start, start + 512)
@@ -431,11 +410,11 @@
                 at_y = relative(y, rel_y)
                 for step in range(shards):
                     at = shard_at(shard, step, shards)
-                    sent.start(
+                    place(
                         grad_pair.at[at_y, rows_at(part * at, part), columns],
                         target.at[rel_x, rel_y, step],
                     )
-                    sent.start(
+                    place(
                         grad_down.at[rows_at(down_part * at + eighth * (2 * block + at_y), eighth)],
                         down_target.at[rel_y, rel_x, step],
                     )
@@ -450,7 +429,6 @@
     grad_from, gain_row = norm_back(h1, norm_recip(h1), gains[1:2], grad_normed)
     grad_one[...] = grad_low.astype(f32) + grad_from
     grad_gain[...] = jnp.broadcast_to(gain_row, grad_gain.shape)
-    sent.wait()
 
 
 def back_heads_kernel(
@@ -525,7 +503,7 @@
     core, x, y, shard = position()
     rows, width = hidden_in.shape
     turned, values, outs = rest[0:KV], rest[KV : 2 * KV], rest[2 * KV : 3 * KV]
-    grad_tokens, keep, send, grad_low, grad_weights, sems = rest[3 * KV :]
+    grad_tokens, keep, send, grad_low, grad_weights = rest[3 * KV :]
     span = RATIO * HD
     grad_low[...] = jnp.concatenate(
         [jnp.zeros((rows, HD), low)]
@@ -552,7 +530,6 @@
     )
     grad_weights[width : width + 16, :] = jnp.zeros((16, grad_weights.shape[1]), low)
     grad_weights[width : width + 16, 0:width] = both.astype(low)
-    copies = Copies(sems)
     for rel_core, target in enumerate((keep, send)):
         for rel_x in range(2):
             for rel_y in range(2):
@@ -562,13 +539,12 @@
                 for step in range(shards):
                     at = shard_at(shard, step, shards)
                     piece = target.at[rel_y, rel_x, step]
-                    copies.start(
+                    place(
                         grad_weights.at[rows_at(part * at + 80 * at_y, 64), columns],
                         piece.at[pl.ds(0, 64)],
                     )
                     last = jnp.where(at_y == 0, part * at + 64, width)
-                    copies.start(grad_weights.at[rows_at(last, 16), columns], piece.at[pl.ds(64, 16)])
-    copies.wait()
+                    place(grad_weights.at[rows_at(last, 16), columns], piece.at[pl.ds(64, 16)])
 
 
 def finish_kernel(
@@ -588,11 +564,9 @@
     attn,
     pair,
     down,
-    sems,
 ):
     core, x, y, shard = position()
     part, width = out_out.shape
-    copies = Copies(sems)
     for rel_core, (p_from, r_from) in enumerate(((pair_pieces, rest_pieces), (pair_other, rest_other))):
         for rel_x in range(2):
             for rel_y in range(2):
@@ -600,10 +574,9 @@
                 block = 2 * relative(core, rel_core) + relative(x, rel_x)
                 columns = rows_at(384 * block, 384, 128)
                 piece = r_from.at[rel_y, rel_x]
-                copies.start(p_from.at[rel_x, rel_y], pair.at[at_y, :, columns])
-                copies.start(piece.at[pl.ds(0, 80)], attn.at[rows_at(80 * at_y, 80), columns])
-                copies.start(piece.at[pl.ds(80, down.shape[1])], down.at[2 * block + at_y])
-    copies.wait()
+                place(p_from.at[rel_x, rel_y], pair.at[at_y, :, columns])
+                place(piece.at[pl.ds(0, 80)], attn.at[rows_at(80 * at_y, 80), columns])
+                place(piece.at[pl.ds(80, down.shape[1])], down.at[2 * block + at_y])
     kv_width = out_key.shape[1]
     out_out[...] = attn[0:part, 0:width].astype(f32)
     rest = attn[0:part, 512:].astype(f32)
@@ -627,7 +600,6 @@
 
 VM = pl.BlockSpec(memory_space=pltpu.VMEM)
 SM = pl.BlockSpec(memory_space=pltpu.SMEM)
-HB = pl.BlockSpec(memory_space=pltpu.HBM)
 
 
 def shape(sizes, kind):
@@ -729,7 +701,7 @@
         functools.partial(project_kernel, shards, part),
         "project",
         (scaled, cosine, sine, own, attn_got, attn_other),
-        [VM, VM, VM, HB, HB, HB],
+        [VM, VM, VM, VM, VM, VM],
         (
             shape((width + 16 * shards, packed), low),
             shape((8, width), f32),
@@ -739,7 +711,7 @@
             shape((KV, rows, HD), low),
         ),
         [VM] * 6,
-        [pltpu.SemaphoreType.DMA((2 + 16 * (shards - 1),))],
+        [],
         5,
         24,
     )
@@ -798,7 +770,7 @@
             down_got,
             down_other,
         ),
-        [VM] * 3 + [SM, VM] + [HB] * 7,
+        [VM] * 3 + [SM, VM] + [VM] * 7,
         (
             shape((width, rows), low),
             shape((rows, width), f32),
@@ -808,7 +780,7 @@
             down_shape,
             down_shape,
         ),
-        [VM] * 3 + [HB] * 4,
+        [VM] * 3 + [VM] * 4,
         [
             pltpu.VMEM((2, shards * part, hidden_width), low),
             pltpu.VMEM((hidden_width, width), low),
@@ -817,10 +789,9 @@
             pltpu.VMEM((rows, hidden_width), low),
             pltpu.VMEM((2, shards * part, hidden_width), low),
             pltpu.VMEM((hidden_width, width), low),
-            pltpu.SemaphoreType.DMA((16 * shards + 3,)),
         ],
         19,
-        40,
+        48,
     )
     pair_sent = flip(pair_send, 0, replicas)
     down_sent = flip(down_send, 0, replicas)
@@ -865,11 +836,10 @@
         ),
         [VM] * (6 + 3 * KV),
         (shape((width, rows), low), attn_shape, attn_shape),
-        [VM, HB, HB],
+        [VM, VM, VM],
         [
             pltpu.VMEM((rows, 1024), low),
             pltpu.VMEM((width + 16, packed), low),
-            pltpu.SemaphoreType.DMA((16 * shards,)),
         ],
         6,
         24,
@@ -887,7 +857,7 @@
         finish_kernel,
         "finish",
         (*pair_pieces, *rest_pieces),
-        [HB] * 4,
+        [VM] * 4,
         (
             shape(w_query.shape, f32),
             shape(w_key.shape, f32),
@@ -904,7 +874,6 @@
             pltpu.VMEM((160, packed), low),
             pltpu.VMEM((2, part, hidden_width), low),
             pltpu.VMEM((8, 2 * eighth, 384), low),
-            pltpu.SemaphoreType.DMA((24,)),
         ],
         5,
         24,

time: 181 us -> 177 us (0.978)
  Pallas kernels: 52.9 us -> 43.5 us
  local copies, waits for them, and re-layouts: 1.5 us -> 7.67 us
    pallas_call x12, Pallas kernels: 52.9 us -> 43.5 us  [call(): pl.pallas_call(kernel, name=name, in_specs=in_specs, out_shape=out_shape,...]
    unnamed x20 -> x48, local copies, waits for them, and re-layouts: 0.05 us -> 6.22 us
  transfers between devices with their start and end apart: 42 -> 42, of which waited for: 25 -> 25; matrix products, arithmetic and copies ran while one was open for 1% -> 1% of each run, Pallas kernels for 14% -> 13%
where the time goes in v3:
time: 177 us; the launch traced here: 175 us
  waiting for transfers between devices  66 us (37%)
  starting transfers between devices  53 us (30%)
  Pallas kernels  43.5 us (25%)
  local copies, waits for them, and re-layouts  7.67 us (4%)
  other arithmetic  3.19 us (2%)
    ppermute x24, waiting for transfers between devices, flip(): lax.ppermute(value, 'rep', [(i, i ^ 1 << bit) for i in range(replicas)])  49.8 us
    pallas_call x12, Pallas kernels, call(): pl.pallas_call(kernel, name=name, in_specs=in_specs, out_shape=out_shape,...  43.5 us
    ppermute x24, starting transfers between devices, flip(): lax.ppermute(value, 'rep', [(i, i ^ 1 << bit) for i in range(replicas)])  24.2 us
    ppermute x9, starting transfers between devices, shift_to(): lax.ppermute(value, 'shard', [(s, (s + step) % shards) for s in range(sha...  14.9 us
    ppermute x9, starting transfers between devices, shift_from(): lax.ppermute(value, 'shard', [((s + step) % shards, s) for s in range(sha...  14 us
    ppermute x9, waiting for transfers between devices, shift_to(): lax.ppermute(value, 'shard', [(s, (s + step) % shards) for s in range(sha...  8.17 us
    ppermute x9, waiting for transfers between devices, shift_from(): lax.ppermute(value, 'shard', [((s + step) % shards, s) for s in range(sha...  8.06 us
    unnamed x48, local copies, waits for them, and re-layouts  6.22 us
  transfers between devices with their start and end apart: 42, of which 25 were waited for; matrix products, arithmetic and copies ran while one was open for 1% of the time, Pallas kernels for 13%

profile of v3, /device:TPU:0, one launch (start us, length us, event | category | flops | bytes accessed | tf_op | source)
XLA Modules:
  0.0 174.8 jit_solution(13779656245728769399)
XLA Ops:
  0.7 0.8 stack.135
  2.7 2.7 %pack.1 = (bf16[160,1536]{1,0:T(8,128)(2,1)}, bf16[80,384]{1,0:T(8,128)(2,1)}, bf16[144,384]{1,0:T(8,128)(2,1)}, bf16[48,576]{1,0:T(8,128)(2,1)}, bf16[384,576]{1,0:T(8,128)(2,1)}) custom-call(bf16[144,576]{1,0:T(8,128)(2,1)} %w_out.1, bf16[144,576]{1,0:T(8,128)(2,1)} %w_query.1, bf16[144,192]{1,0:T(8,128)(2,1)} %w_key.1, bf16[144,192]{1,0:T(8,128)(2,1)} %w_value.1, ...), custom_call_target="tpu_custom_call" | custom-call | flops 20000000 | bytes 1161216 | tf_op jit(solution)/shard_map/pack/pallas_call | solution.py:611
  5.4 3.0 %collective-permute-start.2 = (bf16[80,384]{1,0:T(8,128)(2,1)}, bf16[80,384]{1,0:T(8,128)(2,1)S(1)}, u32[]{:S(2)}, u32[]{:S(2)}) collective-permute-start(bf16[80,384]{1,0:T(8,128)(2,1)} %get-tuple-element.83), channel_id=1, source_target_pairs={{3,0},{0,1},{1,2},{2,3},{7,4},{4,5},{5,6},{6,7},{11,8},{8,9},{9,10... | collective-permute-start | bytes 184328 | tf_op jit(solution)/shard_map/ppermute | solution.py:50
  8.4 2.6 %collective-permute-start.1 = (bf16[80,384]{1,0:T(8,128)(2,1)}, bf16[80,384]{1,0:T(8,128)(2,1)S(1)}, u32[]{:S(2)}, u32[]{:S(2)}) collective-permute-start(bf16[80,384]{1,0:T(8,128)(2,1)} %get-tuple-element.83), channel_id=1, source_target_pairs={{2,0},{3,1},{0,2},{1,3},{6,4},{7,5},{4,6},{5,7},{10,8},{11,9},{8,1... | collective-permute-start | bytes 184328 | tf_op jit(solution)/shard_map/ppermute | solution.py:50
  11.0 1.3 collective-permute-start
  12.4 1.6 prepare.1
  14.0 0.7 collective-permute-start.6
  15.0 2.8 %collective-permute-start.4 = (bf16[144,384]{1,0:T(8,128)(2,1)}, bf16[144,384]{1,0:T(8,128)(2,1)S(1)}, u32[]{:S(2)}, u32[]{:S(2)}) collective-permute-start(bf16[144,384]{1,0:T(8,128)(2,1)} %get-tuple-element.86), channel_id=1, source_target_pairs={{1,0},{2,1},{3,2},{0,3},{5,4},{6,5},{7,6},{4,7},{9,8},{10,9},{11,1... | collective-permute-start | bytes 331784 | tf_op jit(solution)/shard_map/ppermute | solution.py:50
  18.5 1.5 collective-permute-start.8
  20.0 2.0 %collective-permute-done.6 = bf16[144,384]{1,0:T(8,128)(2,1)S(1)} collective-permute-done((bf16[144,384]{1,0:T(8,128)(2,1)}, bf16[144,384]{1,0:T(8,128)(2,1)S(1)}, u32[]{:S(2)}, u32[]{:S(2)}) %collective-permute-start.6) | collective-permute-done | bytes 110624 | tf_op jit(solution)/shard_map/ppermute | solution.py:50
  22.1 1.0 collective-permute-start.7
  23.0 3.2 %collective-permute-done.5 = bf16[144,384]{1,0:T(8,128)(2,1)S(1)} collective-permute-done((bf16[144,384]{1,0:T(8,128)(2,1)}, bf16[144,384]{1,0:T(8,128)(2,1)S(1)}, u32[]{:S(2)}, u32[]{:S(2)}) %collective-permute-start.5) | collective-permute-done | bytes 110624 | tf_op jit(solution)/shard_map/ppermute | solution.py:50
  26.2 1.5 collective-permute-start.3
  28.4 2.8 %collective-permute-done.8 = bf16[48,576]{1,0:T(8,128)(2,1)S(1)} collective-permute-done((bf16[48,576]{1,0:T(8,128)(2,1)S(1)}, bf16[48,576]{1,0:T(8,128)(2,1)S(1)}, u32[]{:S(2)}, u32[]{:S(2)}) %collective-permute-start.8) | collective-permute-done | bytes 55328 | tf_op jit(solution)/shard_map/ppermute | solution.py:50
  31.3 2.5 %collective-permute-done.3 = bf16[3,80,384]{2,1,0:T(8,128)(2,1)S(1)} collective-permute-done((bf16[3,80,384]{2,1,0:T(8,128)(2,1)S(1)}, bf16[3,80,384]{2,1,0:T(8,128)(2,1)S(1)}, u32[]{:S(2)}, u32[]{:S(2)}) %collective-permute-start.3) | collective-permute-done | bytes 184352 | tf_op jit(solution)/shard_map/ppermute | solution.py:46
  33.9 1.6 collective-permute-start.10
  35.4 2.8 %collective-permute-done.11 = bf16[3,144,384]{2,1,0:T(8,128)(2,1)S(1)} collective-permute-done((bf16[3,144,384]{2,1,0:T(8,128)(2,1)S(1)}, bf16[3,144,384]{2,1,0:T(8,128)(2,1)S(1)}, u32[]{:S(2)}, u32[]{:S(2)}) %collective-permute-start.11) | collective-permute-done | bytes 331808 | tf_op jit(solution)/shard_map/ppermute | solution.py:46
  38.3 3.2 %collective-permute-done.10 = bf16[2,3,80,384]{3,2,1,0:T(8,128)(2,1)S(1)} collective-permute-done((bf16[2,3,80,384]{3,2,1,0:T(8,128)(2,1)S(1)}, bf16[2,3,80,384]{3,2,1,0:T(8,128)(2,1)S(1)}, u32[]{:S(2)}, u32[]{:S(2)}) %collective-permute-start.10) | collective-permute-done | bytes 368672 | tf_op jit(solution)/shard_map/ppermute | solution.py:46
  41.6 1.6 collective-permute-start.13
  43.8 2.1 %project.1 = (bf16[640,1536]{1,0:T(8,128)(2,1)S(1)}, f32[8,576]{1,0:T(8,128)S(1)}, bf16[512,576]{1,0:T(8,128)(2,1)S(1)}, bf16[9,512,64]{2,1,0:T(8,128)(2,1)S(1)}...) custom-call(f32[512,576]{1,0:T(8,128)S(1)} %get-tuple-element.79.scaled, ...), custom_call_target="tpu_custom_call" | custom-call | flops 50000000 | bytes 3557376 | tf_op jit(solution)/shard_map/project/pallas_call | solution.py:611
  45.9 3.2 %collective-permute-done.13 = bf16[3,48,576]{2,1,0:T(8,128)(2,1)S(1)} collective-permute-done((bf16[3,48,576]{2,1,0:T(8,128)(2,1)S(1)}, bf16[3,48,576]{2,1,0:T(8,128)(2,1)S(1)}, u32[]{:S(2)}, u32[]{:S(2)}) %collective-permute-start.13) | collective-permute-done | bytes 165920 | tf_op jit(solution)/shard_map/ppermute | solution.py:46
  49.2 1.6 collective-permute-start.14
  50.8 1.9 %attend_1.1 = (bf16[512,192]{1,0:T(8,128)(2,1)S(1)}, f32[3,512,1]{2,1,0:T(8,128)S(1)}) custom-call(f32[512,512]{1,0:T(8,128)S(1)} %get-tuple-element.78.bias, bf16[9,512,64]{2,1,0:T(8,128)(2,1)S(1)} %get-tuple-element.91.query, bf16[3,512,64]{2,1,0:T(8,128)(2,1)S(1)} %get-tuple-element.92.keys, bf16[3,512,64]{2,1,0:T(8,128)(2,1)S(1)} %get-tuple-element.93.values), custom_call_target="tpu_custom_call" | custom-call | flops 30000000 | bytes 202752 | tf_op jit(solution)/shard_map/attend_1/pallas_call | solution.py:611
  52.7 1.9 %attend_0.1 = (bf16[512,192]{1,0:T(8,128)(2,1)S(1)}, f32[3,512,1]{2,1,0:T(8,128)S(1)}) custom-call(f32[512,512]{1,0:T(8,128)S(1)} %get-tuple-element.78.bias, bf16[9,512,64]{2,1,0:T(8,128)(2,1)S(1)} %get-tuple-element.91.query, bf16[3,512,64]{2,1,0:T(8,128)(2,1)S(1)} %get-tuple-element.92.keys, bf16[3,512,64]{2,1,0:T(8,128)(2,1)S(1)} %get-tuple-element.93.values), custom_call_target="tpu_custom_call" | custom-call | flops 30000000 | bytes 202752 | tf_op jit(solution)/shard_map/attend_0/pallas_call | solution.py:611
  54.6 4.4 %collective-permute-done.14 = bf16[2,3,48,576]{3,2,1,0:T(8,128)(2,1)S(1)} collective-permute-done((bf16[2,3,48,576]{3,2,1,0:T(8,128)(2,1)S(1)}, bf16[2,3,48,576]{3,2,1,0:T(8,128)(2,1)S(1)}, u32[]{:S(2)}, u32[]{:S(2)}) %collective-permute-start.14) | collective-permute-done | bytes 331808 | tf_op jit(solution)/shard_map/ppermute | solution.py:46
  59.1 2.7 %attend_2.1 = (bf16[512,192]{1,0:T(8,128)(2,1)S(1)}, f32[3,512,1]{2,1,0:T(8,128)S(1)}, f32[512,576]{1,0:T(8,128)S(1)}, bf16[512,576]{1,0:T(8,128)(2,1)S(1)}) custom-call(f32[512,512]{1,0:T(8,128)S(1)} %get-tuple-element.78.bias, bf16[9,512,64]{2,1,0:T(8,128)(2,1)S(1)} %get-tuple-element.91.query, bf16[3,512,64]{2,1,0:T(8,128)(2,1)S(1)} %get-tuple-element.92.keys, ...), custom_call_target="tpu_custom_call" | custom-call | flops 40000000 | bytes 1972224 | tf_op jit(solution)/shard_map/attend_2/pallas_call | solution.py:611
  63.6 3.6 %collective-permute-done.17.down_other = bf16[2,2,3,48,576]{4,3,2,1,0:T(8,128)(2,1)S(1)} collective-permute-done((bf16[2,2,3,48,576]{4,3,2,1,0:T(8,128)(2,1)S(1)}, bf16[2,2,3,48,576]{4,3,2,1,0:T(8,128)(2,1)S(1)}, u32[]{:S(2)}, u32[]{:S(2)}) %collective-permute-start.17) | collective-permute-done | bytes 663584 | tf_op jit(solution)/shard_map/ppermute | solution.py:46
  67.2 0.9 copy-done.5
  68.1 1.1 copy-done.22
  69.2 1.1 copy-done.6
  70.3 1.1 copy-done.10
  71.4 16.3 %feed.1 = (bf16[576,512]{1,0:T(8,128)(2,1)}, f32[512,576]{1,0:T(8,128)}, f32[8,576]{1,0:T(8,128)S(1)}, bf16[2,2,4,144,384]{4,3,2,1,0:T(8,128)(2,1)}, bf16[2,2,4,...) custom-call(f32[512,576]{1,0:T(8,128)} %copy-done.4, ...), custom_call_target="tpu_custom_call" | custom-call | flops 190000000 | bytes 7096320 | tf_op jit(solution)/shard_map/feed/pallas_call | solution.py:611
  88.2 1.3 copy-done
  89.5 2.9 %back_0.1 = (bf16[512,256]{1,0:T(8,128)(2,1)S(1)}, bf16[512,64]{1,0:T(8,128)(2,1)S(1)}, bf16[192,576]{1,0:T(8,128)(2,1)S(1)}) custom-call(f32[512,512]{1,0:T(8,128)S(1)} %get-tuple-element.78.bias, f32[512,128]{1,0:T(8,128)S(1)} %get-tuple-element.80.cosine, f32[512,128]{1,0:T(8,128)S(1)} %get-tuple-element.81.sine, ...), custom_call_target="tpu_custom_call" | custom-call | flops 50000000 | bytes 548864 | tf_op jit(solution)/shard_map/back_0/pallas_call | solution.py:611
  93.0 1.8 %collective-permute-start.20 = (bf16[2,4,144,384]{3,2,1,0:T(8,128)(2,1)S(1)}, bf16[2,4,144,384]{3,2,1,0:T(8,128)(2,1)S(1)}, u32[]{:S(2)}, u32[]{:S(2)}) collective-permute-start(bf16[2,4,144,384]{3,2,1,0:T(8,128)(2,1)S(1)} %get-tuple-element.146), channel_id=1, source_target_pairs={{0,8},{4,12},{8,0},{12,4},{16,24},{20,28},{24,16},{28,20},{1,9},{5... | collective-permute-start | bytes 2654216 | tf_op jit(solution)/shard_map/ppermute | solution.py:46
  95.1 1.6 collective-permute-start.28
  96.7 3.2 %back_1.1 = (bf16[512,256]{1,0:T(8,128)(2,1)S(1)}, bf16[512,64]{1,0:T(8,128)(2,1)S(1)}, bf16[192,576]{1,0:T(8,128)(2,1)S(1)}) custom-call(f32[512,512]{1,0:T(8,128)S(1)} %get-tuple-element.78.bias, f32[512,128]{1,0:T(8,128)S(1)} %get-tuple-element.80.cosine, f32[512,128]{1,0:T(8,128)S(1)} %get-tuple-element.81.sine, ...), custom_call_target="tpu_custom_call" | custom-call | flops 50000000 | bytes 548864 | tf_op jit(solution)/shard_map/back_1/pallas_call | solution.py:611
  99.8 2.9 %back_2.1 = (bf16[512,256]{1,0:T(8,128)(2,1)S(1)}, bf16[512,64]{1,0:T(8,128)(2,1)S(1)}, bf16[192,576]{1,0:T(8,128)(2,1)S(1)}) custom-call(f32[512,512]{1,0:T(8,128)S(1)} %get-tuple-element.78.bias, f32[512,128]{1,0:T(8,128)S(1)} %get-tuple-element.80.cosine, f32[512,128]{1,0:T(8,128)S(1)} %get-tuple-element.81.sine, ...), custom_call_target="tpu_custom_call" | custom-call | flops 50000000 | bytes 548864 | tf_op jit(solution)/shard_map/back_2/pallas_call | solution.py:611
  102.7 3.4 %back_last.1 = (bf16[576,512]{1,0:T(8,128)(2,1)}, bf16[2,2,4,80,384]{4,3,2,1,0:T(8,128)(2,1)S(1)}, bf16[2,2,4,80,384]{4,3,2,1,0:T(8,128)(2,1)S(1)}) custom-call(f32[512,576]{1,0:T(8,128)S(1)} %get-tuple-element.100.hidden_in, f32[8,576]{1,0:T(8,128)S(1)} %get-tuple-element.101.gains, bf16[640,1536]{1,0:T(8,128)(2,1)S(1)} %get-tuple-element.102.weights, ...), custom_call_target="tpu_custom_call" | custom-call | flops 60000000 | bytes 2555904 | tf_op jit(solution)/shard_map/back_last/pallas_call | solution.py:611
  106.1 2.0 %collective-permute-done.28 = bf16[2,4,48,576]{3,2,1,0:T(8,128)(2,1)S(1)} collective-permute-done((bf16[2,4,48,576]{3,2,1,0:T(8,128)(2,1)S(1)}, bf16[2,4,48,576]{3,2,1,0:T(8,128)(2,1)S(1)}, u32[]{:S(2)}, u32[]{:S(2)}) %collective-permute-start.28) | collective-permute-done | bytes 442400 | tf_op jit(solution)/shard_map/ppermute | solution.py:46
  108.2 6.6 %collective-permute-done.20 = bf16[2,4,144,384]{3,2,1,0:T(8,128)(2,1)S(1)} collective-permute-done((bf16[2,4,144,384]{3,2,1,0:T(8,128)(2,1)S(1)}, bf16[2,4,144,384]{3,2,1,0:T(8,128)(2,1)S(1)}, u32[]{:S(2)}, u32[]{:S(2)}) %collective-permute-start.20) | collective-permute-done | bytes 884768 | tf_op jit(solution)/shard_map/ppermute | solution.py:46
  114.8 2.6 %collective-permute-done.29 = bf16[2,2,4,80,384]{4,3,2,1,0:T(8,128)(2,1)S(1)} collective-permute-done((bf16[2,2,4,80,384]{4,3,2,1,0:T(8,128)(2,1)S(1)}, bf16[2,2,4,80,384]{4,3,2,1,0:T(8,128)(2,1)S(1)}, u32[]{:S(2)}, u32[]{:S(2)}) %collective-permute-start.29) | collective-permute-done | bytes 983072 | tf_op jit(solution)/shard_map/ppermute | solution.py:46
  117.6 1.6 collective-permute-start.30
  119.3 1.8 %collective-permute-start.35 = (bf16[4,48,576]{2,1,0:T(8,128)(2,1)S(1)}, bf16[4,48,576]{2,1,0:T(8,128)(2,1)S(1)}, u32[]{:S(2)}, u32[]{:S(2)}) collective-permute-start(bf16[4,48,576]{2,1,0:T(8,128)(2,1)S(1)} %get-tuple-element.156), channel_id=1, source_target_pairs={{0,8},{4,12},{8,0},{12,4},{16,24},{20,28},{24,16},{28,20},{1,9},{5... | collective-permute-start | bytes 663560 | tf_op jit(solution)/shard_map/ppermute | solution.py:46
  121.1 6.0 %collective-permute-done.35 = bf16[4,48,576]{2,1,0:T(8,128)(2,1)S(1)} collective-permute-done((bf16[4,48,576]{2,1,0:T(8,128)(2,1)S(1)}, bf16[4,48,576]{2,1,0:T(8,128)(2,1)S(1)}, u32[]{:S(2)}, u32[]{:S(2)}) %collective-permute-start.35) | collective-permute-done | bytes 221216 | tf_op jit(solution)/shard_map/ppermute | solution.py:46
  127.1 2.3 %collective-permute-start.36 = (bf16[48,576]{1,0:T(8,128)(2,1)S(1)}, bf16[48,576]{1,0:T(8,128)(2,1)S(1)}, u32[]{:S(2)}, u32[]{:S(2)}) collective-permute-start(bf16[48,576]{1,0:T(8,128)(2,1)S(1)} %get-tuple-element.163), channel_id=1, source_target_pairs={{0,1},{1,2},{2,3},{3,0},{4,5},{5,6},{6,7},{7,4},{8,9},{9,10},{10,1... | collective-permute-start | bytes 165896 | tf_op jit(solution)/shard_map/ppermute | solution.py:54
  129.4 2.8 %collective-permute-start.38 = (bf16[48,576]{1,0:T(8,128)(2,1)S(1)}, bf16[48,576]{1,0:T(8,128)(2,1)S(1)}, u32[]{:S(2)}, u32[]{:S(2)}) collective-permute-start(bf16[48,576]{1,0:T(8,128)(2,1)S(1)} %get-tuple-element.164), channel_id=1, source_target_pairs={{0,3},{1,0},{2,1},{3,2},{4,7},{5,4},{6,5},{7,6},{8,11},{9,8},{10,9... | collective-permute-start | bytes 165896 | tf_op jit(solution)/shard_map/ppermute | solution.py:54
  132.8 1.8 %collective-permute-start.31 = (bf16[4,80,384]{2,1,0:T(8,128)(2,1)S(1)}, bf16[4,80,384]{2,1,0:T(8,128)(2,1)S(1)}, u32[]{:S(2)}, u32[]{:S(2)}) collective-permute-start(bf16[4,80,384]{2,1,0:T(8,128)(2,1)S(1)} %get-tuple-element.154), channel_id=1, source_target_pairs={{0,8},{4,12},{8,0},{12,4},{16,24},{20,28},{24,16},{28,20},{1,9},{5... | collective-permute-start | bytes 737288 | tf_op jit(solution)/shard_map/ppermute | solution.py:46
  135.4 2.5 %collective-permute-done.37 = bf16[48,576]{1,0:T(8,128)(2,1)S(1)} collective-permute-done((bf16[48,576]{1,0:T(8,128)(2,1)S(1)}, bf16[48,576]{1,0:T(8,128)(2,1)S(1)}, u32[]{:S(2)}, u32[]{:S(2)}) %collective-permute-start.37) | collective-permute-done | bytes 55328 | tf_op jit(solution)/shard_map/ppermute | solution.py:54
  138.0 1.2 collective-permute-done.31
  139.2 2.0 %collective-permute-start.32 = (bf16[80,384]{1,0:T(8,128)(2,1)S(1)}, bf16[80,384]{1,0:T(8,128)(2,1)S(1)}, u32[]{:S(2)}, u32[]{:S(2)}) collective-permute-start(bf16[80,384]{1,0:T(8,128)(2,1)S(1)} %get-tuple-element.160), channel_id=1, source_target_pairs={{0,1},{1,2},{2,3},{3,0},{4,5},{5,6},{6,7},{7,4},{8,9},{9,10},{10,1... | collective-permute-start | bytes 184328 | tf_op jit(solution)/shard_map/ppermute | solution.py:54
  141.2 2.2 %collective-permute-start.34 = (bf16[80,384]{1,0:T(8,128)(2,1)S(1)}, bf16[80,384]{1,0:T(8,128)(2,1)S(1)}, u32[]{:S(2)}, u32[]{:S(2)}) collective-permute-start(bf16[80,384]{1,0:T(8,128)(2,1)S(1)} %get-tuple-element.161), channel_id=1, source_target_pairs={{0,3},{1,0},{2,1},{3,2},{4,7},{5,4},{6,5},{7,6},{8,11},{9,8},{10,9... | collective-permute-start | bytes 184328 | tf_op jit(solution)/shard_map/ppermute | solution.py:54
  143.9 1.3 collective-permute-done.21
  145.2 1.8 %collective-permute-start.22 = (bf16[144,384]{1,0:T(8,128)(2,1)S(1)}, bf16[144,384]{1,0:T(8,128)(2,1)S(1)}, u32[]{:S(2)}, u32[]{:S(2)}) collective-permute-start(bf16[144,384]{1,0:T(8,128)(2,1)S(1)} %get-tuple-element.157), channel_id=1, source_target_pairs={{0,1},{1,2},{2,3},{3,0},{4,5},{5,6},{6,7},{7,4},{8,9},{9,10},{10,1... | collective-permute-start | bytes 331784 | tf_op jit(solution)/shard_map/ppermute | solution.py:54
  147.0 2.4 %collective-permute-start.24 = (bf16[144,384]{1,0:T(8,128)(2,1)S(1)}, bf16[144,384]{1,0:T(8,128)(2,1)S(1)}, u32[]{:S(2)}, u32[]{:S(2)}) collective-permute-start(bf16[144,384]{1,0:T(8,128)(2,1)S(1)} %get-tuple-element.158), channel_id=1, source_target_pairs={{0,3},{1,0},{2,1},{3,2},{4,7},{5,4},{6,5},{7,6},{8,11},{9,8},{10,9... | collective-permute-start | bytes 331784 | tf_op jit(solution)/shard_map/ppermute | solution.py:54
  150.7 2.7 %collective-permute-start.39 = (bf16[176,384]{1,0:T(8,128)(2,1)S(1)}, bf16[176,384]{1,0:T(8,128)(2,1)S(1)}, u32[]{:S(2)}, u32[]{:S(2)}) collective-permute-start(bf16[176,384]{1,0:T(8,128)(2,1)S(1)} %get-tuple-element.173), channel_id=1, source_target_pairs={{0,8},{4,12},{8,0},{12,4},{16,24},{20,28},{24,16},{28,20},{1,9},{5... | collective-permute-start | bytes 405512 | tf_op jit(solution)/shard_map/ppermute | solution.py:46
  153.4 5.0 %collective-permute-done.23 = bf16[144,384]{1,0:T(8,128)(2,1)S(1)} collective-permute-done((bf16[144,384]{1,0:T(8,128)(2,1)S(1)}, bf16[144,384]{1,0:T(8,128)(2,1)S(1)}, u32[]{:S(2)}, u32[]{:S(2)}) %collective-permute-start.23) | collective-permute-done | bytes 110624 | tf_op jit(solution)/shard_map/ppermute | solution.py:54
  158.4 1.6 collective-permute-start.25
  160.6 3.7 %collective-permute-done.25 = bf16[144,384]{1,0:T(8,128)(2,1)S(1)} collective-permute-done((bf16[144,384]{1,0:T(8,128)(2,1)S(1)}, bf16[144,384]{1,0:T(8,128)(2,1)S(1)}, u32[]{:S(2)}, u32[]{:S(2)}) %collective-permute-start.25) | collective-permute-done | bytes 110624 | tf_op jit(solution)/shard_map/ppermute | solution.py:46
  164.4 1.6 collective-permute-start.26
  166.0 2.5 %collective-permute-done.40 = bf16[2,176,384]{2,1,0:T(8,128)(2,1)S(1)} collective-permute-done((bf16[2,176,384]{2,1,0:T(8,128)(2,1)S(1)}, bf16[2,176,384]{2,1,0:T(8,128)(2,1)S(1)}, u32[]{:S(2)}, u32[]{:S(2)}) %collective-permute-start.40) | collective-permute-done | bytes 270368 | tf_op jit(solution)/shard_map/ppermute | solution.py:46
  168.6 1.7 collective-permute-done.26
  170.5 1.8 %collective-permute-done.27.pair_other = bf16[2,2,144,384]{3,2,1,0:T(8,128)(2,1)S(1)} collective-permute-done((bf16[2,2,144,384]{3,2,1,0:T(8,128)(2,1)S(1)}, bf16[2,2,144,384]{3,2,1,0:T(8,128)(2,1)S(1)}, u32[]{:S(2)}, u32[]{:S(2)}) %collective-permute-start.27) | collective-permute-done | bytes 442400 | tf_op jit(solution)/shard_map/ppermute | solution.py:46
  172.3 2.1 %finish.1 = (f32[144,576]{1,0:T(8,128)}, f32[144,192]{1,0:T(8,128)}, f32[144,192]{1,0:T(8,128)}, f32[144,576]{1,0:T(8,128)}, f32[1,144]{1,0:T(1,128)}, /*index=5...) custom-call(bf16[2,2,144,384]{3,2,1,0:T(8,128)(2,1)S(1)} %pad_maximum_fusion.5.pair_pieces, ...), custom_call_target="tpu_custom_call" | custom-call | flops 50000000 | bytes 3540096 | tf_op jit(solution)/shard_map/finish/pallas_call | solution.py:611
  (111 shorter events, 12.1 us)
Async XLA Ops:
  0.6 11.7 %copy-start.15 = (f32[520,128]{1,0:T(8,128)S(1)}, f32[520,128]{1,0:T(8,128)}, u32[]{:S(2)}) copy-start(f32[520,128]{1,0:T(8,128)} %constant.8.clone.table_sin) | copy-start | bytes 798724
  0.7 11.7 %copy-start.16 = (f32[520,128]{1,0:T(8,128)S(1)}, f32[520,128]{1,0:T(8,128)}, u32[]{:S(2)}) copy-start(f32[520,128]{1,0:T(8,128)} %constant.7.clone.table_cos) | copy-start | bytes 798724
  0.7 11.7 %copy-start.19 = (s32[1,4]{1,0:T(1,128)S(1)}, s32[1,4]{1,0:T(1,128)}, u32[]{:S(2)}) copy-start(s32[1,4]{1,0:T(1,128)} %lengths.3) | copy-start | bytes 52
  0.7 11.7 %copy-start.12 = (bf16[512,576]{0,1:T(8,128)(2,1)S(1)}, bf16[512,576]{0,1:T(8,128)(2,1)}, u32[]{:S(2)}) copy-start(bf16[512,576]{0,1:T(8,128)(2,1)} %param.25) | copy-start | bytes 1769476
  0.7 11.7 %copy-start.11 = (bf16[512,576]{0,1:T(8,128)(2,1)S(1)}, bf16[512,576]{0,1:T(8,128)(2,1)}, u32[]{:S(2)}) copy-start(bf16[512,576]{0,1:T(8,128)(2,1)} %param.14) | copy-start | bytes 1769476
  5.4 12.5 %copy-start.23 = (bf16[48,576]{1,0:T(8,128)(2,1)S(1)}, bf16[48,576]{1,0:T(8,128)(2,1)}, u32[]{:S(2)}) copy-start(bf16[48,576]{1,0:T(8,128)(2,1)} %get-tuple-element.88) | copy-start | bytes 165892
  5.4 9.6 %collective-permute-start.2 = (bf16[80,384]{1,0:T(8,128)(2,1)}, bf16[80,384]{1,0:T(8,128)(2,1)S(1)}, u32[]{:S(2)}, u32[]{:S(2)}) collective-permute-start(bf16[80,384]{1,0:T(8,128)(2,1)} %get-tuple-element.83), channel_id=1, source_target_pairs={{3,0},{0,1},{1,2},{2,3},{7,4},{4,5},{5,6},{6,7},{11,8},{8,9},{9,10... | collective-permute-start | bytes 184328 | tf_op jit(solution)/shard_map/ppermute | solution.py:50
  8.4 9.4 %collective-permute-start.1 = (bf16[80,384]{1,0:T(8,128)(2,1)}, bf16[80,384]{1,0:T(8,128)(2,1)S(1)}, u32[]{:S(2)}, u32[]{:S(2)}) collective-permute-start(bf16[80,384]{1,0:T(8,128)(2,1)} %get-tuple-element.83), channel_id=1, source_target_pairs={{2,0},{3,1},{0,2},{1,3},{6,4},{7,5},{4,6},{5,7},{10,8},{11,9},{8,1... | collective-permute-start | bytes 184328 | tf_op jit(solution)/shard_map/ppermute | solution.py:50
  11.0 6.8 %collective-permute-start = (bf16[80,384]{1,0:T(8,128)(2,1)}, bf16[80,384]{1,0:T(8,128)(2,1)S(1)}, u32[]{:S(2)}, u32[]{:S(2)}) collective-permute-start(bf16[80,384]{1,0:T(8,128)(2,1)} %get-tuple-element.83), channel_id=1, source_target_pairs={{1,0},{2,1},{3,2},{0,3},{5,4},{6,5},{7,6},{4,7},{9,8},{10,9},{11,1... | collective-permute-start | bytes 184328 | tf_op jit(solution)/shard_map/ppermute | solution.py:50
  14.0 8.1 %collective-permute-start.6 = (bf16[144,384]{1,0:T(8,128)(2,1)}, bf16[144,384]{1,0:T(8,128)(2,1)S(1)}, u32[]{:S(2)}, u32[]{:S(2)}) collective-permute-start(bf16[144,384]{1,0:T(8,128)(2,1)} %get-tuple-element.86), channel_id=1, source_target_pairs={{3,0},{0,1},{1,2},{2,3},{7,4},{4,5},{5,6},{6,7},{11,8},{8,9},{9,10... | collective-permute-start | bytes 331784 | tf_op jit(solution)/shard_map/ppermute | solution.py:50
  14.7 11.6 %collective-permute-start.5 = (bf16[144,384]{1,0:T(8,128)(2,1)}, bf16[144,384]{1,0:T(8,128)(2,1)S(1)}, u32[]{:S(2)}, u32[]{:S(2)}) collective-permute-start(bf16[144,384]{1,0:T(8,128)(2,1)} %get-tuple-element.86), channel_id=1, source_target_pairs={{2,0},{3,1},{0,2},{1,3},{6,4},{7,5},{4,6},{5,7},{10,8},{11,9},{8,1... | collective-permute-start | bytes 331784 | tf_op jit(solution)/shard_map/ppermute | solution.py:50
  15.0 12.7 %collective-permute-start.4 = (bf16[144,384]{1,0:T(8,128)(2,1)}, bf16[144,384]{1,0:T(8,128)(2,1)S(1)}, u32[]{:S(2)}, u32[]{:S(2)}) collective-permute-start(bf16[144,384]{1,0:T(8,128)(2,1)} %get-tuple-element.86), channel_id=1, source_target_pairs={{1,0},{2,1},{3,2},{0,3},{5,4},{6,5},{7,6},{4,7},{9,8},{10,9},{11,1... | collective-permute-start | bytes 331784 | tf_op jit(solution)/shard_map/ppermute | solution.py:50
  17.9 10.5 %collective-permute-start.9 = (bf16[48,576]{1,0:T(8,128)(2,1)S(1)}, bf16[48,576]{1,0:T(8,128)(2,1)S(1)}, u32[]{:S(2)}, u32[]{:S(2)}) collective-permute-start(bf16[48,576]{1,0:T(8,128)(2,1)S(1)} %copy-done.23), channel_id=1, source_target_pairs={{3,0},{0,1},{1,2},{2,3},{7,4},{4,5},{5,6},{6,7},{11,8},{8,9},{9,10... | collective-permute-start | bytes 165896 | tf_op jit(solution)/shard_map/ppermute | solution.py:50
  18.5 12.7 %collective-permute-start.8 = (bf16[48,576]{1,0:T(8,128)(2,1)S(1)}, bf16[48,576]{1,0:T(8,128)(2,1)S(1)}, u32[]{:S(2)}, u32[]{:S(2)}) collective-permute-start(bf16[48,576]{1,0:T(8,128)(2,1)S(1)} %copy-done.23), channel_id=1, source_target_pairs={{2,0},{3,1},{0,2},{1,3},{6,4},{7,5},{4,6},{5,7},{10,8},{11,9},{8,1... | collective-permute-start | bytes 165896 | tf_op jit(solution)/shard_map/ppermute | solution.py:50
  22.1 9.2 %collective-permute-start.7 = (bf16[48,576]{1,0:T(8,128)(2,1)S(1)}, bf16[48,576]{1,0:T(8,128)(2,1)S(1)}, u32[]{:S(2)}, u32[]{:S(2)}) collective-permute-start(bf16[48,576]{1,0:T(8,128)(2,1)S(1)} %copy-done.23), channel_id=1, source_target_pairs={{1,0},{2,1},{3,2},{0,3},{5,4},{6,5},{7,6},{4,7},{9,8},{10,9},{11,1... | collective-permute-start | bytes 165896 | tf_op jit(solution)/shard_map/ppermute | solution.py:50
  26.2 7.6 %collective-permute-start.3 = (bf16[3,80,384]{2,1,0:T(8,128)(2,1)S(1)}, bf16[3,80,384]{2,1,0:T(8,128)(2,1)S(1)}, u32[]{:S(2)}, u32[]{:S(2)}) collective-permute-start(bf16[3,80,384]{2,1,0:T(8,128)(2,1)S(1)} %pad_maximum_fusion.11), channel_id=1, source_target_pairs={{0,16},{4,20},{8,24},{12,28},{16,0},{20,4},{24,8},{28,12},{1,17},{... | collective-permute-start | bytes 552968 | tf_op jit(solution)/shard_map/ppermute | solution.py:46
  27.8 10.3 %collective-permute-start.11 = (bf16[3,144,384]{2,1,0:T(8,128)(2,1)S(1)}, bf16[3,144,384]{2,1,0:T(8,128)(2,1)S(1)}, u32[]{:S(2)}, u32[]{:S(2)}) collective-permute-start(bf16[3,144,384]{2,1,0:T(8,128)(2,1)S(1)} %get-tuple-element.167), channel_id=1, source_target_pairs={{0,16},{4,20},{8,24},{12,28},{16,0},{20,4},{24,8},{28,12},{1,17},{... | collective-permute-start | bytes 995336 | tf_op jit(solution)/shard_map/ppermute | solution.py:46
  33.8 10.0 %copy-start.13 = (bf16[160,1536]{1,0:T(8,128)(2,1)S(1)}, bf16[160,1536]{1,0:T(8,128)(2,1)}, u32[]{:S(2)}) copy-start(bf16[160,1536]{1,0:T(8,128)(2,1)} %get-tuple-element.82.own) | copy-start | bytes 1474564
  33.9 7.6 %collective-permute-start.10 = (bf16[2,3,80,384]{3,2,1,0:T(8,128)(2,1)S(1)}, bf16[2,3,80,384]{3,2,1,0:T(8,128)(2,1)S(1)}, u32[]{:S(2)}, u32[]{:S(2)}) collective-permute-start(bf16[2,3,80,384]{3,2,1,0:T(8,128)(2,1)S(1)} %pad_maximum_fusion.6), channel_id=1, source_target_pairs={{0,8},{4,12},{8,0},{12,4},{16,24},{20,28},{24,16},{28,20},{1,9},{5... | collective-permute-start | bytes 1105928 | tf_op jit(solution)/shard_map/ppermute | solution.py:46
  41.5 2.3 %collective-permute-start.12 = (bf16[2,2,3,80,384]{4,3,2,1,0:T(8,128)(2,1)S(1)}, bf16[2,2,3,80,384]{4,3,2,1,0:T(8,128)(2,1)S(1)}, u32[]{:S(2)}, u32[]{:S(2)}) collective-permute-start(bf16[2,2,3,80,384]{4,3,2,1,0:T(8,128)(2,1)S(1)} %pad_maximum_fusion.1.pieces), channel_id=1, source_target_pairs={{0,4},{4,0},{8,12},{12,8},{16,20},{20,16},{24,28},{28,24},{1,5},{5... | collective-permute-start | bytes 2211848 | tf_op jit(solution)/shard_map/ppermute | solution.py:46
  41.6 7.5 %collective-permute-start.13 = (bf16[3,48,576]{2,1,0:T(8,128)(2,1)S(1)}, bf16[3,48,576]{2,1,0:T(8,128)(2,1)S(1)}, u32[]{:S(2)}, u32[]{:S(2)}) collective-permute-start(bf16[3,48,576]{2,1,0:T(8,128)(2,1)S(1)} %pad_maximum_fusion.12), channel_id=1, source_target_pairs={{0,8},{4,12},{8,0},{12,4},{16,24},{20,28},{24,16},{28,20},{1,9},{5... | collective-permute-start | bytes 497672 | tf_op jit(solution)/shard_map/ppermute | solution.py:46
  43.2 19.7 %collective-permute-start.15 = (bf16[2,3,144,384]{3,2,1,0:T(8,128)(2,1)S(1)}, bf16[2,3,144,384]{3,2,1,0:T(8,128)(2,1)S(1)}, u32[]{:S(2)}, u32[]{:S(2)}) collective-permute-start(bf16[2,3,144,384]{3,2,1,0:T(8,128)(2,1)S(1)} %pad_maximum_fusion.3), channel_id=1, source_target_pairs={{0,8},{4,12},{8,0},{12,4},{16,24},{20,28},{24,16},{28,20},{1,9},{5... | collective-permute-start | bytes 1990664 | tf_op jit(solution)/shard_map/ppermute | solution.py:46
  45.9 6.8 %copy-start.7 = (bf16[512,576]{1,0:T(8,128)(2,1)}, bf16[512,576]{1,0:T(8,128)(2,1)S(1)}, u32[]{:S(2)}) copy-start(bf16[512,576]{1,0:T(8,128)(2,1)S(1)} %get-tuple-element.95.normed) | copy-start | bytes 1769476
  49.2 9.8 %collective-permute-start.14 = (bf16[2,3,48,576]{3,2,1,0:T(8,128)(2,1)S(1)}, bf16[2,3,48,576]{3,2,1,0:T(8,128)(2,1)S(1)}, u32[]{:S(2)}, u32[]{:S(2)}) collective-permute-start(bf16[2,3,48,576]{3,2,1,0:T(8,128)(2,1)S(1)} %pad_maximum_fusion.7), channel_id=1, source_target_pairs={{0,16},{4,20},{8,24},{12,28},{16,0},{20,4},{24,8},{28,12},{1,17},{... | collective-permute-start | bytes 995336 | tf_op jit(solution)/shard_map/ppermute | solution.py:46
  62.4 4.8 %copy-start.4 = (f32[512,576]{1,0:T(8,128)}, f32[512,576]{1,0:T(8,128)S(1)}, u32[]{:S(2)}) copy-start(f32[512,576]{1,0:T(8,128)S(1)} %get-tuple-element.103.hidden_one) | copy-start | bytes 3538948
  62.4 5.7 %copy-start.9 = (bf16[512,576]{1,0:T(8,128)(2,1)}, bf16[512,576]{1,0:T(8,128)(2,1)S(1)}, u32[]{:S(2)}) copy-start(bf16[512,576]{1,0:T(8,128)(2,1)S(1)} %get-tuple-element.104.normed_two) | copy-start | bytes 1769476
  62.4 6.7 %copy-start.2 = (bf16[144,1536]{1,0:T(8,128)(2,1)S(1)}, bf16[144,1536]{1,0:T(8,128)(2,1)}, u32[]{:S(2)}) copy-start(bf16[144,1536]{1,0:T(8,128)(2,1)} %own_gate.1) | copy-start | bytes 1327108
  62.4 6.7 %copy-start.3 = (bf16[144,1536]{1,0:T(8,128)(2,1)S(1)}, bf16[144,1536]{1,0:T(8,128)(2,1)}, u32[]{:S(2)}) copy-start(bf16[144,1536]{1,0:T(8,128)(2,1)} %own_up.1) | copy-start | bytes 1327108
  62.4 6.7 %copy-start.14 = (bf16[384,576]{1,0:T(8,128)(2,1)S(1)}, bf16[384,576]{1,0:T(8,128)(2,1)}, u32[]{:S(2)}) copy-start(bf16[384,576]{1,0:T(8,128)(2,1)} %get-tuple-element.106.own_down) | copy-start | bytes 1327108
  63.0 5.1 %copy-start.20 = (bf16[2,2,3,144,384]{4,3,2,1,0:T(8,128)(2,1)}, bf16[2,2,3,144,384]{4,3,2,1,0:T(8,128)(2,1)S(1)}, u32[]{:S(2)}) copy-start(bf16[2,2,3,144,384]{4,3,2,1,0:T(8,128)(2,1)S(1)} %pad_maximum_fusion.pair_pieces) | copy-start | bytes 3981316
  63.0 5.0 %collective-permute-start.16 = (bf16[2,2,3,144,384]{4,3,2,1,0:T(8,128)(2,1)S(1)}, bf16[2,2,3,144,384]{4,3,2,1,0:T(8,128)(2,1)S(1)}, u32[]{:S(2)}, u32[]{:S(2)}) collective-permute-start(bf16[2,2,3,144,384]{4,3,2,1,0:T(8,128)(2,1)S(1)} %pad_maximum_fusion.pair_pieces), channel_id=1, source_target_pairs={{0,4},{4,0},{8,12},{12,8},{16,20},{20,16},{24,28},{28,24},{1,5},{5... | collective-permute-start | bytes 3981320 | tf_op jit(solution)/shard_map/ppermute | solution.py:46
  63.1 4.1 %collective-permute-start.17 = (bf16[2,2,3,48,576]{4,3,2,1,0:T(8,128)(2,1)S(1)}, bf16[2,2,3,48,576]{4,3,2,1,0:T(8,128)(2,1)S(1)}, u32[]{:S(2)}, u32[]{:S(2)}) collective-permute-start(bf16[2,2,3,48,576]{4,3,2,1,0:T(8,128)(2,1)S(1)} %pad_maximum_fusion.2.down_pieces), channel_id=1, source_target_pairs={{0,4},{4,0},{8,12},{12,8},{16,20},{20,16},{24,28},{28,24},{1,5},{5... | collective-permute-start | bytes 1990664 | tf_op jit(solution)/shard_map/ppermute | solution.py:46
  68.1 1.1 copy-start.22
  69.2 1.1 copy-start.6
  70.3 1.1 copy-start.10
  87.7 4.9 %collective-permute-start.18 = (bf16[2,2,4,144,384]{4,3,2,1,0:T(8,128)(2,1)}, bf16[2,2,4,144,384]{4,3,2,1,0:T(8,128)(2,1)S(1)}, u32[]{:S(2)}, u32[]{:S(2)}) collective-permute-start(bf16[2,2,4,144,384]{4,3,2,1,0:T(8,128)(2,1)} %get-tuple-element.110), channel_id=1, source_target_pairs={{0,4},{4,0},{8,12},{12,8},{16,20},{20,16},{24,28},{28,24},{1,5},{5... | collective-permute-start | bytes 5308424 | tf_op jit(solution)/shard_map/ppermute | solution.py:46
  87.8 7.0 %collective-permute-start.19 = (bf16[2,2,4,48,576]{4,3,2,1,0:T(8,128)(2,1)S(1)}, bf16[2,2,4,48,576]{4,3,2,1,0:T(8,128)(2,1)S(1)}, u32[]{:S(2)}, u32[]{:S(2)}) collective-permute-start(bf16[2,2,4,48,576]{4,3,2,1,0:T(8,128)(2,1)S(1)} %get-tuple-element.111), channel_id=1, source_target_pairs={{0,4},{4,0},{8,12},{12,8},{16,20},{20,16},{24,28},{28,24},{1,5},{5... | collective-permute-start | bytes 2654216 | tf_op jit(solution)/shard_map/ppermute | solution.py:46
  88.2 1.3 copy-start
  89.5 3.1 %copy-start.21 = (bf16[2,2,4,144,384]{4,3,2,1,0:T(8,128)(2,1)S(1)}, bf16[2,2,4,144,384]{4,3,2,1,0:T(8,128)(2,1)}, u32[]{:S(2)}) copy-start(bf16[2,2,4,144,384]{4,3,2,1,0:T(8,128)(2,1)} %get-tuple-element.128) | copy-start | bytes 5308420
  93.0 21.8 %collective-permute-start.20 = (bf16[2,4,144,384]{3,2,1,0:T(8,128)(2,1)S(1)}, bf16[2,4,144,384]{3,2,1,0:T(8,128)(2,1)S(1)}, u32[]{:S(2)}, u32[]{:S(2)}) collective-permute-start(bf16[2,4,144,384]{3,2,1,0:T(8,128)(2,1)S(1)} %get-tuple-element.146), channel_id=1, source_target_pairs={{0,8},{4,12},{8,0},{12,4},{16,24},{20,28},{24,16},{28,20},{1,9},{5... | collective-permute-start | bytes 2654216 | tf_op jit(solution)/shard_map/ppermute | solution.py:46
  95.1 13.0 %collective-permute-start.28 = (bf16[2,4,48,576]{3,2,1,0:T(8,128)(2,1)S(1)}, bf16[2,4,48,576]{3,2,1,0:T(8,128)(2,1)S(1)}, u32[]{:S(2)}, u32[]{:S(2)}) collective-permute-start(bf16[2,4,48,576]{3,2,1,0:T(8,128)(2,1)S(1)} %get-tuple-element.149), channel_id=1, source_target_pairs={{0,16},{4,20},{8,24},{12,28},{16,0},{20,4},{24,8},{28,12},{1,17},{... | collective-permute-start | bytes 1327112 | tf_op jit(solution)/shard_map/ppermute | solution.py:46
  96.7 3.2 %copy-start.18 = (bf16[512,192]{1,0:T(8,128)(2,1)S(1)}, bf16[512,192]{1,0:T(8,128)(2,1)}, u32[]{:S(2)}) copy-start(bf16[512,192]{1,0:T(8,128)(2,1)} %copy-done.17) | copy-start | bytes 589828
  99.8 2.9 %copy-start.1 = (f32[512,576]{1,0:T(8,128)S(1)}, f32[512,576]{1,0:T(8,128)}, u32[]{:S(2)}) copy-start(f32[512,576]{1,0:T(8,128)} %get-tuple-element.112.grad_one) | copy-start | bytes 3538948
  99.8 2.9 %copy-start.8 = (bf16[512,576]{1,0:T(8,128)(2,1)S(1)}, bf16[512,576]{1,0:T(8,128)(2,1)}, u32[]{:S(2)}) copy-start(bf16[512,576]{1,0:T(8,128)(2,1)} %copy-done.7) | copy-start | bytes 1769476
  114.8 2.6 %collective-permute-start.29 = (bf16[2,2,4,80,384]{4,3,2,1,0:T(8,128)(2,1)S(1)}, bf16[2,2,4,80,384]{4,3,2,1,0:T(8,128)(2,1)S(1)}, u32[]{:S(2)}, u32[]{:S(2)}) collective-permute-start(bf16[2,2,4,80,384]{4,3,2,1,0:T(8,128)(2,1)S(1)} %get-tuple-element.134), channel_id=1, source_target_pairs={{0,4},{4,0},{8,12},{12,8},{16,20},{20,16},{24,28},{28,24},{1,5},{5... | collective-permute-start | bytes 2949128 | tf_op jit(solution)/shard_map/ppermute | solution.py:46
  117.6 15.1 %collective-permute-start.30 = (bf16[2,4,80,384]{3,2,1,0:T(8,128)(2,1)S(1)}, bf16[2,4,80,384]{3,2,1,0:T(8,128)(2,1)S(1)}, u32[]{:S(2)}, u32[]{:S(2)}) collective-permute-start(bf16[2,4,80,384]{3,2,1,0:T(8,128)(2,1)S(1)} %get-tuple-element.148), channel_id=1, source_target_pairs={{0,16},{4,20},{8,24},{12,28},{16,0},{20,4},{24,8},{28,12},{1,17},{... | collective-permute-start | bytes 1474568 | tf_op jit(solution)/shard_map/ppermute | solution.py:46
  119.3 7.8 %collective-permute-start.35 = (bf16[4,48,576]{2,1,0:T(8,128)(2,1)S(1)}, bf16[4,48,576]{2,1,0:T(8,128)(2,1)S(1)}, u32[]{:S(2)}, u32[]{:S(2)}) collective-permute-start(bf16[4,48,576]{2,1,0:T(8,128)(2,1)S(1)} %get-tuple-element.156), channel_id=1, source_target_pairs={{0,8},{4,12},{8,0},{12,4},{16,24},{20,28},{24,16},{28,20},{1,9},{5... | collective-permute-start | bytes 663560 | tf_op jit(solution)/shard_map/ppermute | solution.py:46
  127.1 8.3 %collective-permute-start.36 = (bf16[48,576]{1,0:T(8,128)(2,1)S(1)}, bf16[48,576]{1,0:T(8,128)(2,1)S(1)}, u32[]{:S(2)}, u32[]{:S(2)}) collective-permute-start(bf16[48,576]{1,0:T(8,128)(2,1)S(1)} %get-tuple-element.163), channel_id=1, source_target_pairs={{0,1},{1,2},{2,3},{3,0},{4,5},{5,6},{6,7},{7,4},{8,9},{9,10},{10,1... | collective-permute-start | bytes 165896 | tf_op jit(solution)/shard_map/ppermute | solution.py:54
  129.4 6.0 %collective-permute-start.38 = (bf16[48,576]{1,0:T(8,128)(2,1)S(1)}, bf16[48,576]{1,0:T(8,128)(2,1)S(1)}, u32[]{:S(2)}, u32[]{:S(2)}) collective-permute-start(bf16[48,576]{1,0:T(8,128)(2,1)S(1)} %get-tuple-element.164), channel_id=1, source_target_pairs={{0,3},{1,0},{2,1},{3,2},{4,7},{5,4},{6,5},{7,6},{8,11},{9,8},{10,9... | collective-permute-start | bytes 165896 | tf_op jit(solution)/shard_map/ppermute | solution.py:54
  132.2 5.7 %collective-permute-start.37 = (bf16[48,576]{1,0:T(8,128)(2,1)S(1)}, bf16[48,576]{1,0:T(8,128)(2,1)S(1)}, u32[]{:S(2)}, u32[]{:S(2)}) collective-permute-start(bf16[48,576]{1,0:T(8,128)(2,1)S(1)} %get-tuple-element.165), channel_id=1, source_target_pairs={{0,2},{1,3},{2,0},{3,1},{4,6},{5,7},{6,4},{7,5},{8,10},{9,11},{10,... | collective-permute-start | bytes 165896 | tf_op jit(solution)/shard_map/ppermute | solution.py:54
  132.8 6.4 %collective-permute-start.31 = (bf16[4,80,384]{2,1,0:T(8,128)(2,1)S(1)}, bf16[4,80,384]{2,1,0:T(8,128)(2,1)S(1)}, u32[]{:S(2)}, u32[]{:S(2)}) collective-permute-start(bf16[4,80,384]{2,1,0:T(8,128)(2,1)S(1)} %get-tuple-element.154), channel_id=1, source_target_pairs={{0,8},{4,12},{8,0},{12,4},{16,24},{20,28},{24,16},{28,20},{1,9},{5... | collective-permute-start | bytes 737288 | tf_op jit(solution)/shard_map/ppermute | solution.py:46
  134.8 10.3 %collective-permute-start.21 = (bf16[4,144,384]{2,1,0:T(8,128)(2,1)S(1)}, bf16[4,144,384]{2,1,0:T(8,128)(2,1)S(1)}, u32[]{:S(2)}, u32[]{:S(2)}) collective-permute-start(bf16[4,144,384]{2,1,0:T(8,128)(2,1)S(1)} %get-tuple-element.152), channel_id=1, source_target_pairs={{0,16},{4,20},{8,24},{12,28},{16,0},{20,4},{24,8},{28,12},{1,17},{... | collective-permute-start | bytes 1327112 | tf_op jit(solution)/shard_map/ppermute | solution.py:46
  139.2 10.1 %collective-permute-start.32 = (bf16[80,384]{1,0:T(8,128)(2,1)S(1)}, bf16[80,384]{1,0:T(8,128)(2,1)S(1)}, u32[]{:S(2)}, u32[]{:S(2)}) collective-permute-start(bf16[80,384]{1,0:T(8,128)(2,1)S(1)} %get-tuple-element.160), channel_id=1, source_target_pairs={{0,1},{1,2},{2,3},{3,0},{4,5},{5,6},{6,7},{7,4},{8,9},{9,10},{10,1... | collective-permute-start | bytes 184328 | tf_op jit(solution)/shard_map/ppermute | solution.py:54
  141.2 8.7 %collective-permute-start.34 = (bf16[80,384]{1,0:T(8,128)(2,1)S(1)}, bf16[80,384]{1,0:T(8,128)(2,1)S(1)}, u32[]{:S(2)}, u32[]{:S(2)}) collective-permute-start(bf16[80,384]{1,0:T(8,128)(2,1)S(1)} %get-tuple-element.161), channel_id=1, source_target_pairs={{0,3},{1,0},{2,1},{3,2},{4,7},{5,4},{6,5},{7,6},{8,11},{9,8},{10,9... | collective-permute-start | bytes 184328 | tf_op jit(solution)/shard_map/ppermute | solution.py:54
  143.4 7.2 %collective-permute-start.33 = (bf16[80,384]{1,0:T(8,128)(2,1)S(1)}, bf16[80,384]{1,0:T(8,128)(2,1)S(1)}, u32[]{:S(2)}, u32[]{:S(2)}) collective-permute-start(bf16[80,384]{1,0:T(8,128)(2,1)S(1)} %get-tuple-element.162), channel_id=1, source_target_pairs={{0,2},{1,3},{2,0},{3,1},{4,6},{5,7},{6,4},{7,5},{8,10},{9,11},{10,... | collective-permute-start | bytes 184328 | tf_op jit(solution)/shard_map/ppermute | solution.py:54
  145.2 8.1 %collective-permute-start.22 = (bf16[144,384]{1,0:T(8,128)(2,1)S(1)}, bf16[144,384]{1,0:T(8,128)(2,1)S(1)}, u32[]{:S(2)}, u32[]{:S(2)}) collective-permute-start(bf16[144,384]{1,0:T(8,128)(2,1)S(1)} %get-tuple-element.157), channel_id=1, source_target_pairs={{0,1},{1,2},{2,3},{3,0},{4,5},{5,6},{6,7},{7,4},{8,9},{9,10},{10,1... | collective-permute-start | bytes 331784 | tf_op jit(solution)/shard_map/ppermute | solution.py:54
  147.0 6.4 %collective-permute-start.24 = (bf16[144,384]{1,0:T(8,128)(2,1)S(1)}, bf16[144,384]{1,0:T(8,128)(2,1)S(1)}, u32[]{:S(2)}, u32[]{:S(2)}) collective-permute-start(bf16[144,384]{1,0:T(8,128)(2,1)S(1)} %get-tuple-element.158), channel_id=1, source_target_pairs={{0,3},{1,0},{2,1},{3,2},{4,7},{5,4},{6,5},{7,6},{8,11},{9,8},{10,9... | collective-permute-start | bytes 331784 | tf_op jit(solution)/shard_map/ppermute | solution.py:54
  149.4 9.0 %collective-permute-start.23 = (bf16[144,384]{1,0:T(8,128)(2,1)S(1)}, bf16[144,384]{1,0:T(8,128)(2,1)S(1)}, u32[]{:S(2)}, u32[]{:S(2)}) collective-permute-start(bf16[144,384]{1,0:T(8,128)(2,1)S(1)} %get-tuple-element.159), channel_id=1, source_target_pairs={{0,2},{1,3},{2,0},{3,1},{4,6},{5,7},{6,4},{7,5},{8,10},{9,11},{10,... | collective-permute-start | bytes 331784 | tf_op jit(solution)/shard_map/ppermute | solution.py:54
  150.7 9.3 %collective-permute-start.39 = (bf16[176,384]{1,0:T(8,128)(2,1)S(1)}, bf16[176,384]{1,0:T(8,128)(2,1)S(1)}, u32[]{:S(2)}, u32[]{:S(2)}) collective-permute-start(bf16[176,384]{1,0:T(8,128)(2,1)S(1)} %get-tuple-element.173), channel_id=1, source_target_pairs={{0,8},{4,12},{8,0},{12,4},{16,24},{20,28},{24,16},{28,20},{1,9},{5... | collective-permute-start | bytes 405512 | tf_op jit(solution)/shard_map/ppermute | solution.py:46
  158.4 5.9 %collective-permute-start.25 = (bf16[144,384]{1,0:T(8,128)(2,1)S(1)}, bf16[144,384]{1,0:T(8,128)(2,1)S(1)}, u32[]{:S(2)}, u32[]{:S(2)}) collective-permute-start(bf16[144,384]{1,0:T(8,128)(2,1)S(1)} %fusion.20), channel_id=1, source_target_pairs={{0,16},{4,20},{8,24},{12,28},{16,0},{20,4},{24,8},{28,12},{1,17},{... | collective-permute-start | bytes 331784 | tf_op jit(solution)/shard_map/ppermute | solution.py:46
  160.1 8.4 %collective-permute-start.40 = (bf16[2,176,384]{2,1,0:T(8,128)(2,1)S(1)}, bf16[2,176,384]{2,1,0:T(8,128)(2,1)S(1)}, u32[]{:S(2)}, u32[]{:S(2)}) collective-permute-start(bf16[2,176,384]{2,1,0:T(8,128)(2,1)S(1)} %get-tuple-element.169), channel_id=1, source_target_pairs={{0,16},{4,20},{8,24},{12,28},{16,0},{20,4},{24,8},{28,12},{1,17},{... | collective-permute-start | bytes 811016 | tf_op jit(solution)/shard_map/ppermute | solution.py:46
  164.4 6.0 %collective-permute-start.26 = (bf16[2,144,384]{2,1,0:T(8,128)(2,1)S(1)}, bf16[2,144,384]{2,1,0:T(8,128)(2,1)S(1)}, u32[]{:S(2)}, u32[]{:S(2)}) collective-permute-start(bf16[2,144,384]{2,1,0:T(8,128)(2,1)S(1)} %get-tuple-element.171), channel_id=1, source_target_pairs={{0,8},{4,12},{8,0},{12,4},{16,24},{20,28},{24,16},{28,20},{1,9},{5... | collective-permute-start | bytes 663560 | tf_op jit(solution)/shard_map/ppermute | solution.py:46
  168.5 3.7 %collective-permute-start.41 = (bf16[2,2,176,384]{3,2,1,0:T(8,128)(2,1)S(1)}, bf16[2,2,176,384]{3,2,1,0:T(8,128)(2,1)S(1)}, u32[]{:S(2)}, u32[]{:S(2)}) collective-permute-start(bf16[2,2,176,384]{3,2,1,0:T(8,128)(2,1)S(1)} %pad_maximum_fusion.4.rest_pieces), channel_id=1, source_target_pairs={{0,4},{4,0},{8,12},{12,8},{16,20},{20,16},{24,28},{28,24},{1,5},{5... | collective-permute-start | bytes 1622024 | tf_op jit(solution)/shard_map/ppermute | solution.py:46
  170.4 1.9 %collective-permute-start.27 = (bf16[2,2,144,384]{3,2,1,0:T(8,128)(2,1)S(1)}, bf16[2,2,144,384]{3,2,1,0:T(8,128)(2,1)S(1)}, u32[]{:S(2)}, u32[]{:S(2)}) collective-permute-start(bf16[2,2,144,384]{3,2,1,0:T(8,128)(2,1)S(1)} %pad_maximum_fusion.5.pair_pieces), channel_id=1, source_target_pairs={{0,4},{4,0},{8,12},{12,8},{16,20},{20,16},{24,28},{28,24},{1,5},{5... | collective-permute-start | bytes 1327112 | tf_op jit(solution)/shard_map/ppermute | solution.py:46
  (2 other events, 1.6 us)

commit v4 on v3

--- a/solution.py
+++ b/solution.py
@@ -144,7 +144,8 @@
     w_query,
     w_key,
     w_value,
-    both_gains,
+    gain_one,
+    gain_two,
     gate,
     up,
     down_t,
@@ -164,8 +165,8 @@
     row = lax.broadcasted_iota(jnp.int32, (16, part), 0)
     gains = jnp.where(
         row == 0,
-        jnp.broadcast_to(both_gains[0:1].astype(f32), row.shape),
-        jnp.where(row == 1, jnp.broadcast_to(both_gains[1:2].astype(f32), row.shape), 0.0),
+        jnp.broadcast_to(gain_one[...].astype(f32), row.shape),
+        jnp.where(row == 1, jnp.broadcast_to(gain_two[...].astype(f32), row.shape), 0.0),
     )
     gains = jnp.concatenate([gains, jnp.zeros((16, packed - part), f32)], axis=1)
     own[part : part + 16] = pltpu.roll(gains, part * shard, 1).astype(low)
@@ -652,12 +653,13 @@
             w_query,
             w_key,
             w_value,
-            jnp.stack([gain_attn, gain_mlp]),
+            gain_attn[None],
+            gain_mlp[None],
             w_gate,
             w_up,
             w_down.T,
         ),
-        [VM] * 8,
+        [VM] * 9,
         (
             shape((part + 16, packed), low),
             shape((80, 384), low),
@@ -791,7 +793,7 @@
             pltpu.VMEM((hidden_width, width), low),
         ],
         19,
-        48,
+        38,
     )
     pair_sent = flip(pair_send, 0, replicas)
     down_sent = flip(down_send, 0, replicas)
@@ -847,7 +849,7 @@
     attn_left = halve(attn_keep, flip(after(attn_send, down_left[1], pair_left[1]), 0, replicas), 2, replicas)
     pair_left = halve(*pair_left, 2, replicas)
     down_left = halve(down_left[0], after(down_left[1], grad_tokens), 1, replicas)
-    attn_left = halve(*attn_left, 1, replicas)
+    attn_left = halve(attn_left[0], after(attn_left[1], pair_left[1]), 1, replicas)
     down_total = scatter_over_shards(*down_left, shards, replicas)
     pair_total = scatter_over_shards(*pair_left, shards, replicas)
     attn_total = scatter_over_shards(*attn_left, shards, replicas)

time: 177 us -> 179 us (1.011)
  waiting for transfers between devices: 66 us -> 76.8 us
  local copies, waits for them, and re-layouts: 7.67 us -> 2.62 us
  Pallas kernels: 43.5 us -> 41.2 us
    ppermute x24, waiting for transfers between devices: 49.8 us -> 60.8 us  [flip(): lax.ppermute(value, 'rep', [(i, i ^ 1 << bit) for i in range(replicas)])]
    unnamed x48 -> x20, local copies, waits for them, and re-layouts: 6.22 us -> 0.05 us
    broadcast_in_dim x0 -> x2, local copies, waits for them, and re-layouts: none -> 2.56 us  [the longest x1 1.34 us: local(): gain_attn[None]]
    pallas_call x12, Pallas kernels: 43.5 us -> 41.2 us  [call(): pl.pallas_call(kernel, name=name, in_specs=in_specs, out_shape=out_shape,...]
    ppermute x24, starting transfers between devices: 24.2 us -> 22.3 us  [flip(): lax.ppermute(value, 'rep', [(i, i ^ 1 << bit) for i in range(replicas)])]
  transfers between devices with their start and end apart: 42 -> 42, of which waited for: 25 -> 24; matrix products, arithmetic and copies ran while one was open for 1% -> 1% of each run, Pallas kernels for 13% -> 13%
where the time goes in v4:
time: 179 us; the launch traced here: 177 us
  waiting for transfers between devices  76.8 us (43%)
  starting transfers between devices  51.9 us (29%)
  Pallas kernels  41.2 us (23%)
  other arithmetic  2.71 us (2%)
  local copies, waits for them, and re-layouts  2.62 us (1%)
    ppermute x24, waiting for transfers between devices, flip(): lax.ppermute(value, 'rep', [(i, i ^ 1 << bit) for i in range(replicas)])  60.8 us
    pallas_call x12, Pallas kernels, call(): pl.pallas_call(kernel, name=name, in_specs=in_specs, out_shape=out_shape,...  41.2 us
    ppermute x24, starting transfers between devices, flip(): lax.ppermute(value, 'rep', [(i, i ^ 1 << bit) for i in range(replicas)])  22.3 us
    ppermute x9, starting transfers between devices, shift_to(): lax.ppermute(value, 'shard', [(s, (s + step) % shards) for s in range(sha...  15.6 us
    ppermute x9, starting transfers between devices, shift_from(): lax.ppermute(value, 'shard', [((s + step) % shards, s) for s in range(sha...  14 us
    ppermute x9, waiting for transfers between devices, shift_from(): lax.ppermute(value, 'shard', [((s + step) % shards, s) for s in range(sha...  8.06 us
    ppermute x9, waiting for transfers between devices, shift_to(): lax.ppermute(value, 'shard', [(s, (s + step) % shards) for s in range(sha...  7.99 us
  transfers between devices with their start and end apart: 42, of which 24 were waited for; matrix products, arithmetic and copies ran while one was open for 1% of the time, Pallas kernels for 13%

profile of v4, /device:TPU:0, one launch (start us, length us, event | category | flops | bytes accessed | tf_op | source)
XLA Modules:
  0.0 176.7 jit_solution(6631379177075863477)
XLA Ops:
  0.7 1.3 broadcast_in_dim.6.gain_one
  2.0 1.2 broadcast_in_dim.7.gain_two
  3.3 2.7 %pack.1 = (bf16[160,1536]{1,0:T(8,128)(2,1)}, bf16[80,384]{1,0:T(8,128)(2,1)}, bf16[144,384]{1,0:T(8,128)(2,1)}, bf16[48,576]{1,0:T(8,128)(2,1)}, bf16[384,576]{1,0:T(8,128)(2,1)}) custom-call(bf16[144,576]{1,0:T(8,128)(2,1)} %w_out.1, bf16[144,576]{1,0:T(8,128)(2,1)} %w_query.1, bf16[144,192]{1,0:T(8,128)(2,1)} %w_key.1, bf16[144,192]{1,0:T(8,128)(2,1)} %w_value.1, ...), custom_call_target="tpu_custom_call" | custom-call | flops 20000000 | bytes 1161216 | tf_op jit(solution)/shard_map/pack/pallas_call | solution.py:612
  6.0 3.0 %collective-permute-start.2 = (bf16[80,384]{1,0:T(8,128)(2,1)}, bf16[80,384]{1,0:T(8,128)(2,1)S(1)}, u32[]{:S(2)}, u32[]{:S(2)}) collective-permute-start(bf16[80,384]{1,0:T(8,128)(2,1)} %get-tuple-element.84), channel_id=1, source_target_pairs={{3,0},{0,1},{1,2},{2,3},{7,4},{4,5},{5,6},{6,7},{11,8},{8,9},{9,10... | collective-permute-start | bytes 184328 | tf_op jit(solution)/shard_map/ppermute | solution.py:50
  9.0 2.6 %collective-permute-start.1 = (bf16[80,384]{1,0:T(8,128)(2,1)}, bf16[80,384]{1,0:T(8,128)(2,1)S(1)}, u32[]{:S(2)}, u32[]{:S(2)}) collective-permute-start(bf16[80,384]{1,0:T(8,128)(2,1)} %get-tuple-element.84), channel_id=1, source_target_pairs={{2,0},{3,1},{0,2},{1,3},{6,4},{7,5},{4,6},{5,7},{10,8},{11,9},{8,1... | collective-permute-start | bytes 184328 | tf_op jit(solution)/shard_map/ppermute | solution.py:50
  11.6 1.3 collective-permute-start
  12.9 1.6 prepare.1
  14.5 0.7 collective-permute-start.6
  15.6 2.8 %collective-permute-start.4 = (bf16[144,384]{1,0:T(8,128)(2,1)}, bf16[144,384]{1,0:T(8,128)(2,1)S(1)}, u32[]{:S(2)}, u32[]{:S(2)}) collective-permute-start(bf16[144,384]{1,0:T(8,128)(2,1)} %get-tuple-element.87), channel_id=1, source_target_pairs={{1,0},{2,1},{3,2},{0,3},{5,4},{6,5},{7,6},{4,7},{9,8},{10,9},{11,1... | collective-permute-start | bytes 331784 | tf_op jit(solution)/shard_map/ppermute | solution.py:50
  18.4 0.6 collective-permute-start.9
  19.1 1.5 collective-permute-start.8
  20.6 2.0 %collective-permute-done.6 = bf16[144,384]{1,0:T(8,128)(2,1)S(1)} collective-permute-done((bf16[144,384]{1,0:T(8,128)(2,1)}, bf16[144,384]{1,0:T(8,128)(2,1)S(1)}, u32[]{:S(2)}, u32[]{:S(2)}) %collective-permute-start.6) | collective-permute-done | bytes 110624 | tf_op jit(solution)/shard_map/ppermute | solution.py:50
  22.6 1.0 collective-permute-start.7
  23.6 3.2 %collective-permute-done.5 = bf16[144,384]{1,0:T(8,128)(2,1)S(1)} collective-permute-done((bf16[144,384]{1,0:T(8,128)(2,1)}, bf16[144,384]{1,0:T(8,128)(2,1)S(1)}, u32[]{:S(2)}, u32[]{:S(2)}) %collective-permute-start.5) | collective-permute-done | bytes 110624 | tf_op jit(solution)/shard_map/ppermute | solution.py:50
  26.8 1.5 collective-permute-start.3
  29.0 2.8 %collective-permute-done.8 = bf16[48,576]{1,0:T(8,128)(2,1)S(1)} collective-permute-done((bf16[48,576]{1,0:T(8,128)(2,1)S(1)}, bf16[48,576]{1,0:T(8,128)(2,1)S(1)}, u32[]{:S(2)}, u32[]{:S(2)}) %collective-permute-start.8) | collective-permute-done | bytes 55328 | tf_op jit(solution)/shard_map/ppermute | solution.py:50
  31.8 2.5 %collective-permute-done.3 = bf16[3,80,384]{2,1,0:T(8,128)(2,1)S(1)} collective-permute-done((bf16[3,80,384]{2,1,0:T(8,128)(2,1)S(1)}, bf16[3,80,384]{2,1,0:T(8,128)(2,1)S(1)}, u32[]{:S(2)}, u32[]{:S(2)}) %collective-permute-start.3) | collective-permute-done | bytes 184352 | tf_op jit(solution)/shard_map/ppermute | solution.py:46
  34.4 1.6 collective-permute-start.10
  36.0 2.8 %collective-permute-done.11 = bf16[3,144,384]{2,1,0:T(8,128)(2,1)S(1)} collective-permute-done((bf16[3,144,384]{2,1,0:T(8,128)(2,1)S(1)}, bf16[3,144,384]{2,1,0:T(8,128)(2,1)S(1)}, u32[]{:S(2)}, u32[]{:S(2)}) %collective-permute-start.11) | collective-permute-done | bytes 331808 | tf_op jit(solution)/shard_map/ppermute | solution.py:46
  38.8 3.2 %collective-permute-done.10 = bf16[2,3,80,384]{3,2,1,0:T(8,128)(2,1)S(1)} collective-permute-done((bf16[2,3,80,384]{3,2,1,0:T(8,128)(2,1)S(1)}, bf16[2,3,80,384]{3,2,1,0:T(8,128)(2,1)S(1)}, u32[]{:S(2)}, u32[]{:S(2)}) %collective-permute-start.10) | collective-permute-done | bytes 368672 | tf_op jit(solution)/shard_map/ppermute | solution.py:46
  42.2 1.6 collective-permute-start.13
  44.4 2.2 %project.1 = (bf16[640,1536]{1,0:T(8,128)(2,1)S(1)}, f32[8,576]{1,0:T(8,128)S(1)}, bf16[512,576]{1,0:T(8,128)(2,1)S(1)}, bf16[9,512,64]{2,1,0:T(8,128)(2,1)S(1)}...) custom-call(f32[512,576]{1,0:T(8,128)S(1)} %get-tuple-element.80.scaled, ...), custom_call_target="tpu_custom_call" | custom-call | flops 50000000 | bytes 3557376 | tf_op jit(solution)/shard_map/project/pallas_call | solution.py:612
  46.5 3.1 %collective-permute-done.13 = bf16[3,48,576]{2,1,0:T(8,128)(2,1)S(1)} collective-permute-done((bf16[3,48,576]{2,1,0:T(8,128)(2,1)S(1)}, bf16[3,48,576]{2,1,0:T(8,128)(2,1)S(1)}, u32[]{:S(2)}, u32[]{:S(2)}) %collective-permute-start.13) | collective-permute-done | bytes 165920 | tf_op jit(solution)/shard_map/ppermute | solution.py:46
  49.7 1.6 collective-permute-start.14
  51.3 1.9 %attend_1.1 = (bf16[512,192]{1,0:T(8,128)(2,1)S(1)}, f32[3,512,1]{2,1,0:T(8,128)S(1)}) custom-call(f32[512,512]{1,0:T(8,128)S(1)} %get-tuple-element.79.bias, bf16[9,512,64]{2,1,0:T(8,128)(2,1)S(1)} %get-tuple-element.92.query, bf16[3,512,64]{2,1,0:T(8,128)(2,1)S(1)} %get-tuple-element.93.keys, bf16[3,512,64]{2,1,0:T(8,128)(2,1)S(1)} %get-tuple-element.94.values), custom_call_target="tpu_custom_call" | custom-call | flops 30000000 | bytes 202752 | tf_op jit(solution)/shard_map/attend_1/pallas_call | solution.py:612
  53.2 1.9 %attend_0.1 = (bf16[512,192]{1,0:T(8,128)(2,1)S(1)}, f32[3,512,1]{2,1,0:T(8,128)S(1)}) custom-call(f32[512,512]{1,0:T(8,128)S(1)} %get-tuple-element.79.bias, bf16[9,512,64]{2,1,0:T(8,128)(2,1)S(1)} %get-tuple-element.92.query, bf16[3,512,64]{2,1,0:T(8,128)(2,1)S(1)} %get-tuple-element.93.keys, bf16[3,512,64]{2,1,0:T(8,128)(2,1)S(1)} %get-tuple-element.94.values), custom_call_target="tpu_custom_call" | custom-call | flops 30000000 | bytes 202752 | tf_op jit(solution)/shard_map/attend_0/pallas_call | solution.py:612
  55.1 4.4 %collective-permute-done.14 = bf16[2,3,48,576]{3,2,1,0:T(8,128)(2,1)S(1)} collective-permute-done((bf16[2,3,48,576]{3,2,1,0:T(8,128)(2,1)S(1)}, bf16[2,3,48,576]{3,2,1,0:T(8,128)(2,1)S(1)}, u32[]{:S(2)}, u32[]{:S(2)}) %collective-permute-start.14) | collective-permute-done | bytes 331808 | tf_op jit(solution)/shard_map/ppermute | solution.py:46
  59.6 2.7 %attend_2.1 = (bf16[512,192]{1,0:T(8,128)(2,1)S(1)}, f32[3,512,1]{2,1,0:T(8,128)S(1)}, f32[512,576]{1,0:T(8,128)S(1)}, bf16[512,576]{1,0:T(8,128)(2,1)S(1)}) custom-call(f32[512,512]{1,0:T(8,128)S(1)} %get-tuple-element.79.bias, bf16[9,512,64]{2,1,0:T(8,128)(2,1)S(1)} %get-tuple-element.92.query, bf16[3,512,64]{2,1,0:T(8,128)(2,1)S(1)} %get-tuple-element.93.keys, ...), custom_call_target="tpu_custom_call" | custom-call | flops 40000000 | bytes 1972224 | tf_op jit(solution)/shard_map/attend_2/pallas_call | solution.py:612
  62.3 1.1 collective-permute-done.15
  64.2 3.6 %collective-permute-done.17.down_other = bf16[2,2,3,48,576]{4,3,2,1,0:T(8,128)(2,1)S(1)} collective-permute-done((bf16[2,2,3,48,576]{4,3,2,1,0:T(8,128)(2,1)S(1)}, bf16[2,2,3,48,576]{4,3,2,1,0:T(8,128)(2,1)S(1)}, u32[]{:S(2)}, u32[]{:S(2)}) %collective-permute-start.17) | collective-permute-done | bytes 663584 | tf_op jit(solution)/shard_map/ppermute | solution.py:46
  67.8 13.6 %feed.1 = (bf16[576,512]{1,0:T(8,128)(2,1)}, f32[512,576]{1,0:T(8,128)S(1)}, f32[8,576]{1,0:T(8,128)S(1)}, bf16[2,2,4,144,384]{4,3,2,1,0:T(8,128)(2,1)S(1)}, bf1...) custom-call(f32[512,576]{1,0:T(8,128)S(1)} %get-tuple-element.104.hi, ...), custom_call_target="tpu_custom_call" | custom-call | flops 190000000 | bytes 7096320 | tf_op jit(solution)/shard_map/feed/pallas_call | solution.py:612
  81.9 2.9 %back_0.1 = (bf16[512,256]{1,0:T(8,128)(2,1)S(1)}, bf16[512,64]{1,0:T(8,128)(2,1)S(1)}, bf16[192,576]{1,0:T(8,128)(2,1)S(1)}) custom-call(f32[512,512]{1,0:T(8,128)S(1)} %get-tuple-element.79.bias, f32[512,128]{1,0:T(8,128)S(1)} %get-tuple-element.81.cosine, f32[512,128]{1,0:T(8,128)S(1)} %get-tuple-element.82.sine, ...), custom_call_target="tpu_custom_call" | custom-call | flops 50000000 | bytes 548864 | tf_op jit(solution)/shard_map/back_0/pallas_call | solution.py:612
  85.5 1.6 collective-permute-start.20
  87.4 1.6 collective-permute-start.28
  89.0 3.2 %back_1.1 = (bf16[512,256]{1,0:T(8,128)(2,1)S(1)}, bf16[512,64]{1,0:T(8,128)(2,1)S(1)}, bf16[192,576]{1,0:T(8,128)(2,1)S(1)}) custom-call(f32[512,512]{1,0:T(8,128)S(1)} %get-tuple-element.79.bias, f32[512,128]{1,0:T(8,128)S(1)} %get-tuple-element.81.cosine, f32[512,128]{1,0:T(8,128)S(1)} %get-tuple-element.82.sine, ...), custom_call_target="tpu_custom_call" | custom-call | flops 50000000 | bytes 548864 | tf_op jit(solution)/shard_map/back_1/pallas_call | solution.py:612
  92.1 2.9 %back_2.1 = (bf16[512,256]{1,0:T(8,128)(2,1)S(1)}, bf16[512,64]{1,0:T(8,128)(2,1)S(1)}, bf16[192,576]{1,0:T(8,128)(2,1)S(1)}) custom-call(f32[512,512]{1,0:T(8,128)S(1)} %get-tuple-element.79.bias, f32[512,128]{1,0:T(8,128)S(1)} %get-tuple-element.81.cosine, f32[512,128]{1,0:T(8,128)S(1)} %get-tuple-element.82.sine, ...), custom_call_target="tpu_custom_call" | custom-call | flops 50000000 | bytes 548864 | tf_op jit(solution)/shard_map/back_2/pallas_call | solution.py:612
  95.1 3.5 %back_last.1 = (bf16[576,512]{1,0:T(8,128)(2,1)}, bf16[2,2,4,80,384]{4,3,2,1,0:T(8,128)(2,1)S(1)}, bf16[2,2,4,80,384]{4,3,2,1,0:T(8,128)(2,1)S(1)}) custom-call(f32[512,576]{1,0:T(8,128)S(1)} %get-tuple-element.101.hidden_in, f32[8,576]{1,0:T(8,128)S(1)} %get-tuple-element.102.gains, bf16[640,1536]{1,0:T(8,128)(2,1)S(1)} %get-tuple-element.103.weights, ...), custom_call_target="tpu_custom_call" | custom-call | flops 60000000 | bytes 2555904 | tf_op jit(solution)/shard_map/back_last/pallas_call | solution.py:612
  98.6 1.8 %collective-permute-done.28 = bf16[2,4,48,576]{3,2,1,0:T(8,128)(2,1)S(1)} collective-permute-done((bf16[2,4,48,576]{3,2,1,0:T(8,128)(2,1)S(1)}, bf16[2,4,48,576]{3,2,1,0:T(8,128)(2,1)S(1)}, u32[]{:S(2)}, u32[]{:S(2)}) %collective-permute-start.28) | collective-permute-done | bytes 442400 | tf_op jit(solution)/shard_map/ppermute | solution.py:46
  100.4 6.9 %collective-permute-done.20 = bf16[2,4,144,384]{3,2,1,0:T(8,128)(2,1)S(1)} collective-permute-done((bf16[2,4,144,384]{3,2,1,0:T(8,128)(2,1)S(1)}, bf16[2,4,144,384]{3,2,1,0:T(8,128)(2,1)S(1)}, u32[]{:S(2)}, u32[]{:S(2)}) %collective-permute-start.20) | collective-permute-done | bytes 884768 | tf_op jit(solution)/shard_map/ppermute | solution.py:46
  107.4 1.6 collective-permute-start.35
  109.0 0.9 collective-permute-done.29
  110.1 1.6 collective-permute-start.30
  112.5 3.3 %collective-permute-done.35 = bf16[4,48,576]{2,1,0:T(8,128)(2,1)S(1)} collective-permute-done((bf16[4,48,576]{2,1,0:T(8,128)(2,1)S(1)}, bf16[4,48,576]{2,1,0:T(8,128)(2,1)S(1)}, u32[]{:S(2)}, u32[]{:S(2)}) %collective-permute-start.35) | collective-permute-done | bytes 221216 | tf_op jit(solution)/shard_map/ppermute | solution.py:46
  115.9 2.3 %collective-permute-start.36 = (bf16[48,576]{1,0:T(8,128)(2,1)S(1)}, bf16[48,576]{1,0:T(8,128)(2,1)S(1)}, u32[]{:S(2)}, u32[]{:S(2)}) collective-permute-start(bf16[48,576]{1,0:T(8,128)(2,1)S(1)} %get-tuple-element.165), channel_id=1, source_target_pairs={{0,1},{1,2},{2,3},{3,0},{4,5},{5,6},{6,7},{7,4},{8,9},{9,10},{10,1... | collective-permute-start | bytes 165896 | tf_op jit(solution)/shard_map/ppermute | solution.py:54
  118.2 2.8 %collective-permute-start.38 = (bf16[48,576]{1,0:T(8,128)(2,1)S(1)}, bf16[48,576]{1,0:T(8,128)(2,1)S(1)}, u32[]{:S(2)}, u32[]{:S(2)}) collective-permute-start(bf16[48,576]{1,0:T(8,128)(2,1)S(1)} %get-tuple-element.166), channel_id=1, source_target_pairs={{0,3},{1,0},{2,1},{3,2},{4,7},{5,4},{6,5},{7,6},{8,11},{9,8},{10,9... | collective-permute-start | bytes 165896 | tf_op jit(solution)/shard_map/ppermute | solution.py:54
  121.5 11.5 %collective-permute-done.21 = bf16[4,144,384]{2,1,0:T(8,128)(2,1)S(1)} collective-permute-done((bf16[4,144,384]{2,1,0:T(8,128)(2,1)S(1)}, bf16[4,144,384]{2,1,0:T(8,128)(2,1)S(1)}, u32[]{:S(2)}, u32[]{:S(2)}) %collective-permute-start.21) | collective-permute-done | bytes 442400 | tf_op jit(solution)/shard_map/ppermute | solution.py:46
  133.1 1.6 collective-permute-start.31
  134.7 5.6 %collective-permute-done.31 = bf16[4,80,384]{2,1,0:T(8,128)(2,1)S(1)} collective-permute-done((bf16[4,80,384]{2,1,0:T(8,128)(2,1)S(1)}, bf16[4,80,384]{2,1,0:T(8,128)(2,1)S(1)}, u32[]{:S(2)}, u32[]{:S(2)}) %collective-permute-start.31) | collective-permute-done | bytes 245792 | tf_op jit(solution)/shard_map/ppermute | solution.py:46
  140.4 2.3 %collective-permute-start.32 = (bf16[80,384]{1,0:T(8,128)(2,1)S(1)}, bf16[80,384]{1,0:T(8,128)(2,1)S(1)}, u32[]{:S(2)}, u32[]{:S(2)}) collective-permute-start(bf16[80,384]{1,0:T(8,128)(2,1)S(1)} %get-tuple-element.162), channel_id=1, source_target_pairs={{0,1},{1,2},{2,3},{3,0},{4,5},{5,6},{6,7},{7,4},{8,9},{9,10},{10,1... | collective-permute-start | bytes 184328 | tf_op jit(solution)/shard_map/ppermute | solution.py:54
  142.6 2.8 %collective-permute-start.34 = (bf16[80,384]{1,0:T(8,128)(2,1)S(1)}, bf16[80,384]{1,0:T(8,128)(2,1)S(1)}, u32[]{:S(2)}, u32[]{:S(2)}) collective-permute-start(bf16[80,384]{1,0:T(8,128)(2,1)S(1)} %get-tuple-element.163), channel_id=1, source_target_pairs={{0,3},{1,0},{2,1},{3,2},{4,7},{5,4},{6,5},{7,6},{8,11},{9,8},{10,9... | collective-permute-start | bytes 184328 | tf_op jit(solution)/shard_map/ppermute | solution.py:54
  146.0 2.1 %collective-permute-start.22 = (bf16[144,384]{1,0:T(8,128)(2,1)S(1)}, bf16[144,384]{1,0:T(8,128)(2,1)S(1)}, u32[]{:S(2)}, u32[]{:S(2)}) collective-permute-start(bf16[144,384]{1,0:T(8,128)(2,1)S(1)} %get-tuple-element.159), channel_id=1, source_target_pairs={{0,1},{1,2},{2,3},{3,0},{4,5},{5,6},{6,7},{7,4},{8,9},{9,10},{10,1... | collective-permute-start | bytes 331784 | tf_op jit(solution)/shard_map/ppermute | solution.py:54
  148.1 1.8 %collective-permute-start.24 = (bf16[144,384]{1,0:T(8,128)(2,1)S(1)}, bf16[144,384]{1,0:T(8,128)(2,1)S(1)}, u32[]{:S(2)}, u32[]{:S(2)}) collective-permute-start(bf16[144,384]{1,0:T(8,128)(2,1)S(1)} %get-tuple-element.160), channel_id=1, source_target_pairs={{0,3},{1,0},{2,1},{3,2},{4,7},{5,4},{6,5},{7,6},{8,11},{9,8},{10,9... | collective-permute-start | bytes 331784 | tf_op jit(solution)/shard_map/ppermute | solution.py:54
  149.9 0.6 collective-permute-start.23
  150.5 4.4 %collective-permute-done.33 = bf16[80,384]{1,0:T(8,128)(2,1)S(1)} collective-permute-done((bf16[80,384]{1,0:T(8,128)(2,1)S(1)}, bf16[80,384]{1,0:T(8,128)(2,1)S(1)}, u32[]{:S(2)}, u32[]{:S(2)}) %collective-permute-start.33) | collective-permute-done | bytes 61472 | tf_op jit(solution)/shard_map/ppermute | solution.py:54
  155.0 1.6 collective-permute-start.39
  156.6 3.6 %collective-permute-done.23 = bf16[144,384]{1,0:T(8,128)(2,1)S(1)} collective-permute-done((bf16[144,384]{1,0:T(8,128)(2,1)S(1)}, bf16[144,384]{1,0:T(8,128)(2,1)S(1)}, u32[]{:S(2)}, u32[]{:S(2)}) %collective-permute-start.23) | collective-permute-done | bytes 110624 | tf_op jit(solution)/shard_map/ppermute | solution.py:54
  160.2 1.6 collective-permute-start.25
  161.9 0.6 collective-permute-start.40
  162.4 3.8 %collective-permute-done.25 = bf16[144,384]{1,0:T(8,128)(2,1)S(1)} collective-permute-done((bf16[144,384]{1,0:T(8,128)(2,1)S(1)}, bf16[144,384]{1,0:T(8,128)(2,1)S(1)}, u32[]{:S(2)}, u32[]{:S(2)}) %collective-permute-start.25) | collective-permute-done | bytes 110624 | tf_op jit(solution)/shard_map/ppermute | solution.py:46
  166.3 1.6 collective-permute-start.26
  167.8 2.8 %collective-permute-done.40 = bf16[2,176,384]{2,1,0:T(8,128)(2,1)S(1)} collective-permute-done((bf16[2,176,384]{2,1,0:T(8,128)(2,1)S(1)}, bf16[2,176,384]{2,1,0:T(8,128)(2,1)S(1)}, u32[]{:S(2)}, u32[]{:S(2)}) %collective-permute-start.40) | collective-permute-done | bytes 270368 | tf_op jit(solution)/shard_map/ppermute | solution.py:46
  170.8 1.5 collective-permute-done.26
  172.4 1.8 %collective-permute-done.27.pair_other = bf16[2,2,144,384]{3,2,1,0:T(8,128)(2,1)S(1)} collective-permute-done((bf16[2,2,144,384]{3,2,1,0:T(8,128)(2,1)S(1)}, bf16[2,2,144,384]{3,2,1,0:T(8,128)(2,1)S(1)}, u32[]{:S(2)}, u32[]{:S(2)}) %collective-permute-start.27) | collective-permute-done | bytes 442400 | tf_op jit(solution)/shard_map/ppermute | solution.py:46
  174.2 2.1 %finish.1 = (f32[144,576]{1,0:T(8,128)}, f32[144,192]{1,0:T(8,128)}, f32[144,192]{1,0:T(8,128)}, f32[144,576]{1,0:T(8,128)}, f32[1,144]{1,0:T(1,128)}, /*index=5...) custom-call(bf16[2,2,144,384]{3,2,1,0:T(8,128)(2,1)S(1)} %pad_maximum_fusion.5.pair_pieces, ...), custom_call_target="tpu_custom_call" | custom-call | flops 50000000 | bytes 3540096 | tf_op jit(solution)/shard_map/finish/pallas_call | solution.py:612
  (82 shorter events, 7.5 us)
Async XLA Ops:
  0.6 12.3 %copy-start.6 = (f32[520,128]{1,0:T(8,128)S(1)}, f32[520,128]{1,0:T(8,128)}, u32[]{:S(2)}) copy-start(f32[520,128]{1,0:T(8,128)} %constant.8.clone.table_sin) | copy-start | bytes 798724
  0.7 12.3 %copy-start.7 = (f32[520,128]{1,0:T(8,128)S(1)}, f32[520,128]{1,0:T(8,128)}, u32[]{:S(2)}) copy-start(f32[520,128]{1,0:T(8,128)} %constant.7.clone.table_cos) | copy-start | bytes 798724
  0.7 12.3 %copy-start.8 = (s32[1,4]{1,0:T(1,128)S(1)}, s32[1,4]{1,0:T(1,128)}, u32[]{:S(2)}) copy-start(s32[1,4]{1,0:T(1,128)} %lengths.3) | copy-start | bytes 52
  0.7 12.2 %copy-start.3 = (bf16[512,576]{0,1:T(8,128)(2,1)S(1)}, bf16[512,576]{0,1:T(8,128)(2,1)}, u32[]{:S(2)}) copy-start(bf16[512,576]{0,1:T(8,128)(2,1)} %param.25) | copy-start | bytes 1769476
  0.7 12.2 %copy-start.2 = (bf16[512,576]{0,1:T(8,128)(2,1)S(1)}, bf16[512,576]{0,1:T(8,128)(2,1)}, u32[]{:S(2)}) copy-start(bf16[512,576]{0,1:T(8,128)(2,1)} %param.14) | copy-start | bytes 1769476
  6.0 12.5 %copy-start.9 = (bf16[48,576]{1,0:T(8,128)(2,1)S(1)}, bf16[48,576]{1,0:T(8,128)(2,1)}, u32[]{:S(2)}) copy-start(bf16[48,576]{1,0:T(8,128)(2,1)} %get-tuple-element.89) | copy-start | bytes 165892
  6.0 9.6 %collective-permute-start.2 = (bf16[80,384]{1,0:T(8,128)(2,1)}, bf16[80,384]{1,0:T(8,128)(2,1)S(1)}, u32[]{:S(2)}, u32[]{:S(2)}) collective-permute-start(bf16[80,384]{1,0:T(8,128)(2,1)} %get-tuple-element.84), channel_id=1, source_target_pairs={{3,0},{0,1},{1,2},{2,3},{7,4},{4,5},{5,6},{6,7},{11,8},{8,9},{9,10... | collective-permute-start | bytes 184328 | tf_op jit(solution)/shard_map/ppermute | solution.py:50
  9.0 9.4 %collective-permute-start.1 = (bf16[80,384]{1,0:T(8,128)(2,1)}, bf16[80,384]{1,0:T(8,128)(2,1)S(1)}, u32[]{:S(2)}, u32[]{:S(2)}) collective-permute-start(bf16[80,384]{1,0:T(8,128)(2,1)} %get-tuple-element.84), channel_id=1, source_target_pairs={{2,0},{3,1},{0,2},{1,3},{6,4},{7,5},{4,6},{5,7},{10,8},{11,9},{8,1... | collective-permute-start | bytes 184328 | tf_op jit(solution)/shard_map/ppermute | solution.py:50
  11.6 6.8 %collective-permute-start = (bf16[80,384]{1,0:T(8,128)(2,1)}, bf16[80,384]{1,0:T(8,128)(2,1)S(1)}, u32[]{:S(2)}, u32[]{:S(2)}) collective-permute-start(bf16[80,384]{1,0:T(8,128)(2,1)} %get-tuple-element.84), channel_id=1, source_target_pairs={{1,0},{2,1},{3,2},{0,3},{5,4},{6,5},{7,6},{4,7},{9,8},{10,9},{11,1... | collective-permute-start | bytes 184328 | tf_op jit(solution)/shard_map/ppermute | solution.py:50
  14.5 8.1 %collective-permute-start.6 = (bf16[144,384]{1,0:T(8,128)(2,1)}, bf16[144,384]{1,0:T(8,128)(2,1)S(1)}, u32[]{:S(2)}, u32[]{:S(2)}) collective-permute-start(bf16[144,384]{1,0:T(8,128)(2,1)} %get-tuple-element.87), channel_id=1, source_target_pairs={{3,0},{0,1},{1,2},{2,3},{7,4},{4,5},{5,6},{6,7},{11,8},{8,9},{9,10... | collective-permute-start | bytes 331784 | tf_op jit(solution)/shard_map/ppermute | solution.py:50
  15.2 11.6 %collective-permute-start.5 = (bf16[144,384]{1,0:T(8,128)(2,1)}, bf16[144,384]{1,0:T(8,128)(2,1)S(1)}, u32[]{:S(2)}, u32[]{:S(2)}) collective-permute-start(bf16[144,384]{1,0:T(8,128)(2,1)} %get-tuple-element.87), channel_id=1, source_target_pairs={{2,0},{3,1},{0,2},{1,3},{6,4},{7,5},{4,6},{5,7},{10,8},{11,9},{8,1... | collective-permute-start | bytes 331784 | tf_op jit(solution)/shard_map/ppermute | solution.py:50
  15.6 12.7 %collective-permute-start.4 = (bf16[144,384]{1,0:T(8,128)(2,1)}, bf16[144,384]{1,0:T(8,128)(2,1)S(1)}, u32[]{:S(2)}, u32[]{:S(2)}) collective-permute-start(bf16[144,384]{1,0:T(8,128)(2,1)} %get-tuple-element.87), channel_id=1, source_target_pairs={{1,0},{2,1},{3,2},{0,3},{5,4},{6,5},{7,6},{4,7},{9,8},{10,9},{11,1... | collective-permute-start | bytes 331784 | tf_op jit(solution)/shard_map/ppermute | solution.py:50
  18.4 10.5 %collective-permute-start.9 = (bf16[48,576]{1,0:T(8,128)(2,1)S(1)}, bf16[48,576]{1,0:T(8,128)(2,1)S(1)}, u32[]{:S(2)}, u32[]{:S(2)}) collective-permute-start(bf16[48,576]{1,0:T(8,128)(2,1)S(1)} %copy-done.9), channel_id=1, source_target_pairs={{3,0},{0,1},{1,2},{2,3},{7,4},{4,5},{5,6},{6,7},{11,8},{8,9},{9,10... | collective-permute-start | bytes 165896 | tf_op jit(solution)/shard_map/ppermute | solution.py:50
  19.1 12.7 %collective-permute-start.8 = (bf16[48,576]{1,0:T(8,128)(2,1)S(1)}, bf16[48,576]{1,0:T(8,128)(2,1)S(1)}, u32[]{:S(2)}, u32[]{:S(2)}) collective-permute-start(bf16[48,576]{1,0:T(8,128)(2,1)S(1)} %copy-done.9), channel_id=1, source_target_pairs={{2,0},{3,1},{0,2},{1,3},{6,4},{7,5},{4,6},{5,7},{10,8},{11,9},{8,1... | collective-permute-start | bytes 165896 | tf_op jit(solution)/shard_map/ppermute | solution.py:50
  22.6 9.2 %collective-permute-start.7 = (bf16[48,576]{1,0:T(8,128)(2,1)S(1)}, bf16[48,576]{1,0:T(8,128)(2,1)S(1)}, u32[]{:S(2)}, u32[]{:S(2)}) collective-permute-start(bf16[48,576]{1,0:T(8,128)(2,1)S(1)} %copy-done.9), channel_id=1, source_target_pairs={{1,0},{2,1},{3,2},{0,3},{5,4},{6,5},{7,6},{4,7},{9,8},{10,9},{11,1... | collective-permute-start | bytes 165896 | tf_op jit(solution)/shard_map/ppermute | solution.py:50
  26.8 7.6 %collective-permute-start.3 = (bf16[3,80,384]{2,1,0:T(8,128)(2,1)S(1)}, bf16[3,80,384]{2,1,0:T(8,128)(2,1)S(1)}, u32[]{:S(2)}, u32[]{:S(2)}) collective-permute-start(bf16[3,80,384]{2,1,0:T(8,128)(2,1)S(1)} %pad_maximum_fusion.11), channel_id=1, source_target_pairs={{0,16},{4,20},{8,24},{12,28},{16,0},{20,4},{24,8},{28,12},{1,17},{... | collective-permute-start | bytes 552968 | tf_op jit(solution)/shard_map/ppermute | solution.py:46
  28.4 10.3 %collective-permute-start.11 = (bf16[3,144,384]{2,1,0:T(8,128)(2,1)S(1)}, bf16[3,144,384]{2,1,0:T(8,128)(2,1)S(1)}, u32[]{:S(2)}, u32[]{:S(2)}) collective-permute-start(bf16[3,144,384]{2,1,0:T(8,128)(2,1)S(1)} %get-tuple-element.169), channel_id=1, source_target_pairs={{0,16},{4,20},{8,24},{12,28},{16,0},{20,4},{24,8},{28,12},{1,17},{... | collective-permute-start | bytes 995336 | tf_op jit(solution)/shard_map/ppermute | solution.py:46
  34.4 10.0 %copy-start.4 = (bf16[160,1536]{1,0:T(8,128)(2,1)S(1)}, bf16[160,1536]{1,0:T(8,128)(2,1)}, u32[]{:S(2)}) copy-start(bf16[160,1536]{1,0:T(8,128)(2,1)} %get-tuple-element.83.own) | copy-start | bytes 1474564
  34.4 7.6 %collective-permute-start.10 = (bf16[2,3,80,384]{3,2,1,0:T(8,128)(2,1)S(1)}, bf16[2,3,80,384]{3,2,1,0:T(8,128)(2,1)S(1)}, u32[]{:S(2)}, u32[]{:S(2)}) collective-permute-start(bf16[2,3,80,384]{3,2,1,0:T(8,128)(2,1)S(1)} %pad_maximum_fusion.6), channel_id=1, source_target_pairs={{0,8},{4,12},{8,0},{12,4},{16,24},{20,28},{24,16},{28,20},{1,9},{5... | collective-permute-start | bytes 1105928 | tf_op jit(solution)/shard_map/ppermute | solution.py:46
  42.1 2.3 %collective-permute-start.12 = (bf16[2,2,3,80,384]{4,3,2,1,0:T(8,128)(2,1)S(1)}, bf16[2,2,3,80,384]{4,3,2,1,0:T(8,128)(2,1)S(1)}, u32[]{:S(2)}, u32[]{:S(2)}) collective-permute-start(bf16[2,2,3,80,384]{4,3,2,1,0:T(8,128)(2,1)S(1)} %pad_maximum_fusion.1.pieces), channel_id=1, source_target_pairs={{0,4},{4,0},{8,12},{12,8},{16,20},{20,16},{24,28},{28,24},{1,5},{5... | collective-permute-start | bytes 2211848 | tf_op jit(solution)/shard_map/ppermute | solution.py:46
  42.2 7.5 %collective-permute-start.13 = (bf16[3,48,576]{2,1,0:T(8,128)(2,1)S(1)}, bf16[3,48,576]{2,1,0:T(8,128)(2,1)S(1)}, u32[]{:S(2)}, u32[]{:S(2)}) collective-permute-start(bf16[3,48,576]{2,1,0:T(8,128)(2,1)S(1)} %pad_maximum_fusion.12), channel_id=1, source_target_pairs={{0,8},{4,12},{8,0},{12,4},{16,24},{20,28},{24,16},{28,20},{1,9},{5... | collective-permute-start | bytes 497672 | tf_op jit(solution)/shard_map/ppermute | solution.py:46
  43.7 19.7 %collective-permute-start.15 = (bf16[2,3,144,384]{3,2,1,0:T(8,128)(2,1)S(1)}, bf16[2,3,144,384]{3,2,1,0:T(8,128)(2,1)S(1)}, u32[]{:S(2)}, u32[]{:S(2)}) collective-permute-start(bf16[2,3,144,384]{3,2,1,0:T(8,128)(2,1)S(1)} %pad_maximum_fusion.3), channel_id=1, source_target_pairs={{0,8},{4,12},{8,0},{12,4},{16,24},{20,28},{24,16},{28,20},{1,9},{5... | collective-permute-start | bytes 1990664 | tf_op jit(solution)/shard_map/ppermute | solution.py:46
  49.7 9.8 %collective-permute-start.14 = (bf16[2,3,48,576]{3,2,1,0:T(8,128)(2,1)S(1)}, bf16[2,3,48,576]{3,2,1,0:T(8,128)(2,1)S(1)}, u32[]{:S(2)}, u32[]{:S(2)}) collective-permute-start(bf16[2,3,48,576]{3,2,1,0:T(8,128)(2,1)S(1)} %pad_maximum_fusion.7), channel_id=1, source_target_pairs={{0,16},{4,20},{8,24},{12,28},{16,0},{20,4},{24,8},{28,12},{1,17},{... | collective-permute-start | bytes 995336 | tf_op jit(solution)/shard_map/ppermute | solution.py:46
  62.3 5.5 %copy-start = (bf16[144,1536]{1,0:T(8,128)(2,1)S(1)}, bf16[144,1536]{1,0:T(8,128)(2,1)}, u32[]{:S(2)}) copy-start(bf16[144,1536]{1,0:T(8,128)(2,1)} %own_gate.1) | copy-start | bytes 1327108
  62.3 5.5 %copy-start.1 = (bf16[144,1536]{1,0:T(8,128)(2,1)S(1)}, bf16[144,1536]{1,0:T(8,128)(2,1)}, u32[]{:S(2)}) copy-start(bf16[144,1536]{1,0:T(8,128)(2,1)} %own_up.1) | copy-start | bytes 1327108
  62.3 5.5 %copy-start.5 = (bf16[384,576]{1,0:T(8,128)(2,1)S(1)}, bf16[384,576]{1,0:T(8,128)(2,1)}, u32[]{:S(2)}) copy-start(bf16[384,576]{1,0:T(8,128)(2,1)} %get-tuple-element.107.own_down) | copy-start | bytes 1327108
  63.6 4.2 %collective-permute-start.16 = (bf16[2,2,3,144,384]{4,3,2,1,0:T(8,128)(2,1)S(1)}, bf16[2,2,3,144,384]{4,3,2,1,0:T(8,128)(2,1)S(1)}, u32[]{:S(2)}, u32[]{:S(2)}) collective-permute-start(bf16[2,2,3,144,384]{4,3,2,1,0:T(8,128)(2,1)S(1)} %pad_maximum_fusion.pair_pieces), channel_id=1, source_target_pairs={{0,4},{4,0},{8,12},{12,8},{16,20},{20,16},{24,28},{28,24},{1,5},{5... | collective-permute-start | bytes 3981320 | tf_op jit(solution)/shard_map/ppermute | solution.py:46
  63.7 4.1 %collective-permute-start.17 = (bf16[2,2,3,48,576]{4,3,2,1,0:T(8,128)(2,1)S(1)}, bf16[2,2,3,48,576]{4,3,2,1,0:T(8,128)(2,1)S(1)}, u32[]{:S(2)}, u32[]{:S(2)}) collective-permute-start(bf16[2,2,3,48,576]{4,3,2,1,0:T(8,128)(2,1)S(1)} %pad_maximum_fusion.2.down_pieces), channel_id=1, source_target_pairs={{0,4},{4,0},{8,12},{12,8},{16,20},{20,16},{24,28},{28,24},{1,5},{5... | collective-permute-start | bytes 1990664 | tf_op jit(solution)/shard_map/ppermute | solution.py:46
  81.4 3.7 %collective-permute-start.18 = (bf16[2,2,4,144,384]{4,3,2,1,0:T(8,128)(2,1)S(1)}, bf16[2,2,4,144,384]{4,3,2,1,0:T(8,128)(2,1)S(1)}, u32[]{:S(2)}, u32[]{:S(2)}) collective-permute-start(bf16[2,2,4,144,384]{4,3,2,1,0:T(8,128)(2,1)S(1)} %get-tuple-element.111), channel_id=1, source_target_pairs={{0,4},{4,0},{8,12},{12,8},{16,20},{20,16},{24,28},{28,24},{1,5},{5... | collective-permute-start | bytes 5308424 | tf_op jit(solution)/shard_map/ppermute | solution.py:46
  81.5 5.6 %collective-permute-start.19 = (bf16[2,2,4,48,576]{4,3,2,1,0:T(8,128)(2,1)S(1)}, bf16[2,2,4,48,576]{4,3,2,1,0:T(8,128)(2,1)S(1)}, u32[]{:S(2)}, u32[]{:S(2)}) collective-permute-start(bf16[2,2,4,48,576]{4,3,2,1,0:T(8,128)(2,1)S(1)} %get-tuple-element.112), channel_id=1, source_target_pairs={{0,4},{4,0},{8,12},{12,8},{16,20},{20,16},{24,28},{28,24},{1,5},{5... | collective-permute-start | bytes 2654216 | tf_op jit(solution)/shard_map/ppermute | solution.py:46
  85.5 21.8 %collective-permute-start.20 = (bf16[2,4,144,384]{3,2,1,0:T(8,128)(2,1)S(1)}, bf16[2,4,144,384]{3,2,1,0:T(8,128)(2,1)S(1)}, u32[]{:S(2)}, u32[]{:S(2)}) collective-permute-start(bf16[2,4,144,384]{3,2,1,0:T(8,128)(2,1)S(1)} %get-tuple-element.148), channel_id=1, source_target_pairs={{0,8},{4,12},{8,0},{12,4},{16,24},{20,28},{24,16},{28,20},{1,9},{5... | collective-permute-start | bytes 2654216 | tf_op jit(solution)/shard_map/ppermute | solution.py:46
  87.4 13.0 %collective-permute-start.28 = (bf16[2,4,48,576]{3,2,1,0:T(8,128)(2,1)S(1)}, bf16[2,4,48,576]{3,2,1,0:T(8,128)(2,1)S(1)}, u32[]{:S(2)}, u32[]{:S(2)}) collective-permute-start(bf16[2,4,48,576]{3,2,1,0:T(8,128)(2,1)S(1)} %get-tuple-element.151), channel_id=1, source_target_pairs={{0,16},{4,20},{8,24},{12,28},{16,0},{20,4},{24,8},{28,12},{1,17},{... | collective-permute-start | bytes 1327112 | tf_op jit(solution)/shard_map/ppermute | solution.py:46
  107.3 2.6 %collective-permute-start.29 = (bf16[2,2,4,80,384]{4,3,2,1,0:T(8,128)(2,1)S(1)}, bf16[2,2,4,80,384]{4,3,2,1,0:T(8,128)(2,1)S(1)}, u32[]{:S(2)}, u32[]{:S(2)}) collective-permute-start(bf16[2,2,4,80,384]{4,3,2,1,0:T(8,128)(2,1)S(1)} %get-tuple-element.135), channel_id=1, source_target_pairs={{0,4},{4,0},{8,12},{12,8},{16,20},{20,16},{24,28},{28,24},{1,5},{5... | collective-permute-start | bytes 2949128 | tf_op jit(solution)/shard_map/ppermute | solution.py:46
  107.4 8.4 %collective-permute-start.35 = (bf16[4,48,576]{2,1,0:T(8,128)(2,1)S(1)}, bf16[4,48,576]{2,1,0:T(8,128)(2,1)S(1)}, u32[]{:S(2)}, u32[]{:S(2)}) collective-permute-start(bf16[4,48,576]{2,1,0:T(8,128)(2,1)S(1)} %get-tuple-element.158), channel_id=1, source_target_pairs={{0,8},{4,12},{8,0},{12,4},{16,24},{20,28},{24,16},{28,20},{1,9},{5... | collective-permute-start | bytes 663560 | tf_op jit(solution)/shard_map/ppermute | solution.py:46
  110.1 22.8 %collective-permute-start.30 = (bf16[2,4,80,384]{3,2,1,0:T(8,128)(2,1)S(1)}, bf16[2,4,80,384]{3,2,1,0:T(8,128)(2,1)S(1)}, u32[]{:S(2)}, u32[]{:S(2)}) collective-permute-start(bf16[2,4,80,384]{3,2,1,0:T(8,128)(2,1)S(1)} %get-tuple-element.149), channel_id=1, source_target_pairs={{0,16},{4,20},{8,24},{12,28},{16,0},{20,4},{24,8},{28,12},{1,17},{... | collective-permute-start | bytes 1474568 | tf_op jit(solution)/shard_map/ppermute | solution.py:46
  112.0 21.0 %collective-permute-start.21 = (bf16[4,144,384]{2,1,0:T(8,128)(2,1)S(1)}, bf16[4,144,384]{2,1,0:T(8,128)(2,1)S(1)}, u32[]{:S(2)}, u32[]{:S(2)}) collective-permute-start(bf16[4,144,384]{2,1,0:T(8,128)(2,1)S(1)} %get-tuple-element.154), channel_id=1, source_target_pairs={{0,16},{4,20},{8,24},{12,28},{16,0},{20,4},{24,8},{28,12},{1,17},{... | collective-permute-start | bytes 1327112 | tf_op jit(solution)/shard_map/ppermute | solution.py:46
  115.9 18.7 %collective-permute-start.36 = (bf16[48,576]{1,0:T(8,128)(2,1)S(1)}, bf16[48,576]{1,0:T(8,128)(2,1)S(1)}, u32[]{:S(2)}, u32[]{:S(2)}) collective-permute-start(bf16[48,576]{1,0:T(8,128)(2,1)S(1)} %get-tuple-element.165), channel_id=1, source_target_pairs={{0,1},{1,2},{2,3},{3,0},{4,5},{5,6},{6,7},{7,4},{8,9},{9,10},{10,1... | collective-permute-start | bytes 165896 | tf_op jit(solution)/shard_map/ppermute | solution.py:54
  118.2 16.5 %collective-permute-start.38 = (bf16[48,576]{1,0:T(8,128)(2,1)S(1)}, bf16[48,576]{1,0:T(8,128)(2,1)S(1)}, u32[]{:S(2)}, u32[]{:S(2)}) collective-permute-start(bf16[48,576]{1,0:T(8,128)(2,1)S(1)} %get-tuple-element.166), channel_id=1, source_target_pairs={{0,3},{1,0},{2,1},{3,2},{4,7},{5,4},{6,5},{7,6},{8,11},{9,8},{10,9... | collective-permute-start | bytes 165896 | tf_op jit(solution)/shard_map/ppermute | solution.py:54
  121.0 13.7 %collective-permute-start.37 = (bf16[48,576]{1,0:T(8,128)(2,1)S(1)}, bf16[48,576]{1,0:T(8,128)(2,1)S(1)}, u32[]{:S(2)}, u32[]{:S(2)}) collective-permute-start(bf16[48,576]{1,0:T(8,128)(2,1)S(1)} %get-tuple-element.167), channel_id=1, source_target_pairs={{0,2},{1,3},{2,0},{3,1},{4,6},{5,7},{6,4},{7,5},{8,10},{9,11},{10,... | collective-permute-start | bytes 165896 | tf_op jit(solution)/shard_map/ppermute | solution.py:54
  133.1 7.2 %collective-permute-start.31 = (bf16[4,80,384]{2,1,0:T(8,128)(2,1)S(1)}, bf16[4,80,384]{2,1,0:T(8,128)(2,1)S(1)}, u32[]{:S(2)}, u32[]{:S(2)}) collective-permute-start(bf16[4,80,384]{2,1,0:T(8,128)(2,1)S(1)} %get-tuple-element.156), channel_id=1, source_target_pairs={{0,8},{4,12},{8,0},{12,4},{16,24},{20,28},{24,16},{28,20},{1,9},{5... | collective-permute-start | bytes 737288 | tf_op jit(solution)/shard_map/ppermute | solution.py:46
  140.4 9.5 %collective-permute-start.32 = (bf16[80,384]{1,0:T(8,128)(2,1)S(1)}, bf16[80,384]{1,0:T(8,128)(2,1)S(1)}, u32[]{:S(2)}, u32[]{:S(2)}) collective-permute-start(bf16[80,384]{1,0:T(8,128)(2,1)S(1)} %get-tuple-element.162), channel_id=1, source_target_pairs={{0,1},{1,2},{2,3},{3,0},{4,5},{5,6},{6,7},{7,4},{8,9},{9,10},{10,1... | collective-permute-start | bytes 184328 | tf_op jit(solution)/shard_map/ppermute | solution.py:54
  142.6 7.9 %collective-permute-start.34 = (bf16[80,384]{1,0:T(8,128)(2,1)S(1)}, bf16[80,384]{1,0:T(8,128)(2,1)S(1)}, u32[]{:S(2)}, u32[]{:S(2)}) collective-permute-start(bf16[80,384]{1,0:T(8,128)(2,1)S(1)} %get-tuple-element.163), channel_id=1, source_target_pairs={{0,3},{1,0},{2,1},{3,2},{4,7},{5,4},{6,5},{7,6},{8,11},{9,8},{10,9... | collective-permute-start | bytes 184328 | tf_op jit(solution)/shard_map/ppermute | solution.py:54
  145.4 9.5 %collective-permute-start.33 = (bf16[80,384]{1,0:T(8,128)(2,1)S(1)}, bf16[80,384]{1,0:T(8,128)(2,1)S(1)}, u32[]{:S(2)}, u32[]{:S(2)}) collective-permute-start(bf16[80,384]{1,0:T(8,128)(2,1)S(1)} %get-tuple-element.164), channel_id=1, source_target_pairs={{0,2},{1,3},{2,0},{3,1},{4,6},{5,7},{6,4},{7,5},{8,10},{9,11},{10,... | collective-permute-start | bytes 184328 | tf_op jit(solution)/shard_map/ppermute | solution.py:54
  146.0 10.6 %collective-permute-start.22 = (bf16[144,384]{1,0:T(8,128)(2,1)S(1)}, bf16[144,384]{1,0:T(8,128)(2,1)S(1)}, u32[]{:S(2)}, u32[]{:S(2)}) collective-permute-start(bf16[144,384]{1,0:T(8,128)(2,1)S(1)} %get-tuple-element.159), channel_id=1, source_target_pairs={{0,1},{1,2},{2,3},{3,0},{4,5},{5,6},{6,7},{7,4},{8,9},{9,10},{10,1... | collective-permute-start | bytes 331784 | tf_op jit(solution)/shard_map/ppermute | solution.py:54
  148.1 8.5 %collective-permute-start.24 = (bf16[144,384]{1,0:T(8,128)(2,1)S(1)}, bf16[144,384]{1,0:T(8,128)(2,1)S(1)}, u32[]{:S(2)}, u32[]{:S(2)}) collective-permute-start(bf16[144,384]{1,0:T(8,128)(2,1)S(1)} %get-tuple-element.160), channel_id=1, source_target_pairs={{0,3},{1,0},{2,1},{3,2},{4,7},{5,4},{6,5},{7,6},{8,11},{9,8},{10,9... | collective-permute-start | bytes 331784 | tf_op jit(solution)/shard_map/ppermute | solution.py:54
  149.9 10.3 %collective-permute-start.23 = (bf16[144,384]{1,0:T(8,128)(2,1)S(1)}, bf16[144,384]{1,0:T(8,128)(2,1)S(1)}, u32[]{:S(2)}, u32[]{:S(2)}) collective-permute-start(bf16[144,384]{1,0:T(8,128)(2,1)S(1)} %get-tuple-element.161), channel_id=1, source_target_pairs={{0,2},{1,3},{2,0},{3,1},{4,6},{5,7},{6,4},{7,5},{8,10},{9,11},{10,... | collective-permute-start | bytes 331784 | tf_op jit(solution)/shard_map/ppermute | solution.py:54
  155.0 6.8 %collective-permute-start.39 = (bf16[176,384]{1,0:T(8,128)(2,1)S(1)}, bf16[176,384]{1,0:T(8,128)(2,1)S(1)}, u32[]{:S(2)}, u32[]{:S(2)}) collective-permute-start(bf16[176,384]{1,0:T(8,128)(2,1)S(1)} %get-tuple-element.175), channel_id=1, source_target_pairs={{0,8},{4,12},{8,0},{12,4},{16,24},{20,28},{24,16},{28,20},{1,9},{5... | collective-permute-start | bytes 405512 | tf_op jit(solution)/shard_map/ppermute | solution.py:46
  160.2 6.0 %collective-permute-start.25 = (bf16[144,384]{1,0:T(8,128)(2,1)S(1)}, bf16[144,384]{1,0:T(8,128)(2,1)S(1)}, u32[]{:S(2)}, u32[]{:S(2)}) collective-permute-start(bf16[144,384]{1,0:T(8,128)(2,1)S(1)} %fusion.20), channel_id=1, source_target_pairs={{0,16},{4,20},{8,24},{12,28},{16,0},{20,4},{24,8},{28,12},{1,17},{... | collective-permute-start | bytes 331784 | tf_op jit(solution)/shard_map/ppermute | solution.py:46
  161.9 8.8 %collective-permute-start.40 = (bf16[2,176,384]{2,1,0:T(8,128)(2,1)S(1)}, bf16[2,176,384]{2,1,0:T(8,128)(2,1)S(1)}, u32[]{:S(2)}, u32[]{:S(2)}) collective-permute-start(bf16[2,176,384]{2,1,0:T(8,128)(2,1)S(1)} %get-tuple-element.171), channel_id=1, source_target_pairs={{0,16},{4,20},{8,24},{12,28},{16,0},{20,4},{24,8},{28,12},{1,17},{... | collective-permute-start | bytes 811016 | tf_op jit(solution)/shard_map/ppermute | solution.py:46
  166.3 6.0 %collective-permute-start.26 = (bf16[2,144,384]{2,1,0:T(8,128)(2,1)S(1)}, bf16[2,144,384]{2,1,0:T(8,128)(2,1)S(1)}, u32[]{:S(2)}, u32[]{:S(2)}) collective-permute-start(bf16[2,144,384]{2,1,0:T(8,128)(2,1)S(1)} %get-tuple-element.173), channel_id=1, source_target_pairs={{0,8},{4,12},{8,0},{12,4},{16,24},{20,28},{24,16},{28,20},{1,9},{5... | collective-permute-start | bytes 663560 | tf_op jit(solution)/shard_map/ppermute | solution.py:46
  170.7 3.5 %collective-permute-start.41 = (bf16[2,2,176,384]{3,2,1,0:T(8,128)(2,1)S(1)}, bf16[2,2,176,384]{3,2,1,0:T(8,128)(2,1)S(1)}, u32[]{:S(2)}, u32[]{:S(2)}) collective-permute-start(bf16[2,2,176,384]{3,2,1,0:T(8,128)(2,1)S(1)} %pad_maximum_fusion.4.rest_pieces), channel_id=1, source_target_pairs={{0,4},{4,0},{8,12},{12,8},{16,20},{20,16},{24,28},{28,24},{1,5},{5... | collective-permute-start | bytes 1622024 | tf_op jit(solution)/shard_map/ppermute | solution.py:46
  172.3 1.9 %collective-permute-start.27 = (bf16[2,2,144,384]{3,2,1,0:T(8,128)(2,1)S(1)}, bf16[2,2,144,384]{3,2,1,0:T(8,128)(2,1)S(1)}, u32[]{:S(2)}, u32[]{:S(2)}) collective-permute-start(bf16[2,2,144,384]{3,2,1,0:T(8,128)(2,1)S(1)} %pad_maximum_fusion.5.pair_pieces), channel_id=1, source_target_pairs={{0,4},{4,0},{8,12},{12,8},{16,20},{20,16},{24,28},{28,24},{1,5},{5... | collective-permute-start | bytes 1327112 | tf_op jit(solution)/shard_map/ppermute | solution.py:46

commit v5 on v3

--- a/solution.py
+++ b/solution.py
@@ -791,7 +791,7 @@
             pltpu.VMEM((hidden_width, width), low),
         ],
         19,
-        48,
+        38,
     )
     pair_sent = flip(pair_send, 0, replicas)
     down_sent = flip(down_send, 0, replicas)
@@ -844,14 +844,19 @@
         6,
         24,
     )
-    attn_left = halve(attn_keep, flip(after(attn_send, down_left[1], pair_left[1]), 0, replicas), 2, replicas)
+    attn_sent = flip(after(attn_send, down_left[1], pair_left[1]), 0, replicas)
     pair_left = halve(*pair_left, 2, replicas)
+    attn_left = halve(attn_keep, after(attn_sent, pair_left[1]), 2, replicas)
+    pair_total = scatter_over_shards(*pair_left, shards, replicas)
     down_left = halve(down_left[0], after(down_left[1], grad_tokens), 1, replicas)
-    attn_left = halve(*attn_left, 1, replicas)
+    attn_left = halve(attn_left[0], after(attn_left[1], pair_total), 1, replicas)
+    pair_half = gather_bit(pair_total, 2, replicas)
+    attn_left = (attn_left[0], after(attn_left[1], pair_half))
     down_total = scatter_over_shards(*down_left, shards, replicas)
-    pair_total = scatter_over_shards(*pair_left, shards, replicas)
     attn_total = scatter_over_shards(*attn_left, shards, replicas)
-    pair_pieces = spread(pair_total, (2, 1, 0), replicas)
+    pair_half = gather_bit(pair_half, 1, replicas)
+    pair_pieces = spread(pair_half, (0,), replicas)
+    attn_total = after(attn_total, pair_half)
     rest_pieces = spread(jnp.concatenate([attn_total, fold(down_total)]), (1, 2, 0), replicas)
     g_query, g_key, g_value, g_out, g_gain_one, g_gain_two, g_gate, g_up, g_down = call(
         finish_kernel,

time: 177 us -> 177 us (level)
  waiting for transfers between devices: 66 us -> 72.9 us
  local copies, waits for them, and re-layouts: 7.67 us -> 1.5 us
  Pallas kernels: 43.5 us -> 41.2 us
    unnamed x48 -> x20, local copies, waits for them, and re-layouts: 6.22 us -> 0.05 us
    ppermute x24, waiting for transfers between devices: 49.8 us -> 54.6 us  [flip(): lax.ppermute(value, 'rep', [(i, i ^ 1 << bit) for i in range(replicas)])]
    pallas_call x12, Pallas kernels: 43.5 us -> 41.2 us  [call(): pl.pallas_call(kernel, name=name, in_specs=in_specs, out_shape=out_shape,...]
    ppermute x9, waiting for transfers between devices: 8.17 us -> 10.2 us  [shift_to(): lax.ppermute(value, 'shard', [(s, (s + step) % shards) for s in range(sha...]
where the time goes in v5:
time: 177 us; the launch traced here: 174 us
  waiting for transfers between devices  72.9 us (41%)
  starting transfers between devices  54 us (31%)
  Pallas kernels  41.2 us (23%)
  other arithmetic  3.29 us (2%)
    ppermute x24, waiting for transfers between devices, flip(): lax.ppermute(value, 'rep', [(i, i ^ 1 << bit) for i in range(replicas)])  54.6 us
    pallas_call x12, Pallas kernels, call(): pl.pallas_call(kernel, name=name, in_specs=in_specs, out_shape=out_shape,...  41.2 us
    ppermute x24, starting transfers between devices, flip(): lax.ppermute(value, 'rep', [(i, i ^ 1 << bit) for i in range(replicas)])  23.8 us
    ppermute x9, starting transfers between devices, shift_to(): lax.ppermute(value, 'shard', [(s, (s + step) % shards) for s in range(sha...  16.3 us
    ppermute x9, starting transfers between devices, shift_from(): lax.ppermute(value, 'shard', [((s + step) % shards, s) for s in range(sha...  14 us
    ppermute x9, waiting for transfers between devices, shift_to(): lax.ppermute(value, 'shard', [(s, (s + step) % shards) for s in range(sha...  10.2 us
    ppermute x9, waiting for transfers between devices, shift_from(): lax.ppermute(value, 'shard', [((s + step) % shards, s) for s in range(sha...  8.06 us
  transfers between devices with their start and end apart: 42, of which 25 were waited for; matrix products, arithmetic and copies ran while one was open for 1% of the time, Pallas kernels for 13%

profile of v5, /device:TPU:0, one launch (start us, length us, event | category | flops | bytes accessed | tf_op | source)
XLA Modules:
  0.0 174.3 jit_solution(3207652432721483079)
XLA Ops:
  0.7 0.8 stack.135
  1.5 0.7 stack.136
  2.7 2.7 %pack.1 = (bf16[160,1536]{1,0:T(8,128)(2,1)}, bf16[80,384]{1,0:T(8,128)(2,1)}, bf16[144,384]{1,0:T(8,128)(2,1)}, bf16[48,576]{1,0:T(8,128)(2,1)}, bf16[384,576]{1,0:T(8,128)(2,1)}) custom-call(bf16[144,576]{1,0:T(8,128)(2,1)} %w_out.1, bf16[144,576]{1,0:T(8,128)(2,1)} %w_query.1, bf16[144,192]{1,0:T(8,128)(2,1)} %w_key.1, bf16[144,192]{1,0:T(8,128)(2,1)} %w_value.1, ...), custom_call_target="tpu_custom_call" | custom-call | flops 20000000 | bytes 1161216 | tf_op jit(solution)/shard_map/pack/pallas_call | solution.py:611
  5.4 3.0 %collective-permute-start.2 = (bf16[80,384]{1,0:T(8,128)(2,1)}, bf16[80,384]{1,0:T(8,128)(2,1)S(1)}, u32[]{:S(2)}, u32[]{:S(2)}) collective-permute-start(bf16[80,384]{1,0:T(8,128)(2,1)} %get-tuple-element.87), channel_id=1, source_target_pairs={{3,0},{0,1},{1,2},{2,3},{7,4},{4,5},{5,6},{6,7},{11,8},{8,9},{9,10... | collective-permute-start | bytes 184328 | tf_op jit(solution)/shard_map/ppermute | solution.py:50
  8.4 2.6 %collective-permute-start.1 = (bf16[80,384]{1,0:T(8,128)(2,1)}, bf16[80,384]{1,0:T(8,128)(2,1)S(1)}, u32[]{:S(2)}, u32[]{:S(2)}) collective-permute-start(bf16[80,384]{1,0:T(8,128)(2,1)} %get-tuple-element.87), channel_id=1, source_target_pairs={{2,0},{3,1},{0,2},{1,3},{6,4},{7,5},{4,6},{5,7},{10,8},{11,9},{8,1... | collective-permute-start | bytes 184328 | tf_op jit(solution)/shard_map/ppermute | solution.py:50
  11.0 1.3 collective-permute-start
  12.4 1.6 prepare.1
  13.9 0.7 collective-permute-start.6
  15.0 2.8 %collective-permute-start.4 = (bf16[144,384]{1,0:T(8,128)(2,1)}, bf16[144,384]{1,0:T(8,128)(2,1)S(1)}, u32[]{:S(2)}, u32[]{:S(2)}) collective-permute-start(bf16[144,384]{1,0:T(8,128)(2,1)} %get-tuple-element.90), channel_id=1, source_target_pairs={{1,0},{2,1},{3,2},{0,3},{5,4},{6,5},{7,6},{4,7},{9,8},{10,9},{11,1... | collective-permute-start | bytes 331784 | tf_op jit(solution)/shard_map/ppermute | solution.py:50
  17.9 0.6 collective-permute-start.9
  18.5 1.5 collective-permute-start.8
  20.0 2.0 %collective-permute-done.6 = bf16[144,384]{1,0:T(8,128)(2,1)S(1)} collective-permute-done((bf16[144,384]{1,0:T(8,128)(2,1)}, bf16[144,384]{1,0:T(8,128)(2,1)S(1)}, u32[]{:S(2)}, u32[]{:S(2)}) %collective-permute-start.6) | collective-permute-done | bytes 110624 | tf_op jit(solution)/shard_map/ppermute | solution.py:50
  22.1 1.0 collective-permute-start.7
  23.0 3.2 %collective-permute-done.5 = bf16[144,384]{1,0:T(8,128)(2,1)S(1)} collective-permute-done((bf16[144,384]{1,0:T(8,128)(2,1)}, bf16[144,384]{1,0:T(8,128)(2,1)S(1)}, u32[]{:S(2)}, u32[]{:S(2)}) %collective-permute-start.5) | collective-permute-done | bytes 110624 | tf_op jit(solution)/shard_map/ppermute | solution.py:50
  26.2 1.5 collective-permute-start.3
  28.4 2.8 %collective-permute-done.8 = bf16[48,576]{1,0:T(8,128)(2,1)S(1)} collective-permute-done((bf16[48,576]{1,0:T(8,128)(2,1)S(1)}, bf16[48,576]{1,0:T(8,128)(2,1)S(1)}, u32[]{:S(2)}, u32[]{:S(2)}) %collective-permute-start.8) | collective-permute-done | bytes 55328 | tf_op jit(solution)/shard_map/ppermute | solution.py:50
  31.3 2.5 %collective-permute-done.3 = bf16[3,80,384]{2,1,0:T(8,128)(2,1)S(1)} collective-permute-done((bf16[3,80,384]{2,1,0:T(8,128)(2,1)S(1)}, bf16[3,80,384]{2,1,0:T(8,128)(2,1)S(1)}, u32[]{:S(2)}, u32[]{:S(2)}) %collective-permute-start.3) | collective-permute-done | bytes 184352 | tf_op jit(solution)/shard_map/ppermute | solution.py:46
  33.9 1.6 collective-permute-start.10
  35.4 2.8 %collective-permute-done.11 = bf16[3,144,384]{2,1,0:T(8,128)(2,1)S(1)} collective-permute-done((bf16[3,144,384]{2,1,0:T(8,128)(2,1)S(1)}, bf16[3,144,384]{2,1,0:T(8,128)(2,1)S(1)}, u32[]{:S(2)}, u32[]{:S(2)}) %collective-permute-start.11) | collective-permute-done | bytes 331808 | tf_op jit(solution)/shard_map/ppermute | solution.py:46
  38.2 3.2 %collective-permute-done.10 = bf16[2,3,80,384]{3,2,1,0:T(8,128)(2,1)S(1)} collective-permute-done((bf16[2,3,80,384]{3,2,1,0:T(8,128)(2,1)S(1)}, bf16[2,3,80,384]{3,2,1,0:T(8,128)(2,1)S(1)}, u32[]{:S(2)}, u32[]{:S(2)}) %collective-permute-start.10) | collective-permute-done | bytes 368672 | tf_op jit(solution)/shard_map/ppermute | solution.py:46
  41.6 1.6 collective-permute-start.13
  43.8 2.2 %project.1 = (bf16[640,1536]{1,0:T(8,128)(2,1)S(1)}, f32[8,576]{1,0:T(8,128)S(1)}, bf16[512,576]{1,0:T(8,128)(2,1)S(1)}, bf16[9,512,64]{2,1,0:T(8,128)(2,1)S(1)}...) custom-call(f32[512,576]{1,0:T(8,128)S(1)} %get-tuple-element.83.scaled, ...), custom_call_target="tpu_custom_call" | custom-call | flops 50000000 | bytes 3557376 | tf_op jit(solution)/shard_map/project/pallas_call | solution.py:611
  46.0 3.1 %collective-permute-done.13 = bf16[3,48,576]{2,1,0:T(8,128)(2,1)S(1)} collective-permute-done((bf16[3,48,576]{2,1,0:T(8,128)(2,1)S(1)}, bf16[3,48,576]{2,1,0:T(8,128)(2,1)S(1)}, u32[]{:S(2)}, u32[]{:S(2)}) %collective-permute-start.13) | collective-permute-done | bytes 165920 | tf_op jit(solution)/shard_map/ppermute | solution.py:46
  49.2 1.6 collective-permute-start.14
  50.7 1.9 %attend_1.1 = (bf16[512,192]{1,0:T(8,128)(2,1)S(1)}, f32[3,512,1]{2,1,0:T(8,128)S(1)}) custom-call(f32[512,512]{1,0:T(8,128)S(1)} %get-tuple-element.82.bias, bf16[9,512,64]{2,1,0:T(8,128)(2,1)S(1)} %get-tuple-element.95.query, bf16[3,512,64]{2,1,0:T(8,128)(2,1)S(1)} %get-tuple-element.96.keys, bf16[3,512,64]{2,1,0:T(8,128)(2,1)S(1)} %get-tuple-element.97.values), custom_call_target="tpu_custom_call" | custom-call | flops 30000000 | bytes 202752 | tf_op jit(solution)/shard_map/attend_1/pallas_call | solution.py:611
  52.7 1.9 %attend_0.1 = (bf16[512,192]{1,0:T(8,128)(2,1)S(1)}, f32[3,512,1]{2,1,0:T(8,128)S(1)}) custom-call(f32[512,512]{1,0:T(8,128)S(1)} %get-tuple-element.82.bias, bf16[9,512,64]{2,1,0:T(8,128)(2,1)S(1)} %get-tuple-element.95.query, bf16[3,512,64]{2,1,0:T(8,128)(2,1)S(1)} %get-tuple-element.96.keys, bf16[3,512,64]{2,1,0:T(8,128)(2,1)S(1)} %get-tuple-element.97.values), custom_call_target="tpu_custom_call" | custom-call | flops 30000000 | bytes 202752 | tf_op jit(solution)/shard_map/attend_0/pallas_call | solution.py:611
  54.6 4.4 %collective-permute-done.14 = bf16[2,3,48,576]{3,2,1,0:T(8,128)(2,1)S(1)} collective-permute-done((bf16[2,3,48,576]{3,2,1,0:T(8,128)(2,1)S(1)}, bf16[2,3,48,576]{3,2,1,0:T(8,128)(2,1)S(1)}, u32[]{:S(2)}, u32[]{:S(2)}) %collective-permute-start.14) | collective-permute-done | bytes 331808 | tf_op jit(solution)/shard_map/ppermute | solution.py:46
  59.0 2.7 %attend_2.1 = (bf16[512,192]{1,0:T(8,128)(2,1)S(1)}, f32[3,512,1]{2,1,0:T(8,128)S(1)}, f32[512,576]{1,0:T(8,128)S(1)}, bf16[512,576]{1,0:T(8,128)(2,1)S(1)}) custom-call(f32[512,512]{1,0:T(8,128)S(1)} %get-tuple-element.82.bias, bf16[9,512,64]{2,1,0:T(8,128)(2,1)S(1)} %get-tuple-element.95.query, bf16[3,512,64]{2,1,0:T(8,128)(2,1)S(1)} %get-tuple-element.96.keys, ...), custom_call_target="tpu_custom_call" | custom-call | flops 40000000 | bytes 1972224 | tf_op jit(solution)/shard_map/attend_2/pallas_call | solution.py:611
  61.8 1.1 collective-permute-done.15
  63.6 3.6 %collective-permute-done.17.down_other = bf16[2,2,3,48,576]{4,3,2,1,0:T(8,128)(2,1)S(1)} collective-permute-done((bf16[2,2,3,48,576]{4,3,2,1,0:T(8,128)(2,1)S(1)}, bf16[2,2,3,48,576]{4,3,2,1,0:T(8,128)(2,1)S(1)}, u32[]{:S(2)}, u32[]{:S(2)}) %collective-permute-start.17) | collective-permute-done | bytes 663584 | tf_op jit(solution)/shard_map/ppermute | solution.py:46
  67.2 13.6 %feed.1 = (bf16[576,512]{1,0:T(8,128)(2,1)}, f32[512,576]{1,0:T(8,128)S(1)}, f32[8,576]{1,0:T(8,128)S(1)}, bf16[2,2,4,144,384]{4,3,2,1,0:T(8,128)(2,1)S(1)}, bf1...) custom-call(f32[512,576]{1,0:T(8,128)S(1)} %get-tuple-element.107.hi, ...), custom_call_target="tpu_custom_call" | custom-call | flops 190000000 | bytes 7096320 | tf_op jit(solution)/shard_map/feed/pallas_call | solution.py:611
  81.3 2.9 %back_0.1 = (bf16[512,256]{1,0:T(8,128)(2,1)S(1)}, bf16[512,64]{1,0:T(8,128)(2,1)S(1)}, bf16[192,576]{1,0:T(8,128)(2,1)S(1)}) custom-call(f32[512,512]{1,0:T(8,128)S(1)} %get-tuple-element.82.bias, f32[512,128]{1,0:T(8,128)S(1)} %get-tuple-element.84.cosine, f32[512,128]{1,0:T(8,128)S(1)} %get-tuple-element.85.sine, ...), custom_call_target="tpu_custom_call" | custom-call | flops 50000000 | bytes 548864 | tf_op jit(solution)/shard_map/back_0/pallas_call | solution.py:611
  85.0 1.6 collective-permute-start.20
  86.8 1.6 collective-permute-start.28
  88.4 3.2 %back_1.1 = (bf16[512,256]{1,0:T(8,128)(2,1)S(1)}, bf16[512,64]{1,0:T(8,128)(2,1)S(1)}, bf16[192,576]{1,0:T(8,128)(2,1)S(1)}) custom-call(f32[512,512]{1,0:T(8,128)S(1)} %get-tuple-element.82.bias, f32[512,128]{1,0:T(8,128)S(1)} %get-tuple-element.84.cosine, f32[512,128]{1,0:T(8,128)S(1)} %get-tuple-element.85.sine, ...), custom_call_target="tpu_custom_call" | custom-call | flops 50000000 | bytes 548864 | tf_op jit(solution)/shard_map/back_1/pallas_call | solution.py:611
  91.6 2.9 %back_2.1 = (bf16[512,256]{1,0:T(8,128)(2,1)S(1)}, bf16[512,64]{1,0:T(8,128)(2,1)S(1)}, bf16[192,576]{1,0:T(8,128)(2,1)S(1)}) custom-call(f32[512,512]{1,0:T(8,128)S(1)} %get-tuple-element.82.bias, f32[512,128]{1,0:T(8,128)S(1)} %get-tuple-element.84.cosine, f32[512,128]{1,0:T(8,128)S(1)} %get-tuple-element.85.sine, ...), custom_call_target="tpu_custom_call" | custom-call | flops 50000000 | bytes 548864 | tf_op jit(solution)/shard_map/back_2/pallas_call | solution.py:611
  94.5 3.5 %back_last.1 = (bf16[576,512]{1,0:T(8,128)(2,1)}, bf16[2,2,4,80,384]{4,3,2,1,0:T(8,128)(2,1)S(1)}, bf16[2,2,4,80,384]{4,3,2,1,0:T(8,128)(2,1)S(1)}) custom-call(f32[512,576]{1,0:T(8,128)S(1)} %get-tuple-element.104.hidden_in, f32[8,576]{1,0:T(8,128)S(1)} %get-tuple-element.105.gains, bf16[640,1536]{1,0:T(8,128)(2,1)S(1)} %get-tuple-element.106.weights, ...), custom_call_target="tpu_custom_call" | custom-call | flops 60000000 | bytes 2555904 | tf_op jit(solution)/shard_map/back_last/pallas_call | solution.py:611
  98.1 1.8 %collective-permute-done.28 = bf16[2,4,48,576]{3,2,1,0:T(8,128)(2,1)S(1)} collective-permute-done((bf16[2,4,48,576]{3,2,1,0:T(8,128)(2,1)S(1)}, bf16[2,4,48,576]{3,2,1,0:T(8,128)(2,1)S(1)}, u32[]{:S(2)}, u32[]{:S(2)}) %collective-permute-start.28) | collective-permute-done | bytes 442400 | tf_op jit(solution)/shard_map/ppermute | solution.py:46
  99.9 6.9 %collective-permute-done.20 = bf16[2,4,144,384]{3,2,1,0:T(8,128)(2,1)S(1)} collective-permute-done((bf16[2,4,144,384]{3,2,1,0:T(8,128)(2,1)S(1)}, bf16[2,4,144,384]{3,2,1,0:T(8,128)(2,1)S(1)}, u32[]{:S(2)}, u32[]{:S(2)}) %collective-permute-start.20) | collective-permute-done | bytes 884768 | tf_op jit(solution)/shard_map/ppermute | solution.py:46
  107.0 1.6 collective-permute-start.21
  108.7 1.6 collective-permute-start.35
  110.3 9.4 %collective-permute-done.21 = bf16[4,144,384]{2,1,0:T(8,128)(2,1)S(1)} collective-permute-done((bf16[4,144,384]{2,1,0:T(8,128)(2,1)S(1)}, bf16[4,144,384]{2,1,0:T(8,128)(2,1)S(1)}, u32[]{:S(2)}, u32[]{:S(2)}) %collective-permute-start.21) | collective-permute-done | bytes 442400 | tf_op jit(solution)/shard_map/ppermute | solution.py:46
  119.9 1.6 collective-permute-start.30
  121.6 2.3 %collective-permute-start.22 = (bf16[144,384]{1,0:T(8,128)(2,1)S(1)}, bf16[144,384]{1,0:T(8,128)(2,1)S(1)}, u32[]{:S(2)}, u32[]{:S(2)}) collective-permute-start(bf16[144,384]{1,0:T(8,128)(2,1)S(1)} %get-tuple-element.165), channel_id=1, source_target_pairs={{0,1},{1,2},{2,3},{3,0},{4,5},{5,6},{6,7},{7,4},{8,9},{9,10},{10,1... | collective-permute-start | bytes 331784 | tf_op jit(solution)/shard_map/ppermute | solution.py:54
  123.8 2.8 %collective-permute-start.24 = (bf16[144,384]{1,0:T(8,128)(2,1)S(1)}, bf16[144,384]{1,0:T(8,128)(2,1)S(1)}, u32[]{:S(2)}, u32[]{:S(2)}) collective-permute-start(bf16[144,384]{1,0:T(8,128)(2,1)S(1)} %get-tuple-element.166), channel_id=1, source_target_pairs={{0,3},{1,0},{2,1},{3,2},{4,7},{5,4},{6,5},{7,6},{8,11},{9,8},{10,9... | collective-permute-start | bytes 331784 | tf_op jit(solution)/shard_map/ppermute | solution.py:54
  127.2 2.1 %collective-permute-start.36 = (bf16[48,576]{1,0:T(8,128)(2,1)S(1)}, bf16[48,576]{1,0:T(8,128)(2,1)S(1)}, u32[]{:S(2)}, u32[]{:S(2)}) collective-permute-start(bf16[48,576]{1,0:T(8,128)(2,1)S(1)} %get-tuple-element.171), channel_id=1, source_target_pairs={{0,1},{1,2},{2,3},{3,0},{4,5},{5,6},{6,7},{7,4},{8,9},{9,10},{10,1... | collective-permute-start | bytes 165896 | tf_op jit(solution)/shard_map/ppermute | solution.py:54
  129.2 1.0 collective-permute-done.22
  130.2 4.8 %collective-permute-start.38 = (bf16[48,576]{1,0:T(8,128)(2,1)S(1)}, bf16[48,576]{1,0:T(8,128)(2,1)S(1)}, u32[]{:S(2)}, u32[]{:S(2)}) collective-permute-start(bf16[48,576]{1,0:T(8,128)(2,1)S(1)} %get-tuple-element.172), channel_id=1, source_target_pairs={{0,3},{1,0},{2,1},{3,2},{4,7},{5,4},{6,5},{7,6},{8,11},{9,8},{10,9... | collective-permute-start | bytes 165896 | tf_op jit(solution)/shard_map/ppermute | solution.py:54
  135.1 3.5 %collective-permute-done.23 = bf16[144,384]{1,0:T(8,128)(2,1)S(1)} collective-permute-done((bf16[144,384]{1,0:T(8,128)(2,1)S(1)}, bf16[144,384]{1,0:T(8,128)(2,1)S(1)}, u32[]{:S(2)}, u32[]{:S(2)}) %collective-permute-start.23) | collective-permute-done | bytes 110624 | tf_op jit(solution)/shard_map/ppermute | solution.py:54
  138.6 0.6 collective-permute-start.25
  139.3 1.6 collective-permute-start.31
  140.9 0.7 collective-permute-done.37
  141.7 1.8 %collective-permute-done.25 = bf16[144,384]{1,0:T(8,128)(2,1)S(1)} collective-permute-done((bf16[144,384]{1,0:T(8,128)(2,1)S(1)}, bf16[144,384]{1,0:T(8,128)(2,1)S(1)}, u32[]{:S(2)}, u32[]{:S(2)}) %collective-permute-start.25) | collective-permute-done | bytes 110624 | tf_op jit(solution)/shard_map/ppermute | solution.py:46
  143.5 1.6 collective-permute-start.26
  145.0 3.3 %collective-permute-done.31 = bf16[4,80,384]{2,1,0:T(8,128)(2,1)S(1)} collective-permute-done((bf16[4,80,384]{2,1,0:T(8,128)(2,1)S(1)}, bf16[4,80,384]{2,1,0:T(8,128)(2,1)S(1)}, u32[]{:S(2)}, u32[]{:S(2)}) %collective-permute-start.31) | collective-permute-done | bytes 245792 | tf_op jit(solution)/shard_map/ppermute | solution.py:46
  148.4 3.8 %collective-permute-start.34 = (bf16[80,384]{1,0:T(8,128)(2,1)S(1)}, bf16[80,384]{1,0:T(8,128)(2,1)S(1)}, u32[]{:S(2)}, u32[]{:S(2)}) collective-permute-start(bf16[80,384]{1,0:T(8,128)(2,1)S(1)} %get-tuple-element.169), channel_id=1, source_target_pairs={{0,3},{1,0},{2,1},{3,2},{4,7},{5,4},{6,5},{7,6},{8,11},{9,8},{10,9... | collective-permute-start | bytes 184328 | tf_op jit(solution)/shard_map/ppermute | solution.py:54
  152.3 2.1 %collective-permute-done.32 = bf16[80,384]{1,0:T(8,128)(2,1)S(1)} collective-permute-done((bf16[80,384]{1,0:T(8,128)(2,1)S(1)}, bf16[80,384]{1,0:T(8,128)(2,1)S(1)}, u32[]{:S(2)}, u32[]{:S(2)}) %collective-permute-start.32) | collective-permute-done | bytes 61472 | tf_op jit(solution)/shard_map/ppermute | solution.py:54
  154.4 2.9 %collective-permute-done.33 = bf16[80,384]{1,0:T(8,128)(2,1)S(1)} collective-permute-done((bf16[80,384]{1,0:T(8,128)(2,1)S(1)}, bf16[80,384]{1,0:T(8,128)(2,1)S(1)}, u32[]{:S(2)}, u32[]{:S(2)}) %collective-permute-start.33) | collective-permute-done | bytes 61472 | tf_op jit(solution)/shard_map/ppermute | solution.py:54
  157.4 1.6 collective-permute-start.39
  159.0 3.5 %collective-permute-done.39 = bf16[176,384]{1,0:T(8,128)(2,1)S(1)} collective-permute-done((bf16[176,384]{1,0:T(8,128)(2,1)S(1)}, bf16[176,384]{1,0:T(8,128)(2,1)S(1)}, u32[]{:S(2)}, u32[]{:S(2)}) %collective-permute-start.39) | collective-permute-done | bytes 135200 | tf_op jit(solution)/shard_map/ppermute | solution.py:46
  162.6 1.6 collective-permute-start.40
  164.1 4.9 %collective-permute-done.40 = bf16[2,176,384]{2,1,0:T(8,128)(2,1)S(1)} collective-permute-done((bf16[2,176,384]{2,1,0:T(8,128)(2,1)S(1)}, bf16[2,176,384]{2,1,0:T(8,128)(2,1)S(1)}, u32[]{:S(2)}, u32[]{:S(2)}) %collective-permute-start.40) | collective-permute-done | bytes 270368 | tf_op jit(solution)/shard_map/ppermute | solution.py:46
  169.7 2.1 %collective-permute-done.27.pair_other = bf16[2,2,144,384]{3,2,1,0:T(8,128)(2,1)S(1)} collective-permute-done((bf16[2,2,144,384]{3,2,1,0:T(8,128)(2,1)S(1)}, bf16[2,2,144,384]{3,2,1,0:T(8,128)(2,1)S(1)}, u32[]{:S(2)}, u32[]{:S(2)}) %collective-permute-start.27) | collective-permute-done | bytes 442400 | tf_op jit(solution)/shard_map/ppermute | solution.py:46
  171.8 2.1 %finish.1 = (f32[144,576]{1,0:T(8,128)}, f32[144,192]{1,0:T(8,128)}, f32[144,192]{1,0:T(8,128)}, f32[144,576]{1,0:T(8,128)}, f32[1,144]{1,0:T(1,128)}, /*index=5...) custom-call(bf16[2,2,144,384]{3,2,1,0:T(8,128)(2,1)S(1)} %pad_maximum_fusion.5.pair_pieces, ...), custom_call_target="tpu_custom_call" | custom-call | flops 50000000 | bytes 3540096 | tf_op jit(solution)/shard_map/finish/pallas_call | solution.py:611
  (83 shorter events, 7.5 us)
Async XLA Ops:
  0.6 11.7 %copy-start.6 = (f32[520,128]{1,0:T(8,128)S(1)}, f32[520,128]{1,0:T(8,128)}, u32[]{:S(2)}) copy-start(f32[520,128]{1,0:T(8,128)} %constant.8.clone.table_sin) | copy-start | bytes 798724
  0.7 11.7 %copy-start.7 = (f32[520,128]{1,0:T(8,128)S(1)}, f32[520,128]{1,0:T(8,128)}, u32[]{:S(2)}) copy-start(f32[520,128]{1,0:T(8,128)} %constant.7.clone.table_cos) | copy-start | bytes 798724
  0.7 11.7 %copy-start.8 = (s32[1,4]{1,0:T(1,128)S(1)}, s32[1,4]{1,0:T(1,128)}, u32[]{:S(2)}) copy-start(s32[1,4]{1,0:T(1,128)} %lengths.3) | copy-start | bytes 52
  0.7 11.7 %copy-start.3 = (bf16[512,576]{0,1:T(8,128)(2,1)S(1)}, bf16[512,576]{0,1:T(8,128)(2,1)}, u32[]{:S(2)}) copy-start(bf16[512,576]{0,1:T(8,128)(2,1)} %param.25) | copy-start | bytes 1769476
  0.7 11.7 %copy-start.2 = (bf16[512,576]{0,1:T(8,128)(2,1)S(1)}, bf16[512,576]{0,1:T(8,128)(2,1)}, u32[]{:S(2)}) copy-start(bf16[512,576]{0,1:T(8,128)(2,1)} %param.14) | copy-start | bytes 1769476
  5.4 12.5 %copy-start.9 = (bf16[48,576]{1,0:T(8,128)(2,1)S(1)}, bf16[48,576]{1,0:T(8,128)(2,1)}, u32[]{:S(2)}) copy-start(bf16[48,576]{1,0:T(8,128)(2,1)} %get-tuple-element.92) | copy-start | bytes 165892
  5.4 9.6 %collective-permute-start.2 = (bf16[80,384]{1,0:T(8,128)(2,1)}, bf16[80,384]{1,0:T(8,128)(2,1)S(1)}, u32[]{:S(2)}, u32[]{:S(2)}) collective-permute-start(bf16[80,384]{1,0:T(8,128)(2,1)} %get-tuple-element.87), channel_id=1, source_target_pairs={{3,0},{0,1},{1,2},{2,3},{7,4},{4,5},{5,6},{6,7},{11,8},{8,9},{9,10... | collective-permute-start | bytes 184328 | tf_op jit(solution)/shard_map/ppermute | solution.py:50
  8.4 9.4 %collective-permute-start.1 = (bf16[80,384]{1,0:T(8,128)(2,1)}, bf16[80,384]{1,0:T(8,128)(2,1)S(1)}, u32[]{:S(2)}, u32[]{:S(2)}) collective-permute-start(bf16[80,384]{1,0:T(8,128)(2,1)} %get-tuple-element.87), channel_id=1, source_target_pairs={{2,0},{3,1},{0,2},{1,3},{6,4},{7,5},{4,6},{5,7},{10,8},{11,9},{8,1... | collective-permute-start | bytes 184328 | tf_op jit(solution)/shard_map/ppermute | solution.py:50
  11.0 6.8 %collective-permute-start = (bf16[80,384]{1,0:T(8,128)(2,1)}, bf16[80,384]{1,0:T(8,128)(2,1)S(1)}, u32[]{:S(2)}, u32[]{:S(2)}) collective-permute-start(bf16[80,384]{1,0:T(8,128)(2,1)} %get-tuple-element.87), channel_id=1, source_target_pairs={{1,0},{2,1},{3,2},{0,3},{5,4},{6,5},{7,6},{4,7},{9,8},{10,9},{11,1... | collective-permute-start | bytes 184328 | tf_op jit(solution)/shard_map/ppermute | solution.py:50
  13.9 8.1 %collective-permute-start.6 = (bf16[144,384]{1,0:T(8,128)(2,1)}, bf16[144,384]{1,0:T(8,128)(2,1)S(1)}, u32[]{:S(2)}, u32[]{:S(2)}) collective-permute-start(bf16[144,384]{1,0:T(8,128)(2,1)} %get-tuple-element.90), channel_id=1, source_target_pairs={{3,0},{0,1},{1,2},{2,3},{7,4},{4,5},{5,6},{6,7},{11,8},{8,9},{9,10... | collective-permute-start | bytes 331784 | tf_op jit(solution)/shard_map/ppermute | solution.py:50
  14.7 11.6 %collective-permute-start.5 = (bf16[144,384]{1,0:T(8,128)(2,1)}, bf16[144,384]{1,0:T(8,128)(2,1)S(1)}, u32[]{:S(2)}, u32[]{:S(2)}) collective-permute-start(bf16[144,384]{1,0:T(8,128)(2,1)} %get-tuple-element.90), channel_id=1, source_target_pairs={{2,0},{3,1},{0,2},{1,3},{6,4},{7,5},{4,6},{5,7},{10,8},{11,9},{8,1... | collective-permute-start | bytes 331784 | tf_op jit(solution)/shard_map/ppermute | solution.py:50
  15.0 12.7 %collective-permute-start.4 = (bf16[144,384]{1,0:T(8,128)(2,1)}, bf16[144,384]{1,0:T(8,128)(2,1)S(1)}, u32[]{:S(2)}, u32[]{:S(2)}) collective-permute-start(bf16[144,384]{1,0:T(8,128)(2,1)} %get-tuple-element.90), channel_id=1, source_target_pairs={{1,0},{2,1},{3,2},{0,3},{5,4},{6,5},{7,6},{4,7},{9,8},{10,9},{11,1... | collective-permute-start | bytes 331784 | tf_op jit(solution)/shard_map/ppermute | solution.py:50
  17.9 10.5 %collective-permute-start.9 = (bf16[48,576]{1,0:T(8,128)(2,1)S(1)}, bf16[48,576]{1,0:T(8,128)(2,1)S(1)}, u32[]{:S(2)}, u32[]{:S(2)}) collective-permute-start(bf16[48,576]{1,0:T(8,128)(2,1)S(1)} %copy-done.9), channel_id=1, source_target_pairs={{3,0},{0,1},{1,2},{2,3},{7,4},{4,5},{5,6},{6,7},{11,8},{8,9},{9,10... | collective-permute-start | bytes 165896 | tf_op jit(solution)/shard_map/ppermute | solution.py:50
  18.5 12.7 %collective-permute-start.8 = (bf16[48,576]{1,0:T(8,128)(2,1)S(1)}, bf16[48,576]{1,0:T(8,128)(2,1)S(1)}, u32[]{:S(2)}, u32[]{:S(2)}) collective-permute-start(bf16[48,576]{1,0:T(8,128)(2,1)S(1)} %copy-done.9), channel_id=1, source_target_pairs={{2,0},{3,1},{0,2},{1,3},{6,4},{7,5},{4,6},{5,7},{10,8},{11,9},{8,1... | collective-permute-start | bytes 165896 | tf_op jit(solution)/shard_map/ppermute | solution.py:50
  22.1 9.2 %collective-permute-start.7 = (bf16[48,576]{1,0:T(8,128)(2,1)S(1)}, bf16[48,576]{1,0:T(8,128)(2,1)S(1)}, u32[]{:S(2)}, u32[]{:S(2)}) collective-permute-start(bf16[48,576]{1,0:T(8,128)(2,1)S(1)} %copy-done.9), channel_id=1, source_target_pairs={{1,0},{2,1},{3,2},{0,3},{5,4},{6,5},{7,6},{4,7},{9,8},{10,9},{11,1... | collective-permute-start | bytes 165896 | tf_op jit(solution)/shard_map/ppermute | solution.py:50
  26.2 7.6 %collective-permute-start.3 = (bf16[3,80,384]{2,1,0:T(8,128)(2,1)S(1)}, bf16[3,80,384]{2,1,0:T(8,128)(2,1)S(1)}, u32[]{:S(2)}, u32[]{:S(2)}) collective-permute-start(bf16[3,80,384]{2,1,0:T(8,128)(2,1)S(1)} %pad_maximum_fusion.11), channel_id=1, source_target_pairs={{0,16},{4,20},{8,24},{12,28},{16,0},{20,4},{24,8},{28,12},{1,17},{... | collective-permute-start | bytes 552968 | tf_op jit(solution)/shard_map/ppermute | solution.py:46
  27.8 10.3 %collective-permute-start.11 = (bf16[3,144,384]{2,1,0:T(8,128)(2,1)S(1)}, bf16[3,144,384]{2,1,0:T(8,128)(2,1)S(1)}, u32[]{:S(2)}, u32[]{:S(2)}) collective-permute-start(bf16[3,144,384]{2,1,0:T(8,128)(2,1)S(1)} %get-tuple-element.175), channel_id=1, source_target_pairs={{0,16},{4,20},{8,24},{12,28},{16,0},{20,4},{24,8},{28,12},{1,17},{... | collective-permute-start | bytes 995336 | tf_op jit(solution)/shard_map/ppermute | solution.py:46
  33.8 10.0 %copy-start.4 = (bf16[160,1536]{1,0:T(8,128)(2,1)S(1)}, bf16[160,1536]{1,0:T(8,128)(2,1)}, u32[]{:S(2)}) copy-start(bf16[160,1536]{1,0:T(8,128)(2,1)} %get-tuple-element.86.own) | copy-start | bytes 1474564
  33.9 7.6 %collective-permute-start.10 = (bf16[2,3,80,384]{3,2,1,0:T(8,128)(2,1)S(1)}, bf16[2,3,80,384]{3,2,1,0:T(8,128)(2,1)S(1)}, u32[]{:S(2)}, u32[]{:S(2)}) collective-permute-start(bf16[2,3,80,384]{3,2,1,0:T(8,128)(2,1)S(1)} %pad_maximum_fusion.6), channel_id=1, source_target_pairs={{0,8},{4,12},{8,0},{12,4},{16,24},{20,28},{24,16},{28,20},{1,9},{5... | collective-permute-start | bytes 1105928 | tf_op jit(solution)/shard_map/ppermute | solution.py:46
  41.5 2.3 %collective-permute-start.12 = (bf16[2,2,3,80,384]{4,3,2,1,0:T(8,128)(2,1)S(1)}, bf16[2,2,3,80,384]{4,3,2,1,0:T(8,128)(2,1)S(1)}, u32[]{:S(2)}, u32[]{:S(2)}) collective-permute-start(bf16[2,2,3,80,384]{4,3,2,1,0:T(8,128)(2,1)S(1)} %pad_maximum_fusion.1.pieces), channel_id=1, source_target_pairs={{0,4},{4,0},{8,12},{12,8},{16,20},{20,16},{24,28},{28,24},{1,5},{5... | collective-permute-start | bytes 2211848 | tf_op jit(solution)/shard_map/ppermute | solution.py:46
  41.6 7.5 %collective-permute-start.13 = (bf16[3,48,576]{2,1,0:T(8,128)(2,1)S(1)}, bf16[3,48,576]{2,1,0:T(8,128)(2,1)S(1)}, u32[]{:S(2)}, u32[]{:S(2)}) collective-permute-start(bf16[3,48,576]{2,1,0:T(8,128)(2,1)S(1)} %pad_maximum_fusion.12), channel_id=1, source_target_pairs={{0,8},{4,12},{8,0},{12,4},{16,24},{20,28},{24,16},{28,20},{1,9},{5... | collective-permute-start | bytes 497672 | tf_op jit(solution)/shard_map/ppermute | solution.py:46
  43.2 19.7 %collective-permute-start.15 = (bf16[2,3,144,384]{3,2,1,0:T(8,128)(2,1)S(1)}, bf16[2,3,144,384]{3,2,1,0:T(8,128)(2,1)S(1)}, u32[]{:S(2)}, u32[]{:S(2)}) collective-permute-start(bf16[2,3,144,384]{3,2,1,0:T(8,128)(2,1)S(1)} %pad_maximum_fusion.3), channel_id=1, source_target_pairs={{0,8},{4,12},{8,0},{12,4},{16,24},{20,28},{24,16},{28,20},{1,9},{5... | collective-permute-start | bytes 1990664 | tf_op jit(solution)/shard_map/ppermute | solution.py:46
  49.2 9.8 %collective-permute-start.14 = (bf16[2,3,48,576]{3,2,1,0:T(8,128)(2,1)S(1)}, bf16[2,3,48,576]{3,2,1,0:T(8,128)(2,1)S(1)}, u32[]{:S(2)}, u32[]{:S(2)}) collective-permute-start(bf16[2,3,48,576]{3,2,1,0:T(8,128)(2,1)S(1)} %pad_maximum_fusion.7), channel_id=1, source_target_pairs={{0,16},{4,20},{8,24},{12,28},{16,0},{20,4},{24,8},{28,12},{1,17},{... | collective-permute-start | bytes 995336 | tf_op jit(solution)/shard_map/ppermute | solution.py:46
  61.7 5.5 %copy-start = (bf16[144,1536]{1,0:T(8,128)(2,1)S(1)}, bf16[144,1536]{1,0:T(8,128)(2,1)}, u32[]{:S(2)}) copy-start(bf16[144,1536]{1,0:T(8,128)(2,1)} %own_gate.1) | copy-start | bytes 1327108
  61.8 5.5 %copy-start.1 = (bf16[144,1536]{1,0:T(8,128)(2,1)S(1)}, bf16[144,1536]{1,0:T(8,128)(2,1)}, u32[]{:S(2)}) copy-start(bf16[144,1536]{1,0:T(8,128)(2,1)} %own_up.1) | copy-start | bytes 1327108
  61.8 5.5 %copy-start.5 = (bf16[384,576]{1,0:T(8,128)(2,1)S(1)}, bf16[384,576]{1,0:T(8,128)(2,1)}, u32[]{:S(2)}) copy-start(bf16[384,576]{1,0:T(8,128)(2,1)} %get-tuple-element.110.own_down) | copy-start | bytes 1327108
  63.0 4.2 %collective-permute-start.16 = (bf16[2,2,3,144,384]{4,3,2,1,0:T(8,128)(2,1)S(1)}, bf16[2,2,3,144,384]{4,3,2,1,0:T(8,128)(2,1)S(1)}, u32[]{:S(2)}, u32[]{:S(2)}) collective-permute-start(bf16[2,2,3,144,384]{4,3,2,1,0:T(8,128)(2,1)S(1)} %pad_maximum_fusion.pair_pieces), channel_id=1, source_target_pairs={{0,4},{4,0},{8,12},{12,8},{16,20},{20,16},{24,28},{28,24},{1,5},{5... | collective-permute-start | bytes 3981320 | tf_op jit(solution)/shard_map/ppermute | solution.py:46
  63.1 4.1 %collective-permute-start.17 = (bf16[2,2,3,48,576]{4,3,2,1,0:T(8,128)(2,1)S(1)}, bf16[2,2,3,48,576]{4,3,2,1,0:T(8,128)(2,1)S(1)}, u32[]{:S(2)}, u32[]{:S(2)}) collective-permute-start(bf16[2,2,3,48,576]{4,3,2,1,0:T(8,128)(2,1)S(1)} %pad_maximum_fusion.2.down_pieces), channel_id=1, source_target_pairs={{0,4},{4,0},{8,12},{12,8},{16,20},{20,16},{24,28},{28,24},{1,5},{5... | collective-permute-start | bytes 1990664 | tf_op jit(solution)/shard_map/ppermute | solution.py:46
  80.8 3.7 %collective-permute-start.18 = (bf16[2,2,4,144,384]{4,3,2,1,0:T(8,128)(2,1)S(1)}, bf16[2,2,4,144,384]{4,3,2,1,0:T(8,128)(2,1)S(1)}, u32[]{:S(2)}, u32[]{:S(2)}) collective-permute-start(bf16[2,2,4,144,384]{4,3,2,1,0:T(8,128)(2,1)S(1)} %get-tuple-element.114), channel_id=1, source_target_pairs={{0,4},{4,0},{8,12},{12,8},{16,20},{20,16},{24,28},{28,24},{1,5},{5... | collective-permute-start | bytes 5308424 | tf_op jit(solution)/shard_map/ppermute | solution.py:46
  81.0 5.6 %collective-permute-start.19 = (bf16[2,2,4,48,576]{4,3,2,1,0:T(8,128)(2,1)S(1)}, bf16[2,2,4,48,576]{4,3,2,1,0:T(8,128)(2,1)S(1)}, u32[]{:S(2)}, u32[]{:S(2)}) collective-permute-start(bf16[2,2,4,48,576]{4,3,2,1,0:T(8,128)(2,1)S(1)} %get-tuple-element.115), channel_id=1, source_target_pairs={{0,4},{4,0},{8,12},{12,8},{16,20},{20,16},{24,28},{28,24},{1,5},{5... | collective-permute-start | bytes 2654216 | tf_op jit(solution)/shard_map/ppermute | solution.py:46
  85.0 21.8 %collective-permute-start.20 = (bf16[2,4,144,384]{3,2,1,0:T(8,128)(2,1)S(1)}, bf16[2,4,144,384]{3,2,1,0:T(8,128)(2,1)S(1)}, u32[]{:S(2)}, u32[]{:S(2)}) collective-permute-start(bf16[2,4,144,384]{3,2,1,0:T(8,128)(2,1)S(1)} %get-tuple-element.154), channel_id=1, source_target_pairs={{0,8},{4,12},{8,0},{12,4},{16,24},{20,28},{24,16},{28,20},{1,9},{5... | collective-permute-start | bytes 2654216 | tf_op jit(solution)/shard_map/ppermute | solution.py:46
  86.8 13.0 %collective-permute-start.28 = (bf16[2,4,48,576]{3,2,1,0:T(8,128)(2,1)S(1)}, bf16[2,4,48,576]{3,2,1,0:T(8,128)(2,1)S(1)}, u32[]{:S(2)}, u32[]{:S(2)}) collective-permute-start(bf16[2,4,48,576]{3,2,1,0:T(8,128)(2,1)S(1)} %get-tuple-element.157), channel_id=1, source_target_pairs={{0,16},{4,20},{8,24},{12,28},{16,0},{20,4},{24,8},{28,12},{1,17},{... | collective-permute-start | bytes 1327112 | tf_op jit(solution)/shard_map/ppermute | solution.py:46
  106.7 12.9 %collective-permute-start.29 = (bf16[2,2,4,80,384]{4,3,2,1,0:T(8,128)(2,1)S(1)}, bf16[2,2,4,80,384]{4,3,2,1,0:T(8,128)(2,1)S(1)}, u32[]{:S(2)}, u32[]{:S(2)}) collective-permute-start(bf16[2,2,4,80,384]{4,3,2,1,0:T(8,128)(2,1)S(1)} %get-tuple-element.138), channel_id=1, source_target_pairs={{0,4},{4,0},{8,12},{12,8},{16,20},{20,16},{24,28},{28,24},{1,5},{5... | collective-permute-start | bytes 2949128 | tf_op jit(solution)/shard_map/ppermute | solution.py:46
  107.0 12.6 %collective-permute-start.21 = (bf16[4,144,384]{2,1,0:T(8,128)(2,1)S(1)}, bf16[4,144,384]{2,1,0:T(8,128)(2,1)S(1)}, u32[]{:S(2)}, u32[]{:S(2)}) collective-permute-start(bf16[4,144,384]{2,1,0:T(8,128)(2,1)S(1)} %get-tuple-element.160), channel_id=1, source_target_pairs={{0,16},{4,20},{8,24},{12,28},{16,0},{20,4},{24,8},{28,12},{1,17},{... | collective-permute-start | bytes 1327112 | tf_op jit(solution)/shard_map/ppermute | solution.py:46
  108.7 18.4 %collective-permute-start.35 = (bf16[4,48,576]{2,1,0:T(8,128)(2,1)S(1)}, bf16[4,48,576]{2,1,0:T(8,128)(2,1)S(1)}, u32[]{:S(2)}, u32[]{:S(2)}) collective-permute-start(bf16[4,48,576]{2,1,0:T(8,128)(2,1)S(1)} %get-tuple-element.164), channel_id=1, source_target_pairs={{0,8},{4,12},{8,0},{12,4},{16,24},{20,28},{24,16},{28,20},{1,9},{5... | collective-permute-start | bytes 663560 | tf_op jit(solution)/shard_map/ppermute | solution.py:46
  119.9 19.3 %collective-permute-start.30 = (bf16[2,4,80,384]{3,2,1,0:T(8,128)(2,1)S(1)}, bf16[2,4,80,384]{3,2,1,0:T(8,128)(2,1)S(1)}, u32[]{:S(2)}, u32[]{:S(2)}) collective-permute-start(bf16[2,4,80,384]{3,2,1,0:T(8,128)(2,1)S(1)} %get-tuple-element.155), channel_id=1, source_target_pairs={{0,16},{4,20},{8,24},{12,28},{16,0},{20,4},{24,8},{28,12},{1,17},{... | collective-permute-start | bytes 1474568 | tf_op jit(solution)/shard_map/ppermute | solution.py:46
  121.6 8.7 %collective-permute-start.22 = (bf16[144,384]{1,0:T(8,128)(2,1)S(1)}, bf16[144,384]{1,0:T(8,128)(2,1)S(1)}, u32[]{:S(2)}, u32[]{:S(2)}) collective-permute-start(bf16[144,384]{1,0:T(8,128)(2,1)S(1)} %get-tuple-element.165), channel_id=1, source_target_pairs={{0,1},{1,2},{2,3},{3,0},{4,5},{5,6},{6,7},{7,4},{8,9},{9,10},{10,1... | collective-permute-start | bytes 331784 | tf_op jit(solution)/shard_map/ppermute | solution.py:54
  123.8 11.2 %collective-permute-start.24 = (bf16[144,384]{1,0:T(8,128)(2,1)S(1)}, bf16[144,384]{1,0:T(8,128)(2,1)S(1)}, u32[]{:S(2)}, u32[]{:S(2)}) collective-permute-start(bf16[144,384]{1,0:T(8,128)(2,1)S(1)} %get-tuple-element.166), channel_id=1, source_target_pairs={{0,3},{1,0},{2,1},{3,2},{4,7},{5,4},{6,5},{7,6},{8,11},{9,8},{10,9... | collective-permute-start | bytes 331784 | tf_op jit(solution)/shard_map/ppermute | solution.py:54
  126.6 11.9 %collective-permute-start.23 = (bf16[144,384]{1,0:T(8,128)(2,1)S(1)}, bf16[144,384]{1,0:T(8,128)(2,1)S(1)}, u32[]{:S(2)}, u32[]{:S(2)}) collective-permute-start(bf16[144,384]{1,0:T(8,128)(2,1)S(1)} %get-tuple-element.167), channel_id=1, source_target_pairs={{0,2},{1,3},{2,0},{3,1},{4,6},{5,7},{6,4},{7,5},{8,10},{9,11},{10,... | collective-permute-start | bytes 331784 | tf_op jit(solution)/shard_map/ppermute | solution.py:54
  127.2 13.7 %collective-permute-start.36 = (bf16[48,576]{1,0:T(8,128)(2,1)S(1)}, bf16[48,576]{1,0:T(8,128)(2,1)S(1)}, u32[]{:S(2)}, u32[]{:S(2)}) collective-permute-start(bf16[48,576]{1,0:T(8,128)(2,1)S(1)} %get-tuple-element.171), channel_id=1, source_target_pairs={{0,1},{1,2},{2,3},{3,0},{4,5},{5,6},{6,7},{7,4},{8,9},{9,10},{10,1... | collective-permute-start | bytes 165896 | tf_op jit(solution)/shard_map/ppermute | solution.py:54
  130.2 10.7 %collective-permute-start.38 = (bf16[48,576]{1,0:T(8,128)(2,1)S(1)}, bf16[48,576]{1,0:T(8,128)(2,1)S(1)}, u32[]{:S(2)}, u32[]{:S(2)}) collective-permute-start(bf16[48,576]{1,0:T(8,128)(2,1)S(1)} %get-tuple-element.172), channel_id=1, source_target_pairs={{0,3},{1,0},{2,1},{3,2},{4,7},{5,4},{6,5},{7,6},{8,11},{9,8},{10,9... | collective-permute-start | bytes 165896 | tf_op jit(solution)/shard_map/ppermute | solution.py:54
  135.1 6.5 %collective-permute-start.37 = (bf16[48,576]{1,0:T(8,128)(2,1)S(1)}, bf16[48,576]{1,0:T(8,128)(2,1)S(1)}, u32[]{:S(2)}, u32[]{:S(2)}) collective-permute-start(bf16[48,576]{1,0:T(8,128)(2,1)S(1)} %get-tuple-element.173), channel_id=1, source_target_pairs={{0,2},{1,3},{2,0},{3,1},{4,6},{5,7},{6,4},{7,5},{8,10},{9,11},{10,... | collective-permute-start | bytes 165896 | tf_op jit(solution)/shard_map/ppermute | solution.py:54
  138.6 4.8 %collective-permute-start.25 = (bf16[144,384]{1,0:T(8,128)(2,1)S(1)}, bf16[144,384]{1,0:T(8,128)(2,1)S(1)}, u32[]{:S(2)}, u32[]{:S(2)}) collective-permute-start(bf16[144,384]{1,0:T(8,128)(2,1)S(1)} %fusion.20), channel_id=1, source_target_pairs={{0,16},{4,20},{8,24},{12,28},{16,0},{20,4},{24,8},{28,12},{1,17},{... | collective-permute-start | bytes 331784 | tf_op jit(solution)/shard_map/ppermute | solution.py:46
  139.3 9.0 %collective-permute-start.31 = (bf16[4,80,384]{2,1,0:T(8,128)(2,1)S(1)}, bf16[4,80,384]{2,1,0:T(8,128)(2,1)S(1)}, u32[]{:S(2)}, u32[]{:S(2)}) collective-permute-start(bf16[4,80,384]{2,1,0:T(8,128)(2,1)S(1)} %get-tuple-element.161), channel_id=1, source_target_pairs={{0,8},{4,12},{8,0},{12,4},{16,24},{20,28},{24,16},{28,20},{1,9},{5... | collective-permute-start | bytes 737288 | tf_op jit(solution)/shard_map/ppermute | solution.py:46
  143.5 8.8 %collective-permute-start.26 = (bf16[2,144,384]{2,1,0:T(8,128)(2,1)S(1)}, bf16[2,144,384]{2,1,0:T(8,128)(2,1)S(1)}, u32[]{:S(2)}, u32[]{:S(2)}) collective-permute-start(bf16[2,144,384]{2,1,0:T(8,128)(2,1)S(1)} %get-tuple-element.179), channel_id=1, source_target_pairs={{0,8},{4,12},{8,0},{12,4},{16,24},{20,28},{24,16},{28,20},{1,9},{5... | collective-permute-start | bytes 663560 | tf_op jit(solution)/shard_map/ppermute | solution.py:46
  148.3 6.1 %collective-permute-start.32 = (bf16[80,384]{1,0:T(8,128)(2,1)S(1)}, bf16[80,384]{1,0:T(8,128)(2,1)S(1)}, u32[]{:S(2)}, u32[]{:S(2)}) collective-permute-start(bf16[80,384]{1,0:T(8,128)(2,1)S(1)} %get-tuple-element.168), channel_id=1, source_target_pairs={{0,1},{1,2},{2,3},{3,0},{4,5},{5,6},{6,7},{7,4},{8,9},{9,10},{10,1... | collective-permute-start | bytes 184328 | tf_op jit(solution)/shard_map/ppermute | solution.py:54
  148.4 6.0 %collective-permute-start.34 = (bf16[80,384]{1,0:T(8,128)(2,1)S(1)}, bf16[80,384]{1,0:T(8,128)(2,1)S(1)}, u32[]{:S(2)}, u32[]{:S(2)}) collective-permute-start(bf16[80,384]{1,0:T(8,128)(2,1)S(1)} %get-tuple-element.169), channel_id=1, source_target_pairs={{0,3},{1,0},{2,1},{3,2},{4,7},{5,4},{6,5},{7,6},{8,11},{9,8},{10,9... | collective-permute-start | bytes 184328 | tf_op jit(solution)/shard_map/ppermute | solution.py:54
  152.2 5.1 %collective-permute-start.33 = (bf16[80,384]{1,0:T(8,128)(2,1)S(1)}, bf16[80,384]{1,0:T(8,128)(2,1)S(1)}, u32[]{:S(2)}, u32[]{:S(2)}) collective-permute-start(bf16[80,384]{1,0:T(8,128)(2,1)S(1)} %get-tuple-element.170), channel_id=1, source_target_pairs={{0,2},{1,3},{2,0},{3,1},{4,6},{5,7},{6,4},{7,5},{8,10},{9,11},{10,... | collective-permute-start | bytes 184328 | tf_op jit(solution)/shard_map/ppermute | solution.py:54
  157.4 5.1 %collective-permute-start.39 = (bf16[176,384]{1,0:T(8,128)(2,1)S(1)}, bf16[176,384]{1,0:T(8,128)(2,1)S(1)}, u32[]{:S(2)}, u32[]{:S(2)}) collective-permute-start(bf16[176,384]{1,0:T(8,128)(2,1)S(1)} %get-tuple-element.181), channel_id=1, source_target_pairs={{0,8},{4,12},{8,0},{12,4},{16,24},{20,28},{24,16},{28,20},{1,9},{5... | collective-permute-start | bytes 405512 | tf_op jit(solution)/shard_map/ppermute | solution.py:46
  162.6 6.5 %collective-permute-start.40 = (bf16[2,176,384]{2,1,0:T(8,128)(2,1)S(1)}, bf16[2,176,384]{2,1,0:T(8,128)(2,1)S(1)}, u32[]{:S(2)}, u32[]{:S(2)}) collective-permute-start(bf16[2,176,384]{2,1,0:T(8,128)(2,1)S(1)} %get-tuple-element.177), channel_id=1, source_target_pairs={{0,16},{4,20},{8,24},{12,28},{16,0},{20,4},{24,8},{28,12},{1,17},{... | collective-permute-start | bytes 811016 | tf_op jit(solution)/shard_map/ppermute | solution.py:46
  169.1 2.6 %collective-permute-start.41 = (bf16[2,2,176,384]{3,2,1,0:T(8,128)(2,1)S(1)}, bf16[2,2,176,384]{3,2,1,0:T(8,128)(2,1)S(1)}, u32[]{:S(2)}, u32[]{:S(2)}) collective-permute-start(bf16[2,2,176,384]{3,2,1,0:T(8,128)(2,1)S(1)} %pad_maximum_fusion.4.rest_pieces), channel_id=1, source_target_pairs={{0,4},{4,0},{8,12},{12,8},{16,20},{20,16},{24,28},{28,24},{1,5},{5... | collective-permute-start | bytes 1622024 | tf_op jit(solution)/shard_map/ppermute | solution.py:46
  169.2 2.6 %collective-permute-start.27 = (bf16[2,2,144,384]{3,2,1,0:T(8,128)(2,1)S(1)}, bf16[2,2,144,384]{3,2,1,0:T(8,128)(2,1)S(1)}, u32[]{:S(2)}, u32[]{:S(2)}) collective-permute-start(bf16[2,2,144,384]{3,2,1,0:T(8,128)(2,1)S(1)} %pad_maximum_fusion.5.pair_pieces), channel_id=1, source_target_pairs={{0,4},{4,0},{8,12},{12,8},{16,20},{20,16},{24,28},{28,24},{1,5},{5... | collective-permute-start | bytes 1327112 | tf_op jit(solution)/shard_map/ppermute | solution.py:46

commit v6 on v5

--- a/solution.py
+++ b/solution.py
@@ -574,9 +574,11 @@
                 block = 2 * relative(core, rel_core) + relative(x, rel_x)
                 columns = rows_at(384 * block, 384, 128)
                 piece = r_from.at[rel_y, rel_x]
-                place(p_from.at[rel_x, rel_y], pair.at[at_y, :, columns])
-                place(piece.at[pl.ds(0, 80)], attn.at[rows_at(80 * at_y, 80), columns])
-                place(piece.at[pl.ds(80, down.shape[1])], down.at[2 * block + at_y])
+                place(p_from.at[rel_x, rel_y, pl.ds(0, part)], pair.at[at_y, :, columns])
+                place(piece, attn.at[rows_at(80 * at_y, 80), columns])
+                place(
+                    p_from.at[rel_x, rel_y, pl.ds(part, down.shape[1])], down.at[2 * block + at_y]
+                )
     kv_width = out_key.shape[1]
     out_out[...] = attn[0:part, 0:width].astype(f32)
     rest = attn[0:part, 512:].astype(f32)
@@ -850,14 +852,15 @@
     pair_total = scatter_over_shards(*pair_left, shards, replicas)
     down_left = halve(down_left[0], after(down_left[1], grad_tokens), 1, replicas)
     attn_left = halve(attn_left[0], after(attn_left[1], pair_total), 1, replicas)
-    pair_half = gather_bit(pair_total, 2, replicas)
+    down_total = scatter_over_shards(*down_left, shards, replicas)
+    feed_total = jnp.concatenate([pair_total, fold(down_total)])
+    pair_half = gather_bit(feed_total, 2, replicas)
     attn_left = (attn_left[0], after(attn_left[1], pair_half))
-    down_total = scatter_over_shards(*down_left, shards, replicas)
     attn_total = scatter_over_shards(*attn_left, shards, replicas)
     pair_half = gather_bit(pair_half, 1, replicas)
     pair_pieces = spread(pair_half, (0,), replicas)
     attn_total = after(attn_total, pair_half)
-    rest_pieces = spread(jnp.concatenate([attn_total, fold(down_total)]), (1, 2, 0), replicas)
+    rest_pieces = spread(attn_total, (1, 2, 0), replicas)
     g_query, g_key, g_value, g_out, g_gain_one, g_gain_two, g_gate, g_up, g_down = call(
         finish_kernel,
         "finish",

time: 177 us -> 173 us (0.977)
  waiting for transfers between devices: 72.9 us -> 69.4 us
    ppermute x24, waiting for transfers between devices: 54.6 us -> 51.4 us  [flip(): lax.ppermute(value, 'rep', [(i, i ^ 1 << bit) for i in range(replicas)])]
    ppermute x9, starting transfers between devices: 16.3 us -> 19.2 us  [shift_to(): lax.ppermute(value, 'shard', [(s, (s + step) % shards) for s in range(sha...]
    ppermute x24, starting transfers between devices: 23.8 us -> 20.9 us  [flip(): lax.ppermute(value, 'rep', [(i, i ^ 1 << bit) for i in range(replicas)])]
  transfers between devices with their start and end apart: 42 -> 42, of which waited for: 25 -> 27; matrix products, arithmetic and copies ran while one was open for 1% -> 1% of each run, Pallas kernels for 13% -> 13%
where the time goes in v6:
time: 173 us; the launch traced here: 171 us
  waiting for transfers between devices  69.4 us (40%)
  starting transfers between devices  54.1 us (31%)
  Pallas kernels  41.2 us (24%)
  other arithmetic  3.29 us (2%)
    ppermute x24, waiting for transfers between devices, flip(): lax.ppermute(value, 'rep', [(i, i ^ 1 << bit) for i in range(replicas)])  51.4 us
    pallas_call x12, Pallas kernels, call(): pl.pallas_call(kernel, name=name, in_specs=in_specs, out_shape=out_shape,...  41.2 us
    ppermute x24, starting transfers between devices, flip(): lax.ppermute(value, 'rep', [(i, i ^ 1 << bit) for i in range(replicas)])  20.9 us
    ppermute x9, starting transfers between devices, shift_to(): lax.ppermute(value, 'shard', [(s, (s + step) % shards) for s in range(sha...  19.2 us
    ppermute x9, starting transfers between devices, shift_from(): lax.ppermute(value, 'shard', [((s + step) % shards, s) for s in range(sha...  14 us
    ppermute x9, waiting for transfers between devices, shift_to(): lax.ppermute(value, 'shard', [(s, (s + step) % shards) for s in range(sha...  9.91 us
    ppermute x9, waiting for transfers between devices, shift_from(): lax.ppermute(value, 'shard', [((s + step) % shards, s) for s in range(sha...  8.06 us
  transfers between devices with their start and end apart: 42, of which 27 were waited for; matrix products, arithmetic and copies ran while one was open for 1% of the time, Pallas kernels for 13%

profile of v6, /device:TPU:0, one launch (start us, length us, event | category | flops | bytes accessed | tf_op | source)
XLA Modules:
  0.0 170.9 jit_solution(5804371990447296616)
XLA Ops:
  0.7 0.8 stack.135
  1.5 0.7 stack.136
  2.7 2.7 %pack.1 = (bf16[160,1536]{1,0:T(8,128)(2,1)}, bf16[80,384]{1,0:T(8,128)(2,1)}, bf16[144,384]{1,0:T(8,128)(2,1)}, bf16[48,576]{1,0:T(8,128)(2,1)}, bf16[384,576]{1,0:T(8,128)(2,1)}) custom-call(bf16[144,576]{1,0:T(8,128)(2,1)} %w_out.1, bf16[144,576]{1,0:T(8,128)(2,1)} %w_query.1, bf16[144,192]{1,0:T(8,128)(2,1)} %w_key.1, bf16[144,192]{1,0:T(8,128)(2,1)} %w_value.1, ...), custom_call_target="tpu_custom_call" | custom-call | flops 20000000 | bytes 1161216 | tf_op jit(solution)/shard_map/pack/pallas_call | solution.py:613
  5.4 3.0 %collective-permute-start.2 = (bf16[80,384]{1,0:T(8,128)(2,1)}, bf16[80,384]{1,0:T(8,128)(2,1)S(1)}, u32[]{:S(2)}, u32[]{:S(2)}) collective-permute-start(bf16[80,384]{1,0:T(8,128)(2,1)} %get-tuple-element.87), channel_id=1, source_target_pairs={{3,0},{0,1},{1,2},{2,3},{7,4},{4,5},{5,6},{6,7},{11,8},{8,9},{9,10... | collective-permute-start | bytes 184328 | tf_op jit(solution)/shard_map/ppermute | solution.py:50
  8.4 2.6 %collective-permute-start.1 = (bf16[80,384]{1,0:T(8,128)(2,1)}, bf16[80,384]{1,0:T(8,128)(2,1)S(1)}, u32[]{:S(2)}, u32[]{:S(2)}) collective-permute-start(bf16[80,384]{1,0:T(8,128)(2,1)} %get-tuple-element.87), channel_id=1, source_target_pairs={{2,0},{3,1},{0,2},{1,3},{6,4},{7,5},{4,6},{5,7},{10,8},{11,9},{8,1... | collective-permute-start | bytes 184328 | tf_op jit(solution)/shard_map/ppermute | solution.py:50
  11.0 1.3 collective-permute-start
  12.4 1.6 prepare.1
  13.9 0.7 collective-permute-start.6
  15.0 2.8 %collective-permute-start.4 = (bf16[144,384]{1,0:T(8,128)(2,1)}, bf16[144,384]{1,0:T(8,128)(2,1)S(1)}, u32[]{:S(2)}, u32[]{:S(2)}) collective-permute-start(bf16[144,384]{1,0:T(8,128)(2,1)} %get-tuple-element.90), channel_id=1, source_target_pairs={{1,0},{2,1},{3,2},{0,3},{5,4},{6,5},{7,6},{4,7},{9,8},{10,9},{11,1... | collective-permute-start | bytes 331784 | tf_op jit(solution)/shard_map/ppermute | solution.py:50
  17.9 0.6 collective-permute-start.9
  18.5 1.5 collective-permute-start.8
  20.0 2.0 %collective-permute-done.6 = bf16[144,384]{1,0:T(8,128)(2,1)S(1)} collective-permute-done((bf16[144,384]{1,0:T(8,128)(2,1)}, bf16[144,384]{1,0:T(8,128)(2,1)S(1)}, u32[]{:S(2)}, u32[]{:S(2)}) %collective-permute-start.6) | collective-permute-done | bytes 110624 | tf_op jit(solution)/shard_map/ppermute | solution.py:50
  22.1 1.0 collective-permute-start.7
  23.0 3.2 %collective-permute-done.5 = bf16[144,384]{1,0:T(8,128)(2,1)S(1)} collective-permute-done((bf16[144,384]{1,0:T(8,128)(2,1)}, bf16[144,384]{1,0:T(8,128)(2,1)S(1)}, u32[]{:S(2)}, u32[]{:S(2)}) %collective-permute-start.5) | collective-permute-done | bytes 110624 | tf_op jit(solution)/shard_map/ppermute | solution.py:50
  26.2 1.5 collective-permute-start.3
  28.4 2.8 %collective-permute-done.8 = bf16[48,576]{1,0:T(8,128)(2,1)S(1)} collective-permute-done((bf16[48,576]{1,0:T(8,128)(2,1)S(1)}, bf16[48,576]{1,0:T(8,128)(2,1)S(1)}, u32[]{:S(2)}, u32[]{:S(2)}) %collective-permute-start.8) | collective-permute-done | bytes 55328 | tf_op jit(solution)/shard_map/ppermute | solution.py:50
  31.3 2.5 %collective-permute-done.3 = bf16[3,80,384]{2,1,0:T(8,128)(2,1)S(1)} collective-permute-done((bf16[3,80,384]{2,1,0:T(8,128)(2,1)S(1)}, bf16[3,80,384]{2,1,0:T(8,128)(2,1)S(1)}, u32[]{:S(2)}, u32[]{:S(2)}) %collective-permute-start.3) | collective-permute-done | bytes 184352 | tf_op jit(solution)/shard_map/ppermute | solution.py:46
  33.9 1.5 collective-permute-start.10
  35.4 2.8 %collective-permute-done.11 = bf16[3,144,384]{2,1,0:T(8,128)(2,1)S(1)} collective-permute-done((bf16[3,144,384]{2,1,0:T(8,128)(2,1)S(1)}, bf16[3,144,384]{2,1,0:T(8,128)(2,1)S(1)}, u32[]{:S(2)}, u32[]{:S(2)}) %collective-permute-start.11) | collective-permute-done | bytes 331808 | tf_op jit(solution)/shard_map/ppermute | solution.py:46
  38.2 3.2 %collective-permute-done.10 = bf16[2,3,80,384]{3,2,1,0:T(8,128)(2,1)S(1)} collective-permute-done((bf16[2,3,80,384]{3,2,1,0:T(8,128)(2,1)S(1)}, bf16[2,3,80,384]{3,2,1,0:T(8,128)(2,1)S(1)}, u32[]{:S(2)}, u32[]{:S(2)}) %collective-permute-start.10) | collective-permute-done | bytes 368672 | tf_op jit(solution)/shard_map/ppermute | solution.py:46
  41.6 1.5 collective-permute-start.13
  43.8 2.2 %project.1 = (bf16[640,1536]{1,0:T(8,128)(2,1)S(1)}, f32[8,576]{1,0:T(8,128)S(1)}, bf16[512,576]{1,0:T(8,128)(2,1)S(1)}, bf16[9,512,64]{2,1,0:T(8,128)(2,1)S(1)}...) custom-call(f32[512,576]{1,0:T(8,128)S(1)} %get-tuple-element.83.scaled, ...), custom_call_target="tpu_custom_call" | custom-call | flops 50000000 | bytes 3557376 | tf_op jit(solution)/shard_map/project/pallas_call | solution.py:613
  46.0 3.1 %collective-permute-done.13 = bf16[3,48,576]{2,1,0:T(8,128)(2,1)S(1)} collective-permute-done((bf16[3,48,576]{2,1,0:T(8,128)(2,1)S(1)}, bf16[3,48,576]{2,1,0:T(8,128)(2,1)S(1)}, u32[]{:S(2)}, u32[]{:S(2)}) %collective-permute-start.13) | collective-permute-done | bytes 165920 | tf_op jit(solution)/shard_map/ppermute | solution.py:46
  49.2 1.6 collective-permute-start.14
  50.7 1.9 %attend_1.1 = (bf16[512,192]{1,0:T(8,128)(2,1)S(1)}, f32[3,512,1]{2,1,0:T(8,128)S(1)}) custom-call(f32[512,512]{1,0:T(8,128)S(1)} %get-tuple-element.82.bias, bf16[9,512,64]{2,1,0:T(8,128)(2,1)S(1)} %get-tuple-element.95.query, bf16[3,512,64]{2,1,0:T(8,128)(2,1)S(1)} %get-tuple-element.96.keys, bf16[3,512,64]{2,1,0:T(8,128)(2,1)S(1)} %get-tuple-element.97.values), custom_call_target="tpu_custom_call" | custom-call | flops 30000000 | bytes 202752 | tf_op jit(solution)/shard_map/attend_1/pallas_call | solution.py:613
  52.7 1.9 %attend_0.1 = (bf16[512,192]{1,0:T(8,128)(2,1)S(1)}, f32[3,512,1]{2,1,0:T(8,128)S(1)}) custom-call(f32[512,512]{1,0:T(8,128)S(1)} %get-tuple-element.82.bias, bf16[9,512,64]{2,1,0:T(8,128)(2,1)S(1)} %get-tuple-element.95.query, bf16[3,512,64]{2,1,0:T(8,128)(2,1)S(1)} %get-tuple-element.96.keys, bf16[3,512,64]{2,1,0:T(8,128)(2,1)S(1)} %get-tuple-element.97.values), custom_call_target="tpu_custom_call" | custom-call | flops 30000000 | bytes 202752 | tf_op jit(solution)/shard_map/attend_0/pallas_call | solution.py:613
  54.6 4.4 %collective-permute-done.14 = bf16[2,3,48,576]{3,2,1,0:T(8,128)(2,1)S(1)} collective-permute-done((bf16[2,3,48,576]{3,2,1,0:T(8,128)(2,1)S(1)}, bf16[2,3,48,576]{3,2,1,0:T(8,128)(2,1)S(1)}, u32[]{:S(2)}, u32[]{:S(2)}) %collective-permute-start.14) | collective-permute-done | bytes 331808 | tf_op jit(solution)/shard_map/ppermute | solution.py:46
  59.1 2.7 %attend_2.1 = (bf16[512,192]{1,0:T(8,128)(2,1)S(1)}, f32[3,512,1]{2,1,0:T(8,128)S(1)}, f32[512,576]{1,0:T(8,128)S(1)}, bf16[512,576]{1,0:T(8,128)(2,1)S(1)}) custom-call(f32[512,512]{1,0:T(8,128)S(1)} %get-tuple-element.82.bias, bf16[9,512,64]{2,1,0:T(8,128)(2,1)S(1)} %get-tuple-element.95.query, bf16[3,512,64]{2,1,0:T(8,128)(2,1)S(1)} %get-tuple-element.96.keys, ...), custom_call_target="tpu_custom_call" | custom-call | flops 40000000 | bytes 1972224 | tf_op jit(solution)/shard_map/attend_2/pallas_call | solution.py:613
  61.8 1.1 collective-permute-done.15
  63.6 3.6 %collective-permute-done.17.down_other = bf16[2,2,3,48,576]{4,3,2,1,0:T(8,128)(2,1)S(1)} collective-permute-done((bf16[2,2,3,48,576]{4,3,2,1,0:T(8,128)(2,1)S(1)}, bf16[2,2,3,48,576]{4,3,2,1,0:T(8,128)(2,1)S(1)}, u32[]{:S(2)}, u32[]{:S(2)}) %collective-permute-start.17) | collective-permute-done | bytes 663584 | tf_op jit(solution)/shard_map/ppermute | solution.py:46
  67.2 13.6 %feed.1 = (bf16[576,512]{1,0:T(8,128)(2,1)}, f32[512,576]{1,0:T(8,128)S(1)}, f32[8,576]{1,0:T(8,128)S(1)}, bf16[2,2,4,144,384]{4,3,2,1,0:T(8,128)(2,1)S(1)}, bf1...) custom-call(f32[512,576]{1,0:T(8,128)S(1)} %get-tuple-element.107.hi, ...), custom_call_target="tpu_custom_call" | custom-call | flops 190000000 | bytes 7096320 | tf_op jit(solution)/shard_map/feed/pallas_call | solution.py:613
  81.3 2.9 %back_0.1 = (bf16[512,256]{1,0:T(8,128)(2,1)S(1)}, bf16[512,64]{1,0:T(8,128)(2,1)S(1)}, bf16[192,576]{1,0:T(8,128)(2,1)S(1)}) custom-call(f32[512,512]{1,0:T(8,128)S(1)} %get-tuple-element.82.bias, f32[512,128]{1,0:T(8,128)S(1)} %get-tuple-element.84.cosine, f32[512,128]{1,0:T(8,128)S(1)} %get-tuple-element.85.sine, ...), custom_call_target="tpu_custom_call" | custom-call | flops 50000000 | bytes 548864 | tf_op jit(solution)/shard_map/back_0/pallas_call | solution.py:613
  85.0 1.6 collective-permute-start.20
  86.8 1.6 collective-permute-start.25
  88.4 3.2 %back_1.1 = (bf16[512,256]{1,0:T(8,128)(2,1)S(1)}, bf16[512,64]{1,0:T(8,128)(2,1)S(1)}, bf16[192,576]{1,0:T(8,128)(2,1)S(1)}) custom-call(f32[512,512]{1,0:T(8,128)S(1)} %get-tuple-element.82.bias, f32[512,128]{1,0:T(8,128)S(1)} %get-tuple-element.84.cosine, f32[512,128]{1,0:T(8,128)S(1)} %get-tuple-element.85.sine, ...), custom_call_target="tpu_custom_call" | custom-call | flops 50000000 | bytes 548864 | tf_op jit(solution)/shard_map/back_1/pallas_call | solution.py:613
  91.6 2.9 %back_2.1 = (bf16[512,256]{1,0:T(8,128)(2,1)S(1)}, bf16[512,64]{1,0:T(8,128)(2,1)S(1)}, bf16[192,576]{1,0:T(8,128)(2,1)S(1)}) custom-call(f32[512,512]{1,0:T(8,128)S(1)} %get-tuple-element.82.bias, f32[512,128]{1,0:T(8,128)S(1)} %get-tuple-element.84.cosine, f32[512,128]{1,0:T(8,128)S(1)} %get-tuple-element.85.sine, ...), custom_call_target="tpu_custom_call" | custom-call | flops 50000000 | bytes 548864 | tf_op jit(solution)/shard_map/back_2/pallas_call | solution.py:613
  94.5 3.5 %back_last.1 = (bf16[576,512]{1,0:T(8,128)(2,1)}, bf16[2,2,4,80,384]{4,3,2,1,0:T(8,128)(2,1)S(1)}, bf16[2,2,4,80,384]{4,3,2,1,0:T(8,128)(2,1)S(1)}) custom-call(f32[512,576]{1,0:T(8,128)S(1)} %get-tuple-element.104.hidden_in, f32[8,576]{1,0:T(8,128)S(1)} %get-tuple-element.105.gains, bf16[640,1536]{1,0:T(8,128)(2,1)S(1)} %get-tuple-element.106.weights, ...), custom_call_target="tpu_custom_call" | custom-call | flops 60000000 | bytes 2555904 | tf_op jit(solution)/shard_map/back_last/pallas_call | solution.py:613
  98.1 1.8 %collective-permute-done.25 = bf16[2,4,48,576]{3,2,1,0:T(8,128)(2,1)S(1)} collective-permute-done((bf16[2,4,48,576]{3,2,1,0:T(8,128)(2,1)S(1)}, bf16[2,4,48,576]{3,2,1,0:T(8,128)(2,1)S(1)}, u32[]{:S(2)}, u32[]{:S(2)}) %collective-permute-start.25) | collective-permute-done | bytes 442400 | tf_op jit(solution)/shard_map/ppermute | solution.py:46
  99.9 6.9 %collective-permute-done.20 = bf16[2,4,144,384]{3,2,1,0:T(8,128)(2,1)S(1)} collective-permute-done((bf16[2,4,144,384]{3,2,1,0:T(8,128)(2,1)S(1)}, bf16[2,4,144,384]{3,2,1,0:T(8,128)(2,1)S(1)}, u32[]{:S(2)}, u32[]{:S(2)}) %collective-permute-start.20) | collective-permute-done | bytes 884768 | tf_op jit(solution)/shard_map/ppermute | solution.py:46
  106.9 1.6 collective-permute-start.26
  108.7 1.6 collective-permute-start.21
  110.3 5.1 %collective-permute-done.26 = bf16[4,48,576]{2,1,0:T(8,128)(2,1)S(1)} collective-permute-done((bf16[4,48,576]{2,1,0:T(8,128)(2,1)S(1)}, bf16[4,48,576]{2,1,0:T(8,128)(2,1)S(1)}, u32[]{:S(2)}, u32[]{:S(2)}) %collective-permute-start.26) | collective-permute-done | bytes 221216 | tf_op jit(solution)/shard_map/ppermute | solution.py:46
  115.4 2.3 %collective-permute-start.27 = (bf16[48,576]{1,0:T(8,128)(2,1)S(1)}, bf16[48,576]{1,0:T(8,128)(2,1)S(1)}, u32[]{:S(2)}, u32[]{:S(2)}) collective-permute-start(bf16[48,576]{1,0:T(8,128)(2,1)S(1)} %get-tuple-element.171), channel_id=1, source_target_pairs={{0,1},{1,2},{2,3},{3,0},{4,5},{5,6},{6,7},{7,4},{8,9},{9,10},{10,1... | collective-permute-start | bytes 165896 | tf_op jit(solution)/shard_map/ppermute | solution.py:54
  117.6 2.8 %collective-permute-start.29 = (bf16[48,576]{1,0:T(8,128)(2,1)S(1)}, bf16[48,576]{1,0:T(8,128)(2,1)S(1)}, u32[]{:S(2)}, u32[]{:S(2)}) collective-permute-start(bf16[48,576]{1,0:T(8,128)(2,1)S(1)} %get-tuple-element.172), channel_id=1, source_target_pairs={{0,3},{1,0},{2,1},{3,2},{4,7},{5,4},{6,5},{7,6},{8,11},{9,8},{10,9... | collective-permute-start | bytes 165896 | tf_op jit(solution)/shard_map/ppermute | solution.py:54
  121.1 2.3 %collective-permute-start.22 = (bf16[144,384]{1,0:T(8,128)(2,1)S(1)}, bf16[144,384]{1,0:T(8,128)(2,1)S(1)}, u32[]{:S(2)}, u32[]{:S(2)}) collective-permute-start(bf16[144,384]{1,0:T(8,128)(2,1)S(1)} %get-tuple-element.165), channel_id=1, source_target_pairs={{0,1},{1,2},{2,3},{3,0},{4,5},{5,6},{6,7},{7,4},{8,9},{9,10},{10,1... | collective-permute-start | bytes 331784 | tf_op jit(solution)/shard_map/ppermute | solution.py:54
  123.4 2.8 %collective-permute-start.24 = (bf16[144,384]{1,0:T(8,128)(2,1)S(1)}, bf16[144,384]{1,0:T(8,128)(2,1)S(1)}, u32[]{:S(2)}, u32[]{:S(2)}) collective-permute-start(bf16[144,384]{1,0:T(8,128)(2,1)S(1)} %get-tuple-element.166), channel_id=1, source_target_pairs={{0,3},{1,0},{2,1},{3,2},{4,7},{5,4},{6,5},{7,6},{8,11},{9,8},{10,9... | collective-permute-start | bytes 331784 | tf_op jit(solution)/shard_map/ppermute | solution.py:54
  127.0 1.5 collective-permute-start.34
  128.6 1.2 collective-permute-done.22
  129.8 0.9 collective-permute-done.24
  130.7 5.1 %collective-permute-done.23 = bf16[144,384]{1,0:T(8,128)(2,1)S(1)} collective-permute-done((bf16[144,384]{1,0:T(8,128)(2,1)S(1)}, bf16[144,384]{1,0:T(8,128)(2,1)S(1)}, u32[]{:S(2)}, u32[]{:S(2)}) %collective-permute-start.23) | collective-permute-done | bytes 110624 | tf_op jit(solution)/shard_map/ppermute | solution.py:54
  136.0 1.6 collective-permute-start.30
  137.6 1.9 %collective-permute-done.34 = bf16[2,4,80,384]{3,2,1,0:T(8,128)(2,1)S(1)} collective-permute-done((bf16[2,4,80,384]{3,2,1,0:T(8,128)(2,1)S(1)}, bf16[2,4,80,384]{3,2,1,0:T(8,128)(2,1)S(1)}, u32[]{:S(2)}, u32[]{:S(2)}) %collective-permute-start.34) | collective-permute-done | bytes 491552 | tf_op jit(solution)/shard_map/ppermute | solution.py:46
  139.7 3.2 %collective-permute-done.30 = bf16[240,384]{1,0:T(8,128)(2,1)S(1)} collective-permute-done((bf16[240,384]{1,0:T(8,128)(2,1)S(1)}, bf16[240,384]{1,0:T(8,128)(2,1)S(1)}, u32[]{:S(2)}, u32[]{:S(2)}) %collective-permute-start.30) | collective-permute-done | bytes 184352 | tf_op jit(solution)/shard_map/ppermute | solution.py:46
  143.0 0.6 collective-permute-start.31
  143.7 2.8 %collective-permute-done.35 = bf16[4,80,384]{2,1,0:T(8,128)(2,1)S(1)} collective-permute-done((bf16[4,80,384]{2,1,0:T(8,128)(2,1)S(1)}, bf16[4,80,384]{2,1,0:T(8,128)(2,1)S(1)}, u32[]{:S(2)}, u32[]{:S(2)}) %collective-permute-start.35) | collective-permute-done | bytes 245792 | tf_op jit(solution)/shard_map/ppermute | solution.py:46
  146.5 5.2 %collective-permute-start.36 = (bf16[80,384]{1,0:T(8,128)(2,1)S(1)}, bf16[80,384]{1,0:T(8,128)(2,1)S(1)}, u32[]{:S(2)}, u32[]{:S(2)}) collective-permute-start(bf16[80,384]{1,0:T(8,128)(2,1)S(1)} %get-tuple-element.168), channel_id=1, source_target_pairs={{0,1},{1,2},{2,3},{3,0},{4,5},{5,6},{6,7},{7,4},{8,9},{9,10},{10,1... | collective-permute-start | bytes 184328 | tf_op jit(solution)/shard_map/ppermute | solution.py:54
  151.8 2.8 %collective-permute-start.37 = (bf16[80,384]{1,0:T(8,128)(2,1)S(1)}, bf16[80,384]{1,0:T(8,128)(2,1)S(1)}, u32[]{:S(2)}, u32[]{:S(2)}) collective-permute-start(bf16[80,384]{1,0:T(8,128)(2,1)S(1)} %get-tuple-element.170), channel_id=1, source_target_pairs={{0,2},{1,3},{2,0},{3,1},{4,6},{5,7},{6,4},{7,5},{8,10},{9,11},{10,... | collective-permute-start | bytes 184328 | tf_op jit(solution)/shard_map/ppermute | solution.py:54
  154.8 1.2 collective-permute-done.38
  156.0 1.4 collective-permute-done.37
  158.1 3.7 %collective-permute-done.39 = bf16[80,384]{1,0:T(8,128)(2,1)S(1)} collective-permute-done((bf16[80,384]{1,0:T(8,128)(2,1)S(1)}, bf16[80,384]{1,0:T(8,128)(2,1)S(1)}, u32[]{:S(2)}, u32[]{:S(2)}) %collective-permute-start.39) | collective-permute-done | bytes 61472 | tf_op jit(solution)/shard_map/ppermute | solution.py:46
  161.8 1.6 collective-permute-start.40
  163.4 3.4 %collective-permute-done.40 = bf16[2,80,384]{2,1,0:T(8,128)(2,1)S(1)} collective-permute-done((bf16[2,80,384]{2,1,0:T(8,128)(2,1)S(1)}, bf16[2,80,384]{2,1,0:T(8,128)(2,1)S(1)}, u32[]{:S(2)}, u32[]{:S(2)}) %collective-permute-start.40) | collective-permute-done | bytes 122912 | tf_op jit(solution)/shard_map/ppermute | solution.py:46
  166.9 1.5 collective-permute-done.41.rest_other
  168.4 2.1 %finish.1 = (f32[144,576]{1,0:T(8,128)}, f32[144,192]{1,0:T(8,128)}, f32[144,192]{1,0:T(8,128)}, f32[144,576]{1,0:T(8,128)}, f32[1,144]{1,0:T(1,128)}, /*index=5...) custom-call(bf16[2,2,240,384]{3,2,1,0:T(8,128)(2,1)S(1)} %pad_maximum_fusion.3.pair_pieces, ...), custom_call_target="tpu_custom_call" | custom-call | flops 50000000 | bytes 3540096 | tf_op jit(solution)/shard_map/finish/pallas_call | solution.py:613
  (83 shorter events, 8.4 us)
Async XLA Ops:
  0.6 11.7 %copy-start.6 = (f32[520,128]{1,0:T(8,128)S(1)}, f32[520,128]{1,0:T(8,128)}, u32[]{:S(2)}) copy-start(f32[520,128]{1,0:T(8,128)} %constant.8.clone.table_sin) | copy-start | bytes 798724
  0.7 11.7 %copy-start.7 = (f32[520,128]{1,0:T(8,128)S(1)}, f32[520,128]{1,0:T(8,128)}, u32[]{:S(2)}) copy-start(f32[520,128]{1,0:T(8,128)} %constant.7.clone.table_cos) | copy-start | bytes 798724
  0.7 11.7 %copy-start.8 = (s32[1,4]{1,0:T(1,128)S(1)}, s32[1,4]{1,0:T(1,128)}, u32[]{:S(2)}) copy-start(s32[1,4]{1,0:T(1,128)} %lengths.3) | copy-start | bytes 52
  0.7 11.7 %copy-start.3 = (bf16[512,576]{0,1:T(8,128)(2,1)S(1)}, bf16[512,576]{0,1:T(8,128)(2,1)}, u32[]{:S(2)}) copy-start(bf16[512,576]{0,1:T(8,128)(2,1)} %param.25) | copy-start | bytes 1769476
  0.7 11.7 %copy-start.2 = (bf16[512,576]{0,1:T(8,128)(2,1)S(1)}, bf16[512,576]{0,1:T(8,128)(2,1)}, u32[]{:S(2)}) copy-start(bf16[512,576]{0,1:T(8,128)(2,1)} %param.14) | copy-start | bytes 1769476
  5.4 12.5 %copy-start.9 = (bf16[48,576]{1,0:T(8,128)(2,1)S(1)}, bf16[48,576]{1,0:T(8,128)(2,1)}, u32[]{:S(2)}) copy-start(bf16[48,576]{1,0:T(8,128)(2,1)} %get-tuple-element.92) | copy-start | bytes 165892
  5.4 9.6 %collective-permute-start.2 = (bf16[80,384]{1,0:T(8,128)(2,1)}, bf16[80,384]{1,0:T(8,128)(2,1)S(1)}, u32[]{:S(2)}, u32[]{:S(2)}) collective-permute-start(bf16[80,384]{1,0:T(8,128)(2,1)} %get-tuple-element.87), channel_id=1, source_target_pairs={{3,0},{0,1},{1,2},{2,3},{7,4},{4,5},{5,6},{6,7},{11,8},{8,9},{9,10... | collective-permute-start | bytes 184328 | tf_op jit(solution)/shard_map/ppermute | solution.py:50
  8.4 9.4 %collective-permute-start.1 = (bf16[80,384]{1,0:T(8,128)(2,1)}, bf16[80,384]{1,0:T(8,128)(2,1)S(1)}, u32[]{:S(2)}, u32[]{:S(2)}) collective-permute-start(bf16[80,384]{1,0:T(8,128)(2,1)} %get-tuple-element.87), channel_id=1, source_target_pairs={{2,0},{3,1},{0,2},{1,3},{6,4},{7,5},{4,6},{5,7},{10,8},{11,9},{8,1... | collective-permute-start | bytes 184328 | tf_op jit(solution)/shard_map/ppermute | solution.py:50
  11.0 6.8 %collective-permute-start = (bf16[80,384]{1,0:T(8,128)(2,1)}, bf16[80,384]{1,0:T(8,128)(2,1)S(1)}, u32[]{:S(2)}, u32[]{:S(2)}) collective-permute-start(bf16[80,384]{1,0:T(8,128)(2,1)} %get-tuple-element.87), channel_id=1, source_target_pairs={{1,0},{2,1},{3,2},{0,3},{5,4},{6,5},{7,6},{4,7},{9,8},{10,9},{11,1... | collective-permute-start | bytes 184328 | tf_op jit(solution)/shard_map/ppermute | solution.py:50
  13.9 8.1 %collective-permute-start.6 = (bf16[144,384]{1,0:T(8,128)(2,1)}, bf16[144,384]{1,0:T(8,128)(2,1)S(1)}, u32[]{:S(2)}, u32[]{:S(2)}) collective-permute-start(bf16[144,384]{1,0:T(8,128)(2,1)} %get-tuple-element.90), channel_id=1, source_target_pairs={{3,0},{0,1},{1,2},{2,3},{7,4},{4,5},{5,6},{6,7},{11,8},{8,9},{9,10... | collective-permute-start | bytes 331784 | tf_op jit(solution)/shard_map/ppermute | solution.py:50
  14.7 11.6 %collective-permute-start.5 = (bf16[144,384]{1,0:T(8,128)(2,1)}, bf16[144,384]{1,0:T(8,128)(2,1)S(1)}, u32[]{:S(2)}, u32[]{:S(2)}) collective-permute-start(bf16[144,384]{1,0:T(8,128)(2,1)} %get-tuple-element.90), channel_id=1, source_target_pairs={{2,0},{3,1},{0,2},{1,3},{6,4},{7,5},{4,6},{5,7},{10,8},{11,9},{8,1... | collective-permute-start | bytes 331784 | tf_op jit(solution)/shard_map/ppermute | solution.py:50
  15.0 12.7 %collective-permute-start.4 = (bf16[144,384]{1,0:T(8,128)(2,1)}, bf16[144,384]{1,0:T(8,128)(2,1)S(1)}, u32[]{:S(2)}, u32[]{:S(2)}) collective-permute-start(bf16[144,384]{1,0:T(8,128)(2,1)} %get-tuple-element.90), channel_id=1, source_target_pairs={{1,0},{2,1},{3,2},{0,3},{5,4},{6,5},{7,6},{4,7},{9,8},{10,9},{11,1... | collective-permute-start | bytes 331784 | tf_op jit(solution)/shard_map/ppermute | solution.py:50
  17.9 10.5 %collective-permute-start.9 = (bf16[48,576]{1,0:T(8,128)(2,1)S(1)}, bf16[48,576]{1,0:T(8,128)(2,1)S(1)}, u32[]{:S(2)}, u32[]{:S(2)}) collective-permute-start(bf16[48,576]{1,0:T(8,128)(2,1)S(1)} %copy-done.9), channel_id=1, source_target_pairs={{3,0},{0,1},{1,2},{2,3},{7,4},{4,5},{5,6},{6,7},{11,8},{8,9},{9,10... | collective-permute-start | bytes 165896 | tf_op jit(solution)/shard_map/ppermute | solution.py:50
  18.5 12.7 %collective-permute-start.8 = (bf16[48,576]{1,0:T(8,128)(2,1)S(1)}, bf16[48,576]{1,0:T(8,128)(2,1)S(1)}, u32[]{:S(2)}, u32[]{:S(2)}) collective-permute-start(bf16[48,576]{1,0:T(8,128)(2,1)S(1)} %copy-done.9), channel_id=1, source_target_pairs={{2,0},{3,1},{0,2},{1,3},{6,4},{7,5},{4,6},{5,7},{10,8},{11,9},{8,1... | collective-permute-start | bytes 165896 | tf_op jit(solution)/shard_map/ppermute | solution.py:50
  22.1 9.2 %collective-permute-start.7 = (bf16[48,576]{1,0:T(8,128)(2,1)S(1)}, bf16[48,576]{1,0:T(8,128)(2,1)S(1)}, u32[]{:S(2)}, u32[]{:S(2)}) collective-permute-start(bf16[48,576]{1,0:T(8,128)(2,1)S(1)} %copy-done.9), channel_id=1, source_target_pairs={{1,0},{2,1},{3,2},{0,3},{5,4},{6,5},{7,6},{4,7},{9,8},{10,9},{11,1... | collective-permute-start | bytes 165896 | tf_op jit(solution)/shard_map/ppermute | solution.py:50
  26.2 7.6 %collective-permute-start.3 = (bf16[3,80,384]{2,1,0:T(8,128)(2,1)S(1)}, bf16[3,80,384]{2,1,0:T(8,128)(2,1)S(1)}, u32[]{:S(2)}, u32[]{:S(2)}) collective-permute-start(bf16[3,80,384]{2,1,0:T(8,128)(2,1)S(1)} %pad_maximum_fusion.10), channel_id=1, source_target_pairs={{0,16},{4,20},{8,24},{12,28},{16,0},{20,4},{24,8},{28,12},{1,17},{... | collective-permute-start | bytes 552968 | tf_op jit(solution)/shard_map/ppermute | solution.py:46
  27.8 10.3 %collective-permute-start.11 = (bf16[3,144,384]{2,1,0:T(8,128)(2,1)S(1)}, bf16[3,144,384]{2,1,0:T(8,128)(2,1)S(1)}, u32[]{:S(2)}, u32[]{:S(2)}) collective-permute-start(bf16[3,144,384]{2,1,0:T(8,128)(2,1)S(1)} %get-tuple-element.177), channel_id=1, source_target_pairs={{0,16},{4,20},{8,24},{12,28},{16,0},{20,4},{24,8},{28,12},{1,17},{... | collective-permute-start | bytes 995336 | tf_op jit(solution)/shard_map/ppermute | solution.py:46
  33.8 10.0 %copy-start.4 = (bf16[160,1536]{1,0:T(8,128)(2,1)S(1)}, bf16[160,1536]{1,0:T(8,128)(2,1)}, u32[]{:S(2)}) copy-start(bf16[160,1536]{1,0:T(8,128)(2,1)} %get-tuple-element.86.own) | copy-start | bytes 1474564
  33.9 7.6 %collective-permute-start.10 = (bf16[2,3,80,384]{3,2,1,0:T(8,128)(2,1)S(1)}, bf16[2,3,80,384]{3,2,1,0:T(8,128)(2,1)S(1)}, u32[]{:S(2)}, u32[]{:S(2)}) collective-permute-start(bf16[2,3,80,384]{3,2,1,0:T(8,128)(2,1)S(1)} %pad_maximum_fusion.5), channel_id=1, source_target_pairs={{0,8},{4,12},{8,0},{12,4},{16,24},{20,28},{24,16},{28,20},{1,9},{5... | collective-permute-start | bytes 1105928 | tf_op jit(solution)/shard_map/ppermute | solution.py:46
  41.5 2.3 %collective-permute-start.12 = (bf16[2,2,3,80,384]{4,3,2,1,0:T(8,128)(2,1)S(1)}, bf16[2,2,3,80,384]{4,3,2,1,0:T(8,128)(2,1)S(1)}, u32[]{:S(2)}, u32[]{:S(2)}) collective-permute-start(bf16[2,2,3,80,384]{4,3,2,1,0:T(8,128)(2,1)S(1)} %pad_maximum_fusion.1.pieces), channel_id=1, source_target_pairs={{0,4},{4,0},{8,12},{12,8},{16,20},{20,16},{24,28},{28,24},{1,5},{5... | collective-permute-start | bytes 2211848 | tf_op jit(solution)/shard_map/ppermute | solution.py:46
  41.6 7.5 %collective-permute-start.13 = (bf16[3,48,576]{2,1,0:T(8,128)(2,1)S(1)}, bf16[3,48,576]{2,1,0:T(8,128)(2,1)S(1)}, u32[]{:S(2)}, u32[]{:S(2)}) collective-permute-start(bf16[3,48,576]{2,1,0:T(8,128)(2,1)S(1)} %pad_maximum_fusion.11), channel_id=1, source_target_pairs={{0,8},{4,12},{8,0},{12,4},{16,24},{20,28},{24,16},{28,20},{1,9},{5... | collective-permute-start | bytes 497672 | tf_op jit(solution)/shard_map/ppermute | solution.py:46
  43.2 19.7 %collective-permute-start.15 = (bf16[2,3,144,384]{3,2,1,0:T(8,128)(2,1)S(1)}, bf16[2,3,144,384]{3,2,1,0:T(8,128)(2,1)S(1)}, u32[]{:S(2)}, u32[]{:S(2)}) collective-permute-start(bf16[2,3,144,384]{3,2,1,0:T(8,128)(2,1)S(1)} %pad_maximum_fusion.4), channel_id=1, source_target_pairs={{0,8},{4,12},{8,0},{12,4},{16,24},{20,28},{24,16},{28,20},{1,9},{5... | collective-permute-start | bytes 1990664 | tf_op jit(solution)/shard_map/ppermute | solution.py:46
  49.2 9.8 %collective-permute-start.14 = (bf16[2,3,48,576]{3,2,1,0:T(8,128)(2,1)S(1)}, bf16[2,3,48,576]{3,2,1,0:T(8,128)(2,1)S(1)}, u32[]{:S(2)}, u32[]{:S(2)}) collective-permute-start(bf16[2,3,48,576]{3,2,1,0:T(8,128)(2,1)S(1)} %pad_maximum_fusion.6), channel_id=1, source_target_pairs={{0,16},{4,20},{8,24},{12,28},{16,0},{20,4},{24,8},{28,12},{1,17},{... | collective-permute-start | bytes 995336 | tf_op jit(solution)/shard_map/ppermute | solution.py:46
  61.7 5.5 %copy-start = (bf16[144,1536]{1,0:T(8,128)(2,1)S(1)}, bf16[144,1536]{1,0:T(8,128)(2,1)}, u32[]{:S(2)}) copy-start(bf16[144,1536]{1,0:T(8,128)(2,1)} %own_gate.1) | copy-start | bytes 1327108
  61.8 5.5 %copy-start.1 = (bf16[144,1536]{1,0:T(8,128)(2,1)S(1)}, bf16[144,1536]{1,0:T(8,128)(2,1)}, u32[]{:S(2)}) copy-start(bf16[144,1536]{1,0:T(8,128)(2,1)} %own_up.1) | copy-start | bytes 1327108
  61.8 5.5 %copy-start.5 = (bf16[384,576]{1,0:T(8,128)(2,1)S(1)}, bf16[384,576]{1,0:T(8,128)(2,1)}, u32[]{:S(2)}) copy-start(bf16[384,576]{1,0:T(8,128)(2,1)} %get-tuple-element.110.own_down) | copy-start | bytes 1327108
  63.0 4.2 %collective-permute-start.16 = (bf16[2,2,3,144,384]{4,3,2,1,0:T(8,128)(2,1)S(1)}, bf16[2,2,3,144,384]{4,3,2,1,0:T(8,128)(2,1)S(1)}, u32[]{:S(2)}, u32[]{:S(2)}) collective-permute-start(bf16[2,2,3,144,384]{4,3,2,1,0:T(8,128)(2,1)S(1)} %pad_maximum_fusion.pair_pieces), channel_id=1, source_target_pairs={{0,4},{4,0},{8,12},{12,8},{16,20},{20,16},{24,28},{28,24},{1,5},{5... | collective-permute-start | bytes 3981320 | tf_op jit(solution)/shard_map/ppermute | solution.py:46
  63.1 4.1 %collective-permute-start.17 = (bf16[2,2,3,48,576]{4,3,2,1,0:T(8,128)(2,1)S(1)}, bf16[2,2,3,48,576]{4,3,2,1,0:T(8,128)(2,1)S(1)}, u32[]{:S(2)}, u32[]{:S(2)}) collective-permute-start(bf16[2,2,3,48,576]{4,3,2,1,0:T(8,128)(2,1)S(1)} %pad_maximum_fusion.2.down_pieces), channel_id=1, source_target_pairs={{0,4},{4,0},{8,12},{12,8},{16,20},{20,16},{24,28},{28,24},{1,5},{5... | collective-permute-start | bytes 1990664 | tf_op jit(solution)/shard_map/ppermute | solution.py:46
  80.8 3.7 %collective-permute-start.18 = (bf16[2,2,4,144,384]{4,3,2,1,0:T(8,128)(2,1)S(1)}, bf16[2,2,4,144,384]{4,3,2,1,0:T(8,128)(2,1)S(1)}, u32[]{:S(2)}, u32[]{:S(2)}) collective-permute-start(bf16[2,2,4,144,384]{4,3,2,1,0:T(8,128)(2,1)S(1)} %get-tuple-element.114), channel_id=1, source_target_pairs={{0,4},{4,0},{8,12},{12,8},{16,20},{20,16},{24,28},{28,24},{1,5},{5... | collective-permute-start | bytes 5308424 | tf_op jit(solution)/shard_map/ppermute | solution.py:46
  81.0 5.6 %collective-permute-start.19 = (bf16[2,2,4,48,576]{4,3,2,1,0:T(8,128)(2,1)S(1)}, bf16[2,2,4,48,576]{4,3,2,1,0:T(8,128)(2,1)S(1)}, u32[]{:S(2)}, u32[]{:S(2)}) collective-permute-start(bf16[2,2,4,48,576]{4,3,2,1,0:T(8,128)(2,1)S(1)} %get-tuple-element.115), channel_id=1, source_target_pairs={{0,4},{4,0},{8,12},{12,8},{16,20},{20,16},{24,28},{28,24},{1,5},{5... | collective-permute-start | bytes 2654216 | tf_op jit(solution)/shard_map/ppermute | solution.py:46
  85.0 21.8 %collective-permute-start.20 = (bf16[2,4,144,384]{3,2,1,0:T(8,128)(2,1)S(1)}, bf16[2,4,144,384]{3,2,1,0:T(8,128)(2,1)S(1)}, u32[]{:S(2)}, u32[]{:S(2)}) collective-permute-start(bf16[2,4,144,384]{3,2,1,0:T(8,128)(2,1)S(1)} %get-tuple-element.154), channel_id=1, source_target_pairs={{0,8},{4,12},{8,0},{12,4},{16,24},{20,28},{24,16},{28,20},{1,9},{5... | collective-permute-start | bytes 2654216 | tf_op jit(solution)/shard_map/ppermute | solution.py:46
  86.8 13.0 %collective-permute-start.25 = (bf16[2,4,48,576]{3,2,1,0:T(8,128)(2,1)S(1)}, bf16[2,4,48,576]{3,2,1,0:T(8,128)(2,1)S(1)}, u32[]{:S(2)}, u32[]{:S(2)}) collective-permute-start(bf16[2,4,48,576]{3,2,1,0:T(8,128)(2,1)S(1)} %get-tuple-element.157), channel_id=1, source_target_pairs={{0,16},{4,20},{8,24},{12,28},{16,0},{20,4},{24,8},{28,12},{1,17},{... | collective-permute-start | bytes 1327112 | tf_op jit(solution)/shard_map/ppermute | solution.py:46
  106.7 16.7 %collective-permute-start.33 = (bf16[2,2,4,80,384]{4,3,2,1,0:T(8,128)(2,1)S(1)}, bf16[2,2,4,80,384]{4,3,2,1,0:T(8,128)(2,1)S(1)}, u32[]{:S(2)}, u32[]{:S(2)}) collective-permute-start(bf16[2,2,4,80,384]{4,3,2,1,0:T(8,128)(2,1)S(1)} %get-tuple-element.139), channel_id=1, source_target_pairs={{0,4},{4,0},{8,12},{12,8},{16,20},{20,16},{24,28},{28,24},{1,5},{5... | collective-permute-start | bytes 2949128 | tf_op jit(solution)/shard_map/ppermute | solution.py:46
  106.9 8.4 %collective-permute-start.26 = (bf16[4,48,576]{2,1,0:T(8,128)(2,1)S(1)}, bf16[4,48,576]{2,1,0:T(8,128)(2,1)S(1)}, u32[]{:S(2)}, u32[]{:S(2)}) collective-permute-start(bf16[4,48,576]{2,1,0:T(8,128)(2,1)S(1)} %get-tuple-element.164), channel_id=1, source_target_pairs={{0,8},{4,12},{8,0},{12,4},{16,24},{20,28},{24,16},{28,20},{1,9},{5... | collective-permute-start | bytes 663560 | tf_op jit(solution)/shard_map/ppermute | solution.py:46
  108.7 12.4 %collective-permute-start.21 = (bf16[4,144,384]{2,1,0:T(8,128)(2,1)S(1)}, bf16[4,144,384]{2,1,0:T(8,128)(2,1)S(1)}, u32[]{:S(2)}, u32[]{:S(2)}) collective-permute-start(bf16[4,144,384]{2,1,0:T(8,128)(2,1)S(1)} %get-tuple-element.160), channel_id=1, source_target_pairs={{0,16},{4,20},{8,24},{12,28},{16,0},{20,4},{24,8},{28,12},{1,17},{... | collective-permute-start | bytes 1327112 | tf_op jit(solution)/shard_map/ppermute | solution.py:46
  115.4 11.1 %collective-permute-start.27 = (bf16[48,576]{1,0:T(8,128)(2,1)S(1)}, bf16[48,576]{1,0:T(8,128)(2,1)S(1)}, u32[]{:S(2)}, u32[]{:S(2)}) collective-permute-start(bf16[48,576]{1,0:T(8,128)(2,1)S(1)} %get-tuple-element.171), channel_id=1, source_target_pairs={{0,1},{1,2},{2,3},{3,0},{4,5},{5,6},{6,7},{7,4},{8,9},{9,10},{10,1... | collective-permute-start | bytes 165896 | tf_op jit(solution)/shard_map/ppermute | solution.py:54
  117.6 9.4 %collective-permute-start.29 = (bf16[48,576]{1,0:T(8,128)(2,1)S(1)}, bf16[48,576]{1,0:T(8,128)(2,1)S(1)}, u32[]{:S(2)}, u32[]{:S(2)}) collective-permute-start(bf16[48,576]{1,0:T(8,128)(2,1)S(1)} %get-tuple-element.172), channel_id=1, source_target_pairs={{0,3},{1,0},{2,1},{3,2},{4,7},{5,4},{6,5},{7,6},{8,11},{9,8},{10,9... | collective-permute-start | bytes 165896 | tf_op jit(solution)/shard_map/ppermute | solution.py:54
  120.4 8.1 %collective-permute-start.28 = (bf16[48,576]{1,0:T(8,128)(2,1)S(1)}, bf16[48,576]{1,0:T(8,128)(2,1)S(1)}, u32[]{:S(2)}, u32[]{:S(2)}) collective-permute-start(bf16[48,576]{1,0:T(8,128)(2,1)S(1)} %get-tuple-element.173), channel_id=1, source_target_pairs={{0,2},{1,3},{2,0},{3,1},{4,6},{5,7},{6,4},{7,5},{8,10},{9,11},{10,... | collective-permute-start | bytes 165896 | tf_op jit(solution)/shard_map/ppermute | solution.py:54
  121.1 8.7 %collective-permute-start.22 = (bf16[144,384]{1,0:T(8,128)(2,1)S(1)}, bf16[144,384]{1,0:T(8,128)(2,1)S(1)}, u32[]{:S(2)}, u32[]{:S(2)}) collective-permute-start(bf16[144,384]{1,0:T(8,128)(2,1)S(1)} %get-tuple-element.165), channel_id=1, source_target_pairs={{0,1},{1,2},{2,3},{3,0},{4,5},{5,6},{6,7},{7,4},{8,9},{9,10},{10,1... | collective-permute-start | bytes 331784 | tf_op jit(solution)/shard_map/ppermute | solution.py:54
  123.4 7.3 %collective-permute-start.24 = (bf16[144,384]{1,0:T(8,128)(2,1)S(1)}, bf16[144,384]{1,0:T(8,128)(2,1)S(1)}, u32[]{:S(2)}, u32[]{:S(2)}) collective-permute-start(bf16[144,384]{1,0:T(8,128)(2,1)S(1)} %get-tuple-element.166), channel_id=1, source_target_pairs={{0,3},{1,0},{2,1},{3,2},{4,7},{5,4},{6,5},{7,6},{8,11},{9,8},{10,9... | collective-permute-start | bytes 331784 | tf_op jit(solution)/shard_map/ppermute | solution.py:54
  126.5 9.4 %collective-permute-start.23 = (bf16[144,384]{1,0:T(8,128)(2,1)S(1)}, bf16[144,384]{1,0:T(8,128)(2,1)S(1)}, u32[]{:S(2)}, u32[]{:S(2)}) collective-permute-start(bf16[144,384]{1,0:T(8,128)(2,1)S(1)} %get-tuple-element.167), channel_id=1, source_target_pairs={{0,2},{1,3},{2,0},{3,1},{4,6},{5,7},{6,4},{7,5},{8,10},{9,11},{10,... | collective-permute-start | bytes 331784 | tf_op jit(solution)/shard_map/ppermute | solution.py:54
  127.0 12.5 %collective-permute-start.34 = (bf16[2,4,80,384]{3,2,1,0:T(8,128)(2,1)S(1)}, bf16[2,4,80,384]{3,2,1,0:T(8,128)(2,1)S(1)}, u32[]{:S(2)}, u32[]{:S(2)}) collective-permute-start(bf16[2,4,80,384]{3,2,1,0:T(8,128)(2,1)S(1)} %get-tuple-element.155), channel_id=1, source_target_pairs={{0,16},{4,20},{8,24},{12,28},{16,0},{20,4},{24,8},{28,12},{1,17},{... | collective-permute-start | bytes 1474568 | tf_op jit(solution)/shard_map/ppermute | solution.py:46
  136.0 7.0 %collective-permute-start.30 = (bf16[240,384]{1,0:T(8,128)(2,1)S(1)}, bf16[240,384]{1,0:T(8,128)(2,1)S(1)}, u32[]{:S(2)}, u32[]{:S(2)}) collective-permute-start(bf16[240,384]{1,0:T(8,128)(2,1)S(1)} %get-tuple-element.179), channel_id=1, source_target_pairs={{0,16},{4,20},{8,24},{12,28},{16,0},{20,4},{24,8},{28,12},{1,17},{... | collective-permute-start | bytes 552968 | tf_op jit(solution)/shard_map/ppermute | solution.py:46
  139.6 6.9 %collective-permute-start.35 = (bf16[4,80,384]{2,1,0:T(8,128)(2,1)S(1)}, bf16[4,80,384]{2,1,0:T(8,128)(2,1)S(1)}, u32[]{:S(2)}, u32[]{:S(2)}) collective-permute-start(bf16[4,80,384]{2,1,0:T(8,128)(2,1)S(1)} %get-tuple-element.161), channel_id=1, source_target_pairs={{0,8},{4,12},{8,0},{12,4},{16,24},{20,28},{24,16},{28,20},{1,9},{5... | collective-permute-start | bytes 737288 | tf_op jit(solution)/shard_map/ppermute | solution.py:46
  143.0 11.6 %collective-permute-start.31 = (bf16[2,240,384]{2,1,0:T(8,128)(2,1)S(1)}, bf16[2,240,384]{2,1,0:T(8,128)(2,1)S(1)}, u32[]{:S(2)}, u32[]{:S(2)}) collective-permute-start(bf16[2,240,384]{2,1,0:T(8,128)(2,1)S(1)} %get-tuple-element.175), channel_id=1, source_target_pairs={{0,8},{4,12},{8,0},{12,4},{16,24},{20,28},{24,16},{28,20},{1,9},{5... | collective-permute-start | bytes 1105928 | tf_op jit(solution)/shard_map/ppermute | solution.py:46
  146.5 8.2 %collective-permute-start.36 = (bf16[80,384]{1,0:T(8,128)(2,1)S(1)}, bf16[80,384]{1,0:T(8,128)(2,1)S(1)}, u32[]{:S(2)}, u32[]{:S(2)}) collective-permute-start(bf16[80,384]{1,0:T(8,128)(2,1)S(1)} %get-tuple-element.168), channel_id=1, source_target_pairs={{0,1},{1,2},{2,3},{3,0},{4,5},{5,6},{6,7},{7,4},{8,9},{9,10},{10,1... | collective-permute-start | bytes 184328 | tf_op jit(solution)/shard_map/ppermute | solution.py:54
  151.8 4.2 %collective-permute-start.38 = (bf16[80,384]{1,0:T(8,128)(2,1)S(1)}, bf16[80,384]{1,0:T(8,128)(2,1)S(1)}, u32[]{:S(2)}, u32[]{:S(2)}) collective-permute-start(bf16[80,384]{1,0:T(8,128)(2,1)S(1)} %get-tuple-element.169), channel_id=1, source_target_pairs={{0,3},{1,0},{2,1},{3,2},{4,7},{5,4},{6,5},{7,6},{8,11},{9,8},{10,9... | collective-permute-start | bytes 184328 | tf_op jit(solution)/shard_map/ppermute | solution.py:54
  151.8 5.7 %collective-permute-start.37 = (bf16[80,384]{1,0:T(8,128)(2,1)S(1)}, bf16[80,384]{1,0:T(8,128)(2,1)S(1)}, u32[]{:S(2)}, u32[]{:S(2)}) collective-permute-start(bf16[80,384]{1,0:T(8,128)(2,1)S(1)} %get-tuple-element.170), channel_id=1, source_target_pairs={{0,2},{1,3},{2,0},{3,1},{4,6},{5,7},{6,4},{7,5},{8,10},{9,11},{10,... | collective-permute-start | bytes 184328 | tf_op jit(solution)/shard_map/ppermute | solution.py:54
  154.7 12.2 %collective-permute-start.32 = (bf16[2,2,240,384]{3,2,1,0:T(8,128)(2,1)S(1)}, bf16[2,2,240,384]{3,2,1,0:T(8,128)(2,1)S(1)}, u32[]{:S(2)}, u32[]{:S(2)}) collective-permute-start(bf16[2,2,240,384]{3,2,1,0:T(8,128)(2,1)S(1)} %pad_maximum_fusion.3.pair_pieces), channel_id=1, source_target_pairs={{0,4},{4,0},{8,12},{12,8},{16,20},{20,16},{24,28},{28,24},{1,5},{5... | collective-permute-start | bytes 2211848 | tf_op jit(solution)/shard_map/ppermute | solution.py:46
  157.5 4.3 %collective-permute-start.39 = (bf16[80,384]{1,0:T(8,128)(2,1)S(1)}, bf16[80,384]{1,0:T(8,128)(2,1)S(1)}, u32[]{:S(2)}, u32[]{:S(2)}) collective-permute-start(bf16[80,384]{1,0:T(8,128)(2,1)S(1)} %fusion.29), channel_id=1, source_target_pairs={{0,8},{4,12},{8,0},{12,4},{16,24},{20,28},{24,16},{28,20},{1,9},{5... | collective-permute-start | bytes 184328 | tf_op jit(solution)/shard_map/ppermute | solution.py:46
  161.8 4.9 %collective-permute-start.40 = (bf16[2,80,384]{2,1,0:T(8,128)(2,1)S(1)}, bf16[2,80,384]{2,1,0:T(8,128)(2,1)S(1)}, u32[]{:S(2)}, u32[]{:S(2)}) collective-permute-start(bf16[2,80,384]{2,1,0:T(8,128)(2,1)S(1)} %get-tuple-element.181), channel_id=1, source_target_pairs={{0,16},{4,20},{8,24},{12,28},{16,0},{20,4},{24,8},{28,12},{1,17},{... | collective-permute-start | bytes 368648 | tf_op jit(solution)/shard_map/ppermute | solution.py:46
  166.8 1.6 collective-permute-start.41
